TPU v7x, 32 devices: a whole 2x2x4 slice. The times are simulated.
32 devices in a mesh: patch: 4 (over x, core), line: 2 (over y), layer: 4 (over z).
Axes of the slice: x: 2, y: 2, z: 4, core: 2. Of those that a mesh axis runs over, the one named last changes fastest.
Arguments:
- elastic: float32 [4, 5, 1024, 2048], P('patch', None, 'line', 'layer'), may hold values from -6 to 6
- acoustic: float32 [4, 3, 1024, 2048], P('patch', None, 'line', 'layer'), may hold values from -6 to 6
- el_media: float32 [4, 3, 1024, 2048], P('patch', None, 'line', 'layer'), may hold values from 0.2 to 1.5
- ac_media: float32 [4, 2, 1024, 2048], P('patch', None, 'line', 'layer'), may hold values from 0.2 to 1.5
- cont_matrix: float32 [128, 20], replicated, may hold values from -1.25 to 1.25
- fringe_cells: int32 [4, 2, 4, 4, 256], P('patch', 'line', 'layer'), may hold values from 0 to 262143, as said below
- donor_cells: int32 [4, 2, 4, 4, 4, 256], P('patch', 'line', 'layer'), may hold values from 0 to 262143
- donor_weights: float32 [4, 2, 4, 4, 4, 256], P('patch', 'line', 'layer'), may hold values from 0 to 1, as said below
- donor_counts: int32 [4, 2, 4, 4], P('patch', 'line', 'layer'), may hold values from 0 to 256, as said below
- el_pair: int32 [4, 1024], P('patch', 'line'), may hold values from 0 to 511
- ac_pair: int32 [4, 1024], P('patch', 'line'), may hold values from 0 to 511
Outputs:
- new_elastic: float32 [4, 5, 1024, 2048], P('patch', None, 'line', 'layer')
- new_acoustic: float32 [4, 3, 1024, 2048], P('patch', None, 'line', 'layer')
Inputs may be any that keep to these rules, and one draw needn't show every extreme that they name: `fringe_cells`: within one device the 1024 fringe cells are distinct. `donor_weights`: Positive; the four weights of a slot sum to 1. `donor_counts`: 0 where donor and receiver are the same patch; on every device one donor patch fills all 256 slots.
All inputs are finite; a program needn't handle non-finite values.
Results may differ from a plain program's by a relative error of at most 0.0001.
Values sent between devices are 32-bit elements; how exact they have to be, the bound alone decides.
No kernel may reach another device: no remote copies, remote signals or barrier semaphores. Data moves between devices by JAX's collectives and lax.ppermute only.
A program may use at most 512 MiB of HBM per device.

v0:
```python
import functools
import math

import jax
import jax.numpy as jnp
import numpy as np
from jax import lax
from jax.experimental import pallas as pl
from jax.experimental.pallas import tpu as pltpu
from jax.sharding import PartitionSpec as P

STEP = 0.25
PENALTY = 2.0
LANES = 128
VMEM_LIMIT = 56 * 1024 * 1024
HIGH = lax.Precision.HIGH
HIGHEST = lax.Precision.HIGHEST


def derivative_row(period):
    n = np.arange(1, period)
    sign = np.where(n % 2 == 0, 1.0, -1.0)
    row = np.zeros(period)
    row[1:] = (math.pi / period) * sign / np.tan(math.pi * n / period)
    return row


def operator_blocks(cont_matrix, rows, slabs, me):
    cont = cont_matrix.shape[0]
    match = cont_matrix.shape[1] // 2
    points = rows * slabs
    period = points + cont
    row = derivative_row(period)
    j = np.arange(rows)
    blocks = np.stack(
        [
            row[(o * rows + j[:, None] - j[None, :]) % period]
            for o in range(-(slabs - 1), slabs)
        ]
    ).astype(np.float32)
    to_tail = np.stack(
        [
            row[(s * rows + j[:, None] - points - np.arange(cont)[None, :]) % period]
            for s in range(slabs)
        ]
    ).astype(np.float32)
    tail_rows = lax.dynamic_index_in_dim(jnp.asarray(to_tail), me, 0, keepdims=False)
    folded = jnp.dot(tail_rows, cont_matrix, precision=HIGHEST)
    on_last = jnp.pad(folded[:, :match], ((0, 0), (rows - match, 0)))
    on_first = jnp.pad(folded[:, match:], ((0, 0), (0, rows - match)))
    table = jnp.asarray(blocks)
    out = []
    for distance in range(slabs):
        source = (me - distance) % slabs
        block = lax.dynamic_index_in_dim(table, me - source + slabs - 1, 0, keepdims=False)
        block = block + jnp.where(source == slabs - 1, on_last, 0.0)
        out.append(block + jnp.where(source == 0, on_first, 0.0))
    return out


def split(value, size):
    if size & (size - 1) == 0:
        return lax.shift_right_logical(value, size.bit_length() - 1), value & (size - 1)
    return lax.div(value, size), lax.rem(value, size)


def take_kernel(in_ref, out_ref):
    out_ref[...] = in_ref[0, 0]


def take_field(fields, index, tile):
    rows, depth = fields.shape[2:]
    return pl.pallas_call(
        take_kernel,
        grid=(rows // tile,),
        in_specs=[pl.BlockSpec((1, 1, tile, depth), lambda i: (0, index, i, 0))],
        out_specs=pl.BlockSpec((tile, depth), lambda i: (i, 0)),
        out_shape=jax.ShapeDtypeStruct((rows, depth), fields.dtype),
        compiler_params=pltpu.CompilerParams(vmem_limit_bytes=VMEM_LIMIT),
        cost_estimate=pl.CostEstimate(flops=0, bytes_accessed=8 * rows * depth, transcendentals=0),
        name="take_field",
    )(fields)


def gather_kernel(fields, rows, depth, slots, words_ref, weights_ref, elastic_ref, acoustic_ref, out_ref, mixed):
    n_el = elastic_ref.shape[1]
    chunks = depth // LANES
    for f in range(fields):
        source = elastic_ref.at[0, f] if f < n_el else acoustic_ref.at[0, f - n_el]
        for c in range(chunks):
            mixed[pl.ds((c * fields + f) * rows, rows), :] = source[:, c * LANES : (c + 1) * LANES]
    lane = lax.broadcasted_iota(jnp.int32, (fields, LANES), 1)
    groups = out_ref.shape[1]

    def one_group(step, carry):
        def one_slot(r, values):
            first = (step * LANES + r) * 4
            total = None
            for s in range(4):
                start, at = split(words_ref[first + s], LANES)
                picked = mixed[pl.ds(start, fields, stride=rows), :]
                term = jnp.where(lane == at, picked * weights_ref[first + s], 0.0)
                total = term if total is None else total + term
            column = jnp.sum(total, axis=1, keepdims=True)
            return jnp.where(lane == r, column, values)

        values = lax.fori_loop(0, LANES, one_slot, jnp.zeros((fields, LANES), jnp.float32), unroll=16)
        out_ref[step // groups, step % groups] = values
        return carry

    lax.fori_loop(0, out_ref.shape[0] * groups, one_group, 0)


def near_kernel(n_el, d_ref, elastic_ref, acoustic_ref, out_ref):
    value = jnp.where(pl.program_id(0) < n_el, elastic_ref[0, 0], acoustic_ref[0, 0])
    out_ref[0] = jnp.dot(d_ref[...], value, precision=HIGH, preferred_element_type=jnp.float32)


def near_derivatives(operator, elastic, acoustic):
    rows, depth = elastic.shape[2:]
    return pl.pallas_call(
        functools.partial(near_kernel, 4),
        grid=(6,),
        in_specs=[
            pl.BlockSpec((rows, rows), lambda f: (0, 0)),
            pl.BlockSpec((1, 1, rows, depth), lambda f: (0, jnp.where(f < 3, f, 4), 0, 0)),
            pl.BlockSpec((1, 1, rows, depth), lambda f: (0, jnp.maximum(f - 4, 0), 0, 0)),
        ],
        out_specs=pl.BlockSpec((1, rows, depth), lambda f: (f, 0, 0)),
        out_shape=jax.ShapeDtypeStruct((6, rows, depth), jnp.float32),
        compiler_params=pltpu.CompilerParams(vmem_limit_bytes=VMEM_LIMIT),
        cost_estimate=pl.CostEstimate(
            flops=36 * rows * rows * depth, bytes_accessed=48 * rows * depth, transcendentals=0
        ),
        name="near_dx",
    )(operator, elastic, acoustic)


def section_kernel(
    rows, depth, slots, tile,
    words_ref, counts_ref, interp_ref, gates_ref,
    dx_ref, elastic_ref, acoustic_ref, el_media_ref, ac_media_ref, halo_ref,
    el_pair_ref, ac_pair_ref, ocean_row_ref, basin_row_ref,
    new_el_ref, new_ac_ref, open_ref,
):
    step = pl.program_id(0)
    here = pl.ds(pl.multiple_of(step * tile, tile), tile)
    lane = lax.broadcasted_iota(jnp.int32, (tile, depth), 1)

    def dz(value, slot):
        above = halo_ref[:, slot : slot + 1]
        below = halo_ref[:, 6 + slot : 7 + slot]
        following = jnp.where(lane == depth - 1, below, pltpu.roll(value, depth - 1, 1))
        previous = jnp.where(lane == 0, above, pltpu.roll(value, 1, 1))
        return (following - previous) * 0.5

    vx, vz, sxx, szz, sxz = [elastic_ref[0, f] for f in range(5)]
    p, ovx, ovz = [acoustic_ref[0, f] for f in range(3)]
    buoyancy = el_media_ref[0, 0]
    lame = el_media_ref[0, 1]
    shear = el_media_ref[0, 2]
    stiffness = lame + 2.0 * shear
    bulk = ac_media_ref[0, 0]
    ocean_buoyancy = ac_media_ref[0, 1]

    dx_vx = dx_ref[0]
    dz_vz = dz(vz, 1)
    new_el_ref[0, 0, here, :] = vx + STEP * (buoyancy * (dx_ref[2] + dz(sxz, 3)))
    new_el_ref[0, 1, here, :] = vz + STEP * (buoyancy * (dx_ref[3] + dz(szz, 2)))
    new_el_ref[0, 2, here, :] = sxx + STEP * (stiffness * dx_vx + lame * dz_vz)
    choose = lax.broadcasted_iota(jnp.int32, (tile, rows), 1)
    pressure = jnp.sum(jnp.where(el_pair_ref[...] == choose, ocean_row_ref[...], 0.0), axis=1, keepdims=True)
    velocity = jnp.sum(jnp.where(ac_pair_ref[...] == choose, basin_row_ref[...], 0.0), axis=1, keepdims=True)
    rate_szz = lame * dx_vx + stiffness * dz_vz
    rate_szz = rate_szz + jnp.where(lane == 0, gates_ref[0] * (PENALTY * (-pressure - szz)), 0.0)
    new_el_ref[0, 3, here, :] = szz + STEP * rate_szz
    new_el_ref[0, 4, here, :] = sxz + STEP * (shear * (dz(vx, 0) + dx_ref[1]))
    new_ac_ref[0, 0, here, :] = p - STEP * (bulk * (dx_ref[5] + dz(ovz, 5)))
    new_ac_ref[0, 1, here, :] = ovx - STEP * (ocean_buoyancy * dx_ref[4])
    rate_ovz = -ocean_buoyancy * dz(p, 4)
    rate_ovz = rate_ovz + jnp.where(lane == depth - 1, gates_ref[1] * (PENALTY * (velocity - ovz)), 0.0)
    new_ac_ref[0, 2, here, :] = ovz + STEP * rate_ovz
    open_ref[here, :] = jnp.ones((tile, depth), jnp.float32)

    @pl.when(step == pl.num_programs(0) - 1)
    def _():
        place = lax.broadcasted_iota(jnp.int32, (8, LANES), 0) * LANES
        place = place + lax.broadcasted_iota(jnp.int32, (8, LANES), 1)
        n_el = new_el_ref.shape[1]

        def one_patch(q, carry):
            def one_slot(r, inner):
                block, at = split(words_ref[q * slots + r], 8 * LANES)
                high, low = split(block, depth // LANES)
                at_row = pl.ds(pl.multiple_of(high * 8, 8), 8)
                at_lane = pl.ds(pl.multiple_of(low * LANES, LANES), LANES)
                hit = place == at
                group, within = split(r, LANES)
                first = (q * (slots // LANES) + group) * (8 * LANES) + within
                for f in range(8):
                    target = new_el_ref.at[0, f] if f < n_el else new_ac_ref.at[0, f - n_el]
                    target[at_row, at_lane] = jnp.where(hit, interp_ref[first + f * LANES], target[at_row, at_lane])
                open_ref[at_row, at_lane] = jnp.where(hit, 0.0, open_ref[at_row, at_lane])
                return inner

            return lax.fori_loop(0, counts_ref[q], one_slot, carry)

        lax.fori_loop(0, counts_ref.shape[0], one_patch, 0)


def far_kernel(coefficients, d_ref, far_ref, media_ref, open_ref, base_ref, out_ref):
    far = jnp.dot(d_ref[...], far_ref[...], precision=HIGH, preferred_element_type=jnp.float32)
    media = [media_ref[0, i] for i in range(media_ref.shape[1])]
    is_open = open_ref[...] > 0.5
    for i, coefficient in enumerate(coefficients):
        old = base_ref[0, i]
        out_ref[0, i] = jnp.where(is_open, old + (STEP * coefficient(*media)) * far, old)


def add_far(base, operator, far, media, first_media, n_media, first_field, coefficients, opened, tile):
    rows, reach = operator.shape
    depth = far.shape[1]
    n_out = len(coefficients)
    return pl.pallas_call(
        functools.partial(far_kernel, coefficients),
        grid=(depth // tile,),
        in_specs=[
            pl.BlockSpec((rows, reach), lambda i: (0, 0)),
            pl.BlockSpec((reach, tile), lambda i: (0, i)),
            pl.BlockSpec((1, n_media, rows, tile), lambda i: (0, first_media // n_media, 0, i)),
            pl.BlockSpec((rows, tile), lambda i: (0, i)),
            pl.BlockSpec((1, n_out, rows, tile), lambda i: (0, first_field // n_out, 0, i)),
        ],
        out_specs=pl.BlockSpec((1, n_out, rows, tile), lambda i: (0, first_field // n_out, 0, i)),
        out_shape=jax.ShapeDtypeStruct(base.shape, base.dtype),
        input_output_aliases={4: 0},
        compiler_params=pltpu.CompilerParams(vmem_limit_bytes=VMEM_LIMIT),
        cost_estimate=pl.CostEstimate(
            flops=6 * rows * reach * depth,
            bytes_accessed=4 * rows * depth * (3 + n_media + n_out),
            transcendentals=0,
        ),
        name="add_far",
    )(operator, far, media, opened, base)


def per_device(
    elastic,
    acoustic,
    el_media,
    ac_media,
    cont_matrix,
    fringe_cells,
    donor_cells,
    donor_weights,
    donor_counts,
    el_pair,
    ac_pair,
):
    rows, depth = elastic.shape[2], elastic.shape[3]
    slabs = lax.axis_size("line")
    layers = lax.axis_size("layer")
    patches = lax.axis_size("patch")
    slots = fringe_cells.shape[-1]
    groups = slots // LANES
    me = lax.axis_index("line")
    layer = lax.axis_index("layer")
    tile = min(64, rows)

    def other_slabs(value):
        parts = [
            lax.ppermute(value, "line", [(i, (i + distance) % slabs) for i in range(slabs)])
            for distance in range(1, slabs)
        ]
        return parts[0] if slabs == 2 else jnp.concatenate(parts, axis=0)

    far = [
        other_slabs(value)
        for value in [take_field(elastic, f, tile) for f in (0, 1, 2, 4)] + [take_field(acoustic, f, tile) for f in (0, 1)]
    ]

    asked = jnp.concatenate([donor_cells[0, 0, 0].astype(jnp.float32), donor_weights[0, 0, 0]], axis=1)
    asked = lax.all_to_all(asked, "patch", split_axis=0, concat_axis=0, tiled=True)
    x, z = split(jnp.swapaxes(asked[:, :4], 1, 2).astype(jnp.int32), depth)
    chunk, at_lane = split(z, LANES)
    asked_words = ((chunk * (8 * rows) + x) * LANES + at_lane).reshape(-1)
    asked_weights = jnp.swapaxes(asked[:, 4:], 1, 2).reshape(-1)

    smem = pl.BlockSpec(memory_space=pltpu.SMEM)
    vmem = pl.BlockSpec(memory_space=pltpu.VMEM)
    local = pl.pallas_call(
        functools.partial(gather_kernel, 8, rows, depth, slots),
        in_specs=[smem, smem, vmem, vmem],
        out_specs=vmem,
        out_shape=jax.ShapeDtypeStruct((patches, groups, 8, LANES), jnp.float32),
        scratch_shapes=[pltpu.VMEM((8 * rows * (depth // LANES), LANES), jnp.float32)],
        compiler_params=pltpu.CompilerParams(vmem_limit_bytes=VMEM_LIMIT),
        cost_estimate=pl.CostEstimate(flops=10**9, bytes_accessed=32 * rows * depth, transcendentals=0),
        name="donor_gather",
    )(asked_words, asked_weights, elastic, acoustic)
    interp = lax.all_to_all(local, "patch", split_axis=0, concat_axis=0, tiled=True).reshape(-1)

    depth_in = [elastic[0, 0], elastic[0, 1], elastic[0, 3], elastic[0, 4], acoustic[0, 0], acoustic[0, 2]]
    top_cells = jnp.stack([value[:, 0] for value in depth_in])
    bottom_cells = jnp.stack([value[:, depth - 1] for value in depth_in])
    from_above = lax.ppermute(bottom_cells, "layer", [(i, (i + 1) % layers) for i in range(layers)])
    from_below = lax.ppermute(top_cells, "layer", [(i, (i - 1) % layers) for i in range(layers)])
    at_top, at_bottom = layer == 0, layer == layers - 1
    ocean_row = from_above[4:5]
    basin_row = from_below[1:2]
    halo = jnp.concatenate([jnp.where(at_top, 0.0, from_above), jnp.where(at_bottom, 0.0, from_below)]).T
    gates = jnp.stack([at_top, at_bottom]).astype(jnp.float32)

    blocks = operator_blocks(cont_matrix, rows, slabs, me)
    far_operator = blocks[1] if slabs == 2 else jnp.concatenate(blocks[1:], axis=1)

    near = near_derivatives(blocks[0], elastic, acoustic)
    x, z = split(fringe_cells[0, 0, 0], depth)
    (row_block, row), (chunk, at_lane) = split(x, 8), split(z, LANES)
    fringe_words = ((row_block * (depth // LANES) + chunk) * 8 + row) * LANES + at_lane
    new_el, new_ac, opened = pl.pallas_call(
        functools.partial(section_kernel, rows, depth, slots, tile),
        grid=(rows // tile,),
        in_specs=[
            smem,
            smem,
            smem,
            smem,
            pl.BlockSpec((6, tile, depth), lambda i: (0, i, 0)),
            pl.BlockSpec((1, 5, tile, depth), lambda i: (0, 0, i, 0)),
            pl.BlockSpec((1, 3, tile, depth), lambda i: (0, 0, i, 0)),
            pl.BlockSpec((1, 3, tile, depth), lambda i: (0, 0, i, 0)),
            pl.BlockSpec((1, 2, tile, depth), lambda i: (0, 0, i, 0)),
            pl.BlockSpec((tile, 12), lambda i: (i, 0)),
            pl.BlockSpec((tile, 1), lambda i: (i, 0)),
            pl.BlockSpec((tile, 1), lambda i: (i, 0)),
            vmem,
            vmem,
        ],
        out_specs=[vmem, vmem, vmem],
        out_shape=[
            jax.ShapeDtypeStruct(elastic.shape, jnp.float32),
            jax.ShapeDtypeStruct(acoustic.shape, jnp.float32),
            jax.ShapeDtypeStruct((rows, depth), jnp.float32),
        ],
        compiler_params=pltpu.CompilerParams(vmem_limit_bytes=VMEM_LIMIT),
        cost_estimate=pl.CostEstimate(
            flops=100 * rows * depth, bytes_accessed=112 * rows * depth, transcendentals=0
        ),
        name="near_section",
    )(
        fringe_words.reshape(-1),
        donor_counts[0, 0, 0],
        interp,
        gates,
        near,
        elastic,
        acoustic,
        el_media,
        ac_media,
        halo,
        el_pair[0][:, None],
        ac_pair[0][:, None],
        ocean_row,
        basin_row,
    )

    far_tile = min(256, depth)
    new_el = add_far(
        new_el, far_operator, far[0], el_media, 0, 3, 2,
        (lambda b, l, m: l + 2.0 * m, lambda b, l, m: l), opened, far_tile,
    )
    new_el = add_far(new_el, far_operator, far[1], el_media, 2, 1, 4, (lambda m: m,), opened, far_tile)
    new_el = add_far(new_el, far_operator, far[2], el_media, 0, 1, 0, (lambda b: b,), opened, far_tile)
    new_el = add_far(new_el, far_operator, far[3], el_media, 0, 1, 1, (lambda b: b,), opened, far_tile)
    new_ac = add_far(new_ac, far_operator, far[4], ac_media, 1, 1, 1, (lambda b: -b,), opened, far_tile)
    new_ac = add_far(new_ac, far_operator, far[5], ac_media, 0, 1, 0, (lambda k: -k,), opened, far_tile)
    return new_el, new_ac


def solution(mesh):
    placed = (
        P("patch", None, "line", "layer"),
        P("patch", None, "line", "layer"),
        P("patch", None, "line", "layer"),
        P("patch", None, "line", "layer"),
        P(),
        P("patch", "line", "layer", None, None),
        P("patch", "line", "layer", None, None, None),
        P("patch", "line", "layer", None, None, None),
        P("patch", "line", "layer", None),
        P("patch", "line"),
        P("patch", "line"),
    )
    return jax.shard_map(
        per_device,
        mesh=mesh,
        in_specs=placed,
        out_specs=(P("patch", None, "line", "layer"), P("patch", None, "line", "layer")),
        check_vma=False,
    )
```

profile of v0, /device:TPU:0, one launch (start us, length us, event | category | flops | bytes accessed | tf_op | source)
XLA Modules:
  0.0 162.2 jit_solution(17580070521053520186)
XLA Ops:
  0.7 2.8 %slice_bitcast_fusion.2 = (f32[512,512]{1,0:T(8,128)S(1)}, f32[512,512]{1,0:T(8,128)S(1)}, f32[512,512]{1,0:T(8,128)S(1)}, f32[512,512]{1,0:T(8,128)S(1)}) fusion(f32[1,5,512,512]{3,2,1,0:T(8,128)} %in_ref.9), kind=kLoop, calls=%fused_computation.10 | loop fusion | bytes 8388608 | tf_op jit(solution)/shard_map/squeeze | solution.py:303
  5.5 3.1 %collective-permute-start.1 = (f32[6,512]{1,0:T(8,128)S(1)}, f32[6,512]{1,0:T(8,128)S(1)}, u32[]{:S(2)}, u32[]{:S(2)}) collective-permute-start(f32[6,512]{1,0:T(8,128)S(1)} %stack.18), channel_id=1, source_target_pairs={{0,1},{1,2},{2,3},{3,0},{4,5},{5,6},{6,7},{7,4},{8,9},{9,10},{10,1... | collective-permute-start | bytes 36872 | tf_op jit(solution)/shard_map/ppermute | solution.py:306
  8.7 2.1 %collective-permute-start.2 = (f32[6,512]{1,0:T(8,128)S(1)}, f32[6,512]{1,0:T(8,128)S(1)}, u32[]{:S(2)}, u32[]{:S(2)}) collective-permute-start(f32[6,512]{1,0:T(8,128)S(1)} %stack.19), channel_id=1, source_target_pairs={{0,3},{1,0},{2,1},{3,2},{4,7},{5,4},{6,5},{7,6},{8,11},{9,8},{10,9... | collective-permute-start | bytes 36872 | tf_op jit(solution)/shard_map/ppermute | solution.py:307
  11.4 3.3 %all-to-all-start = ((f32[4,8,256]{2,1,0:T(8,128)}), f32[4,8,256]{2,1,0:T(8,128)S(1)}, u32[]{:S(2)}, u32[]{:S(2)}) async-start(f32[4,8,256]{2,1,0:T(8,128)} %pad_maximum_fusion), calls=%async_computation | async-start | bytes 65536 | tf_op jit(solution)/shard_map/all_to_all | solution.py:283
  14.6 5.2 %take_field.11 = f32[512,512]{1,0:T(8,128)} custom-call(f32[1,3,512,512]{3,2,1,0:T(8,128)} %in_ref.11), custom_call_target="tpu_custom_call" | custom-call | bytes 2097152 | tf_op jit(solution)/shard_map/take_field/pallas_call | solution.py:73
  19.8 1.7 %collective-permute-start.7 = (f32[512,512]{1,0:T(8,128)}, f32[512,512]{1,0:T(8,128)}, u32[]{:S(2)}, u32[]{:S(2)}) collective-permute-start(f32[512,512]{1,0:T(8,128)} %take_field.11), channel_id=1, source_target_pairs={{0,4},{4,0},{1,5},{5,1},{2,6},{6,2},{3,7},{7,3},{8,12},{12,8},{9,1... | collective-permute-start | bytes 3145736 | tf_op jit(solution)/shard_map/ppermute | solution.py:272
  21.5 5.1 %take_field.10 = f32[512,512]{1,0:T(8,128)} custom-call(f32[1,3,512,512]{3,2,1,0:T(8,128)} %in_ref.11), custom_call_target="tpu_custom_call" | custom-call | bytes 2097152 | tf_op jit(solution)/shard_map/take_field/pallas_call | solution.py:73
  27.0 5.3 %take_field.9 = f32[512,512]{1,0:T(8,128)} custom-call(f32[1,5,512,512]{3,2,1,0:T(8,128)} %in_ref.9), custom_call_target="tpu_custom_call" | custom-call | bytes 2097152 | tf_op jit(solution)/shard_map/take_field/pallas_call | solution.py:73
  36.0 2.6 %fusion.3 = (f32[512,512]{1,0:T(8,128)}, f32[512,512]{1,0:T(8,128)}) fusion(f32[512,10]{1,0:T(8,128)} %get-tuple-element.29, f32[512,10]{1,0:T(8,128)S(1)} %get-tuple-element.28, f32[3,512,512]{2,1,0:T(8,128)S(1)} %copy-done.2, s32[]{:T(128)S(6)} %select_n.70, pred[]{:T(512)S(6)} %eq.26, pred[]{:T(512)S(6)} %eq.25, pred[]{:T(512)S(6)} %eq.22, pred[]{:T(512)S(6)} %eq.21, ...), kind=kLoop, calls=%fused_computation.7 | loop fusion | flops 2097152 | bytes 4235276 | tf_op jit(solution)/shard_map/add | solution.py:57
  38.5 10.3 %near_dx.1.dx_ref = f32[6,512,512]{2,1,0:T(8,128)} custom-call(f32[512,512]{1,0:T(8,128)} %get-tuple-element.24.d_ref, f32[1,5,512,512]{3,2,1,0:T(8,128)} %in_ref.9, f32[1,3,512,512]{3,2,1,0:T(8,128)} %in_ref.11), custom_call_target="tpu_custom_call" | custom-call | flops 4831838208 | bytes 12582912 | tf_op jit(solution)/shard_map/near_dx/pallas_call | solution.py:121
  49.5 5.2 %take_field.8 = f32[512,512]{1,0:T(8,128)} custom-call(f32[1,5,512,512]{3,2,1,0:T(8,128)} %in_ref.9), custom_call_target="tpu_custom_call" | custom-call | bytes 2097152 | tf_op jit(solution)/shard_map/take_field/pallas_call | solution.py:73
  54.7 5.1 %take_field.7 = f32[512,512]{1,0:T(8,128)} custom-call(f32[1,5,512,512]{3,2,1,0:T(8,128)} %in_ref.9), custom_call_target="tpu_custom_call" | custom-call | bytes 2097152 | tf_op jit(solution)/shard_map/take_field/pallas_call | solution.py:73
  59.8 5.2 %take_field.6 = f32[512,512]{1,0:T(8,128)} custom-call(f32[1,5,512,512]{3,2,1,0:T(8,128)} %in_ref.9), custom_call_target="tpu_custom_call" | custom-call | bytes 2097152 | tf_op jit(solution)/shard_map/take_field/pallas_call | solution.py:73
  72.1 27.0 %donor_gather.1 = f32[4,2,8,128]{3,2,1,0:T(8,128)} custom-call(s32[4096]{0:T(1024)} %reshape.31.words_ref, f32[4096]{0:T(1024)} %reshape.32.weights_ref, f32[1,5,512,512]{3,2,1,0:T(8,128)} %in_ref.9, f32[1,3,512,512]{3,2,1,0:T(8,128)} %in_ref.11), custom_call_target="tpu_custom_call" | custom-call | flops 1000000000 | bytes 8388608 | tf_op jit(solution)/shard_map/donor_gather/pallas_call | solution.py:291
  99.1 3.3 %all-to-all-start.1 = ((f32[4,2,8,128]{3,2,1,0:T(8,128)}), f32[4,2,8,128]{3,2,1,0:T(8,128)S(1)}, u32[]{:S(2)}, u32[]{:S(2)}) async-start(f32[4,2,8,128]{3,2,1,0:T(8,128)} %donor_gather.1), calls=%async_computation.1 | async-start | bytes 65536 | tf_op jit(solution)/shard_map/all_to_all | solution.py:301
  104.5 1.9 %all-to-all-done.1 = f32[4,2,8,128]{3,2,1,0:T(8,128)S(1)} async-done(((f32[4,2,8,128]{3,2,1,0:T(8,128)}), f32[4,2,8,128]{3,2,1,0:T(8,128)S(1)}, u32[]{:S(2)}, u32[]{:S(2)}) %all-to-all-start.1) | async-done | bytes 32800 | tf_op jit(solution)/shard_map/all_to_all | solution.py:301
  106.9 19.5 %near_section.1 = (f32[1,5,512,512]{3,2,1,0:T(8,128)}, f32[1,3,512,512]{3,2,1,0:T(8,128)}, f32[512,512]{1,0:T(8,128)}) custom-call(s32[1024]{0:T(1024)} %bitcast.51, s32[4]{0:T(128)} %bitcast.67, f32[8192]{0:T(1024)} %bitcast.50, f32[2]{0:T(128)} %add_convert_fusion.gates_ref, f32[6,512,512]{2,1,0:T(8,128)} %near_dx.1.dx_ref, f32[1,5,512,512]{3,2,1,0:T(8,128)} %in_ref.9, ...), custom_call_target="tpu_custom_call" | custom-call | flops 26214400 | bytes 29360128 | tf_op jit(solution)/shard_map/near_section/pallas_call | solution.py:321
  126.5 4.2 %add_far.10.base_ref = f32[1,3,512,512]{3,2,1,0:T(8,128)} custom-call(f32[512,512]{1,0:T(8,128)} %get-tuple-element.25.d_ref, f32[512,512]{1,0:T(8,128)} %collective-permute-done.7.far_ref, f32[1,2,512,512]{3,2,1,0:T(8,128)} %media_ref.11, f32[512,512]{1,0:T(8,128)} %get-tuple-element.5.open_ref, ...), custom_call_target="tpu_custom_call", output_to_operand_aliasing={{}: (4, {})} | custom-call | flops 805306368 | bytes 5242880 | tf_op jit(solution)/shard_map/add_far/pallas_call | solution.py:224
  130.7 4.2 %add_far.11 = f32[1,3,512,512]{3,2,1,0:T(8,128)} custom-call(f32[512,512]{1,0:T(8,128)} %get-tuple-element.25.d_ref, f32[512,512]{1,0:T(8,128)} %collective-permute-done.6.far_ref, f32[1,2,512,512]{3,2,1,0:T(8,128)} %media_ref.11, f32[512,512]{1,0:T(8,128)} %get-tuple-element.5.open_ref, ...), custom_call_target="tpu_custom_call", output_to_operand_aliasing={{}: (4, {})} | custom-call | flops 805306368 | bytes 5242880 | tf_op jit(solution)/shard_map/add_far/pallas_call | solution.py:224
  134.9 5.3 %add_far.6.base_ref = f32[1,5,512,512]{3,2,1,0:T(8,128)} custom-call(f32[512,512]{1,0:T(8,128)} %get-tuple-element.25.d_ref, f32[512,512]{1,0:T(8,128)} %collective-permute-done.5.far_ref, f32[1,3,512,512]{3,2,1,0:T(8,128)} %media_ref.9, f32[512,512]{1,0:T(8,128)} %get-tuple-element.5.open_ref, ...), custom_call_target="tpu_custom_call", output_to_operand_aliasing={{}: (4, {})} | custom-call | flops 805306368 | bytes 8388608 | tf_op jit(solution)/shard_map/add_far/pallas_call | solution.py:224
  141.2 4.2 %add_far.7.base_ref = f32[1,5,512,512]{3,2,1,0:T(8,128)} custom-call(f32[512,512]{1,0:T(8,128)} %get-tuple-element.25.d_ref, f32[512,512]{1,0:T(8,128)} %copy-done.3, f32[1,3,512,512]{3,2,1,0:T(8,128)} %media_ref.9, f32[512,512]{1,0:T(8,128)} %get-tuple-element.5.open_ref, f32[1,5,512,512]{3,2,1,0:T(8,128)} %add_far.6.base_ref), custom_call_target="tpu_custom_call", output_to_operand_aliasing={{}: (4, {})} | custom-call | flops 805306368 | bytes 5242880 | tf_op jit(solution)/shard_map/add_far/pallas_call | solution.py:224
  146.4 4.2 %add_far.8.base_ref = f32[1,5,512,512]{3,2,1,0:T(8,128)} custom-call(f32[512,512]{1,0:T(8,128)} %get-tuple-element.25.d_ref, f32[512,512]{1,0:T(8,128)} %copy-done.4, f32[1,3,512,512]{3,2,1,0:T(8,128)} %media_ref.9, f32[512,512]{1,0:T(8,128)} %get-tuple-element.5.open_ref, f32[1,5,512,512]{3,2,1,0:T(8,128)} %add_far.7.base_ref), custom_call_target="tpu_custom_call", output_to_operand_aliasing={{}: (4, {})} | custom-call | flops 805306368 | bytes 5242880 | tf_op jit(solution)/shard_map/add_far/pallas_call | solution.py:224
  150.6 7.4 %collective-permute-done.far_ref = f32[512,512]{1,0:T(8,128)} collective-permute-done((f32[512,512]{1,0:T(8,128)}, f32[512,512]{1,0:T(8,128)}, u32[]{:S(2)}, u32[]{:S(2)}) %collective-permute-start) | collective-permute-done | bytes 1048608 | tf_op jit(solution)/shard_map/ppermute | solution.py:272
  158.0 4.2 %add_far.9 = f32[1,5,512,512]{3,2,1,0:T(8,128)} custom-call(f32[512,512]{1,0:T(8,128)} %get-tuple-element.25.d_ref, f32[512,512]{1,0:T(8,128)} %collective-permute-done.far_ref, f32[1,3,512,512]{3,2,1,0:T(8,128)} %media_ref.9, f32[512,512]{1,0:T(8,128)} %get-tuple-element.5.open_ref, f32[1,5,512,512]{3,2,1,0:T(8,128)} %add_far.8.base_ref), custom_call_target="tpu_custom_call", output_to_operand_aliasing={{}: (4, {})} | custom-call | flops 805306368 | bytes 5242880 | tf_op jit(solution)/shard_map/add_far/pallas_call | solution.py:224
  (62 shorter events, 19.1 us)
Async XLA Ops:
  0.6 33.3 %copy-start = (f32[128,20]{0,1:T(8,128)S(1)}, f32[128,20]{0,1:T(8,128)}, u32[]{:S(2)}) copy-start(f32[128,20]{0,1:T(8,128)} %param.17) | copy-start | bytes 30724
  0.6 3.2 %copy-start.1 = (f32[1,3,512,512]{3,2,1,0:T(8,128)S(1)}, f32[1,3,512,512]{3,2,1,0:T(8,128)}, u32[]{:S(2)}) copy-start(f32[1,3,512,512]{3,2,1,0:T(8,128)} %in_ref.11) | copy-start | bytes 9437188
  3.8 7.0 %copy-start.6 = (s32[1,1,1,4,4,256]{5,4,3,2,1,0:T(4,128)S(1)}, s32[1,1,1,4,4,256]{5,4,3,2,1,0:T(4,128)}, u32[]{:S(2)}) copy-start(s32[1,1,1,4,4,256]{5,4,3,2,1,0:T(4,128)} %param.19) | copy-start | bytes 49156
  3.8 7.0 %copy-start.7 = (f32[1,1,1,4,4,256]{5,4,3,2,1,0:T(4,128)S(1)}, f32[1,1,1,4,4,256]{5,4,3,2,1,0:T(4,128)}, u32[]{:S(2)}) copy-start(f32[1,1,1,4,4,256]{5,4,3,2,1,0:T(4,128)} %param.20) | copy-start | bytes 49156
  5.5 61.8 %collective-permute-start.1 = (f32[6,512]{1,0:T(8,128)S(1)}, f32[6,512]{1,0:T(8,128)S(1)}, u32[]{:S(2)}, u32[]{:S(2)}) collective-permute-start(f32[6,512]{1,0:T(8,128)S(1)} %stack.18), channel_id=1, source_target_pairs={{0,1},{1,2},{2,3},{3,0},{4,5},{5,6},{6,7},{7,4},{8,9},{9,10},{10,1... | collective-permute-start | bytes 36872 | tf_op jit(solution)/shard_map/ppermute | solution.py:306
  8.7 59.2 %collective-permute-start.2 = (f32[6,512]{1,0:T(8,128)S(1)}, f32[6,512]{1,0:T(8,128)S(1)}, u32[]{:S(2)}, u32[]{:S(2)}) collective-permute-start(f32[6,512]{1,0:T(8,128)S(1)} %stack.19), channel_id=1, source_target_pairs={{0,3},{1,0},{2,1},{3,2},{4,7},{5,4},{6,5},{7,6},{8,11},{9,8},{10,9... | collective-permute-start | bytes 36872 | tf_op jit(solution)/shard_map/ppermute | solution.py:307
  11.4 58.5 %all-to-all-start = ((f32[4,8,256]{2,1,0:T(8,128)}), f32[4,8,256]{2,1,0:T(8,128)S(1)}, u32[]{:S(2)}, u32[]{:S(2)}) async-start(f32[4,8,256]{2,1,0:T(8,128)} %pad_maximum_fusion), calls=%async_computation | async-start | bytes 65536 | tf_op jit(solution)/shard_map/all_to_all | solution.py:283
  19.8 49.6 %collective-permute-start.7 = (f32[512,512]{1,0:T(8,128)}, f32[512,512]{1,0:T(8,128)}, u32[]{:S(2)}, u32[]{:S(2)}) collective-permute-start(f32[512,512]{1,0:T(8,128)} %take_field.11), channel_id=1, source_target_pairs={{0,4},{4,0},{1,5},{5,1},{2,6},{6,2},{3,7},{7,3},{8,12},{12,8},{9,1... | collective-permute-start | bytes 3145736 | tf_op jit(solution)/shard_map/ppermute | solution.py:272
  26.7 9.3 %copy-start.2 = (f32[3,512,512]{2,1,0:T(8,128)S(1)}, f32[3,512,512]{2,1,0:T(8,128)}, u32[]{:S(2)}) copy-start(f32[3,512,512]{2,1,0:T(8,128)} %constant.78.clone) | copy-start | bytes 9437188
  26.7 104.0 %collective-permute-start.6 = (f32[512,512]{1,0:T(8,128)}, f32[512,512]{1,0:T(8,128)}, u32[]{:S(2)}, u32[]{:S(2)}) collective-permute-start(f32[512,512]{1,0:T(8,128)} %take_field.10), channel_id=1, source_target_pairs={{0,4},{4,0},{1,5},{5,1},{2,6},{6,2},{3,7},{7,3},{8,12},{12,8},{9,1... | collective-permute-start | bytes 3145736 | tf_op jit(solution)/shard_map/ppermute | solution.py:272
  32.3 102.6 %collective-permute-start.5 = (f32[512,512]{1,0:T(8,128)}, f32[512,512]{1,0:T(8,128)}, u32[]{:S(2)}, u32[]{:S(2)}) collective-permute-start(f32[512,512]{1,0:T(8,128)} %take_field.9), channel_id=1, source_target_pairs={{0,4},{4,0},{1,5},{5,1},{2,6},{6,2},{3,7},{7,3},{8,12},{12,8},{9,1... | collective-permute-start | bytes 3145736 | tf_op jit(solution)/shard_map/ppermute | solution.py:272
  33.9 4.6 %copy-start.8 = (s32[1,1,1,4,256]{4,3,2,1,0:T(4,128)S(1)}, s32[1,1,1,4,256]{4,3,2,1,0:T(4,128)}, u32[]{:S(2)}) copy-start(s32[1,1,1,4,256]{4,3,2,1,0:T(4,128)} %param.18) | copy-start | bytes 12292
  59.8 5.2 %copy-start.9 = (s32[1,512]{1,0:T(1,128)S(1)}, s32[1,512]{1,0:T(1,128)}, u32[]{:S(2)}) copy-start(s32[1,512]{1,0:T(1,128)} %param.22) | copy-start | bytes 6148
  59.8 6.1 %copy-start.10 = (s32[1,512]{1,0:T(1,128)S(1)}, s32[1,512]{1,0:T(1,128)}, u32[]{:S(2)}) copy-start(s32[1,512]{1,0:T(1,128)} %param.23) | copy-start | bytes 6148
  67.4 72.9 %collective-permute-start.4 = (f32[512,512]{1,0:T(8,128)}, f32[512,512]{1,0:T(8,128)S(1)}, u32[]{:S(2)}, u32[]{:S(2)}) collective-permute-start(f32[512,512]{1,0:T(8,128)} %take_field.8), channel_id=1, source_target_pairs={{0,4},{4,0},{1,5},{5,1},{2,6},{6,2},{3,7},{7,3},{8,12},{12,8},{9,1... | collective-permute-start | bytes 3145736 | tf_op jit(solution)/shard_map/ppermute | solution.py:272
  67.8 77.6 %collective-permute-start.3 = (f32[512,512]{1,0:T(8,128)}, f32[512,512]{1,0:T(8,128)S(1)}, u32[]{:S(2)}, u32[]{:S(2)}) collective-permute-start(f32[512,512]{1,0:T(8,128)} %take_field.7), channel_id=1, source_target_pairs={{0,4},{4,0},{1,5},{5,1},{2,6},{6,2},{3,7},{7,3},{8,12},{12,8},{9,1... | collective-permute-start | bytes 3145736 | tf_op jit(solution)/shard_map/ppermute | solution.py:272
  69.4 88.6 %collective-permute-start = (f32[512,512]{1,0:T(8,128)}, f32[512,512]{1,0:T(8,128)}, u32[]{:S(2)}, u32[]{:S(2)}) collective-permute-start(f32[512,512]{1,0:T(8,128)} %take_field.6), channel_id=1, source_target_pairs={{0,4},{4,0},{1,5},{5,1},{2,6},{6,2},{3,7},{7,3},{8,12},{12,8},{9,1... | collective-permute-start | bytes 3145736 | tf_op jit(solution)/shard_map/ppermute | solution.py:272
  99.1 7.2 %all-to-all-start.1 = ((f32[4,2,8,128]{3,2,1,0:T(8,128)}), f32[4,2,8,128]{3,2,1,0:T(8,128)S(1)}, u32[]{:S(2)}, u32[]{:S(2)}) async-start(f32[4,2,8,128]{3,2,1,0:T(8,128)} %donor_gather.1), calls=%async_computation.1 | async-start | bytes 65536 | tf_op jit(solution)/shard_map/all_to_all | solution.py:301
  106.3 0.6 copy-start.5
  140.2 1.0 copy-start.3
  145.4 1.0 copy-start.4
where the time goes:
time: 163 us; the launch traced here: 162 us
  Pallas kernels  114 us (70%)
  starting transfers between devices  17.8 us (11%)
  local copies, waits for them, and re-layouts  14.8 us (9%)
  waiting for transfers between devices  9.28 us (6%)
  other arithmetic  3.87 us (2%)
    pallas_call x6, Pallas kernels, take_field(): pl.pallas_call(take_kernel, grid=(rows // tile,), in_specs=[pl.BlockSpec(...  31.1 us
    pallas_call x1, Pallas kernels, per_device(): pl.pallas_call(functools.partial(gather_kernel, 8, rows, depth, slots), i...  27 us
    pallas_call x6, Pallas kernels, add_far(): pl.pallas_call(functools.partial(far_kernel, coefficients), grid=(depth /...  26.4 us
    pallas_call x1, Pallas kernels, per_device(): pl.pallas_call(functools.partial(section_kernel, rows, depth, slots, tile...  19.5 us
    pallas_call x1, Pallas kernels, near_derivatives(): pl.pallas_call(functools.partial(near_kernel, 4), grid=(6,), in_specs=[pl...  10.3 us
    ppermute x6, waiting for transfers between devices, other_slabs(): lax.ppermute(value, 'line', [(i, (i + distance) % slabs) for i in range(s...  7.4 us
    ppermute x6, starting transfers between devices, other_slabs(): lax.ppermute(value, 'line', [(i, (i + distance) % slabs) for i in range(s...  6.08 us
    unnamed x23, local copies, waits for them, and re-layouts  3.55 us
  transfers between devices with their start and end apart: 10, of which 2 were waited for; matrix products, arithmetic and copies ran while one was open for 8% of the time, Pallas kernels for 68%

commit v1 on v0

--- a/solution.py
+++ b/solution.py
@@ -13,6 +13,7 @@
 PENALTY = 2.0
 LANES = 128
 VMEM_LIMIT = 56 * 1024 * 1024
+FAR_VMEM_LIMIT = 24 * 1024 * 1024
 HIGH = lax.Precision.HIGH
 HIGHEST = lax.Precision.HIGHEST
 
@@ -64,24 +65,6 @@
     return lax.div(value, size), lax.rem(value, size)
 
 
-def take_kernel(in_ref, out_ref):
-    out_ref[...] = in_ref[0, 0]
-
-
-def take_field(fields, index, tile):
-    rows, depth = fields.shape[2:]
-    return pl.pallas_call(
-        take_kernel,
-        grid=(rows // tile,),
-        in_specs=[pl.BlockSpec((1, 1, tile, depth), lambda i: (0, index, i, 0))],
-        out_specs=pl.BlockSpec((tile, depth), lambda i: (i, 0)),
-        out_shape=jax.ShapeDtypeStruct((rows, depth), fields.dtype),
-        compiler_params=pltpu.CompilerParams(vmem_limit_bytes=VMEM_LIMIT),
-        cost_estimate=pl.CostEstimate(flops=0, bytes_accessed=8 * rows * depth, transcendentals=0),
-        name="take_field",
-    )(fields)
-
-
 def gather_kernel(fields, rows, depth, slots, words_ref, weights_ref, elastic_ref, acoustic_ref, out_ref, mixed):
     n_el = elastic_ref.shape[1]
     chunks = depth // LANES
@@ -149,7 +132,7 @@
 
     def dz(value, slot):
         above = halo_ref[:, slot : slot + 1]
-        below = halo_ref[:, 6 + slot : 7 + slot]
+        below = halo_ref[:, 8 + slot : 9 + slot]
         following = jnp.where(lane == depth - 1, below, pltpu.roll(value, depth - 1, 1))
         previous = jnp.where(lane == 0, above, pltpu.roll(value, 1, 1))
         return (following - previous) * 0.5
@@ -165,8 +148,8 @@
 
     dx_vx = dx_ref[0]
     dz_vz = dz(vz, 1)
-    new_el_ref[0, 0, here, :] = vx + STEP * (buoyancy * (dx_ref[2] + dz(sxz, 3)))
-    new_el_ref[0, 1, here, :] = vz + STEP * (buoyancy * (dx_ref[3] + dz(szz, 2)))
+    new_el_ref[0, 0, here, :] = vx + STEP * (buoyancy * (dx_ref[2] + dz(sxz, 4)))
+    new_el_ref[0, 1, here, :] = vz + STEP * (buoyancy * (dx_ref[3] + dz(szz, 3)))
     new_el_ref[0, 2, here, :] = sxx + STEP * (stiffness * dx_vx + lame * dz_vz)
     choose = lax.broadcasted_iota(jnp.int32, (tile, rows), 1)
     pressure = jnp.sum(jnp.where(el_pair_ref[...] == choose, ocean_row_ref[...], 0.0), axis=1, keepdims=True)
@@ -175,9 +158,9 @@
     rate_szz = rate_szz + jnp.where(lane == 0, gates_ref[0] * (PENALTY * (-pressure - szz)), 0.0)
     new_el_ref[0, 3, here, :] = szz + STEP * rate_szz
     new_el_ref[0, 4, here, :] = sxz + STEP * (shear * (dz(vx, 0) + dx_ref[1]))
-    new_ac_ref[0, 0, here, :] = p - STEP * (bulk * (dx_ref[5] + dz(ovz, 5)))
+    new_ac_ref[0, 0, here, :] = p - STEP * (bulk * (dx_ref[5] + dz(ovz, 7)))
     new_ac_ref[0, 1, here, :] = ovx - STEP * (ocean_buoyancy * dx_ref[4])
-    rate_ovz = -ocean_buoyancy * dz(p, 4)
+    rate_ovz = -ocean_buoyancy * dz(p, 5)
     rate_ovz = rate_ovz + jnp.where(lane == depth - 1, gates_ref[1] * (PENALTY * (velocity - ovz)), 0.0)
     new_ac_ref[0, 2, here, :] = ovz + STEP * rate_ovz
     open_ref[here, :] = jnp.ones((tile, depth), jnp.float32)
@@ -208,7 +191,8 @@
         lax.fori_loop(0, counts_ref.shape[0], one_patch, 0)
 
 
-def far_kernel(coefficients, d_ref, far_ref, media_ref, open_ref, base_ref, out_ref):
+def far_kernel(coefficients, turn_ref, d_ref, far_ref, media_ref, open_ref, base_ref, next_ref, out_ref):
+    del turn_ref, next_ref
     far = jnp.dot(d_ref[...], far_ref[...], precision=HIGH, preferred_element_type=jnp.float32)
     media = [media_ref[0, i] for i in range(media_ref.shape[1])]
     is_open = open_ref[...] > 0.5
@@ -217,31 +201,40 @@
         out_ref[0, i] = jnp.where(is_open, old + (STEP * coefficient(*media)) * far, old)
 
 
-def add_far(base, operator, far, media, first_media, n_media, first_field, coefficients, opened, tile):
+def add_far(base, operator, far, at, media, first_media, n_media, first_field, coefficients, opened, turn):
     rows, reach = operator.shape
-    depth = far.shape[1]
+    width = far.shape[1]
+    tile = math.gcd(math.gcd(width, at), 2 * LANES)
     n_out = len(coefficients)
+    shift = at // tile
     return pl.pallas_call(
         functools.partial(far_kernel, coefficients),
-        grid=(depth // tile,),
+        grid=(width // tile,),
         in_specs=[
+            pl.BlockSpec(memory_space=pl.ANY),
             pl.BlockSpec((rows, reach), lambda i: (0, 0)),
             pl.BlockSpec((reach, tile), lambda i: (0, i)),
-            pl.BlockSpec((1, n_media, rows, tile), lambda i: (0, first_media // n_media, 0, i)),
-            pl.BlockSpec((rows, tile), lambda i: (0, i)),
-            pl.BlockSpec((1, n_out, rows, tile), lambda i: (0, first_field // n_out, 0, i)),
-        ],
-        out_specs=pl.BlockSpec((1, n_out, rows, tile), lambda i: (0, first_field // n_out, 0, i)),
-        out_shape=jax.ShapeDtypeStruct(base.shape, base.dtype),
-        input_output_aliases={4: 0},
-        compiler_params=pltpu.CompilerParams(vmem_limit_bytes=VMEM_LIMIT),
+            pl.BlockSpec((1, n_media, rows, tile), lambda i: (0, first_media // n_media, 0, i + shift)),
+            pl.BlockSpec((rows, tile), lambda i: (0, i + shift)),
+            pl.BlockSpec((1, n_out, rows, tile), lambda i: (0, first_field // n_out, 0, i + shift)),
+        ],
+        out_specs=[
+            pl.BlockSpec(memory_space=pl.ANY),
+            pl.BlockSpec((1, n_out, rows, tile), lambda i: (0, first_field // n_out, 0, i + shift)),
+        ],
+        out_shape=[
+            jax.ShapeDtypeStruct(turn.shape, turn.dtype),
+            jax.ShapeDtypeStruct(base.shape, base.dtype),
+        ],
+        input_output_aliases={0: 0, 5: 1},
+        compiler_params=pltpu.CompilerParams(vmem_limit_bytes=FAR_VMEM_LIMIT),
         cost_estimate=pl.CostEstimate(
-            flops=6 * rows * reach * depth,
-            bytes_accessed=4 * rows * depth * (3 + n_media + n_out),
+            flops=6 * rows * reach * width,
+            bytes_accessed=4 * rows * width * (3 + n_media + n_out),
             transcendentals=0,
         ),
         name="add_far",
-    )(operator, far, media, opened, base)
+    )(turn, operator, far, media, opened, base)
 
 
 def per_device(
@@ -274,10 +267,23 @@
         ]
         return parts[0] if slabs == 2 else jnp.concatenate(parts, axis=0)
 
-    far = [
-        other_slabs(value)
-        for value in [take_field(elastic, f, tile) for f in (0, 1, 2, 4)] + [take_field(acoustic, f, tile) for f in (0, 1)]
+    half, quarter = depth // 2, depth // 4
+    pieces = [
+        ("el", 0, 0, depth, "el", 0, 3, 2, (lambda b, l, m: l + 2.0 * m, lambda b, l, m: l)),
+        ("ac", 0, 0, depth, "ac", 1, 1, 1, (lambda b: -b,)),
+        ("ac", 1, 0, depth, "ac", 0, 1, 0, (lambda k: -k,)),
+        ("el", 1, 0, depth, "el", 2, 1, 4, (lambda m: m,)),
+        ("el", 2, 0, depth, "el", 0, 1, 0, (lambda b: b,)),
+        ("el", 4, 0, half, "el", 0, 1, 1, (lambda b: b,)),
+        ("el", 4, half, quarter, "el", 0, 1, 1, (lambda b: b,)),
+        ("el", 4, half + quarter, quarter, "el", 0, 1, 1, (lambda b: b,)),
     ]
+    far = []
+    source = {"el": elastic, "ac": acoustic}
+    for name, field, at, width, *_ in pieces:
+        value = lax.slice(source[name], (0, field, 0, at), (1, field + 1, rows, at + width)).reshape(rows, width)
+        value, source["el"], source["ac"] = lax.optimization_barrier((value, source["el"], source["ac"]))
+        far.append(other_slabs(value))
 
     asked = jnp.concatenate([donor_cells[0, 0, 0].astype(jnp.float32), donor_weights[0, 0, 0]], axis=1)
     asked = lax.all_to_all(asked, "patch", split_axis=0, concat_axis=0, tiled=True)
@@ -300,13 +306,13 @@
     )(asked_words, asked_weights, elastic, acoustic)
     interp = lax.all_to_all(local, "patch", split_axis=0, concat_axis=0, tiled=True).reshape(-1)
 
-    depth_in = [elastic[0, 0], elastic[0, 1], elastic[0, 3], elastic[0, 4], acoustic[0, 0], acoustic[0, 2]]
-    top_cells = jnp.stack([value[:, 0] for value in depth_in])
-    bottom_cells = jnp.stack([value[:, depth - 1] for value in depth_in])
-    from_above = lax.ppermute(bottom_cells, "layer", [(i, (i + 1) % layers) for i in range(layers)])
-    from_below = lax.ppermute(top_cells, "layer", [(i, (i - 1) % layers) for i in range(layers)])
+    top = jnp.concatenate([elastic[0, :, :, 0], acoustic[0, :, :, 0]])
+    bottom = jnp.concatenate([elastic[0, :, :, depth - 1], acoustic[0, :, :, depth - 1]])
+    edges = lax.all_gather(jnp.concatenate([top, bottom]), "layer")
     at_top, at_bottom = layer == 0, layer == layers - 1
-    ocean_row = from_above[4:5]
+    from_above = lax.dynamic_index_in_dim(edges, (layer - 1) % layers, 0, keepdims=False)[8:]
+    from_below = lax.dynamic_index_in_dim(edges, (layer + 1) % layers, 0, keepdims=False)[:8]
+    ocean_row = from_above[5:6]
     basin_row = from_below[1:2]
     halo = jnp.concatenate([jnp.where(at_top, 0.0, from_above), jnp.where(at_bottom, 0.0, from_below)]).T
     gates = jnp.stack([at_top, at_bottom]).astype(jnp.float32)
@@ -331,7 +337,7 @@
             pl.BlockSpec((1, 3, tile, depth), lambda i: (0, 0, i, 0)),
             pl.BlockSpec((1, 3, tile, depth), lambda i: (0, 0, i, 0)),
             pl.BlockSpec((1, 2, tile, depth), lambda i: (0, 0, i, 0)),
-            pl.BlockSpec((tile, 12), lambda i: (i, 0)),
+            pl.BlockSpec((tile, 16), lambda i: (i, 0)),
             pl.BlockSpec((tile, 1), lambda i: (i, 0)),
             pl.BlockSpec((tile, 1), lambda i: (i, 0)),
             vmem,
@@ -365,17 +371,15 @@
         basin_row,
     )
 
-    far_tile = min(256, depth)
-    new_el = add_far(
-        new_el, far_operator, far[0], el_media, 0, 3, 2,
-        (lambda b, l, m: l + 2.0 * m, lambda b, l, m: l), opened, far_tile,
-    )
-    new_el = add_far(new_el, far_operator, far[1], el_media, 2, 1, 4, (lambda m: m,), opened, far_tile)
-    new_el = add_far(new_el, far_operator, far[2], el_media, 0, 1, 0, (lambda b: b,), opened, far_tile)
-    new_el = add_far(new_el, far_operator, far[3], el_media, 0, 1, 1, (lambda b: b,), opened, far_tile)
-    new_ac = add_far(new_ac, far_operator, far[4], ac_media, 1, 1, 1, (lambda b: -b,), opened, far_tile)
-    new_ac = add_far(new_ac, far_operator, far[5], ac_media, 0, 1, 0, (lambda k: -k,), opened, far_tile)
-    return new_el, new_ac
+    turn = jnp.zeros((8, LANES), jnp.float32)
+    section = {"el": new_el, "ac": new_ac}
+    media = {"el": el_media, "ac": ac_media}
+    for value, (_, _, at, _, target, first_media, n_media, first_field, coefficients) in zip(far, pieces):
+        turn, section[target] = add_far(
+            section[target], far_operator, value, at,
+            media[target], first_media, n_media, first_field, coefficients, opened, turn,
+        )
+    return section["el"], section["ac"]
 
 
 def solution(mesh):

time: 163 us -> 162 us (level)
  Pallas kernels: 114 us -> 82.5 us
  local copies, waits for them, and re-layouts: 14.8 us -> 38.7 us
  blocking collectives: 0 us -> 13.7 us
  waiting for transfers between devices: 9.28 us -> 0.03 us
  other arithmetic: 3.87 us -> 7.02 us
    pallas_call x12 -> x8, Pallas kernels: 57.5 us -> 23.8 us  [add_far(): pl.pallas_call(functools.partial(far_kernel, coefficients), grid=(width /...]
    reshape x0 -> x8, local copies, waits for them, and re-layouts: none -> 16 us  [per_device(): lax.slice(source[name], (0, field, 0, at), (1, field + 1, rows, at + width))]
    all_gather x0 -> x1, blocking collectives: none -> 13.7 us  [per_device(): edges = lax.all_gather(jnp.concatenate([top, bottom]), 'layer')]
    ppermute x6 -> x8, waiting for transfers between devices: 7.4 us -> 0.02 us  [other_slabs(): lax.ppermute(value, 'line', [(i, (i + distance) % slabs) for i in range(s...]
    ppermute x2 -> x0, starting transfers between devices: 5.17 us -> none  [the longest x1 3.08 us: per_device(): lax.ppermute(bottom_cells, 'layer', [(i, (i + 1) % layers) for i in range...]
    slice x4 -> x2, local copies, waits for them, and re-layouts: 2.11 us -> 5.71 us  [per_device(): top = jnp.concatenate([elastic[0, :, :, 0], acoustic[0, :, :, 0]])]
    ppermute x6 -> x8, starting transfers between devices: 6.08 us -> 9.68 us  [other_slabs(): lax.ppermute(value, 'line', [(i, (i + distance) % slabs) for i in range(s...]
    squeeze x2 -> x0, local copies, waits for them, and re-layouts: 2.95 us -> none  [the longest x1 2.78 us: per_device(): elastic[0, 4]]
  transfers between devices with their start and end apart: 10 -> 10, of which waited for: 2 -> 0; matrix products, arithmetic and copies ran while one was open for 8% -> 26% of each run, Pallas kernels for 68% -> 50%
where the time goes in v1:
time: 162 us; the launch traced here: 160 us
  Pallas kernels  82.5 us (51%)
  local copies, waits for them, and re-layouts  38.7 us (24%)
  starting transfers between devices  17 us (10%)
  blocking collectives  13.7 us (8%)
  other arithmetic  7.02 us (4%)
    pallas_call x1, Pallas kernels, per_device(): pl.pallas_call(functools.partial(gather_kernel, 8, rows, depth, slots), i...  27 us
    pallas_call x8, Pallas kernels, add_far(): pl.pallas_call(functools.partial(far_kernel, coefficients), grid=(width /...  23.8 us
    pallas_call x1, Pallas kernels, per_device(): pl.pallas_call(functools.partial(section_kernel, rows, depth, slots, tile...  21.3 us
    reshape x8, local copies, waits for them, and re-layouts, per_device(): lax.slice(source[name], (0, field, 0, at), (1, field + 1, rows, at + width))  16 us
    all_gather x1, blocking collectives, per_device(): edges = lax.all_gather(jnp.concatenate([top, bottom]), 'layer')  13.7 us
    pallas_call x1, Pallas kernels, near_derivatives(): pl.pallas_call(functools.partial(near_kernel, 4), grid=(6,), in_specs=[pl...  10.3 us
    ppermute x8, starting transfers between devices, other_slabs(): lax.ppermute(value, 'line', [(i, (i + distance) % slabs) for i in range(s...  9.68 us
    unnamed x27, local copies, waits for them, and re-layouts  6.34 us
  transfers between devices with their start and end apart: 10, of which 0 were waited for; matrix products, arithmetic and copies ran while one was open for 26% of the time, Pallas kernels for 50%

profile of v1, /device:TPU:0, one launch (start us, length us, event | category | flops | bytes accessed | tf_op | source)
XLA Modules:
  0.0 160.0 jit_solution(7826866796691394131)
XLA Ops:
  0.6 2.3 %slice_bitcast_fusion.4 = f32[512,512]{1,0:T(8,128)} fusion(f32[1,5,512,512]{3,2,1,0:T(8,128)} %elastic_ref.5), kind=kLoop, calls=%fused_computation.12 | loop fusion | bytes 2097152 | tf_op jit(solution)/shard_map/reshape | solution.py:284
  2.9 3.0 %collective-permute-start = (f32[512,512]{1,0:T(8,128)}, f32[512,512]{1,0:T(8,128)}, u32[]{:S(2)}, u32[]{:S(2)}) collective-permute-start(f32[512,512]{1,0:T(8,128)} %slice_bitcast_fusion.4), channel_id=1, source_target_pairs={{0,4},{4,0},{1,5},{5,1},{2,6},{6,2},{3,7},{7,3},{8,12},{12,8},{9,1... | collective-permute-start | bytes 3145736 | tf_op jit(solution)/shard_map/ppermute | solution.py:265
  7.9 3.9 %all-to-all-start = ((f32[4,8,256]{2,1,0:T(8,128)}), f32[4,8,256]{2,1,0:T(8,128)}, u32[]{:S(2)}, u32[]{:S(2)}) async-start(f32[4,8,256]{2,1,0:T(8,128)} %pad_maximum_fusion), calls=%async_computation | async-start | bytes 65536 | tf_op jit(solution)/shard_map/all_to_all | solution.py:289
  11.8 2.3 %slice_bitcast_fusion.3 = f32[512,512]{1,0:T(8,128)} fusion(f32[1,3,512,512]{3,2,1,0:T(8,128)} %acoustic_ref.5), kind=kLoop, calls=%fused_computation.11 | loop fusion | bytes 2097152 | tf_op jit(solution)/shard_map/reshape | solution.py:284
  14.1 2.3 %slice_bitcast_fusion.2 = f32[512,512]{1,0:T(8,128)} fusion(f32[1,3,512,512]{3,2,1,0:T(8,128)} %acoustic_ref.5), kind=kLoop, calls=%fused_computation.10 | loop fusion | bytes 2097152 | tf_op jit(solution)/shard_map/reshape | solution.py:284
  16.4 2.0 %collective-permute-start.2 = (f32[512,512]{1,0:T(8,128)}, f32[512,512]{1,0:T(8,128)}, u32[]{:S(2)}, u32[]{:S(2)}) collective-permute-start(f32[512,512]{1,0:T(8,128)} %slice_bitcast_fusion.2), channel_id=1, source_target_pairs={{0,4},{4,0},{1,5},{5,1},{2,6},{6,2},{3,7},{7,3},{8,12},{12,8},{9,1... | collective-permute-start | bytes 3145736 | tf_op jit(solution)/shard_map/ppermute | solution.py:265
  18.4 2.3 %slice_bitcast_fusion.1 = f32[512,512]{1,0:T(8,128)} fusion(f32[1,5,512,512]{3,2,1,0:T(8,128)} %elastic_ref.5), kind=kLoop, calls=%fused_computation.9 | loop fusion | bytes 2097152 | tf_op jit(solution)/shard_map/reshape | solution.py:284
  20.8 2.3 %slice_bitcast_fusion = f32[512,512]{1,0:T(8,128)} fusion(f32[1,5,512,512]{3,2,1,0:T(8,128)} %elastic_ref.5), kind=kLoop, calls=%fused_computation.8 | loop fusion | bytes 2097152 | tf_op jit(solution)/shard_map/reshape | solution.py:284
  25.1 2.1 %slice_reduce_fusion.1 = (f32[3,512]{1,0:T(4,128)S(1)}, f32[3,512]{1,0:T(4,128)S(1)}) fusion(f32[1,3,512,512]{3,2,1,0:T(8,128)} %acoustic_ref.5), kind=kLoop, calls=%fused_computation.14 | loop fusion | bytes 24576 | tf_op jit(solution)/shard_map/slice | solution.py:309
  27.2 3.6 %fusion.10 = (f32[1,5,512,1]{3,2,1,0:T(8,128)}, f32[1,5,512,1]{3,2,1,0:T(8,128)}) fusion(f32[1,5,512,512]{3,2,1,0:T(8,128)} %elastic_ref.5), kind=kLoop, calls=%fused_computation.37 | loop fusion | bytes 40960 | tf_op jit(solution)/shard_map/slice | solution.py:309
  32.0 2.9 %fusion.3 = (f32[512,512]{1,0:T(8,128)}, f32[512,512]{1,0:T(8,128)S(1)}) fusion(f32[512,10]{1,0:T(8,128)} %get-tuple-element.79, f32[512,10]{1,0:T(8,128)S(1)} %get-tuple-element.78, f32[3,512,512]{2,1,0:T(8,128)} %constant.98.clone, s32[]{:T(128)S(6)} %select_n.91, pred[]{:T(512)S(6)} %eq.28, pred[]{:T(512)S(6)} %eq.27, pred[]{:T(512)S(6)} %eq.24, ...), kind=kLoop, calls=%fused_computation.7 | loop fusion | flops 2097152 | bytes 4235276 | tf_op jit(solution)/shard_map/add | solution.py:58
  34.8 10.3 %near_dx.1.dx_ref = f32[6,512,512]{2,1,0:T(8,128)} custom-call(f32[512,512]{1,0:T(8,128)} %get-tuple-element.76.d_ref, f32[1,5,512,512]{3,2,1,0:T(8,128)} %elastic_ref.5, f32[1,3,512,512]{3,2,1,0:T(8,128)} %acoustic_ref.5), custom_call_target="tpu_custom_call" | custom-call | flops 4831838208 | bytes 12582912 | tf_op jit(solution)/shard_map/near_dx/pallas_call | solution.py:104
  51.9 13.7 %all-gather = f32[64,512]{1,0:T(8,128)S(1)} all-gather(f32[16,512]{1,0:T(8,128)S(1)} %pad_maximum_fusion.1), channel_id=2, replica_groups=mesh['patch'=4,'line'=2,'layer'=4] {'layer'}, dimensions={0}, use_global_device_ids=true | all-gather | bytes 163840 | tf_op jit(solution)/shard_map/all_gather | solution.py:311
  76.5 27.0 %donor_gather.1 = f32[4,2,8,128]{3,2,1,0:T(8,128)} custom-call(s32[4096]{0:T(1024)} %reshape.66.words_ref, f32[4096]{0:T(1024)} %reshape.67.weights_ref, f32[1,5,512,512]{3,2,1,0:T(8,128)} %elastic_ref.5, f32[1,3,512,512]{3,2,1,0:T(8,128)} %acoustic_ref.5), custom_call_target="tpu_custom_call" | custom-call | flops 1000000000 | bytes 8388608 | tf_op jit(solution)/shard_map/donor_gather/pallas_call | solution.py:297
  103.5 3.4 %all-to-all-start.1 = ((f32[4,2,8,128]{3,2,1,0:T(8,128)}), f32[4,2,8,128]{3,2,1,0:T(8,128)S(1)}, u32[]{:S(2)}, u32[]{:S(2)}) async-start(f32[4,2,8,128]{3,2,1,0:T(8,128)} %donor_gather.1), calls=%async_computation.1 | async-start | bytes 65536 | tf_op jit(solution)/shard_map/all_to_all | solution.py:307
  111.4 21.3 %near_section.1 = (f32[1,5,512,512]{3,2,1,0:T(8,128)}, f32[1,3,512,512]{3,2,1,0:T(8,128)}, f32[512,512]{1,0:T(8,128)}) custom-call(s32[1024]{0:T(1024)} %bitcast.58, s32[4]{0:T(128)} %bitcast.62, f32[8192]{0:T(1024)} %bitcast.55, f32[2]{0:T(128)} %add_convert_fusion.gates_ref, f32[6,512,512]{2,1,0:T(8,128)} %near_dx.1.dx_ref, ...), custom_call_target="tpu_custom_call" | custom-call | flops 26214400 | bytes 29360128 | tf_op jit(solution)/shard_map/near_section/pallas_call | solution.py:327
  133.9 3.8 %add_far.8 = (f32[8,128]{1,0:T(8,128)S(1)}, f32[1,5,512,512]{3,2,1,0:T(8,128)}) custom-call(f32[8,128]{1,0:T(8,128)S(1)} %broadcast_in_dim.15.turn_ref, f32[512,512]{1,0:T(8,128)S(1)} %get-tuple-element.77.d_ref, f32[512,512]{1,0:T(8,128)} %collective-permute-done.far_ref, ...), custom_call_target="tpu_custom_call", output_to_operand_aliasing={{0}: (0, {}), {1}: (5, {})} | custom-call | flops 805306368 | bytes 8388608 | tf_op jit(solution)/shard_map/add_far/pallas_call | solution.py:210
  139.1 3.2 %add_far.9 = (f32[8,128]{1,0:T(8,128)S(1)}, f32[1,3,512,512]{3,2,1,0:T(8,128)}) custom-call(f32[8,128]{1,0:T(8,128)S(1)} %get-tuple-element.40.turn_ref, f32[512,512]{1,0:T(8,128)S(1)} %get-tuple-element.77.d_ref, f32[512,512]{1,0:T(8,128)} %collective-permute-done.1.far_ref, ...), custom_call_target="tpu_custom_call", output_to_operand_aliasing={{0}: (0, {}), {1}: (5, {})} | custom-call | flops 805306368 | bytes 5242880 | tf_op jit(solution)/shard_map/add_far/pallas_call | solution.py:210
  143.2 3.2 %add_far.10 = (f32[8,128]{1,0:T(8,128)S(1)}, f32[1,3,512,512]{3,2,1,0:T(8,128)}) custom-call(f32[8,128]{1,0:T(8,128)S(1)} %get-tuple-element.45.turn_ref, f32[512,512]{1,0:T(8,128)S(1)} %get-tuple-element.77.d_ref, f32[512,512]{1,0:T(8,128)} %collective-permute-done.2.far_ref, ...), custom_call_target="tpu_custom_call", output_to_operand_aliasing={{0}: (0, {}), {1}: (5, {})} | custom-call | flops 805306368 | bytes 5242880 | tf_op jit(solution)/shard_map/add_far/pallas_call | solution.py:210
  146.4 3.2 %add_far.11 = (f32[8,128]{1,0:T(8,128)S(1)}, f32[1,5,512,512]{3,2,1,0:T(8,128)}) custom-call(f32[8,128]{1,0:T(8,128)S(1)} %get-tuple-element.50.turn_ref, f32[512,512]{1,0:T(8,128)S(1)} %get-tuple-element.77.d_ref, f32[512,512]{1,0:T(8,128)S(1)} %collective-permute-done.3.far_ref, ...), custom_call_target="tpu_custom_call", output_to_operand_aliasing={{0}: (0, {}), {1}: (5, {})} | custom-call | flops 805306368 | bytes 5242880 | tf_op jit(solution)/shard_map/add_far/pallas_call | solution.py:210
  149.6 3.2 %add_far.12 = (f32[8,128]{1,0:T(8,128)S(1)}, f32[1,5,512,512]{3,2,1,0:T(8,128)}) custom-call(f32[8,128]{1,0:T(8,128)S(1)} %get-tuple-element.54.turn_ref, f32[512,512]{1,0:T(8,128)S(1)} %get-tuple-element.77.d_ref, f32[512,512]{1,0:T(8,128)S(1)} %collective-permute-done.4.far_ref, ...), custom_call_target="tpu_custom_call", output_to_operand_aliasing={{0}: (0, {}), {1}: (5, {})} | custom-call | flops 805306368 | bytes 5242880 | tf_op jit(solution)/shard_map/add_far/pallas_call | solution.py:210
  152.7 2.6 %add_far.13 = (f32[8,128]{1,0:T(8,128)S(1)}, f32[1,5,512,512]{3,2,1,0:T(8,128)}) custom-call(f32[8,128]{1,0:T(8,128)S(1)} %get-tuple-element.58.turn_ref, f32[512,512]{1,0:T(8,128)S(1)} %get-tuple-element.77.d_ref, f32[512,256]{1,0:T(8,128)} %collective-permute-done.5.far_ref, ...), custom_call_target="tpu_custom_call", output_to_operand_aliasing={{0}: (0, {}), {1}: (5, {})} | custom-call | flops 402653184 | bytes 2621440 | tf_op jit(solution)/shard_map/add_far/pallas_call | solution.py:210
  155.4 2.3 %add_far.14 = (f32[8,128]{1,0:T(8,128)S(1)}, f32[1,5,512,512]{3,2,1,0:T(8,128)}) custom-call(f32[8,128]{1,0:T(8,128)S(1)} %get-tuple-element.62.turn_ref, f32[512,512]{1,0:T(8,128)S(1)} %get-tuple-element.77.d_ref, f32[512,128]{1,0:T(8,128)S(1)} %collective-permute-done.6.far_ref, ...), custom_call_target="tpu_custom_call", output_to_operand_aliasing={{0}: (0, {}), {1}: (5, {})} | custom-call | flops 201326592 | bytes 1310720 | tf_op jit(solution)/shard_map/add_far/pallas_call | solution.py:210
  157.7 2.3 %add_far.15 = (f32[8,128]{1,0:T(8,128)S(1)}, f32[1,5,512,512]{3,2,1,0:T(8,128)}) custom-call(f32[8,128]{1,0:T(8,128)S(1)} %get-tuple-element.66.turn_ref, f32[512,512]{1,0:T(8,128)S(1)} %get-tuple-element.77.d_ref, f32[512,128]{1,0:T(8,128)S(1)} %collective-permute-done.7.far_ref, ...), custom_call_target="tpu_custom_call", output_to_operand_aliasing={{0}: (0, {}), {1}: (5, {})} | custom-call | flops 201326592 | bytes 1310720 | tf_op jit(solution)/shard_map/add_far/pallas_call | solution.py:210
  (66 shorter events, 30.6 us)
Async XLA Ops:
  0.6 30.2 %copy-start = (f32[128,20]{0,1:T(8,128)S(1)}, f32[128,20]{0,1:T(8,128)}, u32[]{:S(2)}) copy-start(f32[128,20]{0,1:T(8,128)} %param.17) | copy-start | bytes 30724
  2.9 73.0 %collective-permute-start = (f32[512,512]{1,0:T(8,128)}, f32[512,512]{1,0:T(8,128)}, u32[]{:S(2)}, u32[]{:S(2)}) collective-permute-start(f32[512,512]{1,0:T(8,128)} %slice_bitcast_fusion.4), channel_id=1, source_target_pairs={{0,4},{4,0},{1,5},{5,1},{2,6},{6,2},{3,7},{7,3},{8,12},{12,8},{9,1... | collective-permute-start | bytes 3145736 | tf_op jit(solution)/shard_map/ppermute | solution.py:265
  7.9 60.6 %all-to-all-start = ((f32[4,8,256]{2,1,0:T(8,128)}), f32[4,8,256]{2,1,0:T(8,128)}, u32[]{:S(2)}, u32[]{:S(2)}) async-start(f32[4,8,256]{2,1,0:T(8,128)} %pad_maximum_fusion), calls=%async_computation | async-start | bytes 65536 | tf_op jit(solution)/shard_map/all_to_all | solution.py:289
  14.1 123.7 %collective-permute-start.1 = (f32[512,512]{1,0:T(8,128)}, f32[512,512]{1,0:T(8,128)}, u32[]{:S(2)}, u32[]{:S(2)}) collective-permute-start(f32[512,512]{1,0:T(8,128)} %slice_bitcast_fusion.3), channel_id=1, source_target_pairs={{0,4},{4,0},{1,5},{5,1},{2,6},{6,2},{3,7},{7,3},{8,12},{12,8},{9,1... | collective-permute-start | bytes 3145736 | tf_op jit(solution)/shard_map/ppermute | solution.py:265
  16.4 14.4 %copy-start.7 = (f32[2,512,128]{2,1,0:T(8,128)S(1)}, f32[2,512,128]{2,1,0:T(8,128)}, u32[]{:S(2)}) copy-start(f32[2,512,128]{2,1,0:T(8,128)} %constant.97.clone) | copy-start | bytes 1572868
  16.4 125.9 %collective-permute-start.2 = (f32[512,512]{1,0:T(8,128)}, f32[512,512]{1,0:T(8,128)}, u32[]{:S(2)}, u32[]{:S(2)}) collective-permute-start(f32[512,512]{1,0:T(8,128)} %slice_bitcast_fusion.2), channel_id=1, source_target_pairs={{0,4},{4,0},{1,5},{5,1},{2,6},{6,2},{3,7},{7,3},{8,12},{12,8},{9,1... | collective-permute-start | bytes 3145736 | tf_op jit(solution)/shard_map/ppermute | solution.py:265
  20.8 11.2 %copy-start.9 = (s32[1,1,1,4,256]{4,3,2,1,0:T(4,128)S(1)}, s32[1,1,1,4,256]{4,3,2,1,0:T(4,128)}, u32[]{:S(2)}) copy-start(s32[1,1,1,4,256]{4,3,2,1,0:T(4,128)} %param.18) | copy-start | bytes 12292
  20.8 125.7 %collective-permute-start.3 = (f32[512,512]{1,0:T(8,128)}, f32[512,512]{1,0:T(8,128)S(1)}, u32[]{:S(2)}, u32[]{:S(2)}) collective-permute-start(f32[512,512]{1,0:T(8,128)} %slice_bitcast_fusion.1), channel_id=1, source_target_pairs={{0,4},{4,0},{1,5},{5,1},{2,6},{6,2},{3,7},{7,3},{8,12},{12,8},{9,1... | collective-permute-start | bytes 3145736 | tf_op jit(solution)/shard_map/ppermute | solution.py:265
  23.1 126.5 %collective-permute-start.4 = (f32[512,512]{1,0:T(8,128)}, f32[512,512]{1,0:T(8,128)S(1)}, u32[]{:S(2)}, u32[]{:S(2)}) collective-permute-start(f32[512,512]{1,0:T(8,128)} %slice_bitcast_fusion), channel_id=1, source_target_pairs={{0,4},{4,0},{1,5},{5,1},{2,6},{6,2},{3,7},{7,3},{8,12},{12,8},{9,1... | collective-permute-start | bytes 3145736 | tf_op jit(solution)/shard_map/ppermute | solution.py:265
  69.3 38.9 %copy-start.8 = (f32[16,512]{1,0:T(8,128)S(1)}, f32[16,512]{1,0:T(8,128)}, u32[]{:S(2)}) copy-start(f32[16,512]{1,0:T(8,128)} %pad_maximum_fusion.2) | copy-start | bytes 98308
  70.3 38.7 %copy-start.10 = (s32[1,512]{1,0:T(1,128)S(1)}, s32[1,512]{1,0:T(1,128)}, u32[]{:S(2)}) copy-start(s32[1,512]{1,0:T(1,128)} %param.22) | copy-start | bytes 6148
  70.3 39.6 %copy-start.11 = (s32[1,512]{1,0:T(1,128)S(1)}, s32[1,512]{1,0:T(1,128)}, u32[]{:S(2)}) copy-start(s32[1,512]{1,0:T(1,128)} %param.23) | copy-start | bytes 6148
  76.0 76.8 %collective-permute-start.5 = (f32[512,256]{1,0:T(8,128)}, f32[512,256]{1,0:T(8,128)}, u32[]{:S(2)}, u32[]{:S(2)}) collective-permute-start(f32[512,256]{1,0:T(8,128)} %slice_bitcast_fusion.5), channel_id=1, source_target_pairs={{0,4},{4,0},{1,5},{5,1},{2,6},{6,2},{3,7},{7,3},{8,12},{12,8},{9,1... | collective-permute-start | bytes 1572872 | tf_op jit(solution)/shard_map/ppermute | solution.py:265
  103.5 7.3 %all-to-all-start.1 = ((f32[4,2,8,128]{3,2,1,0:T(8,128)}), f32[4,2,8,128]{3,2,1,0:T(8,128)S(1)}, u32[]{:S(2)}, u32[]{:S(2)}) async-start(f32[4,2,8,128]{3,2,1,0:T(8,128)} %donor_gather.1), calls=%async_computation.1 | async-start | bytes 65536 | tf_op jit(solution)/shard_map/all_to_all | solution.py:307
  110.8 0.6 copy-start.6
  111.4 21.3 %copy-start.1 = (f32[1,3,512,512]{3,2,1,0:T(8,128)S(1)}, f32[1,3,512,512]{3,2,1,0:T(8,128)}, u32[]{:S(2)}) copy-start(f32[1,3,512,512]{3,2,1,0:T(8,128)} %media_ref.15) | copy-start | bytes 9437188
  132.7 1.2 copy-start.2
  133.9 5.2 %copy-start.3 = (f32[512,512]{1,0:T(8,128)S(1)}, f32[512,512]{1,0:T(8,128)}, u32[]{:S(2)}) copy-start(f32[512,512]{1,0:T(8,128)} %get-tuple-element.38.open_ref) | copy-start | bytes 3145732
  133.9 5.2 %copy-start.4 = (f32[1,2,512,512]{3,2,1,0:T(8,128)S(1)}, f32[1,2,512,512]{3,2,1,0:T(8,128)}, u32[]{:S(2)}) copy-start(f32[1,2,512,512]{3,2,1,0:T(8,128)} %media_ref.10) | copy-start | bytes 6291460
  137.8 4.6 %copy-start.5 = (f32[512,128]{1,0:T(8,128)S(1)}, f32[512,128]{1,0:T(8,128)}, u32[]{:S(2)}) copy-start(f32[512,128]{1,0:T(8,128)} %slice_bitcast_fusion.6) | copy-start | bytes 786436
  137.8 17.6 %collective-permute-start.6 = (f32[512,128]{1,0:T(8,128)S(1)}, f32[512,128]{1,0:T(8,128)S(1)}, u32[]{:S(2)}, u32[]{:S(2)}) collective-permute-start(f32[512,128]{1,0:T(8,128)S(1)} %slice_bitcast_fusion.7), channel_id=1, source_target_pairs={{0,4},{4,0},{1,5},{5,1},{2,6},{6,2},{3,7},{7,3},{8,12},{12,8},{9,1... | collective-permute-start | bytes 786440 | tf_op jit(solution)/shard_map/ppermute | solution.py:265
  142.3 15.3 %collective-permute-start.7 = (f32[512,128]{1,0:T(8,128)S(1)}, f32[512,128]{1,0:T(8,128)S(1)}, u32[]{:S(2)}, u32[]{:S(2)}) collective-permute-start(f32[512,128]{1,0:T(8,128)S(1)} %copy-done.5), channel_id=1, source_target_pairs={{0,4},{4,0},{1,5},{5,1},{2,6},{6,2},{3,7},{7,3},{8,12},{12,8},{9,1... | collective-permute-start | bytes 786440 | tf_op jit(solution)/shard_map/ppermute | solution.py:265

commit v2 on v1

v2 whole, which is shorter than its diff:
```python
import functools
import math

import jax
import jax.numpy as jnp
import numpy as np
from jax import lax
from jax.experimental import pallas as pl
from jax.experimental.pallas import tpu as pltpu
from jax.sharding import PartitionSpec as P

STEP = 0.25
PENALTY = 2.0
LANES = 128
VMEM_LIMIT = 56 * 1024 * 1024
FAR_VMEM_LIMIT = 24 * 1024 * 1024
HIGHEST = lax.Precision.HIGHEST


def derivative_row(period):
    n = np.arange(1, period)
    sign = np.where(n % 2 == 0, 1.0, -1.0)
    row = np.zeros(period)
    row[1:] = (math.pi / period) * sign / np.tan(math.pi * n / period)
    return row


def operator_tables(rows, slabs, cont):
    points = rows * slabs
    period = points + cont
    row = derivative_row(period)
    j = np.arange(rows)
    own = row[(j[:, None] - j[None, :]) % period]
    far, tail = [], []
    for me in range(slabs):
        mine = me * rows + j[:, None]
        others = np.concatenate([(me - d) % slabs * rows + j for d in range(1, slabs)])
        far.append(row[(mine - others[None, :]) % period])
        tail.append(row[(mine - points - np.arange(cont)[None, :]) % period])
    return tuple(np.asarray(table, np.float32) for table in (own, far, tail))


def continuation_on(cont_matrix, rows, slabs, sources):
    match = cont_matrix.shape[1] // 2
    on_last = jnp.pad(cont_matrix[:, :match], ((0, 0), (rows - match, 0)))
    on_first = jnp.pad(cont_matrix[:, match:], ((0, 0), (0, rows - match)))
    return jnp.concatenate(
        [
            jnp.where(source == slabs - 1, on_last, 0.0) + jnp.where(source == 0, on_first, 0.0)
            for source in sources
        ],
        axis=1,
    )


def split(value, size):
    if size & (size - 1) == 0:
        return lax.shift_right_logical(value, size.bit_length() - 1), value & (size - 1)
    return lax.div(value, size), lax.rem(value, size)


def take_kernel(pieces, elastic_ref, acoustic_ref, after_ref, *refs):
    del after_ref
    outs, semaphores = refs[: len(pieces)], refs[-1]
    copies = []
    for i, (name, field, at, width) in enumerate(pieces):
        source = elastic_ref if name == "el" else acoustic_ref
        copies.append(
            pltpu.make_async_copy(source.at[0, field, :, pl.ds(at, width)], outs[i], semaphores.at[i])
        )
    for copy in copies:
        copy.start()
    return copies


def take_only_kernel(pieces, *refs):
    for copy in take_kernel(pieces, *refs):
        copy.wait()


def take_and_edges_kernel(pieces, layers, elastic_ref, acoustic_ref, after_ref, *refs):
    n = len(pieces)
    edges_ref, tiles, edge_semaphores, semaphores = refs[n:]
    n_el, n_ac = elastic_ref.shape[1], acoustic_ref.shape[1]
    rows, depth = elastic_ref.shape[2:]
    loads = []
    for end, at in enumerate((0, depth - LANES)):
        for k, (source, first, count) in enumerate(((elastic_ref, 0, n_el), (acoustic_ref, n_el, n_ac))):
            loads.append(
                pltpu.make_async_copy(
                    source.at[0, :, :, pl.ds(at, LANES)],
                    tiles.at[end, pl.ds(first, count)],
                    edge_semaphores.at[2 * end + k],
                )
            )
    for load in loads:
        load.start()
    copies = take_kernel(pieces, elastic_ref, acoustic_ref, after_ref, *refs[:n], semaphores)
    for load in loads:
        load.wait()
    lane = lax.broadcasted_iota(jnp.int32, (rows, LANES), 1)
    columns = jnp.zeros((rows, LANES), jnp.float32)
    for f in range(n_el + n_ac):
        columns = jnp.where(lane == f, tiles[0, f, :, 0:1], columns)
        columns = jnp.where(lane == 8 + f, tiles[1, f, :, LANES - 1 : LANES], columns)
    lines = columns.T
    below = lax.rem(lax.axis_index("layer") + 1, layers)
    for to in range(layers):
        edges_ref[to] = jnp.where(to == below, lines[8:16], lines[0:8])
    for copy in copies:
        copy.wait()


def take_pieces(elastic, acoustic, after, pieces, layers=0):
    rows = elastic.shape[2]
    anywhere = pl.BlockSpec(memory_space=pl.ANY)
    out_shape = [jax.ShapeDtypeStruct((rows, width), jnp.float32) for _, _, _, width in pieces]
    out_specs = [anywhere] * len(pieces)
    scratch = [pltpu.SemaphoreType.DMA((len(pieces),))]
    kernel = functools.partial(take_only_kernel, pieces)
    if layers:
        out_shape.append(jax.ShapeDtypeStruct((layers, 8, rows), jnp.float32))
        out_specs.append(pl.BlockSpec(memory_space=pltpu.VMEM))
        scratch = [pltpu.VMEM((2, 8, rows, LANES), jnp.float32), pltpu.SemaphoreType.DMA((4,))] + scratch
        kernel = functools.partial(take_and_edges_kernel, pieces, layers)
    cells = sum(width for _, _, _, width in pieces) * rows
    return pl.pallas_call(
        kernel,
        in_specs=[anywhere] * 3,
        out_specs=out_specs,
        out_shape=out_shape,
        scratch_shapes=scratch,
        compiler_params=pltpu.CompilerParams(vmem_limit_bytes=VMEM_LIMIT),
        cost_estimate=pl.CostEstimate(flops=0, bytes_accessed=8 * cells, transcendentals=0),
        name="take_pieces",
    )(elastic, acoustic, after)


def gather_kernel(fields, rows, depth, words_ref, weights_ref, elastic_ref, acoustic_ref, out_ref, mixed):
    n_el = elastic_ref.shape[1]
    chunks = depth // LANES
    for f in range(fields):
        source = elastic_ref.at[0, f] if f < n_el else acoustic_ref.at[0, f - n_el]
        for c in range(chunks):
            mixed[pl.ds((c * fields + f) * rows, rows), :] = source[:, c * LANES : (c + 1) * LANES]
    lane = lax.broadcasted_iota(jnp.int32, (fields, LANES), 1)
    groups = out_ref.shape[1]

    def one_group(step, carry):
        patch, group = split(step, groups)

        def one_slot(r, values):
            slot = group * LANES + r
            total = None
            for s in range(4):
                start, at = split(words_ref[patch, s, slot], LANES)
                picked = mixed[pl.ds(start, fields, stride=rows), :]
                term = jnp.where(lane == at, picked * weights_ref[patch, 4 + s, slot], 0.0)
                total = term if total is None else total + term
            column = jnp.sum(total, axis=1, keepdims=True)
            return jnp.where(lane == r, column, values)

        values = lax.fori_loop(0, LANES, one_slot, jnp.zeros((fields, LANES), jnp.float32), unroll=16)
        out_ref[patch, group] = values
        return carry

    lax.fori_loop(0, out_ref.shape[0] * groups, one_group, 0)


def bf16_pair(value):
    high = value.astype(jnp.bfloat16)
    return high, (value - high.astype(jnp.float32)).astype(jnp.bfloat16)


def three_left(value):
    high, low = bf16_pair(value)
    return jnp.concatenate([high, high, low], axis=1)


def three_right(value):
    high, low = bf16_pair(value)
    return jnp.concatenate([high, low, high], axis=0)


def near_kernel(
    n_el, me_ref, own_ref, far_ref, tail_ref, own_cont_ref, far_cont_ref, elastic_ref, acoustic_ref,
    out_ref, far_operator_ref, operator,
):
    del me_ref

    @pl.when(pl.program_id(0) == 0)
    def _():
        def folded(table, cont):
            return table + jnp.dot(tail_ref[0], cont, precision=HIGHEST, preferred_element_type=jnp.float32)

        operator[...] = three_left(folded(own_ref[...], own_cont_ref[...]))
        far_operator_ref[...] = three_left(folded(far_ref[0], far_cont_ref[...]))

    value = jnp.where(pl.program_id(0) < n_el, elastic_ref[0, 0], acoustic_ref[0, 0])
    out_ref[0] = jnp.dot(operator[...], three_right(value), preferred_element_type=jnp.float32)


def near_derivatives(elastic, acoustic, cont_matrix, me, slabs):
    rows, depth = elastic.shape[2:]
    cont = cont_matrix.shape[0]
    reach = (slabs - 1) * rows
    own, far, tail = operator_tables(rows, slabs, cont)
    own_cont = continuation_on(cont_matrix, rows, slabs, [me])
    far_cont = continuation_on(cont_matrix, rows, slabs, [(me - d) % slabs for d in range(1, slabs)])
    return pl.pallas_call(
        functools.partial(near_kernel, 4),
        grid_spec=pltpu.PrefetchScalarGridSpec(
            num_scalar_prefetch=1,
            grid=(6,),
            in_specs=[
                pl.BlockSpec((rows, rows), lambda f, me: (0, 0)),
                pl.BlockSpec((1, rows, reach), lambda f, me: (me[0], 0, 0)),
                pl.BlockSpec((1, rows, cont), lambda f, me: (me[0], 0, 0)),
                pl.BlockSpec((cont, rows), lambda f, me: (0, 0)),
                pl.BlockSpec((cont, reach), lambda f, me: (0, 0)),
                pl.BlockSpec((1, 1, rows, depth), lambda f, me: (0, jnp.where(f < 3, f, 4), 0, 0)),
                pl.BlockSpec((1, 1, rows, depth), lambda f, me: (0, jnp.maximum(f - 4, 0), 0, 0)),
            ],
            out_specs=[
                pl.BlockSpec((1, rows, depth), lambda f, me: (f, 0, 0)),
                pl.BlockSpec((rows, 3 * reach), lambda f, me: (0, 0)),
            ],
            scratch_shapes=[pltpu.VMEM((rows, 3 * rows), jnp.bfloat16)],
        ),
        out_shape=[
            jax.ShapeDtypeStruct((6, rows, depth), jnp.float32),
            jax.ShapeDtypeStruct((rows, 3 * reach), jnp.bfloat16),
        ],
        compiler_params=pltpu.CompilerParams(vmem_limit_bytes=VMEM_LIMIT),
        cost_estimate=pl.CostEstimate(
            flops=36 * rows * rows * depth, bytes_accessed=60 * rows * depth, transcendentals=0
        ),
        name="near_dx",
    )(me.reshape(1), own, far, tail, own_cont, far_cont, elastic, acoustic)


def section_kernel(
    layers, rows, depth, tile,
    cells_ref, counts_ref, interp_ref,
    dx_ref, elastic_ref, acoustic_ref, el_media_ref, ac_media_ref, edges_ref, el_pair_ref, ac_pair_ref,
    new_el_ref, new_ac_ref, open_ref,
    columns,
):
    step = pl.program_id(0)
    here = pl.ds(pl.multiple_of(step * tile, tile), tile)
    lane = lax.broadcasted_iota(jnp.int32, (tile, depth), 1)
    layer = lax.axis_index("layer")
    at_top, at_bottom = layer == 0, layer == layers - 1
    from_above = edges_ref[lax.rem(layer + layers - 1, layers)]
    from_below = edges_ref[lax.rem(layer + 1, layers)]
    ocean_row = from_above[5:6]
    basin_row = from_below[1:2]

    @pl.when(step == 0)
    def _():
        pairs = jnp.concatenate([el_pair_ref[...], ac_pair_ref[...]]).astype(jnp.float32)
        lines = [
            jnp.where(at_top, 0.0, from_above),
            jnp.where(at_bottom, 0.0, from_below),
            pairs,
            jnp.zeros((LANES - 18, rows), jnp.float32),
        ]
        columns[...] = jnp.concatenate(lines).T

    halo = columns[here, :]

    def dz(value, slot):
        above = halo[:, slot : slot + 1]
        below = halo[:, 8 + slot : 9 + slot]
        following = jnp.where(lane == depth - 1, below, pltpu.roll(value, depth - 1, 1))
        previous = jnp.where(lane == 0, above, pltpu.roll(value, 1, 1))
        return (following - previous) * 0.5

    vx, vz, sxx, szz, sxz = [elastic_ref[0, f] for f in range(5)]
    p, ovx, ovz = [acoustic_ref[0, f] for f in range(3)]
    buoyancy = el_media_ref[0, 0]
    lame = el_media_ref[0, 1]
    shear = el_media_ref[0, 2]
    stiffness = lame + 2.0 * shear
    bulk = ac_media_ref[0, 0]
    ocean_buoyancy = ac_media_ref[0, 1]

    dx_vx = dx_ref[0]
    dz_vz = dz(vz, 1)
    new_el_ref[0, 0, here, :] = vx + STEP * (buoyancy * (dx_ref[2] + dz(sxz, 4)))
    new_el_ref[0, 1, here, :] = vz + STEP * (buoyancy * (dx_ref[3] + dz(szz, 3)))
    new_el_ref[0, 2, here, :] = sxx + STEP * (stiffness * dx_vx + lame * dz_vz)
    choose = lax.broadcasted_iota(jnp.int32, (tile, rows), 1).astype(jnp.float32)
    pressure = jnp.sum(jnp.where(halo[:, 16:17] == choose, ocean_row, 0.0), axis=1, keepdims=True)
    velocity = jnp.sum(jnp.where(halo[:, 17:18] == choose, basin_row, 0.0), axis=1, keepdims=True)
    rate_szz = lame * dx_vx + stiffness * dz_vz
    rate_szz = rate_szz + jnp.where((lane == 0) & at_top, PENALTY * (-pressure - szz), 0.0)
    new_el_ref[0, 3, here, :] = szz + STEP * rate_szz
    new_el_ref[0, 4, here, :] = sxz + STEP * (shear * (dz(vx, 0) + dx_ref[1]))
    new_ac_ref[0, 0, here, :] = p - STEP * (bulk * (dx_ref[5] + dz(ovz, 7)))
    new_ac_ref[0, 1, here, :] = ovx - STEP * (ocean_buoyancy * dx_ref[4])
    rate_ovz = -ocean_buoyancy * dz(p, 5)
    rate_ovz = rate_ovz + jnp.where((lane == depth - 1) & at_bottom, PENALTY * (velocity - ovz), 0.0)
    new_ac_ref[0, 2, here, :] = ovz + STEP * rate_ovz
    open_ref[here, :] = jnp.ones((tile, depth), jnp.float32)

    @pl.when(step == pl.num_programs(0) - 1)
    def _():
        place = lax.broadcasted_iota(jnp.int32, (8, LANES), 0) * LANES
        place = place + lax.broadcasted_iota(jnp.int32, (8, LANES), 1)
        n_el = new_el_ref.shape[1]

        def one_patch(q, carry):
            def one_slot(r, inner):
                x, z = split(cells_ref[0, 0, 0, q, r], depth)
                (high, row), (low, at) = split(x, 8), split(z, LANES)
                at_row = pl.ds(pl.multiple_of(high * 8, 8), 8)
                at_lane = pl.ds(pl.multiple_of(low * LANES, LANES), LANES)
                hit = place == row * LANES + at
                group, within = split(r, LANES)
                for f in range(8):
                    target = new_el_ref.at[0, f] if f < n_el else new_ac_ref.at[0, f - n_el]
                    target[at_row, at_lane] = jnp.where(hit, interp_ref[q, group, f, within], target[at_row, at_lane])
                open_ref[at_row, at_lane] = jnp.where(hit, 0.0, open_ref[at_row, at_lane])
                return inner

            return lax.fori_loop(0, counts_ref[0, 0, 0, q], one_slot, carry)

        lax.fori_loop(0, counts_ref.shape[3], one_patch, 0)


def far_kernel(coefficients, turn_ref, d_ref, far_ref, media_ref, open_ref, base_ref, next_ref, out_ref):
    del turn_ref, next_ref
    far = jnp.dot(d_ref[...], three_right(far_ref[...]), preferred_element_type=jnp.float32)
    media = [media_ref[0, i] for i in range(media_ref.shape[1])]
    is_open = open_ref[...] > 0.5
    for i, coefficient in enumerate(coefficients):
        old = base_ref[0, i]
        out_ref[0, i] = jnp.where(is_open, old + (STEP * coefficient(*media)) * far, old)


def add_far(base, operator, far, at, media, first_media, n_media, first_field, coefficients, opened, turn):
    rows, reach = operator.shape[0], far.shape[0]
    width = far.shape[1]
    tile = math.gcd(math.gcd(width, at), 2 * LANES)
    n_out = len(coefficients)
    shift = at // tile
    return pl.pallas_call(
        functools.partial(far_kernel, coefficients),
        grid=(width // tile,),
        in_specs=[
            pl.BlockSpec(memory_space=pl.ANY),
            pl.BlockSpec((rows, 3 * reach), lambda i: (0, 0)),
            pl.BlockSpec((reach, tile), lambda i: (0, i)),
            pl.BlockSpec((1, n_media, rows, tile), lambda i: (0, first_media // n_media, 0, i + shift)),
            pl.BlockSpec((rows, tile), lambda i: (0, i + shift)),
            pl.BlockSpec((1, n_out, rows, tile), lambda i: (0, first_field // n_out, 0, i + shift)),
        ],
        out_specs=[
            pl.BlockSpec(memory_space=pl.ANY),
            pl.BlockSpec((1, n_out, rows, tile), lambda i: (0, first_field // n_out, 0, i + shift)),
        ],
        out_shape=[
            jax.ShapeDtypeStruct(turn.shape, turn.dtype),
            jax.ShapeDtypeStruct(base.shape, base.dtype),
        ],
        input_output_aliases={0: 0, 5: 1},
        compiler_params=pltpu.CompilerParams(vmem_limit_bytes=FAR_VMEM_LIMIT),
        cost_estimate=pl.CostEstimate(
            flops=6 * rows * reach * width,
            bytes_accessed=4 * rows * width * (3 + n_media + n_out),
            transcendentals=0,
        ),
        name="add_far",
    )(turn, operator, far, media, opened, base)


def per_device(
    elastic,
    acoustic,
    el_media,
    ac_media,
    cont_matrix,
    fringe_cells,
    donor_cells,
    donor_weights,
    donor_counts,
    el_pair,
    ac_pair,
):
    rows, depth = elastic.shape[2], elastic.shape[3]
    slabs = lax.axis_size("line")
    layers = lax.axis_size("layer")
    patches = lax.axis_size("patch")
    slots = fringe_cells.shape[-1]
    groups = slots // LANES
    me = lax.axis_index("line")
    layer = lax.axis_index("layer")
    tile = min(64, rows)

    def other_slabs(value):
        parts = [
            lax.ppermute(value, "line", [(i, (i + distance) % slabs) for i in range(slabs)])
            for distance in range(1, slabs)
        ]
        return parts[0] if slabs == 2 else jnp.concatenate(parts, axis=0)

    half, quarter = depth // 2, depth // 4
    pieces = [
        ("el", 0, 0, depth, "el", 0, 3, 2, (lambda b, l, m: l + 2.0 * m, lambda b, l, m: l)),
        ("ac", 0, 0, depth, "ac", 1, 1, 1, (lambda b: -b,)),
        ("ac", 1, 0, depth, "ac", 0, 1, 0, (lambda k: -k,)),
        ("el", 1, 0, depth, "el", 2, 1, 4, (lambda m: m,)),
        ("el", 2, 0, depth, "el", 0, 1, 0, (lambda b: b,)),
        ("el", 4, 0, half, "el", 0, 1, 1, (lambda b: b,)),
        ("el", 4, half, quarter, "el", 0, 1, 1, (lambda b: b,)),
        ("el", 4, half + quarter, quarter, "el", 0, 1, 1, (lambda b: b,)),
    ]
    travelling = [piece[:4] for piece in pieces]
    (first,) = take_pieces(elastic, acoustic, cont_matrix, travelling[:1])
    *others, edges = take_pieces(elastic, acoustic, first, travelling[1:], layers)
    far = [other_slabs(value) for value in [first, *others]]

    x, z = split(donor_cells[0, 0, 0], depth)
    chunk, at_lane = split(z, LANES)
    words = (chunk * (8 * rows) + x) * LANES + at_lane
    asked = jnp.concatenate([words.astype(jnp.float32), donor_weights[0, 0, 0]], axis=1)
    asked = lax.all_to_all(asked, "patch", split_axis=0, concat_axis=0, tiled=True)
    asked_words = asked[:, :4].astype(jnp.int32)

    smem = pl.BlockSpec(memory_space=pltpu.SMEM)
    vmem = pl.BlockSpec(memory_space=pltpu.VMEM)
    local = pl.pallas_call(
        functools.partial(gather_kernel, 8, rows, depth),
        in_specs=[smem, smem, vmem, vmem],
        out_specs=vmem,
        out_shape=jax.ShapeDtypeStruct((patches, groups, 8, LANES), jnp.float32),
        scratch_shapes=[pltpu.VMEM((8 * rows * (depth // LANES), LANES), jnp.float32)],
        compiler_params=pltpu.CompilerParams(vmem_limit_bytes=VMEM_LIMIT),
        cost_estimate=pl.CostEstimate(flops=10**9, bytes_accessed=32 * rows * depth, transcendentals=0),
        name="donor_gather",
    )(asked_words, asked, elastic, acoustic)
    interp = lax.all_to_all(local, "patch", split_axis=0, concat_axis=0, tiled=True)
    edges = lax.all_to_all(edges, "layer", split_axis=0, concat_axis=0, tiled=True)

    near, far_operator = near_derivatives(elastic, acoustic, cont_matrix, me, slabs)
    new_el, new_ac, opened = pl.pallas_call(
        functools.partial(section_kernel, layers, rows, depth, tile),
        grid=(rows // tile,),
        in_specs=[
            smem,
            smem,
            smem,
            pl.BlockSpec((6, tile, depth), lambda i: (0, i, 0)),
            pl.BlockSpec((1, 5, tile, depth), lambda i: (0, 0, i, 0)),
            pl.BlockSpec((1, 3, tile, depth), lambda i: (0, 0, i, 0)),
            pl.BlockSpec((1, 3, tile, depth), lambda i: (0, 0, i, 0)),
            pl.BlockSpec((1, 2, tile, depth), lambda i: (0, 0, i, 0)),
            vmem,
            vmem,
            vmem,
        ],
        out_specs=[vmem, vmem, vmem],
        out_shape=[
            jax.ShapeDtypeStruct(elastic.shape, jnp.float32),
            jax.ShapeDtypeStruct(acoustic.shape, jnp.float32),
            jax.ShapeDtypeStruct((rows, depth), jnp.float32),
        ],
        scratch_shapes=[pltpu.VMEM((rows, LANES), jnp.float32)],
        compiler_params=pltpu.CompilerParams(vmem_limit_bytes=VMEM_LIMIT),
        cost_estimate=pl.CostEstimate(
            flops=100 * rows * depth, bytes_accessed=112 * rows * depth, transcendentals=0
        ),
        name="near_section",
    )(
        fringe_cells,
        donor_counts,
        interp,
        near,
        elastic,
        acoustic,
        el_media,
        ac_media,
        edges,
        el_pair,
        ac_pair,
    )

    turn = jnp.zeros((8, LANES), jnp.float32)
    section = {"el": new_el, "ac": new_ac}
    media = {"el": el_media, "ac": ac_media}
    for value, (_, _, at, _, target, first_media, n_media, first_field, coefficients) in zip(far, pieces):
        turn, section[target] = add_far(
            section[target], far_operator, value, at,
            media[target], first_media, n_media, first_field, coefficients, opened, turn,
        )
    return section["el"], section["ac"]


def solution(mesh):
    placed = (
        P("patch", None, "line", "layer"),
        P("patch", None, "line", "layer"),
        P("patch", None, "line", "layer"),
        P("patch", None, "line", "layer"),
        P(),
        P("patch", "line", "layer", None, None),
        P("patch", "line", "layer", None, None, None),
        P("patch", "line", "layer", None, None, None),
        P("patch", "line", "layer", None),
        P("patch", "line"),
        P("patch", "line"),
    )
    return jax.shard_map(
        per_device,
        mesh=mesh,
        in_specs=placed,
        out_specs=(P("patch", None, "line", "layer"), P("patch", None, "line", "layer")),
        check_vma=False,
    )
```

time: 162 us -> 321 us (1.98)
  Pallas kernels: 82.5 us -> 284 us
  local copies, waits for them, and re-layouts: 38.7 us -> 3.41 us
  blocking collectives: 13.7 us -> 0 us
  waiting for transfers between devices: 0.03 us -> 9.08 us
  other arithmetic: 7.02 us -> 2.15 us
  starting transfers between devices: 17 us -> 21.2 us
    pallas_call x3 -> x5, Pallas kernels: 58.6 us -> 260 us  [the longest x2 194 us: take_pieces(): pl.pallas_call(kernel, in_specs=[anywhere] * 3, out_specs=out_specs, out_...]
    reshape x10 -> x0, local copies, waits for them, and re-layouts: 19.9 us -> none  [the longest x8 16 us: per_device(): lax.slice(source[name], (0, field, 0, at), (1, field + 1, rows, at + width))]
    all_gather x1 -> x0, blocking collectives: 13.7 us -> none  [per_device(): edges = lax.all_gather(jnp.concatenate([top, bottom]), 'layer')]
    slice x4 -> x1, local copies, waits for them, and re-layouts: 7.07 us -> 0.08 us  [continuation_on(): on_first = jnp.pad(cont_matrix[:, match:], ((0, 0), (0, rows - match)))]
    ppermute x8, waiting for transfers between devices: 0.02 us -> 6.05 us  [other_slabs(): lax.ppermute(value, 'line', [(i, (i + distance) % slabs) for i in range(s...]
    all_to_all x0 -> x1, starting transfers between devices: none -> 4.89 us  [per_device(): lax.all_to_all(edges, 'layer', split_axis=0, concat_axis=0, tiled=True)]
  transfers between devices with their start and end apart: 10 -> 11, of which waited for: 0 -> 4; matrix products, arithmetic and copies ran while one was open for 26% -> 1% of each run, Pallas kernels for 50% -> 78%
where the time goes in v2:
time: 321 us
  Pallas kernels  284 us (88%)
  starting transfers between devices  21.2 us (7%)
  waiting for transfers between devices  9.08 us (3%)
  local copies, waits for them, and re-layouts  3.41 us (1%)
    pallas_call x2, Pallas kernels, take_pieces(): pl.pallas_call(kernel, in_specs=[anywhere] * 3, out_specs=out_specs, out_...  194 us
    pallas_call x1, Pallas kernels, per_device(): pl.pallas_call(functools.partial(gather_kernel, 8, rows, depth), in_specs...  27.2 us
    pallas_call x1, Pallas kernels, per_device(): pl.pallas_call(functools.partial(section_kernel, layers, rows, depth, til...  26.8 us
    pallas_call x8, Pallas kernels, add_far(): pl.pallas_call(functools.partial(far_kernel, coefficients), grid=(width /...  23.7 us
    pallas_call x1, Pallas kernels, near_derivatives(): pl.pallas_call(functools.partial(near_kernel, 4), grid_spec=pltpu.Prefetc...  12.8 us
    ppermute x8, starting transfers between devices, other_slabs(): lax.ppermute(value, 'line', [(i, (i + distance) % slabs) for i in range(s...  9.8 us
  transfers between devices with their start and end apart: 11, of which 4 were waited for; matrix products, arithmetic and copies ran while one was open for 1% of the time, Pallas kernels for 78%

profile of v2, /device:TPU:0, one launch (start us, length us, event | category | flops | bytes accessed | tf_op | source)
XLA Modules:
  0.0 320.6 jit_solution(14537434606642441586)
XLA Ops:
  0.7 1.4 copy.32.refs_2_
  2.1 32.9 %take_pieces.2.after_ref = f32[512,512]{1,0:T(8,128)} custom-call(f32[1,5,512,512]{3,2,1,0:T(8,128)} %elastic_ref.7, f32[1,3,512,512]{3,2,1,0:T(8,128)} %acoustic_ref.7, f32[128,20]{1,0:T(8,128)} %copy.32.refs_2_), custom_call_target="tpu_custom_call" | custom-call | bytes 2097152 | tf_op jit(solution)/shard_map/take_pieces/pallas_call | solution.py:127
  35.0 3.0 collective-permute-start
  38.7 3.3 %all-to-all-start = ((f32[4,8,256]{2,1,0:T(8,128)}), f32[4,8,256]{2,1,0:T(8,128)S(1)}, u32[]{:S(2)}, u32[]{:S(2)}) async-start(f32[4,8,256]{2,1,0:T(8,128)} %pad_maximum_fusion), calls=%async_computation | async-start | bytes 65536 | tf_op jit(solution)/shard_map/all_to_all | solution.py:428
  41.9 160.7 %take_pieces.3 = (f32[512,512]{1,0:T(8,128)}, f32[512,512]{1,0:T(8,128)}, f32[512,512]{1,0:T(8,128)}, f32[512,512]{1,0:T(8,128)}, f32[512,256]{1,0:T(8,128)}, /*...) custom-call(f32[1,5,512,512]{3,2,1,0:T(8,128)} %elastic_ref.7, f32[1,3,512,512]{3,2,1,0:T(8,128)} %acoustic_ref.7, ...), custom_call_target="tpu_custom_call" | custom-call | bytes 10485760 | tf_op jit(solution)/shard_map/take_pieces/pallas_call | solution.py:127
  202.7 2.0 collective-permute-start.2
  204.8 1.9 collective-permute-start.4
  207.4 27.2 %donor_gather.1 = f32[4,2,8,128]{3,2,1,0:T(8,128)} custom-call(s32[4,4,256]{2,1,0:T(4,128)} %slice_convert_fusion.words_ref, f32[4,8,256]{2,1,0:T(8,128)} %copy-done.6, f32[1,5,512,512]{3,2,1,0:T(8,128)} %elastic_ref.7, f32[1,3,512,512]{3,2,1,0:T(8,128)} %acoustic_ref.7), custom_call_target="tpu_custom_call" | custom-call | flops 1000000000 | bytes 8388608 | tf_op jit(solution)/shard_map/donor_gather/pallas_call | solution.py:433
  234.6 3.3 %all-to-all-start.1 = ((f32[4,2,8,128]{3,2,1,0:T(8,128)}), f32[4,2,8,128]{3,2,1,0:T(8,128)S(1)}, u32[]{:S(2)}, u32[]{:S(2)}) async-start(f32[4,2,8,128]{3,2,1,0:T(8,128)} %donor_gather.1), calls=%async_computation.1 | async-start | bytes 65536 | tf_op jit(solution)/shard_map/all_to_all | solution.py:443
  238.8 3.0 all-to-all-done.1.interp_ref
  241.8 4.9 %all-to-all-start.2 = ((f32[4,8,512]{2,1,0:T(8,128)}), f32[4,8,512]{2,1,0:T(8,128)S(1)}, u32[]{:S(2)}, u32[]{:S(2)}) async-start(f32[4,8,512]{2,1,0:T(8,128)} %get-tuple-element.32), calls=%async_computation.2 | async-start | bytes 131072 | tf_op jit(solution)/shard_map/all_to_all | solution.py:444
  247.2 12.8 %near_dx.1 = (f32[6,512,512]{2,1,0:T(8,128)}, bf16[512,1536]{1,0:T(8,128)(2,1)}) custom-call(s32[1]{0:T(128)} %bitcast.me_ref, f32[512,512]{1,0:T(8,128)} %constant.45.clone.own_ref, f32[2,512,512]{2,1,0:T(8,128)} %constant.46.clone.far_ref, f32[2,512,128]{2,1,0:T(8,128)} %constant.47.clone.tail_ref, f32[128,512]{1,0:T(8,128)} %get-tuple-element.59.own_cont_ref, ...), custom_call_target="tpu_custom_call" | custom-call | flops 4831838208 | bytes 15728640 | tf_op jit(solution)/shard_map/near_dx/pallas_call | solution.py:210
  260.6 26.8 %near_section.1 = (f32[1,5,512,512]{3,2,1,0:T(8,128)}, f32[1,3,512,512]{3,2,1,0:T(8,128)}, f32[512,512]{1,0:T(8,128)}) custom-call(s32[1,1,1,4,256]{4,3,2,1,0:T(4,128)} %cells_ref.1, s32[1,1,1,4]{3,2,1,0:T(1,128)} %counts_ref.1, f32[4,2,8,128]{3,2,1,0:T(8,128)} %copy-done.7, f32[6,512,512]{2,1,0:T(8,128)} %get-tuple-element.31.dx_ref, ...), custom_call_target="tpu_custom_call" | custom-call | flops 26214400 | bytes 29360128 | tf_op jit(solution)/shard_map/near_section/pallas_call | solution.py:447
  288.7 3.9 %add_far.8 = (f32[8,128]{1,0:T(8,128)S(1)}, f32[1,5,512,512]{3,2,1,0:T(8,128)}) custom-call(f32[8,128]{1,0:T(8,128)S(1)} %broadcast_in_dim.10.turn_ref, bf16[512,1536]{1,0:T(8,128)(2,1)S(1)} %copy-done.1, f32[512,512]{1,0:T(8,128)} %collective-permute-done.far_ref, f32[1,3,512,512]{3,2,1,0:T(8,128)S(1)} %copy-done, ...), custom_call_target="tpu_custom_call", output_to_operand_aliasing={{0}: (0, {}), {1}: (5, {})} | custom-call | flops 805306368 | bytes 8388608 | tf_op jit(solution)/shard_map/add_far/pallas_call | solution.py:348
  293.2 3.2 add_far.9
  296.4 1.6 collective-permute-start.7
  298.0 3.1 add_far.10
  301.1 3.1 add_far.11
  304.2 3.1 add_far.12
  307.6 2.6 add_far.13
  310.2 2.9 collective-permute-done.6.far_ref
  313.1 2.3 add_far.14
  315.4 2.9 collective-permute-done.7.far_ref
  318.3 2.3 add_far.15
  (42 shorter events, 5.6 us)
Async XLA Ops:
  0.6 37.4 %copy-start.8 = (s32[1,1,1,4,4,256]{5,4,3,2,1,0:T(4,128)S(1)}, s32[1,1,1,4,4,256]{5,4,3,2,1,0:T(4,128)}, u32[]{:S(2)}) copy-start(s32[1,1,1,4,4,256]{5,4,3,2,1,0:T(4,128)} %param.20) | copy-start | bytes 49156
  0.6 37.4 %copy-start.9 = (f32[1,1,1,4,4,256]{5,4,3,2,1,0:T(4,128)S(1)}, f32[1,1,1,4,4,256]{5,4,3,2,1,0:T(4,128)}, u32[]{:S(2)}) copy-start(f32[1,1,1,4,4,256]{5,4,3,2,1,0:T(4,128)} %param.21) | copy-start | bytes 49156
  35.0 171.8 %copy-start.4 = (f32[128,20]{1,0:T(8,128)S(1)}, f32[128,20]{1,0:T(8,128)}, u32[]{:S(2)}) copy-start(f32[128,20]{1,0:T(8,128)} %copy.32.refs_2_) | copy-start | bytes 30724
  35.0 211.7 %collective-permute-start = (f32[512,512]{1,0:T(8,128)}, f32[512,512]{1,0:T(8,128)}, u32[]{:S(2)}, u32[]{:S(2)}) collective-permute-start(f32[512,512]{1,0:T(8,128)} %take_pieces.2.after_ref), channel_id=1, source_target_pairs={{0,4},{4,0},{1,5},{5,1},{2,6},{6,2},{3,7},{7,3},{8,12},{12,8},{9,1... | collective-permute-start | bytes 3145736 | tf_op jit(solution)/shard_map/ppermute | solution.py:403
  38.7 168.1 %all-to-all-start = ((f32[4,8,256]{2,1,0:T(8,128)}), f32[4,8,256]{2,1,0:T(8,128)S(1)}, u32[]{:S(2)}, u32[]{:S(2)}) async-start(f32[4,8,256]{2,1,0:T(8,128)} %pad_maximum_fusion), calls=%async_computation | async-start | bytes 65536 | tf_op jit(solution)/shard_map/all_to_all | solution.py:428
  202.6 90.0 %collective-permute-start.1 = (f32[512,512]{1,0:T(8,128)}, f32[512,512]{1,0:T(8,128)}, u32[]{:S(2)}, u32[]{:S(2)}) collective-permute-start(f32[512,512]{1,0:T(8,128)} %get-tuple-element.36), channel_id=1, source_target_pairs={{0,4},{4,0},{1,5},{5,1},{2,6},{6,2},{3,7},{7,3},{8,12},{12,8},{9,1... | collective-permute-start | bytes 3145736 | tf_op jit(solution)/shard_map/ppermute | solution.py:403
  202.7 93.7 %collective-permute-start.2 = (f32[512,512]{1,0:T(8,128)}, f32[512,512]{1,0:T(8,128)S(1)}, u32[]{:S(2)}, u32[]{:S(2)}) collective-permute-start(f32[512,512]{1,0:T(8,128)} %get-tuple-element.39), channel_id=1, source_target_pairs={{0,4},{4,0},{1,5},{5,1},{2,6},{6,2},{3,7},{7,3},{8,12},{12,8},{9,1... | collective-permute-start | bytes 3145736 | tf_op jit(solution)/shard_map/ppermute | solution.py:403
  204.7 96.4 %collective-permute-start.3 = (f32[512,512]{1,0:T(8,128)}, f32[512,512]{1,0:T(8,128)S(1)}, u32[]{:S(2)}, u32[]{:S(2)}) collective-permute-start(f32[512,512]{1,0:T(8,128)} %get-tuple-element.42), channel_id=1, source_target_pairs={{0,4},{4,0},{1,5},{5,1},{2,6},{6,2},{3,7},{7,3},{8,12},{12,8},{9,1... | collective-permute-start | bytes 3145736 | tf_op jit(solution)/shard_map/ppermute | solution.py:403
  204.8 99.4 %collective-permute-start.4 = (f32[512,512]{1,0:T(8,128)}, f32[512,512]{1,0:T(8,128)S(1)}, u32[]{:S(2)}, u32[]{:S(2)}) collective-permute-start(f32[512,512]{1,0:T(8,128)} %get-tuple-element.45), channel_id=1, source_target_pairs={{0,4},{4,0},{1,5},{5,1},{2,6},{6,2},{3,7},{7,3},{8,12},{12,8},{9,1... | collective-permute-start | bytes 3145736 | tf_op jit(solution)/shard_map/ppermute | solution.py:403
  206.8 0.6 copy-start.6
  234.6 7.2 %all-to-all-start.1 = ((f32[4,2,8,128]{3,2,1,0:T(8,128)}), f32[4,2,8,128]{3,2,1,0:T(8,128)S(1)}, u32[]{:S(2)}, u32[]{:S(2)}) async-start(f32[4,2,8,128]{3,2,1,0:T(8,128)} %donor_gather.1), calls=%async_computation.1 | async-start | bytes 65536 | tf_op jit(solution)/shard_map/all_to_all | solution.py:443
  241.8 18.2 %copy-start.7 = (f32[4,2,8,128]{3,2,1,0:T(8,128)}, f32[4,2,8,128]{3,2,1,0:T(8,128)S(1)}, u32[]{:S(2)}) copy-start(f32[4,2,8,128]{3,2,1,0:T(8,128)S(1)} %all-to-all-done.1.interp_ref) | copy-start | bytes 98308
  241.8 18.2 %all-to-all-start.2 = ((f32[4,8,512]{2,1,0:T(8,128)}), f32[4,8,512]{2,1,0:T(8,128)S(1)}, u32[]{:S(2)}, u32[]{:S(2)}) async-start(f32[4,8,512]{2,1,0:T(8,128)} %get-tuple-element.32), calls=%async_computation.2 | async-start | bytes 131072 | tf_op jit(solution)/shard_map/all_to_all | solution.py:444
  246.7 60.9 %collective-permute-start.5 = (f32[512,256]{1,0:T(8,128)}, f32[512,256]{1,0:T(8,128)}, u32[]{:S(2)}, u32[]{:S(2)}) collective-permute-start(f32[512,256]{1,0:T(8,128)} %get-tuple-element.48), channel_id=1, source_target_pairs={{0,4},{4,0},{1,5},{5,1},{2,6},{6,2},{3,7},{7,3},{8,12},{12,8},{9,1... | collective-permute-start | bytes 1572872 | tf_op jit(solution)/shard_map/ppermute | solution.py:403
  260.0 0.6 copy-start.5
  260.6 26.9 %copy-start = (f32[1,3,512,512]{3,2,1,0:T(8,128)S(1)}, f32[1,3,512,512]{3,2,1,0:T(8,128)}, u32[]{:S(2)}) copy-start(f32[1,3,512,512]{3,2,1,0:T(8,128)} %media_ref.15) | copy-start | bytes 9437188
  260.6 26.9 %copy-start.1 = (bf16[512,1536]{1,0:T(8,128)(2,1)S(1)}, bf16[512,1536]{1,0:T(8,128)(2,1)}, u32[]{:S(2)}) copy-start(bf16[512,1536]{1,0:T(8,128)(2,1)} %get-tuple-element.30.d_ref) | copy-start | bytes 4718596
  287.5 1.2 copy-start.2
  288.7 3.9 %copy-start.11 = (f32[512,128]{1,0:T(8,128)S(1)}, f32[512,128]{1,0:T(8,128)}, u32[]{:S(2)}) copy-start(f32[512,128]{1,0:T(8,128)} %get-tuple-element.51) | copy-start | bytes 786436
  288.7 4.4 %copy-start.3 = (f32[1,2,512,512]{3,2,1,0:T(8,128)S(1)}, f32[1,2,512,512]{3,2,1,0:T(8,128)}, u32[]{:S(2)}) copy-start(f32[1,2,512,512]{3,2,1,0:T(8,128)} %media_ref.10) | copy-start | bytes 6291460
  292.6 3.8 %copy-start.10 = (f32[512,128]{1,0:T(8,128)S(1)}, f32[512,128]{1,0:T(8,128)}, u32[]{:S(2)}) copy-start(f32[512,128]{1,0:T(8,128)} %get-tuple-element.54) | copy-start | bytes 786436
  292.6 20.5 %collective-permute-start.6 = (f32[512,128]{1,0:T(8,128)S(1)}, f32[512,128]{1,0:T(8,128)S(1)}, u32[]{:S(2)}, u32[]{:S(2)}) collective-permute-start(f32[512,128]{1,0:T(8,128)S(1)} %copy-done.11), channel_id=1, source_target_pairs={{0,4},{4,0},{1,5},{5,1},{2,6},{6,2},{3,7},{7,3},{8,12},{12,8},{9,1... | collective-permute-start | bytes 786440 | tf_op jit(solution)/shard_map/ppermute | solution.py:403
  296.4 21.9 %collective-permute-start.7 = (f32[512,128]{1,0:T(8,128)S(1)}, f32[512,128]{1,0:T(8,128)S(1)}, u32[]{:S(2)}, u32[]{:S(2)}) collective-permute-start(f32[512,128]{1,0:T(8,128)S(1)} %copy-done.10), channel_id=1, source_target_pairs={{0,4},{4,0},{1,5},{5,1},{2,6},{6,2},{3,7},{7,3},{8,12},{12,8},{9,1... | collective-permute-start | bytes 786440 | tf_op jit(solution)/shard_map/ppermute | solution.py:403

commit v3 on v2

--- a/solution.py
+++ b/solution.py
@@ -59,28 +59,37 @@
     return lax.div(value, size), lax.rem(value, size)
 
 
-def take_kernel(pieces, elastic_ref, acoustic_ref, after_ref, *refs):
+def take_kernel(pieces, parts, elastic_ref, acoustic_ref, after_ref, *refs):
     del after_ref
-    outs, semaphores = refs[: len(pieces)], refs[-1]
-    copies = []
+    n = len(pieces)
+    outs, held, in_semaphores, out_semaphores = refs[:n], refs[n : 2 * n], refs[-2], refs[-1]
+    rows = elastic_ref.shape[2]
+    loads, stores = [], []
     for i, (name, field, at, width) in enumerate(pieces):
         source = elastic_ref if name == "el" else acoustic_ref
-        copies.append(
-            pltpu.make_async_copy(source.at[0, field, :, pl.ds(at, width)], outs[i], semaphores.at[i])
-        )
-    for copy in copies:
-        copy.start()
-    return copies
-
-
-def take_only_kernel(pieces, *refs):
-    for copy in take_kernel(pieces, *refs):
-        copy.wait()
-
-
-def take_and_edges_kernel(pieces, layers, elastic_ref, acoustic_ref, after_ref, *refs):
+        for part in range(parts):
+            here = pl.ds(part * (rows // parts), rows // parts)
+            k = i * parts + part
+            loads.append(
+                pltpu.make_async_copy(source.at[0, field, here, pl.ds(at, width)], held[i].at[here], in_semaphores.at[k])
+            )
+            stores.append(pltpu.make_async_copy(held[i].at[here], outs[i].at[here], out_semaphores.at[k]))
+    for load in loads:
+        load.start()
+    for load, store in zip(loads, stores):
+        load.wait()
+        store.start()
+    return stores
+
+
+def take_only_kernel(pieces, parts, *refs):
+    for store in take_kernel(pieces, parts, *refs):
+        store.wait()
+
+
+def take_and_edges_kernel(pieces, parts, layers, elastic_ref, acoustic_ref, after_ref, *refs):
     n = len(pieces)
-    edges_ref, tiles, edge_semaphores, semaphores = refs[n:]
+    edges_ref, tiles, edge_semaphores = refs[n : n + 3]
     n_el, n_ac = elastic_ref.shape[1], acoustic_ref.shape[1]
     rows, depth = elastic_ref.shape[2:]
     loads = []
@@ -95,7 +104,7 @@
             )
     for load in loads:
         load.start()
-    copies = take_kernel(pieces, elastic_ref, acoustic_ref, after_ref, *refs[:n], semaphores)
+    stores = take_kernel(pieces, parts, elastic_ref, acoustic_ref, after_ref, *refs[:n], *refs[n + 3 :])
     for load in loads:
         load.wait()
     lane = lax.broadcasted_iota(jnp.int32, (rows, LANES), 1)
@@ -107,8 +116,8 @@
     below = lax.rem(lax.axis_index("layer") + 1, layers)
     for to in range(layers):
         edges_ref[to] = jnp.where(to == below, lines[8:16], lines[0:8])
-    for copy in copies:
-        copy.wait()
+    for store in stores:
+        store.wait()
 
 
 def take_pieces(elastic, acoustic, after, pieces, layers=0):
@@ -116,13 +125,15 @@
     anywhere = pl.BlockSpec(memory_space=pl.ANY)
     out_shape = [jax.ShapeDtypeStruct((rows, width), jnp.float32) for _, _, _, width in pieces]
     out_specs = [anywhere] * len(pieces)
-    scratch = [pltpu.SemaphoreType.DMA((len(pieces),))]
-    kernel = functools.partial(take_only_kernel, pieces)
+    parts = 2 if layers else 4
+    scratch = [pltpu.VMEM((rows, width), jnp.float32) for _, _, _, width in pieces]
+    scratch += [pltpu.SemaphoreType.DMA((len(pieces) * parts,))] * 2
+    kernel = functools.partial(take_only_kernel, pieces, parts)
     if layers:
         out_shape.append(jax.ShapeDtypeStruct((layers, 8, rows), jnp.float32))
         out_specs.append(pl.BlockSpec(memory_space=pltpu.VMEM))
         scratch = [pltpu.VMEM((2, 8, rows, LANES), jnp.float32), pltpu.SemaphoreType.DMA((4,))] + scratch
-        kernel = functools.partial(take_and_edges_kernel, pieces, layers)
+        kernel = functools.partial(take_and_edges_kernel, pieces, parts, layers)
     cells = sum(width for _, _, _, width in pieces) * rows
     return pl.pallas_call(
         kernel,

time: 321 us -> 146 us (0.45)
  Pallas kernels: 284 us -> 97 us
  waiting for transfers between devices: 9.08 us -> 18.6 us
    pallas_call x2, Pallas kernels: 194 us -> 9.62 us  [take_pieces(): pl.pallas_call(kernel, in_specs=[anywhere] * 3, out_specs=out_specs, out_...]
    ppermute x8, waiting for transfers between devices: 6.05 us -> 15.6 us  [other_slabs(): lax.ppermute(value, 'line', [(i, (i + distance) % slabs) for i in range(s...]
  transfers between devices with their start and end apart: 11 -> 11, of which waited for: 4 -> 5; matrix products, arithmetic and copies ran while one was open for 1% -> 2% of each run, Pallas kernels for 78% -> 64%
where the time goes in v3:
time: 146 us; the launch traced here: 145 us
  Pallas kernels  97 us (66%)
  starting transfers between devices  23.2 us (16%)
  waiting for transfers between devices  18.6 us (13%)
  local copies, waits for them, and re-layouts  3.41 us (2%)
  other arithmetic  2.15 us (1%)
    pallas_call x1, Pallas kernels, per_device(): pl.pallas_call(functools.partial(gather_kernel, 8, rows, depth), in_specs...  27.2 us
    pallas_call x1, Pallas kernels, per_device(): pl.pallas_call(functools.partial(section_kernel, layers, rows, depth, til...  23.8 us
    pallas_call x8, Pallas kernels, add_far(): pl.pallas_call(functools.partial(far_kernel, coefficients), grid=(width /...  23.6 us
    ppermute x8, waiting for transfers between devices, other_slabs(): lax.ppermute(value, 'line', [(i, (i + distance) % slabs) for i in range(s...  15.6 us
    pallas_call x1, Pallas kernels, near_derivatives(): pl.pallas_call(functools.partial(near_kernel, 4), grid_spec=pltpu.Prefetc...  12.8 us
    ppermute x8, starting transfers between devices, other_slabs(): lax.ppermute(value, 'line', [(i, (i + distance) % slabs) for i in range(s...  11.8 us
    pallas_call x2, Pallas kernels, take_pieces(): pl.pallas_call(kernel, in_specs=[anywhere] * 3, out_specs=out_specs, out_...  9.62 us
    all_to_all x1, starting transfers between devices, per_device(): lax.all_to_all(edges, 'layer', split_axis=0, concat_axis=0, tiled=True)  4.89 us
  transfers between devices with their start and end apart: 11, of which 5 were waited for; matrix products, arithmetic and copies ran while one was open for 2% of the time, Pallas kernels for 64%

profile of v3, /device:TPU:0, one launch (start us, length us, event | category | flops | bytes accessed | tf_op | source)
XLA Modules:
  0.0 145.2 jit_solution(4205186916799098402)
XLA Ops:
  2.1 2.0 %take_pieces.2.after_ref = f32[512,512]{1,0:T(8,128)} custom-call(f32[1,5,512,512]{3,2,1,0:T(8,128)} %elastic_ref.7, f32[1,3,512,512]{3,2,1,0:T(8,128)} %acoustic_ref.7, f32[128,20]{1,0:T(8,128)} %copy.32.refs_2_), custom_call_target="tpu_custom_call" | custom-call | bytes 2097152 | tf_op jit(solution)/shard_map/take_pieces/pallas_call | solution.py:138
  4.1 3.0 %collective-permute-start = (f32[512,512]{1,0:T(8,128)}, f32[512,512]{1,0:T(8,128)}, u32[]{:S(2)}, u32[]{:S(2)}) collective-permute-start(f32[512,512]{1,0:T(8,128)} %take_pieces.2.after_ref), channel_id=1, source_target_pairs={{0,4},{4,0},{1,5},{5,1},{2,6},{6,2},{3,7},{7,3},{8,12},{12,8},{9,1... | collective-permute-start | bytes 3145736 | tf_op jit(solution)/shard_map/ppermute | solution.py:414
  7.8 3.3 %all-to-all-start = ((f32[4,8,256]{2,1,0:T(8,128)}), f32[4,8,256]{2,1,0:T(8,128)S(1)}, u32[]{:S(2)}, u32[]{:S(2)}) async-start(f32[4,8,256]{2,1,0:T(8,128)} %pad_maximum_fusion), calls=%async_computation | async-start | bytes 65536 | tf_op jit(solution)/shard_map/all_to_all | solution.py:439
  11.1 7.6 %take_pieces.3 = (f32[512,512]{1,0:T(8,128)}, f32[512,512]{1,0:T(8,128)}, f32[512,512]{1,0:T(8,128)}, f32[512,512]{1,0:T(8,128)}, f32[512,256]{1,0:T(8,128)}, /*...) custom-call(f32[1,5,512,512]{3,2,1,0:T(8,128)} %elastic_ref.7, f32[1,3,512,512]{3,2,1,0:T(8,128)} %acoustic_ref.7, ...), custom_call_target="tpu_custom_call" | custom-call | bytes 10485760 | tf_op jit(solution)/shard_map/take_pieces/pallas_call | solution.py:138
  18.8 2.0 %collective-permute-start.2 = (f32[512,512]{1,0:T(8,128)}, f32[512,512]{1,0:T(8,128)S(1)}, u32[]{:S(2)}, u32[]{:S(2)}) collective-permute-start(f32[512,512]{1,0:T(8,128)} %get-tuple-element.39), channel_id=1, source_target_pairs={{0,4},{4,0},{1,5},{5,1},{2,6},{6,2},{3,7},{7,3},{8,12},{12,8},{9,1... | collective-permute-start | bytes 3145736 | tf_op jit(solution)/shard_map/ppermute | solution.py:414
  23.5 27.2 %donor_gather.1 = f32[4,2,8,128]{3,2,1,0:T(8,128)} custom-call(s32[4,4,256]{2,1,0:T(4,128)} %slice_convert_fusion.words_ref, f32[4,8,256]{2,1,0:T(8,128)} %copy-done.6, f32[1,5,512,512]{3,2,1,0:T(8,128)} %elastic_ref.7, f32[1,3,512,512]{3,2,1,0:T(8,128)} %acoustic_ref.7), custom_call_target="tpu_custom_call" | custom-call | flops 1000000000 | bytes 8388608 | tf_op jit(solution)/shard_map/donor_gather/pallas_call | solution.py:444
  50.7 3.3 %all-to-all-start.1 = ((f32[4,2,8,128]{3,2,1,0:T(8,128)}), f32[4,2,8,128]{3,2,1,0:T(8,128)S(1)}, u32[]{:S(2)}, u32[]{:S(2)}) async-start(f32[4,2,8,128]{3,2,1,0:T(8,128)} %donor_gather.1), calls=%async_computation.1 | async-start | bytes 65536 | tf_op jit(solution)/shard_map/all_to_all | solution.py:454
  54.9 3.0 %all-to-all-done.1.interp_ref = f32[4,2,8,128]{3,2,1,0:T(8,128)S(1)} async-done(((f32[4,2,8,128]{3,2,1,0:T(8,128)}), f32[4,2,8,128]{3,2,1,0:T(8,128)S(1)}, u32[]{:S(2)}, u32[]{:S(2)}) %all-to-all-start.1) | async-done | bytes 32800 | tf_op jit(solution)/shard_map/all_to_all | solution.py:454
  57.9 4.9 %all-to-all-start.2 = ((f32[4,8,512]{2,1,0:T(8,128)}), f32[4,8,512]{2,1,0:T(8,128)S(1)}, u32[]{:S(2)}, u32[]{:S(2)}) async-start(f32[4,8,512]{2,1,0:T(8,128)} %get-tuple-element.32), calls=%async_computation.2 | async-start | bytes 131072 | tf_op jit(solution)/shard_map/all_to_all | solution.py:455
  63.3 12.8 %near_dx.1 = (f32[6,512,512]{2,1,0:T(8,128)}, bf16[512,1536]{1,0:T(8,128)(2,1)}) custom-call(s32[1]{0:T(128)} %bitcast.me_ref, f32[512,512]{1,0:T(8,128)} %constant.45.clone.own_ref, f32[2,512,512]{2,1,0:T(8,128)} %constant.46.clone.far_ref, f32[2,512,128]{2,1,0:T(8,128)} %constant.47.clone.tail_ref, f32[128,512]{1,0:T(8,128)} %get-tuple-element.59.own_cont_ref, ...), custom_call_target="tpu_custom_call" | custom-call | flops 4831838208 | bytes 15728640 | tf_op jit(solution)/shard_map/near_dx/pallas_call | solution.py:221
  76.7 23.8 %near_section.1 = (f32[1,5,512,512]{3,2,1,0:T(8,128)}, f32[1,3,512,512]{3,2,1,0:T(8,128)}, f32[512,512]{1,0:T(8,128)}) custom-call(s32[1,1,1,4,256]{4,3,2,1,0:T(4,128)} %cells_ref.1, s32[1,1,1,4]{3,2,1,0:T(1,128)} %counts_ref.1, f32[4,2,8,128]{3,2,1,0:T(8,128)} %copy-done.7, f32[6,512,512]{2,1,0:T(8,128)} %get-tuple-element.31.dx_ref, ...), custom_call_target="tpu_custom_call" | custom-call | flops 26214400 | bytes 29360128 | tf_op jit(solution)/shard_map/near_section/pallas_call | solution.py:458
  101.8 3.9 %add_far.8 = (f32[8,128]{1,0:T(8,128)S(1)}, f32[1,5,512,512]{3,2,1,0:T(8,128)}) custom-call(f32[8,128]{1,0:T(8,128)S(1)} %broadcast_in_dim.10.turn_ref, bf16[512,1536]{1,0:T(8,128)(2,1)S(1)} %copy-done.1, f32[512,512]{1,0:T(8,128)} %collective-permute-done.far_ref, f32[1,3,512,512]{3,2,1,0:T(8,128)S(1)} %copy-done, ...), custom_call_target="tpu_custom_call", output_to_operand_aliasing={{0}: (0, {}), {1}: (5, {})} | custom-call | flops 805306368 | bytes 8388608 | tf_op jit(solution)/shard_map/add_far/pallas_call | solution.py:359
  105.6 4.0 %collective-permute-start.6 = (f32[512,128]{1,0:T(8,128)S(1)}, f32[512,128]{1,0:T(8,128)S(1)}, u32[]{:S(2)}, u32[]{:S(2)}) collective-permute-start(f32[512,128]{1,0:T(8,128)S(1)} %copy-done.11), channel_id=1, source_target_pairs={{0,4},{4,0},{1,5},{5,1},{2,6},{6,2},{3,7},{7,3},{8,12},{12,8},{9,1... | collective-permute-start | bytes 786440 | tf_op jit(solution)/shard_map/ppermute | solution.py:414
  109.7 3.2 %add_far.9 = (f32[8,128]{1,0:T(8,128)S(1)}, f32[1,3,512,512]{3,2,1,0:T(8,128)}) custom-call(f32[8,128]{1,0:T(8,128)S(1)} %get-tuple-element.35.turn_ref, bf16[512,1536]{1,0:T(8,128)(2,1)S(1)} %copy-done.1, f32[512,512]{1,0:T(8,128)} %collective-permute-done.1.far_ref, ...), custom_call_target="tpu_custom_call", output_to_operand_aliasing={{0}: (0, {}), {1}: (5, {})} | custom-call | flops 805306368 | bytes 5242880 | tf_op jit(solution)/shard_map/add_far/pallas_call | solution.py:359
  113.0 3.1 %add_far.10 = (f32[8,128]{1,0:T(8,128)S(1)}, f32[1,3,512,512]{3,2,1,0:T(8,128)}) custom-call(f32[8,128]{1,0:T(8,128)S(1)} %get-tuple-element.38.turn_ref, bf16[512,1536]{1,0:T(8,128)(2,1)S(1)} %copy-done.1, f32[512,512]{1,0:T(8,128)S(1)} %collective-permute-done.2.far_ref, ...), custom_call_target="tpu_custom_call", output_to_operand_aliasing={{0}: (0, {}), {1}: (5, {})} | custom-call | flops 805306368 | bytes 5242880 | tf_op jit(solution)/shard_map/add_far/pallas_call | solution.py:359
  116.1 3.1 %add_far.11 = (f32[8,128]{1,0:T(8,128)S(1)}, f32[1,5,512,512]{3,2,1,0:T(8,128)}) custom-call(f32[8,128]{1,0:T(8,128)S(1)} %get-tuple-element.41.turn_ref, bf16[512,1536]{1,0:T(8,128)(2,1)S(1)} %copy-done.1, f32[512,512]{1,0:T(8,128)S(1)} %collective-permute-done.3.far_ref, ...), custom_call_target="tpu_custom_call", output_to_operand_aliasing={{0}: (0, {}), {1}: (5, {})} | custom-call | flops 805306368 | bytes 5242880 | tf_op jit(solution)/shard_map/add_far/pallas_call | solution.py:359
  119.2 2.0 %collective-permute-done.4.far_ref = f32[512,512]{1,0:T(8,128)S(1)} collective-permute-done((f32[512,512]{1,0:T(8,128)}, f32[512,512]{1,0:T(8,128)S(1)}, u32[]{:S(2)}, u32[]{:S(2)}) %collective-permute-start.4) | collective-permute-done | bytes 1048608 | tf_op jit(solution)/shard_map/ppermute | solution.py:414
  121.2 3.1 %add_far.12 = (f32[8,128]{1,0:T(8,128)S(1)}, f32[1,5,512,512]{3,2,1,0:T(8,128)}) custom-call(f32[8,128]{1,0:T(8,128)S(1)} %get-tuple-element.44.turn_ref, bf16[512,1536]{1,0:T(8,128)(2,1)S(1)} %copy-done.1, f32[512,512]{1,0:T(8,128)S(1)} %collective-permute-done.4.far_ref, ...), custom_call_target="tpu_custom_call", output_to_operand_aliasing={{0}: (0, {}), {1}: (5, {})} | custom-call | flops 805306368 | bytes 5242880 | tf_op jit(solution)/shard_map/add_far/pallas_call | solution.py:359
  124.3 8.2 %collective-permute-done.5.far_ref = f32[512,256]{1,0:T(8,128)} collective-permute-done((f32[512,256]{1,0:T(8,128)}, f32[512,256]{1,0:T(8,128)}, u32[]{:S(2)}, u32[]{:S(2)}) %collective-permute-start.5) | collective-permute-done | bytes 524320 | tf_op jit(solution)/shard_map/ppermute | solution.py:414
  132.6 2.6 %add_far.13 = (f32[8,128]{1,0:T(8,128)S(1)}, f32[1,5,512,512]{3,2,1,0:T(8,128)}) custom-call(f32[8,128]{1,0:T(8,128)S(1)} %get-tuple-element.47.turn_ref, bf16[512,1536]{1,0:T(8,128)(2,1)S(1)} %copy-done.1, f32[512,256]{1,0:T(8,128)} %collective-permute-done.5.far_ref, f32[1,3,512,512]{3,2,1,0:T(8,128)S(1)} %copy-done, ...), custom_call_target="tpu_custom_call", output_to_operand_aliasing={{0}: (0, {}), {1}: (5, {})} | custom-call | flops 402653184 | bytes 2621440 | tf_op jit(solution)/shard_map/add_far/pallas_call | solution.py:359
  135.1 2.9 %collective-permute-done.6.far_ref = f32[512,128]{1,0:T(8,128)S(1)} collective-permute-done((f32[512,128]{1,0:T(8,128)S(1)}, f32[512,128]{1,0:T(8,128)S(1)}, u32[]{:S(2)}, u32[]{:S(2)}) %collective-permute-start.6) | collective-permute-done | bytes 262176 | tf_op jit(solution)/shard_map/ppermute | solution.py:414
  138.1 2.3 %add_far.14 = (f32[8,128]{1,0:T(8,128)S(1)}, f32[1,5,512,512]{3,2,1,0:T(8,128)}) custom-call(f32[8,128]{1,0:T(8,128)S(1)} %get-tuple-element.50.turn_ref, bf16[512,1536]{1,0:T(8,128)(2,1)S(1)} %copy-done.1, f32[512,128]{1,0:T(8,128)S(1)} %collective-permute-done.6.far_ref, ...), custom_call_target="tpu_custom_call", output_to_operand_aliasing={{0}: (0, {}), {1}: (5, {})} | custom-call | flops 201326592 | bytes 1310720 | tf_op jit(solution)/shard_map/add_far/pallas_call | solution.py:359
  140.4 2.5 %collective-permute-done.7.far_ref = f32[512,128]{1,0:T(8,128)S(1)} collective-permute-done((f32[512,128]{1,0:T(8,128)S(1)}, f32[512,128]{1,0:T(8,128)S(1)}, u32[]{:S(2)}, u32[]{:S(2)}) %collective-permute-start.7) | collective-permute-done | bytes 262176 | tf_op jit(solution)/shard_map/ppermute | solution.py:414
  142.9 2.3 %add_far.15 = (f32[8,128]{1,0:T(8,128)S(1)}, f32[1,5,512,512]{3,2,1,0:T(8,128)}) custom-call(f32[8,128]{1,0:T(8,128)S(1)} %get-tuple-element.53.turn_ref, bf16[512,1536]{1,0:T(8,128)(2,1)S(1)} %copy-done.1, f32[512,128]{1,0:T(8,128)S(1)} %collective-permute-done.7.far_ref, ...), custom_call_target="tpu_custom_call", output_to_operand_aliasing={{0}: (0, {}), {1}: (5, {})} | custom-call | flops 201326592 | bytes 1310720 | tf_op jit(solution)/shard_map/add_far/pallas_call | solution.py:359
  (42 shorter events, 8.3 us)
Async XLA Ops:
  0.6 6.5 %copy-start.8 = (s32[1,1,1,4,4,256]{5,4,3,2,1,0:T(4,128)S(1)}, s32[1,1,1,4,4,256]{5,4,3,2,1,0:T(4,128)}, u32[]{:S(2)}) copy-start(s32[1,1,1,4,4,256]{5,4,3,2,1,0:T(4,128)} %param.20) | copy-start | bytes 49156
  0.6 6.5 %copy-start.9 = (f32[1,1,1,4,4,256]{5,4,3,2,1,0:T(4,128)S(1)}, f32[1,1,1,4,4,256]{5,4,3,2,1,0:T(4,128)}, u32[]{:S(2)}) copy-start(f32[1,1,1,4,4,256]{5,4,3,2,1,0:T(4,128)} %param.21) | copy-start | bytes 49156
  4.1 18.7 %copy-start.4 = (f32[128,20]{1,0:T(8,128)S(1)}, f32[128,20]{1,0:T(8,128)}, u32[]{:S(2)}) copy-start(f32[128,20]{1,0:T(8,128)} %copy.32.refs_2_) | copy-start | bytes 30724
  4.1 58.7 %collective-permute-start = (f32[512,512]{1,0:T(8,128)}, f32[512,512]{1,0:T(8,128)}, u32[]{:S(2)}, u32[]{:S(2)}) collective-permute-start(f32[512,512]{1,0:T(8,128)} %take_pieces.2.after_ref), channel_id=1, source_target_pairs={{0,4},{4,0},{1,5},{5,1},{2,6},{6,2},{3,7},{7,3},{8,12},{12,8},{9,1... | collective-permute-start | bytes 3145736 | tf_op jit(solution)/shard_map/ppermute | solution.py:414
  7.8 15.1 %all-to-all-start = ((f32[4,8,256]{2,1,0:T(8,128)}), f32[4,8,256]{2,1,0:T(8,128)S(1)}, u32[]{:S(2)}, u32[]{:S(2)}) async-start(f32[4,8,256]{2,1,0:T(8,128)} %pad_maximum_fusion), calls=%async_computation | async-start | bytes 65536 | tf_op jit(solution)/shard_map/all_to_all | solution.py:439
  18.7 86.9 %collective-permute-start.1 = (f32[512,512]{1,0:T(8,128)}, f32[512,512]{1,0:T(8,128)}, u32[]{:S(2)}, u32[]{:S(2)}) collective-permute-start(f32[512,512]{1,0:T(8,128)} %get-tuple-element.36), channel_id=1, source_target_pairs={{0,4},{4,0},{1,5},{5,1},{2,6},{6,2},{3,7},{7,3},{8,12},{12,8},{9,1... | collective-permute-start | bytes 3145736 | tf_op jit(solution)/shard_map/ppermute | solution.py:414
  18.8 94.1 %collective-permute-start.2 = (f32[512,512]{1,0:T(8,128)}, f32[512,512]{1,0:T(8,128)S(1)}, u32[]{:S(2)}, u32[]{:S(2)}) collective-permute-start(f32[512,512]{1,0:T(8,128)} %get-tuple-element.39), channel_id=1, source_target_pairs={{0,4},{4,0},{1,5},{5,1},{2,6},{6,2},{3,7},{7,3},{8,12},{12,8},{9,1... | collective-permute-start | bytes 3145736 | tf_op jit(solution)/shard_map/ppermute | solution.py:414
  20.8 95.3 %collective-permute-start.3 = (f32[512,512]{1,0:T(8,128)}, f32[512,512]{1,0:T(8,128)S(1)}, u32[]{:S(2)}, u32[]{:S(2)}) collective-permute-start(f32[512,512]{1,0:T(8,128)} %get-tuple-element.42), channel_id=1, source_target_pairs={{0,4},{4,0},{1,5},{5,1},{2,6},{6,2},{3,7},{7,3},{8,12},{12,8},{9,1... | collective-permute-start | bytes 3145736 | tf_op jit(solution)/shard_map/ppermute | solution.py:414
  20.9 100.3 %collective-permute-start.4 = (f32[512,512]{1,0:T(8,128)}, f32[512,512]{1,0:T(8,128)S(1)}, u32[]{:S(2)}, u32[]{:S(2)}) collective-permute-start(f32[512,512]{1,0:T(8,128)} %get-tuple-element.45), channel_id=1, source_target_pairs={{0,4},{4,0},{1,5},{5,1},{2,6},{6,2},{3,7},{7,3},{8,12},{12,8},{9,1... | collective-permute-start | bytes 3145736 | tf_op jit(solution)/shard_map/ppermute | solution.py:414
  22.9 0.6 copy-start.6
  50.7 7.2 %all-to-all-start.1 = ((f32[4,2,8,128]{3,2,1,0:T(8,128)}), f32[4,2,8,128]{3,2,1,0:T(8,128)S(1)}, u32[]{:S(2)}, u32[]{:S(2)}) async-start(f32[4,2,8,128]{3,2,1,0:T(8,128)} %donor_gather.1), calls=%async_computation.1 | async-start | bytes 65536 | tf_op jit(solution)/shard_map/all_to_all | solution.py:454
  57.9 18.2 %copy-start.7 = (f32[4,2,8,128]{3,2,1,0:T(8,128)}, f32[4,2,8,128]{3,2,1,0:T(8,128)S(1)}, u32[]{:S(2)}) copy-start(f32[4,2,8,128]{3,2,1,0:T(8,128)S(1)} %all-to-all-done.1.interp_ref) | copy-start | bytes 98308
  57.9 18.2 %all-to-all-start.2 = ((f32[4,8,512]{2,1,0:T(8,128)}), f32[4,8,512]{2,1,0:T(8,128)S(1)}, u32[]{:S(2)}, u32[]{:S(2)}) async-start(f32[4,8,512]{2,1,0:T(8,128)} %get-tuple-element.32), calls=%async_computation.2 | async-start | bytes 131072 | tf_op jit(solution)/shard_map/all_to_all | solution.py:455
  62.8 69.8 %collective-permute-start.5 = (f32[512,256]{1,0:T(8,128)}, f32[512,256]{1,0:T(8,128)}, u32[]{:S(2)}, u32[]{:S(2)}) collective-permute-start(f32[512,256]{1,0:T(8,128)} %get-tuple-element.48), channel_id=1, source_target_pairs={{0,4},{4,0},{1,5},{5,1},{2,6},{6,2},{3,7},{7,3},{8,12},{12,8},{9,1... | collective-permute-start | bytes 1572872 | tf_op jit(solution)/shard_map/ppermute | solution.py:414
  76.1 0.6 copy-start.5
  76.7 23.8 %copy-start = (f32[1,3,512,512]{3,2,1,0:T(8,128)S(1)}, f32[1,3,512,512]{3,2,1,0:T(8,128)}, u32[]{:S(2)}) copy-start(f32[1,3,512,512]{3,2,1,0:T(8,128)} %media_ref.15) | copy-start | bytes 9437188
  76.7 23.8 %copy-start.1 = (bf16[512,1536]{1,0:T(8,128)(2,1)S(1)}, bf16[512,1536]{1,0:T(8,128)(2,1)}, u32[]{:S(2)}) copy-start(bf16[512,1536]{1,0:T(8,128)(2,1)} %get-tuple-element.30.d_ref) | copy-start | bytes 4718596
  100.5 1.2 copy-start.2
  101.8 3.9 %copy-start.11 = (f32[512,128]{1,0:T(8,128)S(1)}, f32[512,128]{1,0:T(8,128)}, u32[]{:S(2)}) copy-start(f32[512,128]{1,0:T(8,128)} %get-tuple-element.51) | copy-start | bytes 786436
  101.8 7.9 %copy-start.3 = (f32[1,2,512,512]{3,2,1,0:T(8,128)S(1)}, f32[1,2,512,512]{3,2,1,0:T(8,128)}, u32[]{:S(2)}) copy-start(f32[1,2,512,512]{3,2,1,0:T(8,128)} %media_ref.10) | copy-start | bytes 6291460
  105.6 7.2 %copy-start.10 = (f32[512,128]{1,0:T(8,128)S(1)}, f32[512,128]{1,0:T(8,128)}, u32[]{:S(2)}) copy-start(f32[512,128]{1,0:T(8,128)} %get-tuple-element.54) | copy-start | bytes 786436
  105.6 32.4 %collective-permute-start.6 = (f32[512,128]{1,0:T(8,128)S(1)}, f32[512,128]{1,0:T(8,128)S(1)}, u32[]{:S(2)}, u32[]{:S(2)}) collective-permute-start(f32[512,128]{1,0:T(8,128)S(1)} %copy-done.11), channel_id=1, source_target_pairs={{0,4},{4,0},{1,5},{5,1},{2,6},{6,2},{3,7},{7,3},{8,12},{12,8},{9,1... | collective-permute-start | bytes 786440 | tf_op jit(solution)/shard_map/ppermute | solution.py:414
  112.9 30.0 %collective-permute-start.7 = (f32[512,128]{1,0:T(8,128)S(1)}, f32[512,128]{1,0:T(8,128)S(1)}, u32[]{:S(2)}, u32[]{:S(2)}) collective-permute-start(f32[512,128]{1,0:T(8,128)S(1)} %copy-done.10), channel_id=1, source_target_pairs={{0,4},{4,0},{1,5},{5,1},{2,6},{6,2},{3,7},{7,3},{8,12},{12,8},{9,1... | collective-permute-start | bytes 786440 | tf_op jit(solution)/shard_map/ppermute | solution.py:414

commit v4 on v2

--- a/solution.py
+++ b/solution.py
@@ -12,8 +12,7 @@
 STEP = 0.25
 PENALTY = 2.0
 LANES = 128
-VMEM_LIMIT = 56 * 1024 * 1024
-FAR_VMEM_LIMIT = 24 * 1024 * 1024
+MIB = 1024 * 1024
 HIGHEST = lax.Precision.HIGHEST
 
 
@@ -31,13 +30,15 @@
     row = derivative_row(period)
     j = np.arange(rows)
     own = row[(j[:, None] - j[None, :]) % period]
-    far, tail = [], []
+    far, sent, tail = [], [], []
     for me in range(slabs):
         mine = me * rows + j[:, None]
         others = np.concatenate([(me - d) % slabs * rows + j for d in range(1, slabs)])
         far.append(row[(mine - others[None, :]) % period])
+        toward = np.concatenate([(me + d) % slabs * rows + j for d in range(1, slabs)])
+        sent.append(row[(toward[:, None] - me * rows - j[None, :]) % period])
         tail.append(row[(mine - points - np.arange(cont)[None, :]) % period])
-    return tuple(np.asarray(table, np.float32) for table in (own, far, tail))
+    return tuple(np.asarray(table, np.float32) for table in (own, far, sent, tail))
 
 
 def continuation_on(cont_matrix, rows, slabs, sources):
@@ -59,28 +60,24 @@
     return lax.div(value, size), lax.rem(value, size)
 
 
-def take_kernel(pieces, elastic_ref, acoustic_ref, after_ref, *refs):
-    del after_ref
-    outs, semaphores = refs[: len(pieces)], refs[-1]
+def take_kernel(pieces, elastic_ref, acoustic_ref, outs, semaphores):
     copies = []
     for i, (name, field, at, width) in enumerate(pieces):
         source = elastic_ref if name == "el" else acoustic_ref
-        copies.append(
-            pltpu.make_async_copy(source.at[0, field, :, pl.ds(at, width)], outs[i], semaphores.at[i])
-        )
+        copies.append(pltpu.make_async_copy(source.at[0, field, :, pl.ds(at, width)], outs[i], semaphores.at[i]))
     for copy in copies:
         copy.start()
     return copies
 
 
-def take_only_kernel(pieces, *refs):
-    for copy in take_kernel(pieces, *refs):
+def take_only_kernel(pieces, elastic_ref, *refs):
+    for copy in take_kernel(pieces, elastic_ref, None, refs[:-1], refs[-1]):
         copy.wait()
 
 
-def take_and_edges_kernel(pieces, layers, elastic_ref, acoustic_ref, after_ref, *refs):
-    n = len(pieces)
-    edges_ref, tiles, edge_semaphores, semaphores = refs[n:]
+def take_and_edges_kernel(pieces, layers, after_ref, elastic_ref, acoustic_ref, *refs):
+    del after_ref
+    edges_ref, tiles, edge_semaphores, semaphores = refs[len(pieces) :]
     n_el, n_ac = elastic_ref.shape[1], acoustic_ref.shape[1]
     rows, depth = elastic_ref.shape[2:]
     loads = []
@@ -93,9 +90,9 @@
                     edge_semaphores.at[2 * end + k],
                 )
             )
+    copies = take_kernel(pieces, elastic_ref, acoustic_ref, refs[: len(pieces)], semaphores)
     for load in loads:
         load.start()
-    copies = take_kernel(pieces, elastic_ref, acoustic_ref, after_ref, *refs[:n], semaphores)
     for load in loads:
         load.wait()
     lane = lax.broadcasted_iota(jnp.int32, (rows, LANES), 1)
@@ -111,29 +108,28 @@
         copy.wait()
 
 
-def take_pieces(elastic, acoustic, after, pieces, layers=0):
+def take_pieces(elastic, acoustic, pieces, after=None, layers=0):
     rows = elastic.shape[2]
     anywhere = pl.BlockSpec(memory_space=pl.ANY)
+    vmem = pl.BlockSpec(memory_space=pltpu.VMEM)
     out_shape = [jax.ShapeDtypeStruct((rows, width), jnp.float32) for _, _, _, width in pieces]
-    out_specs = [anywhere] * len(pieces)
     scratch = [pltpu.SemaphoreType.DMA((len(pieces),))]
-    kernel = functools.partial(take_only_kernel, pieces)
+    kernel, operands = functools.partial(take_only_kernel, pieces), (elastic,)
     if layers:
         out_shape.append(jax.ShapeDtypeStruct((layers, 8, rows), jnp.float32))
-        out_specs.append(pl.BlockSpec(memory_space=pltpu.VMEM))
         scratch = [pltpu.VMEM((2, 8, rows, LANES), jnp.float32), pltpu.SemaphoreType.DMA((4,))] + scratch
-        kernel = functools.partial(take_and_edges_kernel, pieces, layers)
+        kernel, operands = functools.partial(take_and_edges_kernel, pieces, layers), (after, elastic, acoustic)
     cells = sum(width for _, _, _, width in pieces) * rows
     return pl.pallas_call(
         kernel,
-        in_specs=[anywhere] * 3,
-        out_specs=out_specs,
+        in_specs=[anywhere] * len(operands),
+        out_specs=[vmem] * len(out_shape),
         out_shape=out_shape,
         scratch_shapes=scratch,
-        compiler_params=pltpu.CompilerParams(vmem_limit_bytes=VMEM_LIMIT),
+        compiler_params=pltpu.CompilerParams(vmem_limit_bytes=(14 if layers else 60) * MIB),
         cost_estimate=pl.CostEstimate(flops=0, bytes_accessed=8 * cells, transcendentals=0),
         name="take_pieces",
-    )(elastic, acoustic, after)
+    )(*operands)
 
 
 def gather_kernel(fields, rows, depth, words_ref, weights_ref, elastic_ref, acoustic_ref, out_ref, mixed):
@@ -200,11 +196,11 @@
     out_ref[0] = jnp.dot(operator[...], three_right(value), preferred_element_type=jnp.float32)
 
 
-def near_derivatives(elastic, acoustic, cont_matrix, me, slabs):
+def near_derivatives(elastic, acoustic, cont_matrix, tables, me, slabs):
     rows, depth = elastic.shape[2:]
     cont = cont_matrix.shape[0]
     reach = (slabs - 1) * rows
-    own, far, tail = operator_tables(rows, slabs, cont)
+    own, far, _, tail = tables
     own_cont = continuation_on(cont_matrix, rows, slabs, [me])
     far_cont = continuation_on(cont_matrix, rows, slabs, [(me - d) % slabs for d in range(1, slabs)])
     return pl.pallas_call(
@@ -231,12 +227,53 @@
             jax.ShapeDtypeStruct((6, rows, depth), jnp.float32),
             jax.ShapeDtypeStruct((rows, 3 * reach), jnp.bfloat16),
         ],
-        compiler_params=pltpu.CompilerParams(vmem_limit_bytes=VMEM_LIMIT),
+        compiler_params=pltpu.CompilerParams(vmem_limit_bytes=28 * MIB),
         cost_estimate=pl.CostEstimate(
             flops=36 * rows * rows * depth, bytes_accessed=60 * rows * depth, transcendentals=0
         ),
         name="near_dx",
     )(me.reshape(1), own, far, tail, own_cont, far_cont, elastic, acoustic)
+
+
+def sent_kernel(rows, me_ref, turn_ref, sent_ref, tail_ref, cont_ref, piece_ref, out_ref):
+    del turn_ref
+    me, slabs = me_ref[0], tail_ref.shape[0]
+    value = three_right(piece_ref[...])
+    for d in range(1, slabs):
+        here = pl.ds((d - 1) * rows, rows)
+        tail = tail_ref[lax.rem(me + d, slabs)]
+        block = sent_ref[0, here, :] + jnp.dot(
+            tail, cont_ref[...], precision=HIGHEST, preferred_element_type=jnp.float32
+        )
+        out_ref[here, :] = jnp.dot(three_left(block), value, preferred_element_type=jnp.float32)
+
+
+def sent_products(piece, cont_matrix, tables, me, slabs, turn):
+    rows, width = piece.shape
+    cont = cont_matrix.shape[0]
+    reach = (slabs - 1) * rows
+    _, _, sent, tail = tables
+    return pl.pallas_call(
+        functools.partial(sent_kernel, rows),
+        grid_spec=pltpu.PrefetchScalarGridSpec(
+            num_scalar_prefetch=1,
+            grid=(1,),
+            in_specs=[
+                pl.BlockSpec(memory_space=pl.ANY),
+                pl.BlockSpec((1, reach, rows), lambda i, me: (me[0], 0, 0)),
+                pl.BlockSpec((slabs, rows, cont), lambda i, me: (0, 0, 0)),
+                pl.BlockSpec((cont, rows), lambda i, me: (0, 0)),
+                pl.BlockSpec((rows, width), lambda i, me: (0, 0)),
+            ],
+            out_specs=pl.BlockSpec((reach, width), lambda i, me: (0, 0)),
+        ),
+        out_shape=jax.ShapeDtypeStruct((reach, width), jnp.float32),
+        compiler_params=pltpu.CompilerParams(vmem_limit_bytes=16 * MIB),
+        cost_estimate=pl.CostEstimate(
+            flops=6 * rows * reach * width, bytes_accessed=4 * rows * reach, transcendentals=0
+        ),
+        name="sent_products",
+    )(me.reshape(1), turn, sent, tail, continuation_on(cont_matrix, rows, slabs, [me]), piece)
 
 
 def section_kernel(
@@ -365,7 +402,7 @@
             jax.ShapeDtypeStruct(base.shape, base.dtype),
         ],
         input_output_aliases={0: 0, 5: 1},
-        compiler_params=pltpu.CompilerParams(vmem_limit_bytes=FAR_VMEM_LIMIT),
+        compiler_params=pltpu.CompilerParams(vmem_limit_bytes=20 * MIB),
         cost_estimate=pl.CostEstimate(
             flops=6 * rows * reach * width,
             bytes_accessed=4 * rows * width * (3 + n_media + n_out),
@@ -417,9 +454,10 @@
         ("el", 4, half + quarter, quarter, "el", 0, 1, 1, (lambda b: b,)),
     ]
     travelling = [piece[:4] for piece in pieces]
-    (first,) = take_pieces(elastic, acoustic, cont_matrix, travelling[:1])
-    *others, edges = take_pieces(elastic, acoustic, first, travelling[1:], layers)
+    (first,) = take_pieces(elastic, acoustic, travelling[:1])
+    *others, last, edges = take_pieces(elastic, acoustic, travelling[1:], first, layers)
     far = [other_slabs(value) for value in [first, *others]]
+    tables = operator_tables(rows, slabs, cont_matrix.shape[0])
 
     x, z = split(donor_cells[0, 0, 0], depth)
     chunk, at_lane = split(z, LANES)
@@ -436,14 +474,14 @@
         out_specs=vmem,
         out_shape=jax.ShapeDtypeStruct((patches, groups, 8, LANES), jnp.float32),
         scratch_shapes=[pltpu.VMEM((8 * rows * (depth // LANES), LANES), jnp.float32)],
-        compiler_params=pltpu.CompilerParams(vmem_limit_bytes=VMEM_LIMIT),
+        compiler_params=pltpu.CompilerParams(vmem_limit_bytes=24 * MIB),
         cost_estimate=pl.CostEstimate(flops=10**9, bytes_accessed=32 * rows * depth, transcendentals=0),
         name="donor_gather",
     )(asked_words, asked, elastic, acoustic)
     interp = lax.all_to_all(local, "patch", split_axis=0, concat_axis=0, tiled=True)
     edges = lax.all_to_all(edges, "layer", split_axis=0, concat_axis=0, tiled=True)
 
-    near, far_operator = near_derivatives(elastic, acoustic, cont_matrix, me, slabs)
+    near, far_operator = near_derivatives(elastic, acoustic, cont_matrix, tables, me, slabs)
     new_el, new_ac, opened = pl.pallas_call(
         functools.partial(section_kernel, layers, rows, depth, tile),
         grid=(rows // tile,),
@@ -467,7 +505,7 @@
             jax.ShapeDtypeStruct((rows, depth), jnp.float32),
         ],
         scratch_shapes=[pltpu.VMEM((rows, LANES), jnp.float32)],
-        compiler_params=pltpu.CompilerParams(vmem_limit_bytes=VMEM_LIMIT),
+        compiler_params=pltpu.CompilerParams(vmem_limit_bytes=28 * MIB),
         cost_estimate=pl.CostEstimate(
             flops=100 * rows * depth, bytes_accessed=112 * rows * depth, transcendentals=0
         ),
@@ -489,11 +527,30 @@
     turn = jnp.zeros((8, LANES), jnp.float32)
     section = {"el": new_el, "ac": new_ac}
     media = {"el": el_media, "ac": ac_media}
+    turns = []
     for value, (_, _, at, _, target, first_media, n_media, first_field, coefficients) in zip(far, pieces):
         turn, section[target] = add_far(
             section[target], far_operator, value, at,
             media[target], first_media, n_media, first_field, coefficients, opened, turn,
         )
+        turns.append(turn)
+    products = sent_products(last, cont_matrix, tables, me, slabs, turns[2])
+    products = [
+        lax.ppermute(
+            lax.slice_in_dim(products, (d - 1) * rows, d * rows),
+            "line",
+            [(i, (i + d) % slabs) for i in range(slabs)],
+        )
+        for d in range(1, slabs)
+    ]
+
+    _, _, at, width, target, first_media, _, first_field, (coefficient,) = pieces[-1]
+    corner = (0, first_field, 0, at)
+    old = lax.dynamic_slice(section[target], corner, (1, 1, rows, width))
+    scale = STEP * coefficient(media[target][:, first_media : first_media + 1, :, at : at + width])
+    is_open = opened[None, None, :, at : at + width] > 0.5
+    new = jnp.where(is_open, old + scale * functools.reduce(jnp.add, products)[None, None], old)
+    section[target] = lax.dynamic_update_slice(section[target], new, corner)
     return section["el"], section["ac"]
 
 

time: 321 us -> 149 us (0.46)
  Pallas kernels: 284 us -> 89 us
  local copies, waits for them, and re-layouts: 3.41 us -> 31.8 us
  waiting for transfers between devices: 9.08 us -> 2.31 us
    pallas_call x2 -> x3, Pallas kernels: 194 us -> 8.8 us  [the longest x2 6.75 us: take_pieces(): pl.pallas_call(kernel, in_specs=[anywhere] * len(operands), out_specs=[vm...]
    unnamed x25 -> x68, local copies, waits for them, and re-layouts: 3.33 us -> 31.8 us
    ppermute x8 -> x7, waiting for transfers between devices: 6.05 us -> 0.02 us  [other_slabs(): lax.ppermute(value, 'line', [(i, (i + distance) % slabs) for i in range(s...]
    pallas_call x1, Pallas kernels: 12.8 us -> 8.05 us  [near_derivatives(): pl.pallas_call(functools.partial(near_kernel, 4), grid_spec=pltpu.Prefetc...]
    pallas_call x8 -> x7, Pallas kernels: 23.7 us -> 21.6 us  [add_far(): pl.pallas_call(functools.partial(far_kernel, coefficients), grid=(width /...]
    ppermute x8 -> x7, starting transfers between devices: 9.8 us -> 8.13 us  [other_slabs(): lax.ppermute(value, 'line', [(i, (i + distance) % slabs) for i in range(s...]
  transfers between devices with their start and end apart: 11 -> 11, of which waited for: 4 -> 1; matrix products, arithmetic and copies ran while one was open for 1% -> 2% of each run, Pallas kernels for 78% -> 58%
where the time goes in v4:
time: 149 us
  Pallas kernels  89 us (60%)
  local copies, waits for them, and re-layouts  31.8 us (21%)
  starting transfers between devices  21.1 us (14%)
  other arithmetic  4.03 us (3%)
  waiting for transfers between devices  2.31 us (2%)
    unnamed x68, local copies, waits for them, and re-layouts  31.8 us
    pallas_call x1, Pallas kernels, per_device(): pl.pallas_call(functools.partial(section_kernel, layers, rows, depth, til...  25.6 us
    pallas_call x1, Pallas kernels, per_device(): pl.pallas_call(functools.partial(gather_kernel, 8, rows, depth), in_specs...  25 us
    pallas_call x7, Pallas kernels, add_far(): pl.pallas_call(functools.partial(far_kernel, coefficients), grid=(width /...  21.6 us
    ppermute x7, starting transfers between devices, other_slabs(): lax.ppermute(value, 'line', [(i, (i + distance) % slabs) for i in range(s...  8.13 us
    pallas_call x1, Pallas kernels, near_derivatives(): pl.pallas_call(functools.partial(near_kernel, 4), grid_spec=pltpu.Prefetc...  8.05 us
    pallas_call x2, Pallas kernels, take_pieces(): pl.pallas_call(kernel, in_specs=[anywhere] * len(operands), out_specs=[vm...  6.75 us
    all_to_all x1, starting transfers between devices, per_device(): lax.all_to_all(edges, 'layer', split_axis=0, concat_axis=0, tiled=True)  4.89 us
  transfers between devices with their start and end apart: 11, of which 1 were waited for; matrix products, arithmetic and copies ran while one was open for 2% of the time, Pallas kernels for 58%

profile of v4, /device:TPU:0, one launch (start us, length us, event | category | flops | bytes accessed | tf_op | source)
XLA Modules:
  0.0 149.2 jit_solution(18014011878913695844)
XLA Ops:
  0.7 2.4 %take_pieces.2.after_ref = f32[512,512]{1,0:T(8,128)} custom-call(f32[1,5,512,512]{3,2,1,0:T(8,128)} %elastic_ref.9), custom_call_target="tpu_custom_call" | custom-call | bytes 2097152 | tf_op jit(solution)/shard_map/take_pieces/pallas_call | solution.py:123
  3.0 3.0 %collective-permute-start = (f32[512,512]{1,0:T(8,128)}, f32[512,512]{1,0:T(8,128)}, u32[]{:S(2)}, u32[]{:S(2)}) collective-permute-start(f32[512,512]{1,0:T(8,128)} %take_pieces.2.after_ref), channel_id=1, source_target_pairs={{0,4},{4,0},{1,5},{5,1},{2,6},{6,2},{3,7},{7,3},{8,12},{12,8},{9,1... | collective-permute-start | bytes 3145736 | tf_op jit(solution)/shard_map/ppermute | solution.py:440
  6.7 3.3 %all-to-all-start = ((f32[4,8,256]{2,1,0:T(8,128)}), f32[4,8,256]{2,1,0:T(8,128)S(1)}, u32[]{:S(2)}, u32[]{:S(2)}) async-start(f32[4,8,256]{2,1,0:T(8,128)} %pad_maximum_fusion), calls=%async_computation | async-start | bytes 65536 | tf_op jit(solution)/shard_map/all_to_all | solution.py:466
  10.0 2.5 %copy-done.1 = f32[1,5,512,512]{3,2,1,0:T(8,128)S(1)} copy-done((f32[1,5,512,512]{3,2,1,0:T(8,128)S(1)}, f32[1,5,512,512]{3,2,1,0:T(8,128)}, u32[]{:S(2)}) %copy-start.1) | copy-done | bytes 5242904
  13.7 4.4 %take_pieces.3 = (f32[512,512]{1,0:T(8,128)}, f32[512,512]{1,0:T(8,128)}, f32[512,512]{1,0:T(8,128)}, f32[512,512]{1,0:T(8,128)}, f32[512,256]{1,0:T(8,128)S(1)}...) custom-call(f32[512,512]{1,0:T(8,128)S(1)} %copy-done.13, ...), custom_call_target="tpu_custom_call" | custom-call | bytes 10485760 | tf_op jit(solution)/shard_map/take_pieces/pallas_call | solution.py:123
  25.9 2.5 %copy-done.2 = f32[1,5,512,512]{3,2,1,0:T(8,128)S(1)} copy-done((f32[1,5,512,512]{3,2,1,0:T(8,128)S(1)}, f32[1,5,512,512]{3,2,1,0:T(8,128)}, u32[]{:S(2)}) %copy-start.2) | copy-done | bytes 5242904
  28.4 25.0 %donor_gather.1 = f32[4,2,8,128]{3,2,1,0:T(8,128)} custom-call(s32[4,4,256]{2,1,0:T(4,128)S(1)} %slice_convert_fusion.words_ref, f32[4,8,256]{2,1,0:T(8,128)S(1)} %all-to-all-done.weights_ref, f32[1,5,512,512]{3,2,1,0:T(8,128)S(1)} %copy-done.2, f32[1,3,512,512]{3,2,1,0:T(8,128)S(1)} %copy-done.7), custom_call_target="tpu_custom_call" | custom-call | flops 1000000000 | bytes 8388608 | tf_op jit(solution)/shard_map/donor_gather/pallas_call | solution.py:471
  53.4 3.3 %all-to-all-start.1 = ((f32[4,2,8,128]{3,2,1,0:T(8,128)}), f32[4,2,8,128]{3,2,1,0:T(8,128)S(1)}, u32[]{:S(2)}, u32[]{:S(2)}) async-start(f32[4,2,8,128]{3,2,1,0:T(8,128)} %donor_gather.1), calls=%async_computation.1 | async-start | bytes 65536 | tf_op jit(solution)/shard_map/all_to_all | solution.py:481
  58.3 2.3 %all-to-all-done.1.interp_ref = f32[4,2,8,128]{3,2,1,0:T(8,128)S(1)} async-done(((f32[4,2,8,128]{3,2,1,0:T(8,128)}), f32[4,2,8,128]{3,2,1,0:T(8,128)S(1)}, u32[]{:S(2)}, u32[]{:S(2)}) %all-to-all-start.1) | async-done | bytes 32800 | tf_op jit(solution)/shard_map/all_to_all | solution.py:481
  60.6 4.9 %all-to-all-start.2 = ((f32[4,8,512]{2,1,0:T(8,128)}), f32[4,8,512]{2,1,0:T(8,128)S(1)}, u32[]{:S(2)}, u32[]{:S(2)}) async-start(f32[4,8,512]{2,1,0:T(8,128)} %copy-done.20), calls=%async_computation.2 | async-start | bytes 131072 | tf_op jit(solution)/shard_map/all_to_all | solution.py:482
  66.0 2.5 %copy-done.3 = f32[1,5,512,512]{3,2,1,0:T(8,128)S(1)} copy-done((f32[1,5,512,512]{3,2,1,0:T(8,128)S(1)}, f32[1,5,512,512]{3,2,1,0:T(8,128)}, u32[]{:S(2)}) %copy-start.3) | copy-done | bytes 5242904
  75.2 8.1 %near_dx.1 = (f32[6,512,512]{2,1,0:T(8,128)S(1)}, bf16[512,1536]{1,0:T(8,128)(2,1)S(1)}) custom-call(s32[1]{0:T(128)} %bitcast.me_ref, f32[512,512]{1,0:T(8,128)S(1)} %copy-done.29, f32[2,512,512]{2,1,0:T(8,128)S(1)} %copy-done.28, f32[2,512,128]{2,1,0:T(8,128)S(1)} %copy-done.15, f32[128,512]{1,0:T(8,128)S(1)} %get-tuple-element.55.own_cont_ref.cont_ref, ...), custom_call_target="tpu_custom_call" | custom-call | flops 4831838208 | bytes 15728640 | tf_op jit(solution)/shard_map/near_dx/pallas_call | solution.py:206
  84.5 2.7 %copy-done.11 = f32[6,512,512]{2,1,0:T(8,128)} copy-done((f32[6,512,512]{2,1,0:T(8,128)}, f32[6,512,512]{2,1,0:T(8,128)S(1)}, u32[]{:S(2)}) %copy-start.11) | copy-done | bytes 6291480
  87.3 2.5 %copy-done.4 = f32[1,5,512,512]{3,2,1,0:T(8,128)S(1)} copy-done((f32[1,5,512,512]{3,2,1,0:T(8,128)S(1)}, f32[1,5,512,512]{3,2,1,0:T(8,128)}, u32[]{:S(2)}) %copy-start.4) | copy-done | bytes 5242904
  93.2 2.8 %copy-done.12 = f32[6,512,512]{2,1,0:T(8,128)S(1)} copy-done((f32[6,512,512]{2,1,0:T(8,128)S(1)}, f32[6,512,512]{2,1,0:T(8,128)}, u32[]{:S(2)}) %copy-start.12) | copy-done | bytes 6291480
  96.0 25.6 %near_section.1 = (f32[1,5,512,512]{3,2,1,0:T(8,128)}, f32[1,3,512,512]{3,2,1,0:T(8,128)}, f32[512,512]{1,0:T(8,128)S(1)}) custom-call(s32[1,1,1,4,256]{4,3,2,1,0:T(4,128)S(1)} %copy-done.21, s32[1,1,1,4]{3,2,1,0:T(1,128)S(1)} %copy-done.24, f32[4,2,8,128]{3,2,1,0:T(8,128)S(1)} %all-to-all-done.1.interp_ref, f32[6,512,512]{2,1,0:T(8,128)S(1)} %copy-done.12, ...), custom_call_target="tpu_custom_call" | custom-call | flops 26214400 | bytes 29360128 | tf_op jit(solution)/shard_map/near_section/pallas_call | solution.py:485
  121.6 3.7 %add_far.7 = (f32[8,128]{1,0:T(8,128)S(1)}, f32[1,5,512,512]{3,2,1,0:T(8,128)}) custom-call(f32[8,128]{1,0:T(8,128)S(1)} %broadcast_in_dim.16.turn_ref, bf16[512,1536]{1,0:T(8,128)(2,1)S(1)} %copy-done.6, f32[512,512]{1,0:T(8,128)} %collective-permute-done.far_ref, f32[1,3,512,512]{3,2,1,0:T(8,128)S(1)} %copy-done, ...), custom_call_target="tpu_custom_call", output_to_operand_aliasing={{0}: (0, {}), {1}: (5, {})} | custom-call | flops 805306368 | bytes 8388608 | tf_op jit(solution)/shard_map/add_far/pallas_call | solution.py:385
  125.9 3.2 %add_far.8 = (f32[8,128]{1,0:T(8,128)S(1)}, f32[1,3,512,512]{3,2,1,0:T(8,128)}) custom-call(f32[8,128]{1,0:T(8,128)S(1)} %get-tuple-element.33.turn_ref, bf16[512,1536]{1,0:T(8,128)(2,1)S(1)} %copy-done.6, f32[512,512]{1,0:T(8,128)} %collective-permute-done.1.far_ref, ...), custom_call_target="tpu_custom_call", output_to_operand_aliasing={{0}: (0, {}), {1}: (5, {})} | custom-call | flops 805306368 | bytes 5242880 | tf_op jit(solution)/shard_map/add_far/pallas_call | solution.py:385
  129.1 3.4 %add_far.9 = (f32[8,128]{1,0:T(8,128)S(1)}, f32[1,3,512,512]{3,2,1,0:T(8,128)}) custom-call(f32[8,128]{1,0:T(8,128)S(1)} %get-tuple-element.36.turn_ref, bf16[512,1536]{1,0:T(8,128)(2,1)S(1)} %copy-done.6, f32[512,512]{1,0:T(8,128)} %collective-permute-done.2.far_ref, ...), custom_call_target="tpu_custom_call", output_to_operand_aliasing={{0}: (0, {}), {1}: (5, {})} | custom-call | flops 805306368 | bytes 5242880 | tf_op jit(solution)/shard_map/add_far/pallas_call | solution.py:385
  132.5 2.0 %sent_products.1 = f32[512,128]{1,0:T(8,128)S(1)} custom-call(s32[1]{0:T(128)} %bitcast.me_ref, f32[8,128]{1,0:T(8,128)S(1)} %get-tuple-element.39.turn_ref, f32[2,512,512]{2,1,0:T(8,128)S(1)} %copy-done.14, f32[2,512,128]{2,1,0:T(8,128)S(1)} %copy-done.16, f32[128,512]{1,0:T(8,128)S(1)} %get-tuple-element.55.own_cont_ref.cont_ref, f32[512,128]{1,0:T(8,128)S(1)} %copy-done.18), custom_call_target="tpu_custom_call" | custom-call | flops 201326592 | bytes 1048576 | tf_op jit(solution)/shard_map/sent_products/pallas_call | solution.py:256
  136.1 3.2 %add_far.10 = (f32[8,128]{1,0:T(8,128)S(1)}, f32[1,5,512,512]{3,2,1,0:T(8,128)}) custom-call(f32[8,128]{1,0:T(8,128)S(1)} %get-tuple-element.39.turn_ref, bf16[512,1536]{1,0:T(8,128)(2,1)S(1)} %copy-done.6, f32[512,512]{1,0:T(8,128)} %collective-permute-done.3.far_ref, f32[1,3,512,512]{3,2,1,0:T(8,128)S(1)} %copy-done, ...), custom_call_target="tpu_custom_call", output_to_operand_aliasing={{0}: (0, {}), {1}: (5, {})} | custom-call | flops 805306368 | bytes 5242880 | tf_op jit(solution)/shard_map/add_far/pallas_call | solution.py:385
  139.3 3.2 %add_far.11 = (f32[8,128]{1,0:T(8,128)S(1)}, f32[1,5,512,512]{3,2,1,0:T(8,128)}) custom-call(f32[8,128]{1,0:T(8,128)S(1)} %get-tuple-element.42.turn_ref, bf16[512,1536]{1,0:T(8,128)(2,1)S(1)} %copy-done.6, f32[512,512]{1,0:T(8,128)} %collective-permute-done.4.far_ref, f32[1,3,512,512]{3,2,1,0:T(8,128)S(1)} %copy-done, ...), custom_call_target="tpu_custom_call", output_to_operand_aliasing={{0}: (0, {}), {1}: (5, {})} | custom-call | flops 805306368 | bytes 5242880 | tf_op jit(solution)/shard_map/add_far/pallas_call | solution.py:385
  142.5 2.6 %add_far.12 = (f32[8,128]{1,0:T(8,128)S(1)}, f32[1,5,512,512]{3,2,1,0:T(8,128)}) custom-call(f32[8,128]{1,0:T(8,128)S(1)} %get-tuple-element.45.turn_ref, bf16[512,1536]{1,0:T(8,128)(2,1)S(1)} %copy-done.6, f32[512,256]{1,0:T(8,128)} %collective-permute-done.5.far_ref, f32[1,3,512,512]{3,2,1,0:T(8,128)S(1)} %copy-done, ...), custom_call_target="tpu_custom_call", output_to_operand_aliasing={{0}: (0, {}), {1}: (5, {})} | custom-call | flops 402653184 | bytes 2621440 | tf_op jit(solution)/shard_map/add_far/pallas_call | solution.py:385
  145.1 2.3 %add_far.13 = (f32[8,128]{1,0:T(8,128)S(1)}, f32[1,5,512,512]{3,2,1,0:T(8,128)}) custom-call(f32[8,128]{1,0:T(8,128)S(1)} %get-tuple-element.48.turn_ref, bf16[512,1536]{1,0:T(8,128)(2,1)S(1)} %copy-done.6, f32[512,128]{1,0:T(8,128)S(1)} %collective-permute-done.6.far_ref, ...), custom_call_target="tpu_custom_call", output_to_operand_aliasing={{0}: (0, {}), {1}: (5, {})} | custom-call | flops 201326592 | bytes 1310720 | tf_op jit(solution)/shard_map/add_far/pallas_call | solution.py:385
  (86 shorter events, 27.2 us)
Async XLA Ops:
  0.6 5.4 %copy-start.31 = (s32[1,1,1,4,4,256]{5,4,3,2,1,0:T(4,128)S(1)}, s32[1,1,1,4,4,256]{5,4,3,2,1,0:T(4,128)}, u32[]{:S(2)}) copy-start(s32[1,1,1,4,4,256]{5,4,3,2,1,0:T(4,128)} %param.21) | copy-start | bytes 49156
  0.6 5.5 %copy-start.32 = (f32[1,1,1,4,4,256]{5,4,3,2,1,0:T(4,128)S(1)}, f32[1,1,1,4,4,256]{5,4,3,2,1,0:T(4,128)}, u32[]{:S(2)}) copy-start(f32[1,1,1,4,4,256]{5,4,3,2,1,0:T(4,128)} %param.22) | copy-start | bytes 49156
  0.6 9.3 %copy-start.7 = (f32[1,3,512,512]{3,2,1,0:T(8,128)S(1)}, f32[1,3,512,512]{3,2,1,0:T(8,128)}, u32[]{:S(2)}) copy-start(f32[1,3,512,512]{3,2,1,0:T(8,128)} %acoustic_ref.7) | copy-start | bytes 9437188
  3.0 22.0 %copy-start.30 = (f32[128,20]{0,1:T(8,128)S(1)}, f32[128,20]{0,1:T(8,128)}, u32[]{:S(2)}) copy-start(f32[128,20]{0,1:T(8,128)} %param.19) | copy-start | bytes 30724
  3.0 62.5 %collective-permute-start = (f32[512,512]{1,0:T(8,128)}, f32[512,512]{1,0:T(8,128)}, u32[]{:S(2)}, u32[]{:S(2)}) collective-permute-start(f32[512,512]{1,0:T(8,128)} %take_pieces.2.after_ref), channel_id=1, source_target_pairs={{0,4},{4,0},{1,5},{5,1},{2,6},{6,2},{3,7},{7,3},{8,12},{12,8},{9,1... | collective-permute-start | bytes 3145736 | tf_op jit(solution)/shard_map/ppermute | solution.py:440
  6.7 19.2 %all-to-all-start = ((f32[4,8,256]{2,1,0:T(8,128)}), f32[4,8,256]{2,1,0:T(8,128)S(1)}, u32[]{:S(2)}, u32[]{:S(2)}) async-start(f32[4,8,256]{2,1,0:T(8,128)} %pad_maximum_fusion), calls=%async_computation | async-start | bytes 65536 | tf_op jit(solution)/shard_map/all_to_all | solution.py:466
  21.0 104.3 %collective-permute-start.1 = (f32[512,512]{1,0:T(8,128)}, f32[512,512]{1,0:T(8,128)}, u32[]{:S(2)}, u32[]{:S(2)}) collective-permute-start(f32[512,512]{1,0:T(8,128)} %get-tuple-element.34), channel_id=1, source_target_pairs={{0,4},{4,0},{1,5},{5,1},{2,6},{6,2},{3,7},{7,3},{8,12},{12,8},{9,1... | collective-permute-start | bytes 3145736 | tf_op jit(solution)/shard_map/ppermute | solution.py:440
  21.0 108.1 %collective-permute-start.2 = (f32[512,512]{1,0:T(8,128)}, f32[512,512]{1,0:T(8,128)}, u32[]{:S(2)}, u32[]{:S(2)}) collective-permute-start(f32[512,512]{1,0:T(8,128)} %get-tuple-element.37), channel_id=1, source_target_pairs={{0,4},{4,0},{1,5},{5,1},{2,6},{6,2},{3,7},{7,3},{8,12},{12,8},{9,1... | collective-permute-start | bytes 3145736 | tf_op jit(solution)/shard_map/ppermute | solution.py:440
  23.0 113.1 %collective-permute-start.3 = (f32[512,512]{1,0:T(8,128)}, f32[512,512]{1,0:T(8,128)}, u32[]{:S(2)}, u32[]{:S(2)}) collective-permute-start(f32[512,512]{1,0:T(8,128)} %get-tuple-element.40), channel_id=1, source_target_pairs={{0,4},{4,0},{1,5},{5,1},{2,6},{6,2},{3,7},{7,3},{8,12},{12,8},{9,1... | collective-permute-start | bytes 3145736 | tf_op jit(solution)/shard_map/ppermute | solution.py:440
  23.1 116.3 %collective-permute-start.4 = (f32[512,512]{1,0:T(8,128)}, f32[512,512]{1,0:T(8,128)}, u32[]{:S(2)}, u32[]{:S(2)}) collective-permute-start(f32[512,512]{1,0:T(8,128)} %get-tuple-element.43), channel_id=1, source_target_pairs={{0,4},{4,0},{1,5},{5,1},{2,6},{6,2},{3,7},{7,3},{8,12},{12,8},{9,1... | collective-permute-start | bytes 3145736 | tf_op jit(solution)/shard_map/ppermute | solution.py:440
  53.4 7.2 %all-to-all-start.1 = ((f32[4,2,8,128]{3,2,1,0:T(8,128)}), f32[4,2,8,128]{3,2,1,0:T(8,128)S(1)}, u32[]{:S(2)}, u32[]{:S(2)}) async-start(f32[4,2,8,128]{3,2,1,0:T(8,128)} %donor_gather.1), calls=%async_computation.1 | async-start | bytes 65536 | tf_op jit(solution)/shard_map/all_to_all | solution.py:481
  60.6 26.6 %all-to-all-start.2 = ((f32[4,8,512]{2,1,0:T(8,128)}), f32[4,8,512]{2,1,0:T(8,128)S(1)}, u32[]{:S(2)}, u32[]{:S(2)}) async-start(f32[4,8,512]{2,1,0:T(8,128)} %copy-done.20), calls=%async_computation.2 | async-start | bytes 131072 | tf_op jit(solution)/shard_map/all_to_all | solution.py:482
  65.5 77.0 %collective-permute-start.5 = (f32[512,256]{1,0:T(8,128)}, f32[512,256]{1,0:T(8,128)}, u32[]{:S(2)}, u32[]{:S(2)}) collective-permute-start(f32[512,256]{1,0:T(8,128)} %copy-done.25), channel_id=1, source_target_pairs={{0,4},{4,0},{1,5},{5,1},{2,6},{6,2},{3,7},{7,3},{8,12},{12,8},{9,1... | collective-permute-start | bytes 1572872 | tf_op jit(solution)/shard_map/ppermute | solution.py:440
  75.2 12.0 %copy-start = (f32[1,3,512,512]{3,2,1,0:T(8,128)S(1)}, f32[1,3,512,512]{3,2,1,0:T(8,128)}, u32[]{:S(2)}) copy-start(f32[1,3,512,512]{3,2,1,0:T(8,128)} %media_ref.13) | copy-start | bytes 9437188
  75.2 12.0 %copy-start.21 = (s32[1,1,1,4,256]{4,3,2,1,0:T(4,128)S(1)}, s32[1,1,1,4,256]{4,3,2,1,0:T(4,128)}, u32[]{:S(2)}) copy-start(s32[1,1,1,4,256]{4,3,2,1,0:T(4,128)} %cells_ref.1) | copy-start | bytes 12292
  75.2 12.0 %copy-start.22 = (s32[1,512]{1,0:T(1,128)S(1)}, s32[1,512]{1,0:T(1,128)}, u32[]{:S(2)}) copy-start(s32[1,512]{1,0:T(1,128)} %el_pair_ref.1) | copy-start | bytes 6148
  75.2 12.0 %copy-start.23 = (s32[1,512]{1,0:T(1,128)S(1)}, s32[1,512]{1,0:T(1,128)}, u32[]{:S(2)}) copy-start(s32[1,512]{1,0:T(1,128)} %ac_pair_ref.1) | copy-start | bytes 6148
  75.2 12.0 %copy-start.24 = (s32[1,1,1,4]{3,2,1,0:T(1,128)S(1)}, s32[1,1,1,4]{3,2,1,0:T(1,128)}, u32[]{:S(2)}) copy-start(s32[1,1,1,4]{3,2,1,0:T(1,128)} %counts_ref.1) | copy-start | bytes 52
  96.0 25.6 %copy-start.6 = (bf16[512,1536]{1,0:T(8,128)(2,1)S(1)}, bf16[512,1536]{1,0:T(8,128)(2,1)}, u32[]{:S(2)}) copy-start(bf16[512,1536]{1,0:T(8,128)(2,1)} %copy-done.5) | copy-start | bytes 4718596
  121.6 3.7 %copy-start.27 = (f32[512,128]{1,0:T(8,128)S(1)}, f32[512,128]{1,0:T(8,128)}, u32[]{:S(2)}) copy-start(f32[512,128]{1,0:T(8,128)} %copy-done.26) | copy-start | bytes 786436
  125.3 19.8 %collective-permute-start.6 = (f32[512,128]{1,0:T(8,128)S(1)}, f32[512,128]{1,0:T(8,128)S(1)}, u32[]{:S(2)}, u32[]{:S(2)}) collective-permute-start(f32[512,128]{1,0:T(8,128)S(1)} %copy-done.27), channel_id=1, source_target_pairs={{0,4},{4,0},{1,5},{5,1},{2,6},{6,2},{3,7},{7,3},{8,12},{12,8},{9,1... | collective-permute-start | bytes 786440 | tf_op jit(solution)/shard_map/ppermute | solution.py:440
  129.1 3.4 %copy-start.16 = (f32[2,512,128]{2,1,0:T(8,128)S(1)}, f32[2,512,128]{2,1,0:T(8,128)}, u32[]{:S(2)}) copy-start(f32[2,512,128]{2,1,0:T(8,128)} %constant.55.clone.tail_ref) | copy-start | bytes 1572868
  129.1 3.4 %copy-start.18 = (f32[512,128]{1,0:T(8,128)S(1)}, f32[512,128]{1,0:T(8,128)}, u32[]{:S(2)}) copy-start(f32[512,128]{1,0:T(8,128)} %copy-done.17) | copy-start | bytes 786436
  134.5 12.9 %collective-permute-start.7 = (f32[512,128]{1,0:T(8,128)S(1)}, f32[512,128]{1,0:T(8,128)S(1)}, u32[]{:S(2)}, u32[]{:S(2)}) collective-permute-start(f32[512,128]{1,0:T(8,128)S(1)} %sent_products.1), channel_id=1, source_target_pairs={{0,4},{4,0},{1,5},{5,1},{2,6},{6,2},{3,7},{7,3},{8,12},{12,8},{9,1... | collective-permute-start | bytes 786440 | tf_op jit(solution)/shard_map/ppermute | solution.py:539
  (20 other events, 34.3 us)

commit v5 on v4

--- a/solution.py
+++ b/solution.py
@@ -12,7 +12,8 @@
 STEP = 0.25
 PENALTY = 2.0
 LANES = 128
-MIB = 1024 * 1024
+VMEM_LIMIT = 56 * 1024 * 1024
+FAR_VMEM_LIMIT = 24 * 1024 * 1024
 HIGHEST = lax.Precision.HIGHEST
 
 
@@ -60,26 +61,62 @@
     return lax.div(value, size), lax.rem(value, size)
 
 
-def take_kernel(pieces, elastic_ref, acoustic_ref, outs, semaphores):
+def through_vmem(parts, in_semaphores, out_semaphores):
+    loads, stores = [], []
+    for i, (source, target, buffer) in enumerate(parts):
+        loads.append(pltpu.make_async_copy(source, buffer, in_semaphores.at[i]))
+        stores.append(pltpu.make_async_copy(buffer, target, out_semaphores.at[i]))
+    for load in loads:
+        load.start()
+    for load, store in zip(loads, stores):
+        load.wait()
+        store.start()
+    return stores
+
+
+def take_rows_kernel(field, first, parts, *refs):
+    elastic_ref = refs[-5]
+    out_ref, held, in_semaphores, out_semaphores = refs[-4:]
+    size = out_ref.shape[0] // parts
     copies = []
+    for part in range(parts):
+        here = pl.ds(part * size, size)
+        source = elastic_ref.at[0, field, pl.ds(first + part * size, size)]
+        copies.append((source, out_ref.at[here], held.at[here]))
+    for store in through_vmem(copies, in_semaphores, out_semaphores):
+        store.wait()
+
+
+def take_rows(elastic, field, first, count, after=None):
+    depth = elastic.shape[3]
+    parts = 2 if count % 32 == 0 else 1
+    anywhere = pl.BlockSpec(memory_space=pl.ANY)
+    operands = (elastic,) if after is None else (after, elastic)
+    return pl.pallas_call(
+        functools.partial(take_rows_kernel, field, first, parts),
+        in_specs=[anywhere] * len(operands),
+        out_specs=anywhere,
+        out_shape=jax.ShapeDtypeStruct((count, depth), jnp.float32),
+        scratch_shapes=[pltpu.VMEM((count, depth), jnp.float32)] + [pltpu.SemaphoreType.DMA((parts,))] * 2,
+        compiler_params=pltpu.CompilerParams(vmem_limit_bytes=VMEM_LIMIT),
+        cost_estimate=pl.CostEstimate(flops=0, bytes_accessed=8 * count * depth, transcendentals=0),
+        name="take_rows",
+    )(*operands)
+
+
+def take_pieces_kernel(
+    pieces, layers, after_ref, elastic_ref, acoustic_ref, cells_ref, weights_ref, *refs
+):
+    del after_ref
+    n = len(pieces)
+    outs, (edges_ref, asked_ref), held = refs[:n], refs[n : n + 2], refs[n + 2 : 2 * n + 2]
+    tiles, edge_semaphores, in_semaphores, out_semaphores = refs[2 * n + 2 :]
+    n_el, n_ac = elastic_ref.shape[1], acoustic_ref.shape[1]
+    rows, depth = elastic_ref.shape[2:]
+    parts = []
     for i, (name, field, at, width) in enumerate(pieces):
         source = elastic_ref if name == "el" else acoustic_ref
-        copies.append(pltpu.make_async_copy(source.at[0, field, :, pl.ds(at, width)], outs[i], semaphores.at[i]))
-    for copy in copies:
-        copy.start()
-    return copies
-
-
-def take_only_kernel(pieces, elastic_ref, *refs):
-    for copy in take_kernel(pieces, elastic_ref, None, refs[:-1], refs[-1]):
-        copy.wait()
-
-
-def take_and_edges_kernel(pieces, layers, after_ref, elastic_ref, acoustic_ref, *refs):
-    del after_ref
-    edges_ref, tiles, edge_semaphores, semaphores = refs[len(pieces) :]
-    n_el, n_ac = elastic_ref.shape[1], acoustic_ref.shape[1]
-    rows, depth = elastic_ref.shape[2:]
+        parts.append((source.at[0, field, :, pl.ds(at, width)], outs[i], held[i]))
     loads = []
     for end, at in enumerate((0, depth - LANES)):
         for k, (source, first, count) in enumerate(((elastic_ref, 0, n_el), (acoustic_ref, n_el, n_ac))):
@@ -90,9 +127,15 @@
                     edge_semaphores.at[2 * end + k],
                 )
             )
-    copies = take_kernel(pieces, elastic_ref, acoustic_ref, refs[: len(pieces)], semaphores)
+    stores = through_vmem(parts, in_semaphores, out_semaphores)
     for load in loads:
         load.start()
+
+    x, z = split(cells_ref[0, 0, 0], depth)
+    chunk, lane = split(z, LANES)
+    words = (chunk * ((n_el + n_ac) * rows) + x) * LANES + lane
+    asked_ref[...] = jnp.concatenate([words.astype(jnp.float32), weights_ref[0, 0, 0]], axis=1)
+
     for load in loads:
         load.wait()
     lane = lax.broadcasted_iota(jnp.int32, (rows, LANES), 1)
@@ -104,32 +147,34 @@
     below = lax.rem(lax.axis_index("layer") + 1, layers)
     for to in range(layers):
         edges_ref[to] = jnp.where(to == below, lines[8:16], lines[0:8])
-    for copy in copies:
-        copy.wait()
-
-
-def take_pieces(elastic, acoustic, pieces, after=None, layers=0):
+    for store in stores:
+        store.wait()
+
+
+def take_pieces(elastic, acoustic, cells, weights, pieces, after, layers):
     rows = elastic.shape[2]
+    patches, corners, slots = cells.shape[3:]
+    n = len(pieces)
     anywhere = pl.BlockSpec(memory_space=pl.ANY)
     vmem = pl.BlockSpec(memory_space=pltpu.VMEM)
-    out_shape = [jax.ShapeDtypeStruct((rows, width), jnp.float32) for _, _, _, width in pieces]
-    scratch = [pltpu.SemaphoreType.DMA((len(pieces),))]
-    kernel, operands = functools.partial(take_only_kernel, pieces), (elastic,)
-    if layers:
-        out_shape.append(jax.ShapeDtypeStruct((layers, 8, rows), jnp.float32))
-        scratch = [pltpu.VMEM((2, 8, rows, LANES), jnp.float32), pltpu.SemaphoreType.DMA((4,))] + scratch
-        kernel, operands = functools.partial(take_and_edges_kernel, pieces, layers), (after, elastic, acoustic)
-    cells = sum(width for _, _, _, width in pieces) * rows
+    travelling = [jax.ShapeDtypeStruct((rows, width), jnp.float32) for _, _, _, width in pieces]
+    cost = sum(width for _, _, _, width in pieces) * rows
     return pl.pallas_call(
-        kernel,
-        in_specs=[anywhere] * len(operands),
-        out_specs=[vmem] * len(out_shape),
-        out_shape=out_shape,
-        scratch_shapes=scratch,
-        compiler_params=pltpu.CompilerParams(vmem_limit_bytes=(14 if layers else 60) * MIB),
-        cost_estimate=pl.CostEstimate(flops=0, bytes_accessed=8 * cells, transcendentals=0),
+        functools.partial(take_pieces_kernel, pieces, layers),
+        in_specs=[anywhere] * 3 + [vmem] * 2,
+        out_specs=[anywhere] * n + [vmem] * 2,
+        out_shape=travelling
+        + [
+            jax.ShapeDtypeStruct((layers, 8, rows), jnp.float32),
+            jax.ShapeDtypeStruct((patches, 2 * corners, slots), jnp.float32),
+        ],
+        scratch_shapes=[pltpu.VMEM(piece.shape, jnp.float32) for piece in travelling]
+        + [pltpu.VMEM((2, 8, rows, LANES), jnp.float32), pltpu.SemaphoreType.DMA((4,))]
+        + [pltpu.SemaphoreType.DMA((n,))] * 2,
+        compiler_params=pltpu.CompilerParams(vmem_limit_bytes=VMEM_LIMIT),
+        cost_estimate=pl.CostEstimate(flops=0, bytes_accessed=8 * cost, transcendentals=0),
         name="take_pieces",
-    )(*operands)
+    )(after, elastic, acoustic, cells, weights)
 
 
 def gather_kernel(fields, rows, depth, words_ref, weights_ref, elastic_ref, acoustic_ref, out_ref, mixed):
@@ -227,7 +272,7 @@
             jax.ShapeDtypeStruct((6, rows, depth), jnp.float32),
             jax.ShapeDtypeStruct((rows, 3 * reach), jnp.bfloat16),
         ],
-        compiler_params=pltpu.CompilerParams(vmem_limit_bytes=28 * MIB),
+        compiler_params=pltpu.CompilerParams(vmem_limit_bytes=VMEM_LIMIT),
         cost_estimate=pl.CostEstimate(
             flops=36 * rows * rows * depth, bytes_accessed=60 * rows * depth, transcendentals=0
         ),
@@ -268,7 +313,7 @@
             out_specs=pl.BlockSpec((reach, width), lambda i, me: (0, 0)),
         ),
         out_shape=jax.ShapeDtypeStruct((reach, width), jnp.float32),
-        compiler_params=pltpu.CompilerParams(vmem_limit_bytes=16 * MIB),
+        compiler_params=pltpu.CompilerParams(vmem_limit_bytes=VMEM_LIMIT),
         cost_estimate=pl.CostEstimate(
             flops=6 * rows * reach * width, bytes_accessed=4 * rows * reach, transcendentals=0
         ),
@@ -366,9 +411,12 @@
         lax.fori_loop(0, counts_ref.shape[3], one_patch, 0)
 
 
-def far_kernel(coefficients, turn_ref, d_ref, far_ref, media_ref, open_ref, base_ref, next_ref, out_ref):
-    del turn_ref, next_ref
-    far = jnp.dot(d_ref[...], three_right(far_ref[...]), preferred_element_type=jnp.float32)
+def far_kernel(coefficients, turn_ref, d_ref, media_ref, open_ref, base_ref, *refs):
+    del turn_ref
+    *far_refs, next_ref, out_ref = refs
+    del next_ref
+    far_field = jnp.concatenate([far_ref[...] for far_ref in far_refs], axis=0)
+    far = jnp.dot(d_ref[...], three_right(far_field), preferred_element_type=jnp.float32)
     media = [media_ref[0, i] for i in range(media_ref.shape[1])]
     is_open = open_ref[...] > 0.5
     for i, coefficient in enumerate(coefficients):
@@ -377,8 +425,8 @@
 
 
 def add_far(base, operator, far, at, media, first_media, n_media, first_field, coefficients, opened, turn):
-    rows, reach = operator.shape[0], far.shape[0]
-    width = far.shape[1]
+    rows, reach = operator.shape[0], operator.shape[1] // 3
+    width = far[0].shape[1]
     tile = math.gcd(math.gcd(width, at), 2 * LANES)
     n_out = len(coefficients)
     shift = at // tile
@@ -388,11 +436,11 @@
         in_specs=[
             pl.BlockSpec(memory_space=pl.ANY),
             pl.BlockSpec((rows, 3 * reach), lambda i: (0, 0)),
-            pl.BlockSpec((reach, tile), lambda i: (0, i)),
             pl.BlockSpec((1, n_media, rows, tile), lambda i: (0, first_media // n_media, 0, i + shift)),
             pl.BlockSpec((rows, tile), lambda i: (0, i + shift)),
             pl.BlockSpec((1, n_out, rows, tile), lambda i: (0, first_field // n_out, 0, i + shift)),
-        ],
+        ]
+        + [pl.BlockSpec((part.shape[0], tile), lambda i: (0, i)) for part in far],
         out_specs=[
             pl.BlockSpec(memory_space=pl.ANY),
             pl.BlockSpec((1, n_out, rows, tile), lambda i: (0, first_field // n_out, 0, i + shift)),
@@ -401,15 +449,15 @@
             jax.ShapeDtypeStruct(turn.shape, turn.dtype),
             jax.ShapeDtypeStruct(base.shape, base.dtype),
         ],
-        input_output_aliases={0: 0, 5: 1},
-        compiler_params=pltpu.CompilerParams(vmem_limit_bytes=20 * MIB),
+        input_output_aliases={0: 0, 4: 1},
+        compiler_params=pltpu.CompilerParams(vmem_limit_bytes=FAR_VMEM_LIMIT),
         cost_estimate=pl.CostEstimate(
             flops=6 * rows * reach * width,
             bytes_accessed=4 * rows * width * (3 + n_media + n_out),
             transcendentals=0,
         ),
         name="add_far",
-    )(turn, operator, far, media, opened, base)
+    )(turn, operator, media, opened, base, *far)
 
 
 def per_device(
@@ -435,34 +483,31 @@
     layer = lax.axis_index("layer")
     tile = min(64, rows)
 
-    def other_slabs(value):
-        parts = [
+    def to_others(value):
+        return [
             lax.ppermute(value, "line", [(i, (i + distance) % slabs) for i in range(slabs)])
             for distance in range(1, slabs)
         ]
-        return parts[0] if slabs == 2 else jnp.concatenate(parts, axis=0)
-
-    half, quarter = depth // 2, depth // 4
+
+    most = depth - depth // 4
     pieces = [
         ("el", 0, 0, depth, "el", 0, 3, 2, (lambda b, l, m: l + 2.0 * m, lambda b, l, m: l)),
         ("ac", 0, 0, depth, "ac", 1, 1, 1, (lambda b: -b,)),
         ("ac", 1, 0, depth, "ac", 0, 1, 0, (lambda k: -k,)),
         ("el", 1, 0, depth, "el", 2, 1, 4, (lambda m: m,)),
         ("el", 2, 0, depth, "el", 0, 1, 0, (lambda b: b,)),
-        ("el", 4, 0, half, "el", 0, 1, 1, (lambda b: b,)),
-        ("el", 4, half, quarter, "el", 0, 1, 1, (lambda b: b,)),
-        ("el", 4, half + quarter, quarter, "el", 0, 1, 1, (lambda b: b,)),
+        ("el", 4, 0, most, "el", 0, 1, 1, (lambda b: b,)),
+        ("el", 4, most, depth - most, "el", 0, 1, 1, (lambda b: b,)),
     ]
-    travelling = [piece[:4] for piece in pieces]
-    (first,) = take_pieces(elastic, acoustic, travelling[:1])
-    *others, last, edges = take_pieces(elastic, acoustic, travelling[1:], first, layers)
-    far = [other_slabs(value) for value in [first, *others]]
-    tables = operator_tables(rows, slabs, cont_matrix.shape[0])
-
-    x, z = split(donor_cells[0, 0, 0], depth)
-    chunk, at_lane = split(z, LANES)
-    words = (chunk * (8 * rows) + x) * LANES + at_lane
-    asked = jnp.concatenate([words.astype(jnp.float32), donor_weights[0, 0, 0]], axis=1)
+    early = rows // 4
+    first = take_rows(elastic, 0, 0, early)
+    second = take_rows(elastic, 0, early, rows - early, first)
+    *others, last, edges, asked = take_pieces(
+        elastic, acoustic, donor_cells, donor_weights, [piece[:4] for piece in pieces[1:]], second, layers
+    )
+    far = [[part for pair in zip(to_others(first), to_others(second)) for part in pair]]
+    far += [to_others(value) for value in others]
+
     asked = lax.all_to_all(asked, "patch", split_axis=0, concat_axis=0, tiled=True)
     asked_words = asked[:, :4].astype(jnp.int32)
 
@@ -474,13 +519,14 @@
         out_specs=vmem,
         out_shape=jax.ShapeDtypeStruct((patches, groups, 8, LANES), jnp.float32),
         scratch_shapes=[pltpu.VMEM((8 * rows * (depth // LANES), LANES), jnp.float32)],
-        compiler_params=pltpu.CompilerParams(vmem_limit_bytes=24 * MIB),
+        compiler_params=pltpu.CompilerParams(vmem_limit_bytes=VMEM_LIMIT),
         cost_estimate=pl.CostEstimate(flops=10**9, bytes_accessed=32 * rows * depth, transcendentals=0),
         name="donor_gather",
     )(asked_words, asked, elastic, acoustic)
     interp = lax.all_to_all(local, "patch", split_axis=0, concat_axis=0, tiled=True)
     edges = lax.all_to_all(edges, "layer", split_axis=0, concat_axis=0, tiled=True)
 
+    tables = operator_tables(rows, slabs, cont_matrix.shape[0])
     near, far_operator = near_derivatives(elastic, acoustic, cont_matrix, tables, me, slabs)
     new_el, new_ac, opened = pl.pallas_call(
         functools.partial(section_kernel, layers, rows, depth, tile),
@@ -505,7 +551,7 @@
             jax.ShapeDtypeStruct((rows, depth), jnp.float32),
         ],
         scratch_shapes=[pltpu.VMEM((rows, LANES), jnp.float32)],
-        compiler_params=pltpu.CompilerParams(vmem_limit_bytes=28 * MIB),
+        compiler_params=pltpu.CompilerParams(vmem_limit_bytes=VMEM_LIMIT),
         cost_estimate=pl.CostEstimate(
             flops=100 * rows * depth, bytes_accessed=112 * rows * depth, transcendentals=0
         ),
@@ -534,23 +580,25 @@
             media[target], first_media, n_media, first_field, coefficients, opened, turn,
         )
         turns.append(turn)
+
     products = sent_products(last, cont_matrix, tables, me, slabs, turns[2])
-    products = [
-        lax.ppermute(
-            lax.slice_in_dim(products, (d - 1) * rows, d * rows),
-            "line",
-            [(i, (i + d) % slabs) for i in range(slabs)],
-        )
-        for d in range(1, slabs)
-    ]
-
     _, _, at, width, target, first_media, _, first_field, (coefficient,) = pieces[-1]
-    corner = (0, first_field, 0, at)
-    old = lax.dynamic_slice(section[target], corner, (1, 1, rows, width))
-    scale = STEP * coefficient(media[target][:, first_media : first_media + 1, :, at : at + width])
-    is_open = opened[None, None, :, at : at + width] > 0.5
-    new = jnp.where(is_open, old + scale * functools.reduce(jnp.add, products)[None, None], old)
-    section[target] = lax.dynamic_update_slice(section[target], new, corner)
+    for start, count in ((0, rows - early), (rows - early, early)):
+        received = [
+            lax.ppermute(
+                lax.slice_in_dim(products, (d - 1) * rows + start, (d - 1) * rows + start + count),
+                "line",
+                [(i, (i + d) % slabs) for i in range(slabs)],
+            )
+            for d in range(1, slabs)
+        ]
+        corner = (0, first_field, start, at)
+        here = (slice(start, start + count), slice(at, at + width))
+        old = lax.dynamic_slice(section[target], corner, (1, 1, count, width))
+        scale = STEP * coefficient(media[target][(slice(None), slice(first_media, first_media + 1)) + here])
+        far_part = functools.reduce(jnp.add, received)[None, None]
+        new = jnp.where(opened[here] > 0.5, old + scale * far_part, old)
+        section[target] = lax.optimization_barrier(lax.dynamic_update_slice(section[target], new, corner))
     return section["el"], section["ac"]
 
 

time: 149 us -> 150 us (level)
  local copies, waits for them, and re-layouts: 31.8 us -> 5.14 us
  Pallas kernels: 89 us -> 104 us
  waiting for transfers between devices: 2.31 us -> 10.6 us
  starting transfers between devices: 21.1 us -> 24.2 us
    unnamed x68 -> x24, local copies, waits for them, and re-layouts: 31.8 us -> 3.35 us
    ppermute x8 -> x9, waiting for transfers between devices: 0.02 us -> 7.56 us  [the longest x7 7.56 us: to_others(): lax.ppermute(value, 'line', [(i, (i + distance) % slabs) for i in range(s...]
    pallas_call x2 -> x3, Pallas kernels: 6.75 us -> 12 us  [the longest x1 8.37 us: take_pieces(): pl.pallas_call(functools.partial(take_pieces_kernel, pieces, layers), in_...]
    pallas_call x1, Pallas kernels: 8.05 us -> 12.7 us  [near_derivatives(): pl.pallas_call(functools.partial(near_kernel, 4), grid_spec=pltpu.Prefetc...]
    ppermute x8 -> x9, starting transfers between devices: 9.73 us -> 12.1 us  [the longest x7 9.75 us: to_others(): lax.ppermute(value, 'line', [(i, (i + distance) % slabs) for i in range(s...]
    pallas_call x1, Pallas kernels: 2.04 us -> 4.25 us  [sent_products(): pl.pallas_call(functools.partial(sent_kernel, rows), grid_spec=pltpu.Pref...]
    pallas_call x1, Pallas kernels: 25 us -> 27.2 us  [per_device(): pl.pallas_call(functools.partial(gather_kernel, 8, rows, depth), in_specs...]
    slice x0 -> x2, local copies, waits for them, and re-layouts: none -> 1.79 us  [per_device(): lax.slice_in_dim(products, (d - 1) * rows + start, (d - 1) * rows + start...]
  transfers between devices with their start and end apart: 11 -> 12, of which waited for: 1 -> 2; matrix products, arithmetic and copies ran while one was open for 2% -> 4% of each run, Pallas kernels for 58% -> 67%
where the time goes in v5:
time: 150 us
  Pallas kernels  104 us (69%)
  starting transfers between devices  24.2 us (16%)
  waiting for transfers between devices  10.6 us (7%)
  other arithmetic  5.41 us (4%)
  local copies, waits for them, and re-layouts  5.14 us (3%)
    pallas_call x1, Pallas kernels, per_device(): pl.pallas_call(functools.partial(gather_kernel, 8, rows, depth), in_specs...  27.2 us
    pallas_call x1, Pallas kernels, per_device(): pl.pallas_call(functools.partial(section_kernel, layers, rows, depth, til...  26.8 us
    pallas_call x6, Pallas kernels, add_far(): pl.pallas_call(functools.partial(far_kernel, coefficients), grid=(width /...  20.7 us
    pallas_call x1, Pallas kernels, near_derivatives(): pl.pallas_call(functools.partial(near_kernel, 4), grid_spec=pltpu.Prefetc...  12.7 us
    ppermute x7, starting transfers between devices, to_others(): lax.ppermute(value, 'line', [(i, (i + distance) % slabs) for i in range(s...  9.75 us
    pallas_call x1, Pallas kernels, take_pieces(): pl.pallas_call(functools.partial(take_pieces_kernel, pieces, layers), in_...  8.37 us
    ppermute x7, waiting for transfers between devices, to_others(): lax.ppermute(value, 'line', [(i, (i + distance) % slabs) for i in range(s...  7.56 us
    all_to_all x1, starting transfers between devices, per_device(): lax.all_to_all(edges, 'layer', split_axis=0, concat_axis=0, tiled=True)  4.87 us
  transfers between devices with their start and end apart: 12, of which 2 were waited for; matrix products, arithmetic and copies ran while one was open for 4% of the time, Pallas kernels for 67%

profile of v5, /device:TPU:0, one launch (start us, length us, event | category | flops | bytes accessed | tf_op | source)
XLA Modules:
  0.0 149.7 jit_solution(8182008187819248404)
XLA Ops:
  0.6 1.7 %take_rows.2.refs_0_ = f32[128,512]{1,0:T(8,128)} custom-call(f32[1,5,512,512]{3,2,1,0:T(8,128)} %elastic_ref.7), custom_call_target="tpu_custom_call" | custom-call | bytes 524288 | tf_op jit(solution)/shard_map/take_rows/pallas_call | solution.py:95
  2.3 1.9 %take_rows.3.after_ref = f32[384,512]{1,0:T(8,128)} custom-call(f32[128,512]{1,0:T(8,128)} %take_rows.2.refs_0_, f32[1,5,512,512]{3,2,1,0:T(8,128)} %elastic_ref.7), custom_call_target="tpu_custom_call" | custom-call | bytes 1572864 | tf_op jit(solution)/shard_map/take_rows/pallas_call | solution.py:95
  4.3 3.0 %collective-permute-start.1 = (f32[384,512]{1,0:T(8,128)}, f32[384,512]{1,0:T(8,128)S(1)}, u32[]{:S(2)}, u32[]{:S(2)}) collective-permute-start(f32[384,512]{1,0:T(8,128)} %take_rows.3.after_ref), channel_id=1, source_target_pairs={{0,4},{4,0},{1,5},{5,1},{2,6},{6,2},{3,7},{7,3},{8,12},{12,8},{9,1... | collective-permute-start | bytes 2359304 | tf_op jit(solution)/shard_map/ppermute | solution.py:488
  7.4 8.4 %take_pieces.1 = (f32[512,512]{1,0:T(8,128)}, f32[512,512]{1,0:T(8,128)}, f32[512,512]{1,0:T(8,128)}, f32[512,512]{1,0:T(8,128)}, f32[512,384]{1,0:T(8,128)}, /*...) custom-call(f32[384,512]{1,0:T(8,128)} %take_rows.3.after_ref, f32[1,5,512,512]{3,2,1,0:T(8,128)} %elastic_ref.7, ...), custom_call_target="tpu_custom_call" | custom-call | bytes 10485760 | tf_op jit(solution)/shard_map/take_pieces/pallas_call | solution.py:162
  15.8 3.9 %all-to-all-start = ((f32[4,8,256]{2,1,0:T(8,128)}), f32[4,8,256]{2,1,0:T(8,128)}, u32[]{:S(2)}, u32[]{:S(2)}) async-start(f32[4,8,256]{2,1,0:T(8,128)} %get-tuple-element.27), calls=%async_computation | async-start | bytes 65536 | tf_op jit(solution)/shard_map/all_to_all | solution.py:511
  19.7 2.0 %collective-permute-start.2 = (f32[512,512]{1,0:T(8,128)}, f32[512,512]{1,0:T(8,128)}, u32[]{:S(2)}, u32[]{:S(2)}) collective-permute-start(f32[512,512]{1,0:T(8,128)} %get-tuple-element.34), channel_id=1, source_target_pairs={{0,4},{4,0},{1,5},{5,1},{2,6},{6,2},{3,7},{7,3},{8,12},{12,8},{9,1... | collective-permute-start | bytes 3145736 | tf_op jit(solution)/shard_map/ppermute | solution.py:488
  21.8 1.9 %collective-permute-start.4 = (f32[512,512]{1,0:T(8,128)}, f32[512,512]{1,0:T(8,128)S(1)}, u32[]{:S(2)}, u32[]{:S(2)}) collective-permute-start(f32[512,512]{1,0:T(8,128)} %get-tuple-element.40), channel_id=1, source_target_pairs={{0,4},{4,0},{1,5},{5,1},{2,6},{6,2},{3,7},{7,3},{8,12},{12,8},{9,1... | collective-permute-start | bytes 3145736 | tf_op jit(solution)/shard_map/ppermute | solution.py:488
  24.0 7.5 %collective-permute-done.refs_0_ = f32[128,512]{1,0:T(8,128)S(1)} collective-permute-done((f32[128,512]{1,0:T(8,128)S(1)}, f32[128,512]{1,0:T(8,128)S(1)}, u32[]{:S(2)}, u32[]{:S(2)}) %collective-permute-start) | collective-permute-done | bytes 262176 | tf_op jit(solution)/shard_map/ppermute | solution.py:488
  31.5 2.1 %collective-permute-start.5 = (f32[512,512]{1,0:T(8,128)}, f32[512,512]{1,0:T(8,128)}, u32[]{:S(2)}, u32[]{:S(2)}) collective-permute-start(f32[512,512]{1,0:T(8,128)} %get-tuple-element.43), channel_id=1, source_target_pairs={{0,4},{4,0},{1,5},{5,1},{2,6},{6,2},{3,7},{7,3},{8,12},{12,8},{9,1... | collective-permute-start | bytes 3145736 | tf_op jit(solution)/shard_map/ppermute | solution.py:488
  34.9 27.2 %donor_gather.1 = f32[4,2,8,128]{3,2,1,0:T(8,128)} custom-call(s32[4,4,256]{2,1,0:T(4,128)} %slice_convert_fusion.words_ref, f32[4,8,256]{2,1,0:T(8,128)} %all-to-all-done.weights_ref, f32[1,5,512,512]{3,2,1,0:T(8,128)} %elastic_ref.7, f32[1,3,512,512]{3,2,1,0:T(8,128)} %acoustic_ref.7), custom_call_target="tpu_custom_call" | custom-call | flops 1000000000 | bytes 8388608 | tf_op jit(solution)/shard_map/donor_gather/pallas_call | solution.py:516
  62.1 3.3 %all-to-all-start.1 = ((f32[4,2,8,128]{3,2,1,0:T(8,128)}), f32[4,2,8,128]{3,2,1,0:T(8,128)S(1)}, u32[]{:S(2)}, u32[]{:S(2)}) async-start(f32[4,2,8,128]{3,2,1,0:T(8,128)} %donor_gather.1), calls=%async_computation.1 | async-start | bytes 65536 | tf_op jit(solution)/shard_map/all_to_all | solution.py:526
  66.3 3.0 %all-to-all-done.1.interp_ref = f32[4,2,8,128]{3,2,1,0:T(8,128)S(1)} async-done(((f32[4,2,8,128]{3,2,1,0:T(8,128)}), f32[4,2,8,128]{3,2,1,0:T(8,128)S(1)}, u32[]{:S(2)}, u32[]{:S(2)}) %all-to-all-start.1) | async-done | bytes 32800 | tf_op jit(solution)/shard_map/all_to_all | solution.py:526
  69.3 4.9 %all-to-all-start.2 = ((f32[4,8,512]{2,1,0:T(8,128)}), f32[4,8,512]{2,1,0:T(8,128)S(1)}, u32[]{:S(2)}, u32[]{:S(2)}) async-start(f32[4,8,512]{2,1,0:T(8,128)} %get-tuple-element.29), calls=%async_computation.2 | async-start | bytes 131072 | tf_op jit(solution)/shard_map/all_to_all | solution.py:527
  74.7 12.7 %near_dx.1 = (f32[6,512,512]{2,1,0:T(8,128)}, bf16[512,1536]{1,0:T(8,128)(2,1)}) custom-call(s32[1]{0:T(128)} %bitcast.me_ref, f32[512,512]{1,0:T(8,128)} %constant.43.clone.own_ref, f32[2,512,512]{2,1,0:T(8,128)} %constant.44.clone.far_ref, f32[2,512,128]{2,1,0:T(8,128)} %constant.45.clone.tail_ref, f32[128,512]{1,0:T(8,128)} %get-tuple-element.51.own_cont_ref.cont_ref, ...), custom_call_target="tpu_custom_call" | custom-call | flops 4831838208 | bytes 15728640 | tf_op jit(solution)/shard_map/near_dx/pallas_call | solution.py:251
  88.0 26.8 %near_section.1 = (f32[1,5,512,512]{3,2,1,0:T(8,128)}, f32[1,3,512,512]{3,2,1,0:T(8,128)}, f32[512,512]{1,0:T(8,128)}) custom-call(s32[1,1,1,4,256]{4,3,2,1,0:T(4,128)} %cells_ref.3, s32[1,1,1,4]{3,2,1,0:T(1,128)} %counts_ref.1, f32[4,2,8,128]{3,2,1,0:T(8,128)} %copy-done.9, f32[6,512,512]{2,1,0:T(8,128)} %get-tuple-element.28.dx_ref, ...), custom_call_target="tpu_custom_call" | custom-call | flops 26214400 | bytes 29360128 | tf_op jit(solution)/shard_map/near_section/pallas_call | solution.py:531
  116.1 3.8 %add_far.6 = (f32[8,128]{1,0:T(8,128)S(1)}, f32[1,5,512,512]{3,2,1,0:T(8,128)}) custom-call(f32[8,128]{1,0:T(8,128)S(1)} %broadcast_in_dim.26.turn_ref, bf16[512,1536]{1,0:T(8,128)(2,1)S(1)} %copy-done.1, f32[1,3,512,512]{3,2,1,0:T(8,128)S(1)} %copy-done, f32[512,512]{1,0:T(8,128)S(1)} %copy-done.2, ...), custom_call_target="tpu_custom_call", output_to_operand_aliasing={{0}: (0, {}), {1}: (4, {})} | custom-call | flops 805306368 | bytes 8388608 | tf_op jit(solution)/shard_map/add_far/pallas_call | solution.py:433
  119.8 3.3 %add_far.7 = (f32[8,128]{1,0:T(8,128)S(1)}, f32[1,3,512,512]{3,2,1,0:T(8,128)}) custom-call(f32[8,128]{1,0:T(8,128)S(1)} %get-tuple-element.32.turn_ref, bf16[512,1536]{1,0:T(8,128)(2,1)S(1)} %copy-done.1, f32[1,2,512,512]{3,2,1,0:T(8,128)S(1)} %copy-done.4, f32[512,512]{1,0:T(8,128)S(1)} %copy-done.2, ...), custom_call_target="tpu_custom_call", output_to_operand_aliasing={{0}: (0, {}), {1}: (4, {})} | custom-call | flops 805306368 | bytes 5242880 | tf_op jit(solution)/shard_map/add_far/pallas_call | solution.py:433
  123.1 3.2 %add_far.8 = (f32[8,128]{1,0:T(8,128)S(1)}, f32[1,3,512,512]{3,2,1,0:T(8,128)}) custom-call(f32[8,128]{1,0:T(8,128)S(1)} %get-tuple-element.35.turn_ref, bf16[512,1536]{1,0:T(8,128)(2,1)S(1)} %copy-done.1, f32[1,2,512,512]{3,2,1,0:T(8,128)S(1)} %copy-done.4, f32[512,512]{1,0:T(8,128)S(1)} %copy-done.2, ...), custom_call_target="tpu_custom_call", output_to_operand_aliasing={{0}: (0, {}), {1}: (4, {})} | custom-call | flops 805306368 | bytes 5242880 | tf_op jit(solution)/shard_map/add_far/pallas_call | solution.py:433
  126.9 4.2 %sent_products.1 = f32[512,128]{1,0:T(8,128)} custom-call(s32[1]{0:T(128)} %bitcast.me_ref, f32[8,128]{1,0:T(8,128)} %copy-done.5, f32[2,512,512]{2,1,0:T(8,128)} %constant.46.clone.sent_ref, f32[2,512,128]{2,1,0:T(8,128)} %constant.45.clone.tail_ref, f32[128,512]{1,0:T(8,128)} %get-tuple-element.51.own_cont_ref.cont_ref, f32[512,128]{1,0:T(8,128)} %get-tuple-element.48.piece_ref), custom_call_target="tpu_custom_call" | custom-call | flops 201326592 | bytes 1048576 | tf_op jit(solution)/shard_map/sent_products/pallas_call | solution.py:301
  132.9 2.4 %collective-permute-start.7 = (f32[384,128]{1,0:T(8,128)S(1)}, f32[384,128]{1,0:T(8,128)S(1)}, u32[]{:S(2)}, u32[]{:S(2)}) collective-permute-start(f32[384,128]{1,0:T(8,128)S(1)} %slice.41), channel_id=1, source_target_pairs={{0,4},{4,0},{1,5},{5,1},{2,6},{6,2},{3,7},{7,3},{8,12},{12,8},{9,1... | collective-permute-start | bytes 589832 | tf_op jit(solution)/shard_map/ppermute | solution.py:588
  136.0 3.1 %add_far.9 = (f32[8,128]{1,0:T(8,128)S(1)}, f32[1,5,512,512]{3,2,1,0:T(8,128)}) custom-call(f32[8,128]{1,0:T(8,128)S(1)} %copy-done.6, bf16[512,1536]{1,0:T(8,128)(2,1)S(1)} %copy-done.1, f32[1,3,512,512]{3,2,1,0:T(8,128)S(1)} %copy-done, f32[512,512]{1,0:T(8,128)S(1)} %copy-done.3, ...), custom_call_target="tpu_custom_call", output_to_operand_aliasing={{0}: (0, {}), {1}: (4, {})} | custom-call | flops 805306368 | bytes 5242880 | tf_op jit(solution)/shard_map/add_far/pallas_call | solution.py:433
  139.1 3.3 %add_far.10 = (f32[8,128]{1,0:T(8,128)S(1)}, f32[1,5,512,512]{3,2,1,0:T(8,128)}) custom-call(f32[8,128]{1,0:T(8,128)S(1)} %get-tuple-element.41.turn_ref, bf16[512,1536]{1,0:T(8,128)(2,1)S(1)} %copy-done.1, f32[1,3,512,512]{3,2,1,0:T(8,128)S(1)} %copy-done, f32[512,512]{1,0:T(8,128)S(1)} %copy-done.3, ...), custom_call_target="tpu_custom_call", output_to_operand_aliasing={{0}: (0, {}), {1}: (4, {})} | custom-call | flops 805306368 | bytes 5242880 | tf_op jit(solution)/shard_map/add_far/pallas_call | solution.py:433
  142.4 4.1 %add_far.11 = (f32[8,128]{1,0:T(8,128)S(1)}, f32[1,5,512,512]{3,2,1,0:T(8,128)}) custom-call(f32[8,128]{1,0:T(8,128)S(1)} %get-tuple-element.44.turn_ref, bf16[512,1536]{1,0:T(8,128)(2,1)S(1)} %copy-done.1, f32[1,3,512,512]{3,2,1,0:T(8,128)S(1)} %copy-done, f32[512,512]{1,0:T(8,128)S(1)} %copy-done.3, ...), custom_call_target="tpu_custom_call", output_to_operand_aliasing={{0}: (0, {}), {1}: (4, {})} | custom-call | flops 603979776 | bytes 3932160 | tf_op jit(solution)/shard_map/add_far/pallas_call | solution.py:433
  146.5 1.7 %fusion.2 = f32[1,5,512,512]{3,2,1,0:T(8,128)} fusion(f32[1,5,512,512]{3,2,1,0:T(8,128)} %get-tuple-element.47, f32[384,128]{1,0:T(8,128)S(1)} %collective-permute-done.7, f32[1,3,512,512]{3,2,1,0:T(8,128)S(1)} %copy-done, f32[512,512]{1,0:T(8,128)S(1)} %copy-done.3), kind=kLoop, calls=%fused_computation.7 | loop fusion | flops 245760 | bytes 983040 | tf_op jit(solution)/shard_map/dynamic_update_slice | solution.py:601
  (45 shorter events, 9.6 us)
Async XLA Ops:
  2.3 5.0 %copy-start.7 = (f32[128,512]{1,0:T(8,128)S(1)}, f32[128,512]{1,0:T(8,128)}, u32[]{:S(2)}) copy-start(f32[128,512]{1,0:T(8,128)} %take_rows.2.refs_0_) | copy-start | bytes 786436
  4.3 19.5 %copy-start.10 = (f32[128,20]{0,1:T(8,128)S(1)}, f32[128,20]{0,1:T(8,128)}, u32[]{:S(2)}) copy-start(f32[128,20]{0,1:T(8,128)} %param.19) | copy-start | bytes 30724
  4.3 69.9 %collective-permute-start.1 = (f32[384,512]{1,0:T(8,128)}, f32[384,512]{1,0:T(8,128)S(1)}, u32[]{:S(2)}, u32[]{:S(2)}) collective-permute-start(f32[384,512]{1,0:T(8,128)} %take_rows.3.after_ref), channel_id=1, source_target_pairs={{0,4},{4,0},{1,5},{5,1},{2,6},{6,2},{3,7},{7,3},{8,12},{12,8},{9,1... | collective-permute-start | bytes 2359304 | tf_op jit(solution)/shard_map/ppermute | solution.py:488
  7.3 24.2 %collective-permute-start = (f32[128,512]{1,0:T(8,128)S(1)}, f32[128,512]{1,0:T(8,128)S(1)}, u32[]{:S(2)}, u32[]{:S(2)}) collective-permute-start(f32[128,512]{1,0:T(8,128)S(1)} %copy-done.7), channel_id=1, source_target_pairs={{0,4},{4,0},{1,5},{5,1},{2,6},{6,2},{3,7},{7,3},{8,12},{12,8},{9,1... | collective-permute-start | bytes 786440 | tf_op jit(solution)/shard_map/ppermute | solution.py:488
  15.8 17.8 %all-to-all-start = ((f32[4,8,256]{2,1,0:T(8,128)}), f32[4,8,256]{2,1,0:T(8,128)}, u32[]{:S(2)}, u32[]{:S(2)}) async-start(f32[4,8,256]{2,1,0:T(8,128)} %get-tuple-element.27), calls=%async_computation | async-start | bytes 65536 | tf_op jit(solution)/shard_map/all_to_all | solution.py:511
  19.7 100.2 %collective-permute-start.2 = (f32[512,512]{1,0:T(8,128)}, f32[512,512]{1,0:T(8,128)}, u32[]{:S(2)}, u32[]{:S(2)}) collective-permute-start(f32[512,512]{1,0:T(8,128)} %get-tuple-element.34), channel_id=1, source_target_pairs={{0,4},{4,0},{1,5},{5,1},{2,6},{6,2},{3,7},{7,3},{8,12},{12,8},{9,1... | collective-permute-start | bytes 3145736 | tf_op jit(solution)/shard_map/ppermute | solution.py:488
  21.7 101.4 %collective-permute-start.3 = (f32[512,512]{1,0:T(8,128)}, f32[512,512]{1,0:T(8,128)S(1)}, u32[]{:S(2)}, u32[]{:S(2)}) collective-permute-start(f32[512,512]{1,0:T(8,128)} %get-tuple-element.37), channel_id=1, source_target_pairs={{0,4},{4,0},{1,5},{5,1},{2,6},{6,2},{3,7},{7,3},{8,12},{12,8},{9,1... | collective-permute-start | bytes 3145736 | tf_op jit(solution)/shard_map/ppermute | solution.py:488
  21.8 113.5 %collective-permute-start.4 = (f32[512,512]{1,0:T(8,128)}, f32[512,512]{1,0:T(8,128)S(1)}, u32[]{:S(2)}, u32[]{:S(2)}) collective-permute-start(f32[512,512]{1,0:T(8,128)} %get-tuple-element.40), channel_id=1, source_target_pairs={{0,4},{4,0},{1,5},{5,1},{2,6},{6,2},{3,7},{7,3},{8,12},{12,8},{9,1... | collective-permute-start | bytes 3145736 | tf_op jit(solution)/shard_map/ppermute | solution.py:488
  31.5 107.6 %collective-permute-start.5 = (f32[512,512]{1,0:T(8,128)}, f32[512,512]{1,0:T(8,128)}, u32[]{:S(2)}, u32[]{:S(2)}) collective-permute-start(f32[512,512]{1,0:T(8,128)} %get-tuple-element.43), channel_id=1, source_target_pairs={{0,4},{4,0},{1,5},{5,1},{2,6},{6,2},{3,7},{7,3},{8,12},{12,8},{9,1... | collective-permute-start | bytes 3145736 | tf_op jit(solution)/shard_map/ppermute | solution.py:488
  62.1 7.2 %all-to-all-start.1 = ((f32[4,2,8,128]{3,2,1,0:T(8,128)}), f32[4,2,8,128]{3,2,1,0:T(8,128)S(1)}, u32[]{:S(2)}, u32[]{:S(2)}) async-start(f32[4,2,8,128]{3,2,1,0:T(8,128)} %donor_gather.1), calls=%async_computation.1 | async-start | bytes 65536 | tf_op jit(solution)/shard_map/all_to_all | solution.py:526
  69.3 18.1 %copy-start.9 = (f32[4,2,8,128]{3,2,1,0:T(8,128)}, f32[4,2,8,128]{3,2,1,0:T(8,128)S(1)}, u32[]{:S(2)}) copy-start(f32[4,2,8,128]{3,2,1,0:T(8,128)S(1)} %all-to-all-done.1.interp_ref) | copy-start | bytes 98308
  69.3 18.1 %all-to-all-start.2 = ((f32[4,8,512]{2,1,0:T(8,128)}), f32[4,8,512]{2,1,0:T(8,128)S(1)}, u32[]{:S(2)}, u32[]{:S(2)}) async-start(f32[4,8,512]{2,1,0:T(8,128)} %get-tuple-element.29), calls=%async_computation.2 | async-start | bytes 131072 | tf_op jit(solution)/shard_map/all_to_all | solution.py:527
  74.2 68.2 %collective-permute-start.6 = (f32[512,384]{1,0:T(8,128)}, f32[512,384]{1,0:T(8,128)}, u32[]{:S(2)}, u32[]{:S(2)}) collective-permute-start(f32[512,384]{1,0:T(8,128)} %get-tuple-element.46), channel_id=1, source_target_pairs={{0,4},{4,0},{1,5},{5,1},{2,6},{6,2},{3,7},{7,3},{8,12},{12,8},{9,1... | collective-permute-start | bytes 2359304 | tf_op jit(solution)/shard_map/ppermute | solution.py:488
  87.4 0.6 copy-start.8
  88.0 26.8 %copy-start = (f32[1,3,512,512]{3,2,1,0:T(8,128)S(1)}, f32[1,3,512,512]{3,2,1,0:T(8,128)}, u32[]{:S(2)}) copy-start(f32[1,3,512,512]{3,2,1,0:T(8,128)} %media_ref.11) | copy-start | bytes 9437188
  88.0 26.8 %copy-start.1 = (bf16[512,1536]{1,0:T(8,128)(2,1)S(1)}, bf16[512,1536]{1,0:T(8,128)(2,1)}, u32[]{:S(2)}) copy-start(bf16[512,1536]{1,0:T(8,128)(2,1)} %get-tuple-element.26.d_ref) | copy-start | bytes 4718596
  114.9 1.2 copy-start.2
  116.1 3.8 %copy-start.4 = (f32[1,2,512,512]{3,2,1,0:T(8,128)S(1)}, f32[1,2,512,512]{3,2,1,0:T(8,128)}, u32[]{:S(2)}) copy-start(f32[1,2,512,512]{3,2,1,0:T(8,128)} %media_ref.8) | copy-start | bytes 6291460
  123.1 12.2 %copy-start.3 = (f32[512,512]{1,0:T(8,128)S(1)}, f32[512,512]{1,0:T(8,128)}, u32[]{:S(2)}) copy-start(f32[512,512]{1,0:T(8,128)} %get-tuple-element.30.open_ref) | copy-start | bytes 3145732
  126.3 0.6 copy-start.5
  132.9 13.6 %collective-permute-start.7 = (f32[384,128]{1,0:T(8,128)S(1)}, f32[384,128]{1,0:T(8,128)S(1)}, u32[]{:S(2)}, u32[]{:S(2)}) collective-permute-start(f32[384,128]{1,0:T(8,128)S(1)} %slice.41), channel_id=1, source_target_pairs={{0,4},{4,0},{1,5},{5,1},{2,6},{6,2},{3,7},{7,3},{8,12},{12,8},{9,1... | collective-permute-start | bytes 589832 | tf_op jit(solution)/shard_map/ppermute | solution.py:588
  135.3 12.9 %collective-permute-start.8 = (f32[128,128]{1,0:T(8,128)S(1)}, f32[128,128]{1,0:T(8,128)S(1)}, u32[]{:S(2)}, u32[]{:S(2)}) collective-permute-start(f32[128,128]{1,0:T(8,128)S(1)} %slice.42), channel_id=1, source_target_pairs={{0,4},{4,0},{1,5},{5,1},{2,6},{6,2},{3,7},{7,3},{8,12},{12,8},{9,1... | collective-permute-start | bytes 196616 | tf_op jit(solution)/shard_map/ppermute | solution.py:588
  135.3 0.7 copy-start.6

commit v6 on v3

--- a/solution.py
+++ b/solution.py
@@ -59,8 +59,7 @@
     return lax.div(value, size), lax.rem(value, size)
 
 
-def take_kernel(pieces, parts, elastic_ref, acoustic_ref, after_ref, *refs):
-    del after_ref
+def take_kernel(pieces, parts, elastic_ref, acoustic_ref, *refs):
     n = len(pieces)
     outs, held, in_semaphores, out_semaphores = refs[:n], refs[n : 2 * n], refs[-2], refs[-1]
     rows = elastic_ref.shape[2]
@@ -82,14 +81,17 @@
     return stores
 
 
-def take_only_kernel(pieces, parts, *refs):
-    for store in take_kernel(pieces, parts, *refs):
+def take_only_kernel(pieces, parts, elastic_ref, *refs):
+    for store in take_kernel(pieces, parts, elastic_ref, None, *refs):
         store.wait()
 
 
-def take_and_edges_kernel(pieces, parts, layers, elastic_ref, acoustic_ref, after_ref, *refs):
+def take_and_edges_kernel(
+    pieces, parts, layers, after_ref, elastic_ref, acoustic_ref, cells_ref, weights_ref, *refs
+):
+    del after_ref
     n = len(pieces)
-    edges_ref, tiles, edge_semaphores = refs[n : n + 3]
+    edges_ref, asked_ref, tiles, edge_semaphores = refs[n : n + 4]
     n_el, n_ac = elastic_ref.shape[1], acoustic_ref.shape[1]
     rows, depth = elastic_ref.shape[2:]
     loads = []
@@ -104,7 +106,13 @@
             )
     for load in loads:
         load.start()
-    stores = take_kernel(pieces, parts, elastic_ref, acoustic_ref, after_ref, *refs[:n], *refs[n + 3 :])
+    stores = take_kernel(pieces, parts, elastic_ref, acoustic_ref, *refs[:n], *refs[n + 4 :])
+
+    x, z = split(cells_ref[0, 0, 0], depth)
+    chunk, at_lane = split(z, LANES)
+    words = (chunk * ((n_el + n_ac) * rows) + x) * LANES + at_lane
+    asked_ref[...] = jnp.concatenate([words.astype(jnp.float32), weights_ref[0, 0, 0]], axis=1)
+
     for load in loads:
         load.wait()
     lane = lax.broadcasted_iota(jnp.int32, (rows, LANES), 1)
@@ -120,31 +128,35 @@
         store.wait()
 
 
-def take_pieces(elastic, acoustic, after, pieces, layers=0):
+def take_pieces(elastic, acoustic, pieces, after=None, cells=None, weights=None, layers=0):
     rows = elastic.shape[2]
     anywhere = pl.BlockSpec(memory_space=pl.ANY)
+    vmem = pl.BlockSpec(memory_space=pltpu.VMEM)
     out_shape = [jax.ShapeDtypeStruct((rows, width), jnp.float32) for _, _, _, width in pieces]
-    out_specs = [anywhere] * len(pieces)
+    in_specs, out_specs = [anywhere], [anywhere] * len(pieces)
     parts = 2 if layers else 4
     scratch = [pltpu.VMEM((rows, width), jnp.float32) for _, _, _, width in pieces]
     scratch += [pltpu.SemaphoreType.DMA((len(pieces) * parts,))] * 2
-    kernel = functools.partial(take_only_kernel, pieces, parts)
+    kernel, operands = functools.partial(take_only_kernel, pieces, parts), (elastic,)
     if layers:
+        patches, corners, slots = cells.shape[3:]
         out_shape.append(jax.ShapeDtypeStruct((layers, 8, rows), jnp.float32))
-        out_specs.append(pl.BlockSpec(memory_space=pltpu.VMEM))
+        out_shape.append(jax.ShapeDtypeStruct((patches, 2 * corners, slots), jnp.float32))
+        in_specs, out_specs = [anywhere] * 3 + [vmem] * 2, out_specs + [vmem] * 2
         scratch = [pltpu.VMEM((2, 8, rows, LANES), jnp.float32), pltpu.SemaphoreType.DMA((4,))] + scratch
         kernel = functools.partial(take_and_edges_kernel, pieces, parts, layers)
-    cells = sum(width for _, _, _, width in pieces) * rows
+        operands = (after, elastic, acoustic, cells, weights)
+    cost = sum(width for _, _, _, width in pieces) * rows
     return pl.pallas_call(
         kernel,
-        in_specs=[anywhere] * 3,
+        in_specs=in_specs,
         out_specs=out_specs,
         out_shape=out_shape,
         scratch_shapes=scratch,
         compiler_params=pltpu.CompilerParams(vmem_limit_bytes=VMEM_LIMIT),
-        cost_estimate=pl.CostEstimate(flops=0, bytes_accessed=8 * cells, transcendentals=0),
+        cost_estimate=pl.CostEstimate(flops=0, bytes_accessed=8 * cost, transcendentals=0),
         name="take_pieces",
-    )(elastic, acoustic, after)
+    )(*operands)
 
 
 def gather_kernel(fields, rows, depth, words_ref, weights_ref, elastic_ref, acoustic_ref, out_ref, mixed):
@@ -428,14 +440,12 @@
         ("el", 4, half + quarter, quarter, "el", 0, 1, 1, (lambda b: b,)),
     ]
     travelling = [piece[:4] for piece in pieces]
-    (first,) = take_pieces(elastic, acoustic, cont_matrix, travelling[:1])
-    *others, edges = take_pieces(elastic, acoustic, first, travelling[1:], layers)
+    (first,) = take_pieces(elastic, acoustic, travelling[:1])
+    *others, edges, asked = take_pieces(
+        elastic, acoustic, travelling[1:], first, donor_cells, donor_weights, layers
+    )
     far = [other_slabs(value) for value in [first, *others]]
 
-    x, z = split(donor_cells[0, 0, 0], depth)
-    chunk, at_lane = split(z, LANES)
-    words = (chunk * (8 * rows) + x) * LANES + at_lane
-    asked = jnp.concatenate([words.astype(jnp.float32), donor_weights[0, 0, 0]], axis=1)
     asked = lax.all_to_all(asked, "patch", split_axis=0, concat_axis=0, tiled=True)
     asked_words = asked[:, :4].astype(jnp.int32)
 

time: 146 us -> 145 us (level)
  Pallas kernels: 97 us -> 98.5 us
  starting transfers between devices: 23.2 us -> 21.7 us
    unnamed x25 -> x22, local copies, waits for them, and re-layouts: 3.33 us -> 2.11 us
  transfers between devices with their start and end apart: 11 -> 11, of which waited for: 5 -> 5; matrix products, arithmetic and copies ran while one was open for 2% -> 1% of each run, Pallas kernels for 64% -> 66%
where the time goes in v6:
time: 145 us; the launch traced here: 144 us
  Pallas kernels  98.5 us (68%)
  starting transfers between devices  21.7 us (15%)
  waiting for transfers between devices  19.1 us (13%)
  local copies, waits for them, and re-layouts  2.12 us (1%)
  other arithmetic  1.52 us (1%)
    pallas_call x1, Pallas kernels, per_device(): pl.pallas_call(functools.partial(gather_kernel, 8, rows, depth), in_specs...  27.2 us
    pallas_call x1, Pallas kernels, per_device(): pl.pallas_call(functools.partial(section_kernel, layers, rows, depth, til...  24.5 us
    pallas_call x8, Pallas kernels, add_far(): pl.pallas_call(functools.partial(far_kernel, coefficients), grid=(width /...  23.7 us
    ppermute x8, waiting for transfers between devices, other_slabs(): lax.ppermute(value, 'line', [(i, (i + distance) % slabs) for i in range(s...  16.1 us
    pallas_call x1, Pallas kernels, near_derivatives(): pl.pallas_call(functools.partial(near_kernel, 4), grid_spec=pltpu.Prefetc...  12.8 us
    pallas_call x2, Pallas kernels, take_pieces(): pl.pallas_call(kernel, in_specs=in_specs, out_specs=out_specs, out_shape=...  10.4 us
    ppermute x8, starting transfers between devices, other_slabs(): lax.ppermute(value, 'line', [(i, (i + distance) % slabs) for i in range(s...  10.3 us
    all_to_all x1, starting transfers between devices, per_device(): lax.all_to_all(edges, 'layer', split_axis=0, concat_axis=0, tiled=True)  4.89 us
  transfers between devices with their start and end apart: 11, of which 5 were waited for; matrix products, arithmetic and copies ran while one was open for 1% of the time, Pallas kernels for 66%

profile of v6, /device:TPU:0, one launch (start us, length us, event | category | flops | bytes accessed | tf_op | source)
XLA Modules:
  0.0 143.7 jit_solution(14518184436331616989)
XLA Ops:
  0.6 2.0 %take_pieces.2.after_ref = f32[512,512]{1,0:T(8,128)} custom-call(f32[1,5,512,512]{3,2,1,0:T(8,128)} %elastic_ref.9), custom_call_target="tpu_custom_call" | custom-call | bytes 2097152 | tf_op jit(solution)/shard_map/take_pieces/pallas_call | solution.py:150
  2.6 3.0 %collective-permute-start = (f32[512,512]{1,0:T(8,128)}, f32[512,512]{1,0:T(8,128)}, u32[]{:S(2)}, u32[]{:S(2)}) collective-permute-start(f32[512,512]{1,0:T(8,128)} %take_pieces.2.after_ref), channel_id=1, source_target_pairs={{0,4},{4,0},{1,5},{5,1},{2,6},{6,2},{3,7},{7,3},{8,12},{12,8},{9,1... | collective-permute-start | bytes 3145736 | tf_op jit(solution)/shard_map/ppermute | solution.py:426
  5.7 8.4 %take_pieces.3 = (f32[512,512]{1,0:T(8,128)}, f32[512,512]{1,0:T(8,128)}, f32[512,512]{1,0:T(8,128)}, f32[512,512]{1,0:T(8,128)}, f32[512,256]{1,0:T(8,128)}, /*...) custom-call(f32[512,512]{1,0:T(8,128)} %take_pieces.2.after_ref, ...), custom_call_target="tpu_custom_call" | custom-call | bytes 10485760 | tf_op jit(solution)/shard_map/take_pieces/pallas_call | solution.py:150
  14.1 3.3 %all-to-all-start = ((f32[4,8,256]{2,1,0:T(8,128)}), f32[4,8,256]{2,1,0:T(8,128)S(1)}, u32[]{:S(2)}, u32[]{:S(2)}) async-start(f32[4,8,256]{2,1,0:T(8,128)} %get-tuple-element.32), calls=%async_computation | async-start | bytes 65536 | tf_op jit(solution)/shard_map/all_to_all | solution.py:449
  17.4 2.0 %collective-permute-start.2 = (f32[512,512]{1,0:T(8,128)}, f32[512,512]{1,0:T(8,128)S(1)}, u32[]{:S(2)}, u32[]{:S(2)}) collective-permute-start(f32[512,512]{1,0:T(8,128)} %get-tuple-element.41), channel_id=1, source_target_pairs={{0,4},{4,0},{1,5},{5,1},{2,6},{6,2},{3,7},{7,3},{8,12},{12,8},{9,1... | collective-permute-start | bytes 3145736 | tf_op jit(solution)/shard_map/ppermute | solution.py:426
  22.3 27.2 %donor_gather.1 = f32[4,2,8,128]{3,2,1,0:T(8,128)} custom-call(s32[4,4,256]{2,1,0:T(4,128)} %slice_convert_fusion.words_ref, f32[4,8,256]{2,1,0:T(8,128)} %copy-done.5, f32[1,5,512,512]{3,2,1,0:T(8,128)} %elastic_ref.9, f32[1,3,512,512]{3,2,1,0:T(8,128)} %acoustic_ref.7), custom_call_target="tpu_custom_call" | custom-call | flops 1000000000 | bytes 8388608 | tf_op jit(solution)/shard_map/donor_gather/pallas_call | solution.py:454
  49.5 3.3 %all-to-all-start.1 = ((f32[4,2,8,128]{3,2,1,0:T(8,128)}), f32[4,2,8,128]{3,2,1,0:T(8,128)S(1)}, u32[]{:S(2)}, u32[]{:S(2)}) async-start(f32[4,2,8,128]{3,2,1,0:T(8,128)} %donor_gather.1), calls=%async_computation.1 | async-start | bytes 65536 | tf_op jit(solution)/shard_map/all_to_all | solution.py:464
  53.7 3.0 %all-to-all-done.1.interp_ref = f32[4,2,8,128]{3,2,1,0:T(8,128)S(1)} async-done(((f32[4,2,8,128]{3,2,1,0:T(8,128)}), f32[4,2,8,128]{3,2,1,0:T(8,128)S(1)}, u32[]{:S(2)}, u32[]{:S(2)}) %all-to-all-start.1) | async-done | bytes 32800 | tf_op jit(solution)/shard_map/all_to_all | solution.py:464
  56.7 4.9 %all-to-all-start.2 = ((f32[4,8,512]{2,1,0:T(8,128)}), f32[4,8,512]{2,1,0:T(8,128)S(1)}, u32[]{:S(2)}, u32[]{:S(2)}) async-start(f32[4,8,512]{2,1,0:T(8,128)} %get-tuple-element.34), calls=%async_computation.2 | async-start | bytes 131072 | tf_op jit(solution)/shard_map/all_to_all | solution.py:465
  62.1 12.8 %near_dx.1 = (f32[6,512,512]{2,1,0:T(8,128)}, bf16[512,1536]{1,0:T(8,128)(2,1)}) custom-call(s32[1]{0:T(128)} %bitcast.me_ref, f32[512,512]{1,0:T(8,128)} %constant.33.clone.own_ref, f32[2,512,512]{2,1,0:T(8,128)} %constant.34.clone.far_ref, f32[2,512,128]{2,1,0:T(8,128)} %constant.35.clone.tail_ref, f32[128,512]{1,0:T(8,128)} %get-tuple-element.61.own_cont_ref, ...), custom_call_target="tpu_custom_call" | custom-call | flops 4831838208 | bytes 15728640 | tf_op jit(solution)/shard_map/near_dx/pallas_call | solution.py:233
  75.5 24.5 %near_section.1 = (f32[1,5,512,512]{3,2,1,0:T(8,128)}, f32[1,3,512,512]{3,2,1,0:T(8,128)}, f32[512,512]{1,0:T(8,128)}) custom-call(s32[1,1,1,4,256]{4,3,2,1,0:T(4,128)} %cells_ref.3, s32[1,1,1,4]{3,2,1,0:T(1,128)} %counts_ref.1, f32[4,2,8,128]{3,2,1,0:T(8,128)} %copy-done.6, f32[6,512,512]{2,1,0:T(8,128)} %get-tuple-element.33.dx_ref, ...), custom_call_target="tpu_custom_call" | custom-call | flops 26214400 | bytes 29360128 | tf_op jit(solution)/shard_map/near_section/pallas_call | solution.py:468
  101.3 3.9 %add_far.8 = (f32[8,128]{1,0:T(8,128)S(1)}, f32[1,5,512,512]{3,2,1,0:T(8,128)}) custom-call(f32[8,128]{1,0:T(8,128)S(1)} %broadcast_in_dim.10.turn_ref, bf16[512,1536]{1,0:T(8,128)(2,1)S(1)} %copy-done.1, f32[512,512]{1,0:T(8,128)} %collective-permute-done.far_ref, f32[1,3,512,512]{3,2,1,0:T(8,128)S(1)} %copy-done, ...), custom_call_target="tpu_custom_call", output_to_operand_aliasing={{0}: (0, {}), {1}: (5, {})} | custom-call | flops 805306368 | bytes 8388608 | tf_op jit(solution)/shard_map/add_far/pallas_call | solution.py:371
  105.1 2.6 %collective-permute-start.6 = (f32[512,128]{1,0:T(8,128)S(1)}, f32[512,128]{1,0:T(8,128)S(1)}, u32[]{:S(2)}, u32[]{:S(2)}) collective-permute-start(f32[512,128]{1,0:T(8,128)S(1)} %copy-done.9), channel_id=1, source_target_pairs={{0,4},{4,0},{1,5},{5,1},{2,6},{6,2},{3,7},{7,3},{8,12},{12,8},{9,1... | collective-permute-start | bytes 786440 | tf_op jit(solution)/shard_map/ppermute | solution.py:426
  107.7 3.2 %add_far.9 = (f32[8,128]{1,0:T(8,128)S(1)}, f32[1,3,512,512]{3,2,1,0:T(8,128)}) custom-call(f32[8,128]{1,0:T(8,128)S(1)} %get-tuple-element.37.turn_ref, bf16[512,1536]{1,0:T(8,128)(2,1)S(1)} %copy-done.1, f32[512,512]{1,0:T(8,128)} %collective-permute-done.1.far_ref, ...), custom_call_target="tpu_custom_call", output_to_operand_aliasing={{0}: (0, {}), {1}: (5, {})} | custom-call | flops 805306368 | bytes 5242880 | tf_op jit(solution)/shard_map/add_far/pallas_call | solution.py:371
  111.0 3.1 %add_far.10 = (f32[8,128]{1,0:T(8,128)S(1)}, f32[1,3,512,512]{3,2,1,0:T(8,128)}) custom-call(f32[8,128]{1,0:T(8,128)S(1)} %get-tuple-element.40.turn_ref, bf16[512,1536]{1,0:T(8,128)(2,1)S(1)} %copy-done.1, f32[512,512]{1,0:T(8,128)S(1)} %collective-permute-done.2.far_ref, ...), custom_call_target="tpu_custom_call", output_to_operand_aliasing={{0}: (0, {}), {1}: (5, {})} | custom-call | flops 805306368 | bytes 5242880 | tf_op jit(solution)/shard_map/add_far/pallas_call | solution.py:371
  114.2 3.1 %add_far.11 = (f32[8,128]{1,0:T(8,128)S(1)}, f32[1,5,512,512]{3,2,1,0:T(8,128)}) custom-call(f32[8,128]{1,0:T(8,128)S(1)} %get-tuple-element.43.turn_ref, bf16[512,1536]{1,0:T(8,128)(2,1)S(1)} %copy-done.1, f32[512,512]{1,0:T(8,128)S(1)} %collective-permute-done.3.far_ref, ...), custom_call_target="tpu_custom_call", output_to_operand_aliasing={{0}: (0, {}), {1}: (5, {})} | custom-call | flops 805306368 | bytes 5242880 | tf_op jit(solution)/shard_map/add_far/pallas_call | solution.py:371
  117.3 2.5 %collective-permute-done.4.far_ref = f32[512,512]{1,0:T(8,128)S(1)} collective-permute-done((f32[512,512]{1,0:T(8,128)}, f32[512,512]{1,0:T(8,128)S(1)}, u32[]{:S(2)}, u32[]{:S(2)}) %collective-permute-start.4) | collective-permute-done | bytes 1048608 | tf_op jit(solution)/shard_map/ppermute | solution.py:426
  119.7 3.1 %add_far.12 = (f32[8,128]{1,0:T(8,128)S(1)}, f32[1,5,512,512]{3,2,1,0:T(8,128)}) custom-call(f32[8,128]{1,0:T(8,128)S(1)} %get-tuple-element.46.turn_ref, bf16[512,1536]{1,0:T(8,128)(2,1)S(1)} %copy-done.1, f32[512,512]{1,0:T(8,128)S(1)} %collective-permute-done.4.far_ref, ...), custom_call_target="tpu_custom_call", output_to_operand_aliasing={{0}: (0, {}), {1}: (5, {})} | custom-call | flops 805306368 | bytes 5242880 | tf_op jit(solution)/shard_map/add_far/pallas_call | solution.py:371
  122.9 8.2 %collective-permute-done.5.far_ref = f32[512,256]{1,0:T(8,128)} collective-permute-done((f32[512,256]{1,0:T(8,128)}, f32[512,256]{1,0:T(8,128)}, u32[]{:S(2)}, u32[]{:S(2)}) %collective-permute-start.5) | collective-permute-done | bytes 524320 | tf_op jit(solution)/shard_map/ppermute | solution.py:426
  131.1 2.6 %add_far.13 = (f32[8,128]{1,0:T(8,128)S(1)}, f32[1,5,512,512]{3,2,1,0:T(8,128)}) custom-call(f32[8,128]{1,0:T(8,128)S(1)} %get-tuple-element.49.turn_ref, bf16[512,1536]{1,0:T(8,128)(2,1)S(1)} %copy-done.1, f32[512,256]{1,0:T(8,128)} %collective-permute-done.5.far_ref, f32[1,3,512,512]{3,2,1,0:T(8,128)S(1)} %copy-done, ...), custom_call_target="tpu_custom_call", output_to_operand_aliasing={{0}: (0, {}), {1}: (5, {})} | custom-call | flops 402653184 | bytes 2621440 | tf_op jit(solution)/shard_map/add_far/pallas_call | solution.py:371
  133.7 2.9 %collective-permute-done.6.far_ref = f32[512,128]{1,0:T(8,128)S(1)} collective-permute-done((f32[512,128]{1,0:T(8,128)S(1)}, f32[512,128]{1,0:T(8,128)S(1)}, u32[]{:S(2)}, u32[]{:S(2)}) %collective-permute-start.6) | collective-permute-done | bytes 262176 | tf_op jit(solution)/shard_map/ppermute | solution.py:426
  136.6 2.3 %add_far.14 = (f32[8,128]{1,0:T(8,128)S(1)}, f32[1,5,512,512]{3,2,1,0:T(8,128)}) custom-call(f32[8,128]{1,0:T(8,128)S(1)} %get-tuple-element.52.turn_ref, bf16[512,1536]{1,0:T(8,128)(2,1)S(1)} %copy-done.1, f32[512,128]{1,0:T(8,128)S(1)} %collective-permute-done.6.far_ref, ...), custom_call_target="tpu_custom_call", output_to_operand_aliasing={{0}: (0, {}), {1}: (5, {})} | custom-call | flops 201326592 | bytes 1310720 | tf_op jit(solution)/shard_map/add_far/pallas_call | solution.py:371
  138.9 2.5 %collective-permute-done.7.far_ref = f32[512,128]{1,0:T(8,128)S(1)} collective-permute-done((f32[512,128]{1,0:T(8,128)S(1)}, f32[512,128]{1,0:T(8,128)S(1)}, u32[]{:S(2)}, u32[]{:S(2)}) %collective-permute-start.7) | collective-permute-done | bytes 262176 | tf_op jit(solution)/shard_map/ppermute | solution.py:426
  141.4 2.3 %add_far.15 = (f32[8,128]{1,0:T(8,128)S(1)}, f32[1,5,512,512]{3,2,1,0:T(8,128)}) custom-call(f32[8,128]{1,0:T(8,128)S(1)} %get-tuple-element.55.turn_ref, bf16[512,1536]{1,0:T(8,128)(2,1)S(1)} %copy-done.1, f32[512,128]{1,0:T(8,128)S(1)} %collective-permute-done.7.far_ref, ...), custom_call_target="tpu_custom_call", output_to_operand_aliasing={{0}: (0, {}), {1}: (5, {})} | custom-call | flops 201326592 | bytes 1310720 | tf_op jit(solution)/shard_map/add_far/pallas_call | solution.py:371
  (37 shorter events, 6.4 us)
Async XLA Ops:
  2.6 18.8 %copy-start.7 = (f32[128,20]{0,1:T(8,128)S(1)}, f32[128,20]{0,1:T(8,128)}, u32[]{:S(2)}) copy-start(f32[128,20]{0,1:T(8,128)} %param.18) | copy-start | bytes 30724
  2.6 58.9 %collective-permute-start = (f32[512,512]{1,0:T(8,128)}, f32[512,512]{1,0:T(8,128)}, u32[]{:S(2)}, u32[]{:S(2)}) collective-permute-start(f32[512,512]{1,0:T(8,128)} %take_pieces.2.after_ref), channel_id=1, source_target_pairs={{0,4},{4,0},{1,5},{5,1},{2,6},{6,2},{3,7},{7,3},{8,12},{12,8},{9,1... | collective-permute-start | bytes 3145736 | tf_op jit(solution)/shard_map/ppermute | solution.py:426
  14.1 7.6 %all-to-all-start = ((f32[4,8,256]{2,1,0:T(8,128)}), f32[4,8,256]{2,1,0:T(8,128)S(1)}, u32[]{:S(2)}, u32[]{:S(2)}) async-start(f32[4,8,256]{2,1,0:T(8,128)} %get-tuple-element.32), calls=%async_computation | async-start | bytes 65536 | tf_op jit(solution)/shard_map/all_to_all | solution.py:449
  17.3 87.8 %collective-permute-start.1 = (f32[512,512]{1,0:T(8,128)}, f32[512,512]{1,0:T(8,128)}, u32[]{:S(2)}, u32[]{:S(2)}) collective-permute-start(f32[512,512]{1,0:T(8,128)} %get-tuple-element.38), channel_id=1, source_target_pairs={{0,4},{4,0},{1,5},{5,1},{2,6},{6,2},{3,7},{7,3},{8,12},{12,8},{9,1... | collective-permute-start | bytes 3145736 | tf_op jit(solution)/shard_map/ppermute | solution.py:426
  17.4 93.5 %collective-permute-start.2 = (f32[512,512]{1,0:T(8,128)}, f32[512,512]{1,0:T(8,128)S(1)}, u32[]{:S(2)}, u32[]{:S(2)}) collective-permute-start(f32[512,512]{1,0:T(8,128)} %get-tuple-element.41), channel_id=1, source_target_pairs={{0,4},{4,0},{1,5},{5,1},{2,6},{6,2},{3,7},{7,3},{8,12},{12,8},{9,1... | collective-permute-start | bytes 3145736 | tf_op jit(solution)/shard_map/ppermute | solution.py:426
  19.4 94.7 %collective-permute-start.3 = (f32[512,512]{1,0:T(8,128)}, f32[512,512]{1,0:T(8,128)S(1)}, u32[]{:S(2)}, u32[]{:S(2)}) collective-permute-start(f32[512,512]{1,0:T(8,128)} %get-tuple-element.44), channel_id=1, source_target_pairs={{0,4},{4,0},{1,5},{5,1},{2,6},{6,2},{3,7},{7,3},{8,12},{12,8},{9,1... | collective-permute-start | bytes 3145736 | tf_op jit(solution)/shard_map/ppermute | solution.py:426
  19.5 100.2 %collective-permute-start.4 = (f32[512,512]{1,0:T(8,128)}, f32[512,512]{1,0:T(8,128)S(1)}, u32[]{:S(2)}, u32[]{:S(2)}) collective-permute-start(f32[512,512]{1,0:T(8,128)} %get-tuple-element.47), channel_id=1, source_target_pairs={{0,4},{4,0},{1,5},{5,1},{2,6},{6,2},{3,7},{7,3},{8,12},{12,8},{9,1... | collective-permute-start | bytes 3145736 | tf_op jit(solution)/shard_map/ppermute | solution.py:426
  21.7 0.6 copy-start.5
  49.5 7.2 %all-to-all-start.1 = ((f32[4,2,8,128]{3,2,1,0:T(8,128)}), f32[4,2,8,128]{3,2,1,0:T(8,128)S(1)}, u32[]{:S(2)}, u32[]{:S(2)}) async-start(f32[4,2,8,128]{3,2,1,0:T(8,128)} %donor_gather.1), calls=%async_computation.1 | async-start | bytes 65536 | tf_op jit(solution)/shard_map/all_to_all | solution.py:464
  56.7 18.2 %copy-start.6 = (f32[4,2,8,128]{3,2,1,0:T(8,128)}, f32[4,2,8,128]{3,2,1,0:T(8,128)S(1)}, u32[]{:S(2)}) copy-start(f32[4,2,8,128]{3,2,1,0:T(8,128)S(1)} %all-to-all-done.1.interp_ref) | copy-start | bytes 98308
  56.7 18.2 %all-to-all-start.2 = ((f32[4,8,512]{2,1,0:T(8,128)}), f32[4,8,512]{2,1,0:T(8,128)S(1)}, u32[]{:S(2)}, u32[]{:S(2)}) async-start(f32[4,8,512]{2,1,0:T(8,128)} %get-tuple-element.34), calls=%async_computation.2 | async-start | bytes 131072 | tf_op jit(solution)/shard_map/all_to_all | solution.py:465
  61.6 69.5 %collective-permute-start.5 = (f32[512,256]{1,0:T(8,128)}, f32[512,256]{1,0:T(8,128)}, u32[]{:S(2)}, u32[]{:S(2)}) collective-permute-start(f32[512,256]{1,0:T(8,128)} %get-tuple-element.50), channel_id=1, source_target_pairs={{0,4},{4,0},{1,5},{5,1},{2,6},{6,2},{3,7},{7,3},{8,12},{12,8},{9,1... | collective-permute-start | bytes 1572872 | tf_op jit(solution)/shard_map/ppermute | solution.py:426
  74.8 0.6 copy-start.4
  75.5 24.6 %copy-start = (f32[1,3,512,512]{3,2,1,0:T(8,128)S(1)}, f32[1,3,512,512]{3,2,1,0:T(8,128)}, u32[]{:S(2)}) copy-start(f32[1,3,512,512]{3,2,1,0:T(8,128)} %media_ref.15) | copy-start | bytes 9437188
  75.5 24.6 %copy-start.1 = (bf16[512,1536]{1,0:T(8,128)(2,1)S(1)}, bf16[512,1536]{1,0:T(8,128)(2,1)}, u32[]{:S(2)}) copy-start(bf16[512,1536]{1,0:T(8,128)(2,1)} %get-tuple-element.31.d_ref) | copy-start | bytes 4718596
  100.0 1.2 copy-start.2
  101.3 3.9 %copy-start.9 = (f32[512,128]{1,0:T(8,128)S(1)}, f32[512,128]{1,0:T(8,128)}, u32[]{:S(2)}) copy-start(f32[512,128]{1,0:T(8,128)} %get-tuple-element.53) | copy-start | bytes 786436
  101.3 6.4 %copy-start.3 = (f32[1,2,512,512]{3,2,1,0:T(8,128)S(1)}, f32[1,2,512,512]{3,2,1,0:T(8,128)}, u32[]{:S(2)}) copy-start(f32[1,2,512,512]{3,2,1,0:T(8,128)} %media_ref.10) | copy-start | bytes 6291460
  105.1 5.8 %copy-start.8 = (f32[512,128]{1,0:T(8,128)S(1)}, f32[512,128]{1,0:T(8,128)}, u32[]{:S(2)}) copy-start(f32[512,128]{1,0:T(8,128)} %get-tuple-element.56) | copy-start | bytes 786436
  105.1 31.4 %collective-permute-start.6 = (f32[512,128]{1,0:T(8,128)S(1)}, f32[512,128]{1,0:T(8,128)S(1)}, u32[]{:S(2)}, u32[]{:S(2)}) collective-permute-start(f32[512,128]{1,0:T(8,128)S(1)} %copy-done.9), channel_id=1, source_target_pairs={{0,4},{4,0},{1,5},{5,1},{2,6},{6,2},{3,7},{7,3},{8,12},{12,8},{9,1... | collective-permute-start | bytes 786440 | tf_op jit(solution)/shard_map/ppermute | solution.py:426
  110.9 30.5 %collective-permute-start.7 = (f32[512,128]{1,0:T(8,128)S(1)}, f32[512,128]{1,0:T(8,128)S(1)}, u32[]{:S(2)}, u32[]{:S(2)}) collective-permute-start(f32[512,128]{1,0:T(8,128)S(1)} %copy-done.8), channel_id=1, source_target_pairs={{0,4},{4,0},{1,5},{5,1},{2,6},{6,2},{3,7},{7,3},{8,12},{12,8},{9,1... | collective-permute-start | bytes 786440 | tf_op jit(solution)/shard_map/ppermute | solution.py:426

commit v7 on v6

--- a/solution.py
+++ b/solution.py
@@ -12,9 +12,12 @@
 STEP = 0.25
 PENALTY = 2.0
 LANES = 128
-VMEM_LIMIT = 56 * 1024 * 1024
-FAR_VMEM_LIMIT = 24 * 1024 * 1024
+MIB = 1024 * 1024
 HIGHEST = lax.Precision.HIGHEST
+
+
+def in_hbm(array):
+    return pltpu.with_memory_space_constraint(array, pltpu.HBM)
 
 
 def derivative_row(period):
@@ -37,7 +40,7 @@
         others = np.concatenate([(me - d) % slabs * rows + j for d in range(1, slabs)])
         far.append(row[(mine - others[None, :]) % period])
         tail.append(row[(mine - points - np.arange(cont)[None, :]) % period])
-    return tuple(np.asarray(table, np.float32) for table in (own, far, tail))
+    return tuple(jnp.asarray(np.asarray(table, np.float32)) for table in (own, far, tail))
 
 
 def continuation_on(cont_matrix, rows, slabs, sources):
@@ -59,39 +62,27 @@
     return lax.div(value, size), lax.rem(value, size)
 
 
-def take_kernel(pieces, parts, elastic_ref, acoustic_ref, *refs):
-    n = len(pieces)
-    outs, held, in_semaphores, out_semaphores = refs[:n], refs[n : 2 * n], refs[-2], refs[-1]
-    rows = elastic_ref.shape[2]
-    loads, stores = [], []
+def take_kernel(pieces, elastic_ref, acoustic_ref, outs, semaphores):
+    copies = []
     for i, (name, field, at, width) in enumerate(pieces):
         source = elastic_ref if name == "el" else acoustic_ref
-        for part in range(parts):
-            here = pl.ds(part * (rows // parts), rows // parts)
-            k = i * parts + part
-            loads.append(
-                pltpu.make_async_copy(source.at[0, field, here, pl.ds(at, width)], held[i].at[here], in_semaphores.at[k])
-            )
-            stores.append(pltpu.make_async_copy(held[i].at[here], outs[i].at[here], out_semaphores.at[k]))
-    for load in loads:
-        load.start()
-    for load, store in zip(loads, stores):
-        load.wait()
-        store.start()
-    return stores
-
-
-def take_only_kernel(pieces, parts, elastic_ref, *refs):
-    for store in take_kernel(pieces, parts, elastic_ref, None, *refs):
-        store.wait()
+        copies.append(pltpu.make_async_copy(source.at[0, field, :, pl.ds(at, width)], outs[i], semaphores.at[i]))
+    for copy in copies:
+        copy.start()
+    return copies
+
+
+def take_only_kernel(pieces, elastic_ref, *refs):
+    for copy in take_kernel(pieces, elastic_ref, None, refs[:-1], refs[-1]):
+        copy.wait()
 
 
 def take_and_edges_kernel(
-    pieces, parts, layers, after_ref, elastic_ref, acoustic_ref, cells_ref, weights_ref, *refs
+    pieces, layers, after_ref, elastic_ref, acoustic_ref, cells_ref, weights_ref, *refs
 ):
     del after_ref
     n = len(pieces)
-    edges_ref, asked_ref, tiles, edge_semaphores = refs[n : n + 4]
+    edges_ref, asked_ref, tiles, edge_semaphores, semaphores = refs[n:]
     n_el, n_ac = elastic_ref.shape[1], acoustic_ref.shape[1]
     rows, depth = elastic_ref.shape[2:]
     loads = []
@@ -104,9 +95,9 @@
                     edge_semaphores.at[2 * end + k],
                 )
             )
+    copies = take_kernel(pieces, elastic_ref, acoustic_ref, refs[:n], semaphores)
     for load in loads:
         load.start()
-    stores = take_kernel(pieces, parts, elastic_ref, acoustic_ref, *refs[:n], *refs[n + 4 :])
 
     x, z = split(cells_ref[0, 0, 0], depth)
     chunk, at_lane = split(z, LANES)
@@ -124,28 +115,26 @@
     below = lax.rem(lax.axis_index("layer") + 1, layers)
     for to in range(layers):
         edges_ref[to] = jnp.where(to == below, lines[8:16], lines[0:8])
-    for store in stores:
-        store.wait()
+    for copy in copies:
+        copy.wait()
 
 
 def take_pieces(elastic, acoustic, pieces, after=None, cells=None, weights=None, layers=0):
     rows = elastic.shape[2]
     anywhere = pl.BlockSpec(memory_space=pl.ANY)
     vmem = pl.BlockSpec(memory_space=pltpu.VMEM)
-    out_shape = [jax.ShapeDtypeStruct((rows, width), jnp.float32) for _, _, _, width in pieces]
-    in_specs, out_specs = [anywhere], [anywhere] * len(pieces)
-    parts = 2 if layers else 4
-    scratch = [pltpu.VMEM((rows, width), jnp.float32) for _, _, _, width in pieces]
-    scratch += [pltpu.SemaphoreType.DMA((len(pieces) * parts,))] * 2
-    kernel, operands = functools.partial(take_only_kernel, pieces, parts), (elastic,)
+    out_shape = [pltpu.VMEM((rows, width), jnp.float32) for _, _, _, width in pieces]
+    in_specs, out_specs = [anywhere], [vmem] * len(pieces)
+    scratch = [pltpu.SemaphoreType.DMA((len(pieces),))]
+    kernel, operands = functools.partial(take_only_kernel, pieces), (in_hbm(elastic),)
     if layers:
         patches, corners, slots = cells.shape[3:]
         out_shape.append(jax.ShapeDtypeStruct((layers, 8, rows), jnp.float32))
         out_shape.append(jax.ShapeDtypeStruct((patches, 2 * corners, slots), jnp.float32))
         in_specs, out_specs = [anywhere] * 3 + [vmem] * 2, out_specs + [vmem] * 2
         scratch = [pltpu.VMEM((2, 8, rows, LANES), jnp.float32), pltpu.SemaphoreType.DMA((4,))] + scratch
-        kernel = functools.partial(take_and_edges_kernel, pieces, parts, layers)
-        operands = (after, elastic, acoustic, cells, weights)
+        kernel = functools.partial(take_and_edges_kernel, pieces, layers)
+        operands = (after, in_hbm(elastic), in_hbm(acoustic), cells, weights)
     cost = sum(width for _, _, _, width in pieces) * rows
     return pl.pallas_call(
         kernel,
@@ -153,7 +142,7 @@
         out_specs=out_specs,
         out_shape=out_shape,
         scratch_shapes=scratch,
-        compiler_params=pltpu.CompilerParams(vmem_limit_bytes=VMEM_LIMIT),
+        compiler_params=pltpu.CompilerParams(vmem_limit_bytes=16 * MIB),
         cost_estimate=pl.CostEstimate(flops=0, bytes_accessed=8 * cost, transcendentals=0),
         name="take_pieces",
     )(*operands)
@@ -251,15 +240,17 @@
             scratch_shapes=[pltpu.VMEM((rows, 3 * rows), jnp.bfloat16)],
         ),
         out_shape=[
-            jax.ShapeDtypeStruct((6, rows, depth), jnp.float32),
-            jax.ShapeDtypeStruct((rows, 3 * reach), jnp.bfloat16),
-        ],
-        compiler_params=pltpu.CompilerParams(vmem_limit_bytes=VMEM_LIMIT),
+            pltpu.VMEM((6, rows, depth), jnp.float32),
+            pltpu.VMEM((rows, 3 * reach), jnp.bfloat16),
+        ],
+        compiler_params=pltpu.CompilerParams(vmem_limit_bytes=24 * MIB),
         cost_estimate=pl.CostEstimate(
             flops=36 * rows * rows * depth, bytes_accessed=60 * rows * depth, transcendentals=0
         ),
         name="near_dx",
-    )(me.reshape(1), own, far, tail, own_cont, far_cont, elastic, acoustic)
+    )(
+        me.reshape(1), in_hbm(own), in_hbm(far), in_hbm(tail), own_cont, far_cont, in_hbm(elastic), in_hbm(acoustic)
+    )
 
 
 def section_kernel(
@@ -388,14 +379,14 @@
             jax.ShapeDtypeStruct(base.shape, base.dtype),
         ],
         input_output_aliases={0: 0, 5: 1},
-        compiler_params=pltpu.CompilerParams(vmem_limit_bytes=FAR_VMEM_LIMIT),
+        compiler_params=pltpu.CompilerParams(vmem_limit_bytes=16 * MIB),
         cost_estimate=pl.CostEstimate(
             flops=6 * rows * reach * width,
             bytes_accessed=4 * rows * width * (3 + n_media + n_out),
             transcendentals=0,
         ),
         name="add_far",
-    )(turn, operator, far, media, opened, base)
+    )(turn, operator, far, in_hbm(media), opened, base)
 
 
 def per_device(
@@ -457,10 +448,10 @@
         out_specs=vmem,
         out_shape=jax.ShapeDtypeStruct((patches, groups, 8, LANES), jnp.float32),
         scratch_shapes=[pltpu.VMEM((8 * rows * (depth // LANES), LANES), jnp.float32)],
-        compiler_params=pltpu.CompilerParams(vmem_limit_bytes=VMEM_LIMIT),
+        compiler_params=pltpu.CompilerParams(vmem_limit_bytes=24 * MIB),
         cost_estimate=pl.CostEstimate(flops=10**9, bytes_accessed=32 * rows * depth, transcendentals=0),
         name="donor_gather",
-    )(asked_words, asked, elastic, acoustic)
+    )(asked_words, asked, in_hbm(elastic), in_hbm(acoustic))
     interp = lax.all_to_all(local, "patch", split_axis=0, concat_axis=0, tiled=True)
     edges = lax.all_to_all(edges, "layer", split_axis=0, concat_axis=0, tiled=True)
 
@@ -485,10 +476,10 @@
         out_shape=[
             jax.ShapeDtypeStruct(elastic.shape, jnp.float32),
             jax.ShapeDtypeStruct(acoustic.shape, jnp.float32),
-            jax.ShapeDtypeStruct((rows, depth), jnp.float32),
+            pltpu.VMEM((rows, depth), jnp.float32),
         ],
         scratch_shapes=[pltpu.VMEM((rows, LANES), jnp.float32)],
-        compiler_params=pltpu.CompilerParams(vmem_limit_bytes=VMEM_LIMIT),
+        compiler_params=pltpu.CompilerParams(vmem_limit_bytes=32 * MIB),
         cost_estimate=pl.CostEstimate(
             flops=100 * rows * depth, bytes_accessed=112 * rows * depth, transcendentals=0
         ),
@@ -498,10 +489,10 @@
         donor_counts,
         interp,
         near,
-        elastic,
-        acoustic,
-        el_media,
-        ac_media,
+        in_hbm(elastic),
+        in_hbm(acoustic),
+        in_hbm(el_media),
+        in_hbm(ac_media),
         edges,
         el_pair,
         ac_pair,

time: 145 us -> 144 us (level)
  local copies, waits for them, and re-layouts: 2.12 us -> 8.81 us
  Pallas kernels: 98.5 us -> 94.4 us
  waiting for transfers between devices: 19.1 us -> 16.8 us
    unnamed x22 -> x32, local copies, waits for them, and re-layouts: 2.11 us -> 8.81 us
    ppermute x8, waiting for transfers between devices: 16.1 us -> 13.6 us  [other_slabs(): lax.ppermute(value, 'line', [(i, (i + distance) % slabs) for i in range(s...]
    pallas_call x2, Pallas kernels: 10.4 us -> 8.39 us  [take_pieces(): pl.pallas_call(kernel, in_specs=in_specs, out_specs=out_specs, out_shape=...]
    pallas_call x1, Pallas kernels: 12.8 us -> 10.8 us  [near_derivatives(): pl.pallas_call(functools.partial(near_kernel, 4), grid_spec=pltpu.Prefetc...]
    pallas_call x1, Pallas kernels: 24.5 us -> 23 us  [per_device(): pl.pallas_call(functools.partial(section_kernel, layers, rows, depth, til...]
  transfers between devices with their start and end apart: 11 -> 11, of which waited for: 5 -> 5; matrix products, arithmetic and copies ran while one was open for 1% -> 1% of each run, Pallas kernels for 66% -> 64%
where the time goes in v7:
time: 144 us; the launch traced here: 143 us
  Pallas kernels  94.4 us (66%)
  starting transfers between devices  21.2 us (15%)
  waiting for transfers between devices  16.8 us (12%)
  local copies, waits for them, and re-layouts  8.81 us (6%)
    pallas_call x1, Pallas kernels, per_device(): pl.pallas_call(functools.partial(gather_kernel, 8, rows, depth), in_specs...  27.2 us
    pallas_call x8, Pallas kernels, add_far(): pl.pallas_call(functools.partial(far_kernel, coefficients), grid=(width /...  25 us
    pallas_call x1, Pallas kernels, per_device(): pl.pallas_call(functools.partial(section_kernel, layers, rows, depth, til...  23 us
    ppermute x8, waiting for transfers between devices, other_slabs(): lax.ppermute(value, 'line', [(i, (i + distance) % slabs) for i in range(s...  13.6 us
    pallas_call x1, Pallas kernels, near_derivatives(): pl.pallas_call(functools.partial(near_kernel, 4), grid_spec=pltpu.Prefetc...  10.8 us
    ppermute x8, starting transfers between devices, other_slabs(): lax.ppermute(value, 'line', [(i, (i + distance) % slabs) for i in range(s...  9.8 us
    unnamed x32, local copies, waits for them, and re-layouts  8.81 us
    pallas_call x2, Pallas kernels, take_pieces(): pl.pallas_call(kernel, in_specs=in_specs, out_specs=out_specs, out_shape=...  8.39 us
  transfers between devices with their start and end apart: 11, of which 5 were waited for; matrix products, arithmetic and copies ran while one was open for 1% of the time, Pallas kernels for 64%

profile of v7, /device:TPU:0, one launch (start us, length us, event | category | flops | bytes accessed | tf_op | source)
XLA Modules:
  0.0 142.8 jit_solution(15608087987222588774)
XLA Ops:
  1.9 3.0 %collective-permute-start = (f32[512,512]{1,0:T(8,128)S(1)}, f32[512,512]{1,0:T(8,128)}, u32[]{:S(2)}, u32[]{:S(2)}) collective-permute-start(f32[512,512]{1,0:T(8,128)S(1)} %take_pieces.2.after_ref), channel_id=1, source_target_pairs={{0,4},{4,0},{1,5},{5,1},{2,6},{6,2},{3,7},{7,3},{8,12},{12,8},{9,1... | collective-permute-start | bytes 3145736 | tf_op jit(solution)/shard_map/ppermute | solution.py:417
  5.0 7.1 %take_pieces.3 = (f32[512,512]{1,0:T(8,128)}, f32[512,512]{1,0:T(8,128)}, f32[512,512]{1,0:T(8,128)}, f32[512,512]{1,0:T(8,128)}, f32[512,256]{1,0:T(8,128)S(1)}...) custom-call(f32[512,512]{1,0:T(8,128)S(1)} %take_pieces.2.after_ref, ...), custom_call_target="tpu_custom_call" | custom-call | bytes 10485760 | tf_op jit(solution)/shard_map/take_pieces/pallas_call | solution.py:139
  14.3 3.3 %all-to-all-start = ((f32[4,8,256]{2,1,0:T(8,128)}), f32[4,8,256]{2,1,0:T(8,128)S(1)}, u32[]{:S(2)}, u32[]{:S(2)}) async-start(f32[4,8,256]{2,1,0:T(8,128)} %get-tuple-element.32), calls=%async_computation | async-start | bytes 65536 | tf_op jit(solution)/shard_map/all_to_all | solution.py:440
  17.7 2.0 %collective-permute-start.2 = (f32[512,512]{1,0:T(8,128)}, f32[512,512]{1,0:T(8,128)}, u32[]{:S(2)}, u32[]{:S(2)}) collective-permute-start(f32[512,512]{1,0:T(8,128)} %get-tuple-element.41), channel_id=1, source_target_pairs={{0,4},{4,0},{1,5},{5,1},{2,6},{6,2},{3,7},{7,3},{8,12},{12,8},{9,1... | collective-permute-start | bytes 3145736 | tf_op jit(solution)/shard_map/ppermute | solution.py:417
  21.9 27.2 %donor_gather.1 = f32[4,2,8,128]{3,2,1,0:T(8,128)} custom-call(s32[4,4,256]{2,1,0:T(4,128)S(1)} %slice_convert_fusion.words_ref, f32[4,8,256]{2,1,0:T(8,128)S(1)} %all-to-all-done.weights_ref, f32[1,5,512,512]{3,2,1,0:T(8,128)} %elastic_ref.9, f32[1,3,512,512]{3,2,1,0:T(8,128)} %acoustic_ref.7), custom_call_target="tpu_custom_call" | custom-call | flops 1000000000 | bytes 8388608 | tf_op jit(solution)/shard_map/donor_gather/pallas_call | solution.py:445
  49.1 3.3 %all-to-all-start.1 = ((f32[4,2,8,128]{3,2,1,0:T(8,128)}), f32[4,2,8,128]{3,2,1,0:T(8,128)S(1)}, u32[]{:S(2)}, u32[]{:S(2)}) async-start(f32[4,2,8,128]{3,2,1,0:T(8,128)} %donor_gather.1), calls=%async_computation.1 | async-start | bytes 65536 | tf_op jit(solution)/shard_map/all_to_all | solution.py:455
  53.2 3.1 %all-to-all-done.1.interp_ref = f32[4,2,8,128]{3,2,1,0:T(8,128)S(1)} async-done(((f32[4,2,8,128]{3,2,1,0:T(8,128)}), f32[4,2,8,128]{3,2,1,0:T(8,128)S(1)}, u32[]{:S(2)}, u32[]{:S(2)}) %all-to-all-start.1) | async-done | bytes 32800 | tf_op jit(solution)/shard_map/all_to_all | solution.py:455
  56.3 4.9 %all-to-all-start.2 = ((f32[4,8,512]{2,1,0:T(8,128)}), f32[4,8,512]{2,1,0:T(8,128)S(1)}, u32[]{:S(2)}, u32[]{:S(2)}) async-start(f32[4,8,512]{2,1,0:T(8,128)} %get-tuple-element.34), calls=%async_computation.2 | async-start | bytes 131072 | tf_op jit(solution)/shard_map/all_to_all | solution.py:456
  62.6 10.8 %near_dx.1 = (f32[6,512,512]{2,1,0:T(8,128)S(1)}, bf16[512,1536]{1,0:T(8,128)(2,1)S(1)}) custom-call(s32[1]{0:T(128)} %bitcast.me_ref, f32[512,512]{1,0:T(8,128)} %constant.33.clone.own_ref, f32[2,512,512]{2,1,0:T(8,128)} %constant.34.clone.far_ref, f32[2,512,128]{2,1,0:T(8,128)} %constant.35.clone.tail_ref, f32[128,512]{1,0:T(8,128)S(1)} %copy-done.2, ...), custom_call_target="tpu_custom_call" | custom-call | flops 4831838208 | bytes 15728640 | tf_op jit(solution)/shard_map/near_dx/pallas_call | solution.py:222
  73.5 2.6 %copy-done = f32[6,512,512]{2,1,0:T(8,128)} copy-done((f32[6,512,512]{2,1,0:T(8,128)}, f32[6,512,512]{2,1,0:T(8,128)S(1)}, u32[]{:S(2)}) %copy-start) | copy-done | bytes 6291480
  76.1 2.8 %copy-done.1 = f32[6,512,512]{2,1,0:T(8,128)S(1)} copy-done((f32[6,512,512]{2,1,0:T(8,128)S(1)}, f32[6,512,512]{2,1,0:T(8,128)}, u32[]{:S(2)}) %copy-start.1) | copy-done | bytes 6291480
  78.9 23.0 %near_section.1 = (f32[1,5,512,512]{3,2,1,0:T(8,128)}, f32[1,3,512,512]{3,2,1,0:T(8,128)}, f32[512,512]{1,0:T(8,128)S(1)}) custom-call(s32[1,1,1,4,256]{4,3,2,1,0:T(4,128)S(1)} %copy-done.5, s32[1,1,1,4]{3,2,1,0:T(1,128)S(1)} %copy-done.8, f32[4,2,8,128]{3,2,1,0:T(8,128)S(1)} %all-to-all-done.1.interp_ref, f32[6,512,512]{2,1,0:T(8,128)S(1)} %copy-done.1, ...), custom_call_target="tpu_custom_call" | custom-call | flops 26214400 | bytes 29360128 | tf_op jit(solution)/shard_map/near_section/pallas_call | solution.py:459
  102.0 4.5 %add_far.8 = (f32[8,128]{1,0:T(8,128)S(1)}, f32[1,5,512,512]{3,2,1,0:T(8,128)}) custom-call(f32[8,128]{1,0:T(8,128)S(1)} %broadcast_in_dim.10.turn_ref, bf16[512,1536]{1,0:T(8,128)(2,1)S(1)} %get-tuple-element.31.d_ref, f32[512,512]{1,0:T(8,128)} %collective-permute-done.far_ref, ...), custom_call_target="tpu_custom_call", output_to_operand_aliasing={{0}: (0, {}), {1}: (5, {})} | custom-call | flops 805306368 | bytes 8388608 | tf_op jit(solution)/shard_map/add_far/pallas_call | solution.py:362
  106.5 2.0 %collective-permute-start.6 = (f32[512,128]{1,0:T(8,128)S(1)}, f32[512,128]{1,0:T(8,128)S(1)}, u32[]{:S(2)}, u32[]{:S(2)}) collective-permute-start(f32[512,128]{1,0:T(8,128)S(1)} %copy-done.13), channel_id=1, source_target_pairs={{0,4},{4,0},{1,5},{5,1},{2,6},{6,2},{3,7},{7,3},{8,12},{12,8},{9,1... | collective-permute-start | bytes 786440 | tf_op jit(solution)/shard_map/ppermute | solution.py:417
  108.4 3.4 %add_far.9 = (f32[8,128]{1,0:T(8,128)S(1)}, f32[1,3,512,512]{3,2,1,0:T(8,128)}) custom-call(f32[8,128]{1,0:T(8,128)S(1)} %get-tuple-element.37.turn_ref, bf16[512,1536]{1,0:T(8,128)(2,1)S(1)} %get-tuple-element.31.d_ref, f32[512,512]{1,0:T(8,128)} %collective-permute-done.1.far_ref, ...), custom_call_target="tpu_custom_call", output_to_operand_aliasing={{0}: (0, {}), {1}: (5, {})} | custom-call | flops 805306368 | bytes 5242880 | tf_op jit(solution)/shard_map/add_far/pallas_call | solution.py:362
  112.0 3.4 %add_far.10 = (f32[8,128]{1,0:T(8,128)S(1)}, f32[1,3,512,512]{3,2,1,0:T(8,128)}) custom-call(f32[8,128]{1,0:T(8,128)S(1)} %get-tuple-element.40.turn_ref, bf16[512,1536]{1,0:T(8,128)(2,1)S(1)} %get-tuple-element.31.d_ref, f32[512,512]{1,0:T(8,128)} %collective-permute-done.2.far_ref, ...), custom_call_target="tpu_custom_call", output_to_operand_aliasing={{0}: (0, {}), {1}: (5, {})} | custom-call | flops 805306368 | bytes 5242880 | tf_op jit(solution)/shard_map/add_far/pallas_call | solution.py:362
  115.3 3.4 %add_far.11 = (f32[8,128]{1,0:T(8,128)S(1)}, f32[1,5,512,512]{3,2,1,0:T(8,128)}) custom-call(f32[8,128]{1,0:T(8,128)S(1)} %get-tuple-element.43.turn_ref, bf16[512,1536]{1,0:T(8,128)(2,1)S(1)} %get-tuple-element.31.d_ref, f32[512,512]{1,0:T(8,128)} %collective-permute-done.3.far_ref, ...), custom_call_target="tpu_custom_call", output_to_operand_aliasing={{0}: (0, {}), {1}: (5, {})} | custom-call | flops 805306368 | bytes 5242880 | tf_op jit(solution)/shard_map/add_far/pallas_call | solution.py:362
  118.8 3.2 %add_far.12 = (f32[8,128]{1,0:T(8,128)S(1)}, f32[1,5,512,512]{3,2,1,0:T(8,128)}) custom-call(f32[8,128]{1,0:T(8,128)S(1)} %get-tuple-element.46.turn_ref, bf16[512,1536]{1,0:T(8,128)(2,1)S(1)} %get-tuple-element.31.d_ref, f32[512,512]{1,0:T(8,128)S(1)} %collective-permute-done.4.far_ref, ...), custom_call_target="tpu_custom_call", output_to_operand_aliasing={{0}: (0, {}), {1}: (5, {})} | custom-call | flops 805306368 | bytes 5242880 | tf_op jit(solution)/shard_map/add_far/pallas_call | solution.py:362
  122.0 8.0 %collective-permute-done.5.far_ref = f32[512,256]{1,0:T(8,128)S(1)} collective-permute-done((f32[512,256]{1,0:T(8,128)}, f32[512,256]{1,0:T(8,128)S(1)}, u32[]{:S(2)}, u32[]{:S(2)}) %collective-permute-start.5) | collective-permute-done | bytes 524320 | tf_op jit(solution)/shard_map/ppermute | solution.py:417
  130.1 2.6 %add_far.13 = (f32[8,128]{1,0:T(8,128)S(1)}, f32[1,5,512,512]{3,2,1,0:T(8,128)}) custom-call(f32[8,128]{1,0:T(8,128)S(1)} %get-tuple-element.49.turn_ref, bf16[512,1536]{1,0:T(8,128)(2,1)S(1)} %get-tuple-element.31.d_ref, f32[512,256]{1,0:T(8,128)S(1)} %collective-permute-done.5.far_ref, ...), custom_call_target="tpu_custom_call", output_to_operand_aliasing={{0}: (0, {}), {1}: (5, {})} | custom-call | flops 402653184 | bytes 2621440 | tf_op jit(solution)/shard_map/add_far/pallas_call | solution.py:362
  132.6 3.0 %collective-permute-done.6.far_ref = f32[512,128]{1,0:T(8,128)S(1)} collective-permute-done((f32[512,128]{1,0:T(8,128)S(1)}, f32[512,128]{1,0:T(8,128)S(1)}, u32[]{:S(2)}, u32[]{:S(2)}) %collective-permute-start.6) | collective-permute-done | bytes 262176 | tf_op jit(solution)/shard_map/ppermute | solution.py:417
  135.7 2.3 %add_far.14 = (f32[8,128]{1,0:T(8,128)S(1)}, f32[1,5,512,512]{3,2,1,0:T(8,128)}) custom-call(f32[8,128]{1,0:T(8,128)S(1)} %get-tuple-element.52.turn_ref, bf16[512,1536]{1,0:T(8,128)(2,1)S(1)} %get-tuple-element.31.d_ref, f32[512,128]{1,0:T(8,128)S(1)} %collective-permute-done.6.far_ref, ...), custom_call_target="tpu_custom_call", output_to_operand_aliasing={{0}: (0, {}), {1}: (5, {})} | custom-call | flops 201326592 | bytes 1310720 | tf_op jit(solution)/shard_map/add_far/pallas_call | solution.py:362
  138.0 2.5 %collective-permute-done.7.far_ref = f32[512,128]{1,0:T(8,128)S(1)} collective-permute-done((f32[512,128]{1,0:T(8,128)S(1)}, f32[512,128]{1,0:T(8,128)S(1)}, u32[]{:S(2)}, u32[]{:S(2)}) %collective-permute-start.7) | collective-permute-done | bytes 262176 | tf_op jit(solution)/shard_map/ppermute | solution.py:417
  140.5 2.3 %add_far.15 = (f32[8,128]{1,0:T(8,128)S(1)}, f32[1,5,512,512]{3,2,1,0:T(8,128)}) custom-call(f32[8,128]{1,0:T(8,128)S(1)} %get-tuple-element.55.turn_ref, bf16[512,1536]{1,0:T(8,128)(2,1)S(1)} %get-tuple-element.31.d_ref, f32[512,128]{1,0:T(8,128)S(1)} %collective-permute-done.7.far_ref, ...), custom_call_target="tpu_custom_call", output_to_operand_aliasing={{0}: (0, {}), {1}: (5, {})} | custom-call | flops 201326592 | bytes 1310720 | tf_op jit(solution)/shard_map/add_far/pallas_call | solution.py:362
  (47 shorter events, 8.4 us)
Async XLA Ops:
  0.6 4.3 %copy-start.3 = (s32[1,1,1,4,4,256]{5,4,3,2,1,0:T(4,128)S(1)}, s32[1,1,1,4,4,256]{5,4,3,2,1,0:T(4,128)}, u32[]{:S(2)}) copy-start(s32[1,1,1,4,4,256]{5,4,3,2,1,0:T(4,128)} %cells_ref.2) | copy-start | bytes 49156
  0.6 4.3 %copy-start.4 = (f32[1,1,1,4,4,256]{5,4,3,2,1,0:T(4,128)S(1)}, f32[1,1,1,4,4,256]{5,4,3,2,1,0:T(4,128)}, u32[]{:S(2)}) copy-start(f32[1,1,1,4,4,256]{5,4,3,2,1,0:T(4,128)} %weights_ref.1) | copy-start | bytes 49156
  1.9 19.8 %copy-start.14 = (f32[128,20]{0,1:T(8,128)S(1)}, f32[128,20]{0,1:T(8,128)}, u32[]{:S(2)}) copy-start(f32[128,20]{0,1:T(8,128)} %param.18) | copy-start | bytes 30724
  1.9 59.3 %collective-permute-start = (f32[512,512]{1,0:T(8,128)S(1)}, f32[512,512]{1,0:T(8,128)}, u32[]{:S(2)}, u32[]{:S(2)}) collective-permute-start(f32[512,512]{1,0:T(8,128)S(1)} %take_pieces.2.after_ref), channel_id=1, source_target_pairs={{0,4},{4,0},{1,5},{5,1},{2,6},{6,2},{3,7},{7,3},{8,12},{12,8},{9,1... | collective-permute-start | bytes 3145736 | tf_op jit(solution)/shard_map/ppermute | solution.py:417
  12.1 0.8 copy-start.9
  14.3 7.6 %all-to-all-start = ((f32[4,8,256]{2,1,0:T(8,128)}), f32[4,8,256]{2,1,0:T(8,128)S(1)}, u32[]{:S(2)}, u32[]{:S(2)}) async-start(f32[4,8,256]{2,1,0:T(8,128)} %get-tuple-element.32), calls=%async_computation | async-start | bytes 65536 | tf_op jit(solution)/shard_map/all_to_all | solution.py:440
  17.6 88.9 %collective-permute-start.1 = (f32[512,512]{1,0:T(8,128)}, f32[512,512]{1,0:T(8,128)}, u32[]{:S(2)}, u32[]{:S(2)}) collective-permute-start(f32[512,512]{1,0:T(8,128)} %get-tuple-element.38), channel_id=1, source_target_pairs={{0,4},{4,0},{1,5},{5,1},{2,6},{6,2},{3,7},{7,3},{8,12},{12,8},{9,1... | collective-permute-start | bytes 3145736 | tf_op jit(solution)/shard_map/ppermute | solution.py:417
  17.7 94.1 %collective-permute-start.2 = (f32[512,512]{1,0:T(8,128)}, f32[512,512]{1,0:T(8,128)}, u32[]{:S(2)}, u32[]{:S(2)}) collective-permute-start(f32[512,512]{1,0:T(8,128)} %get-tuple-element.41), channel_id=1, source_target_pairs={{0,4},{4,0},{1,5},{5,1},{2,6},{6,2},{3,7},{7,3},{8,12},{12,8},{9,1... | collective-permute-start | bytes 3145736 | tf_op jit(solution)/shard_map/ppermute | solution.py:417
  19.7 95.7 %collective-permute-start.3 = (f32[512,512]{1,0:T(8,128)}, f32[512,512]{1,0:T(8,128)}, u32[]{:S(2)}, u32[]{:S(2)}) collective-permute-start(f32[512,512]{1,0:T(8,128)} %get-tuple-element.44), channel_id=1, source_target_pairs={{0,4},{4,0},{1,5},{5,1},{2,6},{6,2},{3,7},{7,3},{8,12},{12,8},{9,1... | collective-permute-start | bytes 3145736 | tf_op jit(solution)/shard_map/ppermute | solution.py:417
  19.8 99.1 %collective-permute-start.4 = (f32[512,512]{1,0:T(8,128)}, f32[512,512]{1,0:T(8,128)S(1)}, u32[]{:S(2)}, u32[]{:S(2)}) collective-permute-start(f32[512,512]{1,0:T(8,128)} %get-tuple-element.47), channel_id=1, source_target_pairs={{0,4},{4,0},{1,5},{5,1},{2,6},{6,2},{3,7},{7,3},{8,12},{12,8},{9,1... | collective-permute-start | bytes 3145736 | tf_op jit(solution)/shard_map/ppermute | solution.py:417
  49.1 7.2 %all-to-all-start.1 = ((f32[4,2,8,128]{3,2,1,0:T(8,128)}), f32[4,2,8,128]{3,2,1,0:T(8,128)S(1)}, u32[]{:S(2)}, u32[]{:S(2)}) async-start(f32[4,2,8,128]{3,2,1,0:T(8,128)} %donor_gather.1), calls=%async_computation.1 | async-start | bytes 65536 | tf_op jit(solution)/shard_map/all_to_all | solution.py:455
  56.3 19.8 %all-to-all-start.2 = ((f32[4,8,512]{2,1,0:T(8,128)}), f32[4,8,512]{2,1,0:T(8,128)S(1)}, u32[]{:S(2)}, u32[]{:S(2)}) async-start(f32[4,8,512]{2,1,0:T(8,128)} %get-tuple-element.34), calls=%async_computation.2 | async-start | bytes 131072 | tf_op jit(solution)/shard_map/all_to_all | solution.py:456
  61.2 68.9 %collective-permute-start.5 = (f32[512,256]{1,0:T(8,128)}, f32[512,256]{1,0:T(8,128)S(1)}, u32[]{:S(2)}, u32[]{:S(2)}) collective-permute-start(f32[512,256]{1,0:T(8,128)} %copy-done.9), channel_id=1, source_target_pairs={{0,4},{4,0},{1,5},{5,1},{2,6},{6,2},{3,7},{7,3},{8,12},{12,8},{9,1... | collective-permute-start | bytes 1572872 | tf_op jit(solution)/shard_map/ppermute | solution.py:417
  61.7 0.9 copy-start.2
  62.6 13.5 %copy-start.5 = (s32[1,1,1,4,256]{4,3,2,1,0:T(4,128)S(1)}, s32[1,1,1,4,256]{4,3,2,1,0:T(4,128)}, u32[]{:S(2)}) copy-start(s32[1,1,1,4,256]{4,3,2,1,0:T(4,128)} %cells_ref.3) | copy-start | bytes 12292
  62.6 13.5 %copy-start.6 = (s32[1,512]{1,0:T(1,128)S(1)}, s32[1,512]{1,0:T(1,128)}, u32[]{:S(2)}) copy-start(s32[1,512]{1,0:T(1,128)} %el_pair_ref.1) | copy-start | bytes 6148
  62.6 13.5 %copy-start.7 = (s32[1,512]{1,0:T(1,128)S(1)}, s32[1,512]{1,0:T(1,128)}, u32[]{:S(2)}) copy-start(s32[1,512]{1,0:T(1,128)} %ac_pair_ref.1) | copy-start | bytes 6148
  62.6 13.5 %copy-start.8 = (s32[1,1,1,4]{3,2,1,0:T(1,128)S(1)}, s32[1,1,1,4]{3,2,1,0:T(1,128)}, u32[]{:S(2)}) copy-start(s32[1,1,1,4]{3,2,1,0:T(1,128)} %counts_ref.1) | copy-start | bytes 52
  73.5 2.6 %copy-start = (f32[6,512,512]{2,1,0:T(8,128)}, f32[6,512,512]{2,1,0:T(8,128)S(1)}, u32[]{:S(2)}) copy-start(f32[6,512,512]{2,1,0:T(8,128)S(1)} %get-tuple-element.33.dx_ref) | copy-start | bytes 18874372
  76.1 2.8 %copy-start.1 = (f32[6,512,512]{2,1,0:T(8,128)S(1)}, f32[6,512,512]{2,1,0:T(8,128)}, u32[]{:S(2)}) copy-start(f32[6,512,512]{2,1,0:T(8,128)} %copy-done) | copy-start | bytes 18874372
  102.0 4.5 %copy-start.13 = (f32[512,128]{1,0:T(8,128)S(1)}, f32[512,128]{1,0:T(8,128)}, u32[]{:S(2)}) copy-start(f32[512,128]{1,0:T(8,128)} %copy-done.12) | copy-start | bytes 786436
  106.4 5.3 %copy-start.11 = (f32[512,128]{1,0:T(8,128)S(1)}, f32[512,128]{1,0:T(8,128)}, u32[]{:S(2)}) copy-start(f32[512,128]{1,0:T(8,128)} %copy-done.10) | copy-start | bytes 786436
  106.5 29.2 %collective-permute-start.6 = (f32[512,128]{1,0:T(8,128)S(1)}, f32[512,128]{1,0:T(8,128)S(1)}, u32[]{:S(2)}, u32[]{:S(2)}) collective-permute-start(f32[512,128]{1,0:T(8,128)S(1)} %copy-done.13), channel_id=1, source_target_pairs={{0,4},{4,0},{1,5},{5,1},{2,6},{6,2},{3,7},{7,3},{8,12},{12,8},{9,1... | collective-permute-start | bytes 786440 | tf_op jit(solution)/shard_map/ppermute | solution.py:417
  111.8 28.7 %collective-permute-start.7 = (f32[512,128]{1,0:T(8,128)S(1)}, f32[512,128]{1,0:T(8,128)S(1)}, u32[]{:S(2)}, u32[]{:S(2)}) collective-permute-start(f32[512,128]{1,0:T(8,128)S(1)} %copy-done.11), channel_id=1, source_target_pairs={{0,4},{4,0},{1,5},{5,1},{2,6},{6,2},{3,7},{7,3},{8,12},{12,8},{9,1... | collective-permute-start | bytes 786440 | tf_op jit(solution)/shard_map/ppermute | solution.py:417
  (2 other events, 1.4 us)

commit v8 on v6

--- a/solution.py
+++ b/solution.py
@@ -12,9 +12,12 @@
 STEP = 0.25
 PENALTY = 2.0
 LANES = 128
-VMEM_LIMIT = 56 * 1024 * 1024
-FAR_VMEM_LIMIT = 24 * 1024 * 1024
+MIB = 1024 * 1024
 HIGHEST = lax.Precision.HIGHEST
+
+
+def in_hbm(array):
+    return pltpu.with_memory_space_constraint(array, pltpu.HBM)
 
 
 def derivative_row(period):
@@ -37,7 +40,7 @@
         others = np.concatenate([(me - d) % slabs * rows + j for d in range(1, slabs)])
         far.append(row[(mine - others[None, :]) % period])
         tail.append(row[(mine - points - np.arange(cont)[None, :]) % period])
-    return tuple(np.asarray(table, np.float32) for table in (own, far, tail))
+    return tuple(jnp.asarray(np.asarray(table, np.float32)) for table in (own, far, tail))
 
 
 def continuation_on(cont_matrix, rows, slabs, sources):
@@ -81,9 +84,24 @@
     return stores
 
 
-def take_only_kernel(pieces, parts, elastic_ref, *refs):
-    for store in take_kernel(pieces, parts, elastic_ref, None, *refs):
-        store.wait()
+def take_first_kernel(field, elastic_ref, out_ref, semaphore):
+    copy = pltpu.make_async_copy(elastic_ref.at[0, field], out_ref, semaphore)
+    copy.start()
+    copy.wait()
+
+
+def take_first(elastic, field):
+    rows, depth = elastic.shape[2:]
+    return pl.pallas_call(
+        functools.partial(take_first_kernel, field),
+        in_specs=[pl.BlockSpec(memory_space=pl.ANY)],
+        out_specs=pl.BlockSpec(memory_space=pltpu.VMEM),
+        out_shape=pltpu.VMEM((rows, depth), jnp.float32),
+        scratch_shapes=[pltpu.SemaphoreType.DMA],
+        compiler_params=pltpu.CompilerParams(vmem_limit_bytes=16 * MIB),
+        cost_estimate=pl.CostEstimate(flops=0, bytes_accessed=8 * rows * depth, transcendentals=0),
+        name="take_first",
+    )(in_hbm(elastic))
 
 
 def take_and_edges_kernel(
@@ -128,35 +146,29 @@
         store.wait()
 
 
-def take_pieces(elastic, acoustic, pieces, after=None, cells=None, weights=None, layers=0):
+def take_pieces(elastic, acoustic, pieces, after, cells, weights, layers):
     rows = elastic.shape[2]
     anywhere = pl.BlockSpec(memory_space=pl.ANY)
     vmem = pl.BlockSpec(memory_space=pltpu.VMEM)
     out_shape = [jax.ShapeDtypeStruct((rows, width), jnp.float32) for _, _, _, width in pieces]
-    in_specs, out_specs = [anywhere], [anywhere] * len(pieces)
-    parts = 2 if layers else 4
-    scratch = [pltpu.VMEM((rows, width), jnp.float32) for _, _, _, width in pieces]
+    parts = 2
+    scratch = [pltpu.VMEM((2, 8, rows, LANES), jnp.float32), pltpu.SemaphoreType.DMA((4,))]
+    scratch += [pltpu.VMEM((rows, width), jnp.float32) for _, _, _, width in pieces]
     scratch += [pltpu.SemaphoreType.DMA((len(pieces) * parts,))] * 2
-    kernel, operands = functools.partial(take_only_kernel, pieces, parts), (elastic,)
-    if layers:
-        patches, corners, slots = cells.shape[3:]
-        out_shape.append(jax.ShapeDtypeStruct((layers, 8, rows), jnp.float32))
-        out_shape.append(jax.ShapeDtypeStruct((patches, 2 * corners, slots), jnp.float32))
-        in_specs, out_specs = [anywhere] * 3 + [vmem] * 2, out_specs + [vmem] * 2
-        scratch = [pltpu.VMEM((2, 8, rows, LANES), jnp.float32), pltpu.SemaphoreType.DMA((4,))] + scratch
-        kernel = functools.partial(take_and_edges_kernel, pieces, parts, layers)
-        operands = (after, elastic, acoustic, cells, weights)
+    patches, corners, slots = cells.shape[3:]
+    out_shape.append(jax.ShapeDtypeStruct((layers, 8, rows), jnp.float32))
+    out_shape.append(jax.ShapeDtypeStruct((patches, 2 * corners, slots), jnp.float32))
     cost = sum(width for _, _, _, width in pieces) * rows
     return pl.pallas_call(
-        kernel,
-        in_specs=in_specs,
-        out_specs=out_specs,
+        functools.partial(take_and_edges_kernel, pieces, parts, layers),
+        in_specs=[anywhere] * 3 + [vmem] * 2,
+        out_specs=[anywhere] * len(pieces) + [vmem] * 2,
         out_shape=out_shape,
         scratch_shapes=scratch,
-        compiler_params=pltpu.CompilerParams(vmem_limit_bytes=VMEM_LIMIT),
+        compiler_params=pltpu.CompilerParams(vmem_limit_bytes=24 * MIB),
         cost_estimate=pl.CostEstimate(flops=0, bytes_accessed=8 * cost, transcendentals=0),
         name="take_pieces",
-    )(*operands)
+    )(after, in_hbm(elastic), in_hbm(acoustic), cells, weights)
 
 
 def gather_kernel(fields, rows, depth, words_ref, weights_ref, elastic_ref, acoustic_ref, out_ref, mixed):
@@ -251,15 +263,17 @@
             scratch_shapes=[pltpu.VMEM((rows, 3 * rows), jnp.bfloat16)],
         ),
         out_shape=[
-            jax.ShapeDtypeStruct((6, rows, depth), jnp.float32),
-            jax.ShapeDtypeStruct((rows, 3 * reach), jnp.bfloat16),
-        ],
-        compiler_params=pltpu.CompilerParams(vmem_limit_bytes=VMEM_LIMIT),
+            pltpu.HBM((6, rows, depth), jnp.float32),
+            pltpu.VMEM((rows, 3 * reach), jnp.bfloat16),
+        ],
+        compiler_params=pltpu.CompilerParams(vmem_limit_bytes=24 * MIB),
         cost_estimate=pl.CostEstimate(
             flops=36 * rows * rows * depth, bytes_accessed=60 * rows * depth, transcendentals=0
         ),
         name="near_dx",
-    )(me.reshape(1), own, far, tail, own_cont, far_cont, elastic, acoustic)
+    )(
+        me.reshape(1), in_hbm(own), in_hbm(far), in_hbm(tail), own_cont, far_cont, in_hbm(elastic), in_hbm(acoustic)
+    )
 
 
 def section_kernel(
@@ -388,14 +402,87 @@
             jax.ShapeDtypeStruct(base.shape, base.dtype),
         ],
         input_output_aliases={0: 0, 5: 1},
-        compiler_params=pltpu.CompilerParams(vmem_limit_bytes=FAR_VMEM_LIMIT),
+        compiler_params=pltpu.CompilerParams(vmem_limit_bytes=16 * MIB),
         cost_estimate=pl.CostEstimate(
             flops=6 * rows * reach * width,
             bytes_accessed=4 * rows * width * (3 + n_media + n_out),
             transcendentals=0,
         ),
         name="add_far",
-    )(turn, operator, far, media, opened, base)
+    )(turn, operator, far, in_hbm(media), opened, base)
+
+
+def prepare_kernel(coefficient, field, at, base_ref, media_ref, open_ref, same_ref, old_ref, scale_ref, semaphore):
+    del same_ref
+    load = pltpu.make_async_copy(base_ref.at[0, field, :, pl.ds(at, old_ref.shape[1])], old_ref, semaphore)
+    load.start()
+    scale_ref[...] = jnp.where(open_ref[...] > 0.5, STEP * coefficient(media_ref[0, 0]), 0.0)
+    load.wait()
+
+
+def prepare_last(base, media, first_media, field, coefficient, opened, at, width):
+    rows = opened.shape[0]
+    anywhere = pl.BlockSpec(memory_space=pl.ANY)
+    vmem = pl.BlockSpec(memory_space=pltpu.VMEM)
+    return pl.pallas_call(
+        functools.partial(prepare_kernel, coefficient, field, at),
+        grid=(1,),
+        in_specs=[
+            anywhere,
+            pl.BlockSpec((1, 1, rows, width), lambda i: (0, first_media, 0, at // width)),
+            pl.BlockSpec((rows, width), lambda i: (0, at // width)),
+        ],
+        out_specs=[anywhere, vmem, vmem],
+        out_shape=[
+            jax.ShapeDtypeStruct(base.shape, base.dtype),
+            pltpu.VMEM((rows, width), jnp.float32),
+            pltpu.VMEM((rows, width), jnp.float32),
+        ],
+        scratch_shapes=[pltpu.SemaphoreType.DMA],
+        input_output_aliases={0: 0},
+        compiler_params=pltpu.CompilerParams(vmem_limit_bytes=16 * MIB),
+        cost_estimate=pl.CostEstimate(flops=rows * width, bytes_accessed=20 * rows * width, transcendentals=0),
+        name="prepare_last",
+    )(base, in_hbm(media), opened)
+
+
+def finish_kernel(field, at, parts, d_ref, far_ref, old_ref, scale_ref, base_ref, out_ref, held, semaphores):
+    del base_ref
+    rows, width = old_ref.shape[0] // parts, old_ref.shape[1]
+    far_field = three_right(far_ref[...])
+    stores = []
+    for part in range(parts):
+        here = pl.ds(part * rows, rows)
+        far = jnp.dot(d_ref[here, :], far_field, preferred_element_type=jnp.float32)
+        held[here, :] = old_ref[here, :] + scale_ref[here, :] * far
+        stores.append(
+            pltpu.make_async_copy(
+                held.at[here], out_ref.at[0, field, here, pl.ds(at, width)], semaphores.at[part]
+            )
+        )
+        stores[-1].start()
+    for store in stores:
+        store.wait()
+
+
+def finish_last(base, operator, far, old, scale, field, at):
+    rows, width = old.shape
+    parts = 4
+    anywhere = pl.BlockSpec(memory_space=pl.ANY)
+    vmem = pl.BlockSpec(memory_space=pltpu.VMEM)
+    return pl.pallas_call(
+        functools.partial(finish_kernel, field, at, parts),
+        in_specs=[vmem] * 4 + [anywhere],
+        out_specs=anywhere,
+        out_shape=jax.ShapeDtypeStruct(base.shape, base.dtype),
+        scratch_shapes=[pltpu.VMEM((rows, width), jnp.float32), pltpu.SemaphoreType.DMA((parts,))],
+        input_output_aliases={4: 0},
+        compiler_params=pltpu.CompilerParams(vmem_limit_bytes=16 * MIB),
+        cost_estimate=pl.CostEstimate(
+            flops=2 * rows * operator.shape[1] * width, bytes_accessed=4 * rows * width, transcendentals=0
+        ),
+        name="finish_last",
+    )(operator, far, old, scale, base)
 
 
 def per_device(
@@ -440,7 +527,7 @@
         ("el", 4, half + quarter, quarter, "el", 0, 1, 1, (lambda b: b,)),
     ]
     travelling = [piece[:4] for piece in pieces]
-    (first,) = take_pieces(elastic, acoustic, travelling[:1])
+    first = take_first(elastic, travelling[0][1])
     *others, edges, asked = take_pieces(
         elastic, acoustic, travelling[1:], first, donor_cells, donor_weights, layers
     )
@@ -457,10 +544,10 @@
         out_specs=vmem,
         out_shape=jax.ShapeDtypeStruct((patches, groups, 8, LANES), jnp.float32),
         scratch_shapes=[pltpu.VMEM((8 * rows * (depth // LANES), LANES), jnp.float32)],
-        compiler_params=pltpu.CompilerParams(vmem_limit_bytes=VMEM_LIMIT),
+        compiler_params=pltpu.CompilerParams(vmem_limit_bytes=24 * MIB),
         cost_estimate=pl.CostEstimate(flops=10**9, bytes_accessed=32 * rows * depth, transcendentals=0),
         name="donor_gather",
-    )(asked_words, asked, elastic, acoustic)
+    )(asked_words, asked, in_hbm(elastic), in_hbm(acoustic))
     interp = lax.all_to_all(local, "patch", split_axis=0, concat_axis=0, tiled=True)
     edges = lax.all_to_all(edges, "layer", split_axis=0, concat_axis=0, tiled=True)
 
@@ -485,10 +572,10 @@
         out_shape=[
             jax.ShapeDtypeStruct(elastic.shape, jnp.float32),
             jax.ShapeDtypeStruct(acoustic.shape, jnp.float32),
-            jax.ShapeDtypeStruct((rows, depth), jnp.float32),
+            pltpu.VMEM((rows, depth), jnp.float32),
         ],
         scratch_shapes=[pltpu.VMEM((rows, LANES), jnp.float32)],
-        compiler_params=pltpu.CompilerParams(vmem_limit_bytes=VMEM_LIMIT),
+        compiler_params=pltpu.CompilerParams(vmem_limit_bytes=32 * MIB),
         cost_estimate=pl.CostEstimate(
             flops=100 * rows * depth, bytes_accessed=112 * rows * depth, transcendentals=0
         ),
@@ -498,10 +585,10 @@
         donor_counts,
         interp,
         near,
-        elastic,
-        acoustic,
-        el_media,
-        ac_media,
+        in_hbm(elastic),
+        in_hbm(acoustic),
+        in_hbm(el_media),
+        in_hbm(ac_media),
         edges,
         el_pair,
         ac_pair,
@@ -510,11 +597,17 @@
     turn = jnp.zeros((8, LANES), jnp.float32)
     section = {"el": new_el, "ac": new_ac}
     media = {"el": el_media, "ac": ac_media}
-    for value, (_, _, at, _, target, first_media, n_media, first_field, coefficients) in zip(far, pieces):
+    for value, (_, _, at, _, target, first_media, n_media, first_field, coefficients) in zip(far[:-1], pieces):
         turn, section[target] = add_far(
             section[target], far_operator, value, at,
             media[target], first_media, n_media, first_field, coefficients, opened, turn,
         )
+
+    _, _, at, width, target, first_media, _, field, (coefficient,) = pieces[-1]
+    base, old, scale = prepare_last(
+        section[target], media[target], first_media, field, coefficient, opened, at, width
+    )
+    section[target] = finish_last(base, far_operator, far[-1], old, scale, field, at)
     return section["el"], section["ac"]
 
 

time: 145 us -> 143 us (0.986)
  waiting for transfers between devices: 19.1 us -> 13.8 us
  local copies, waits for them, and re-layouts: 2.12 us -> 6.19 us
    ppermute x8, waiting for transfers between devices: 16.1 us -> 10.6 us  [other_slabs(): lax.ppermute(value, 'line', [(i, (i + distance) % slabs) for i in range(s...]
    unnamed x22 -> x30, local copies, waits for them, and re-layouts: 2.11 us -> 6.18 us
    pallas_call x2 -> x4, Pallas kernels: 10.4 us -> 12 us  [the longest x1 7.57 us: take_pieces(): pl.pallas_call(functools.partial(take_and_edges_kernel, pieces, parts, la...]
    pallas_call x8 -> x7, Pallas kernels: 23.7 us -> 22.7 us  [add_far(): pl.pallas_call(functools.partial(far_kernel, coefficients), grid=(width /...]
  transfers between devices with their start and end apart: 11 -> 11, of which waited for: 5 -> 4; matrix products, arithmetic and copies ran while one was open for 1% -> 1% of each run, Pallas kernels for 66% -> 68%
where the time goes in v8:
time: 143 us; the launch traced here: 142 us
  Pallas kernels  99 us (69%)
  starting transfers between devices  21.2 us (15%)
  waiting for transfers between devices  13.8 us (10%)
  local copies, waits for them, and re-layouts  6.19 us (4%)
    pallas_call x1, Pallas kernels, per_device(): pl.pallas_call(functools.partial(gather_kernel, 8, rows, depth), in_specs...  27.2 us
    pallas_call x1, Pallas kernels, per_device(): pl.pallas_call(functools.partial(section_kernel, layers, rows, depth, til...  24.6 us
    pallas_call x7, Pallas kernels, add_far(): pl.pallas_call(functools.partial(far_kernel, coefficients), grid=(width /...  22.7 us
    pallas_call x1, Pallas kernels, near_derivatives(): pl.pallas_call(functools.partial(near_kernel, 4), grid_spec=pltpu.Prefetc...  12.6 us
    ppermute x8, waiting for transfers between devices, other_slabs(): lax.ppermute(value, 'line', [(i, (i + distance) % slabs) for i in range(s...  10.6 us
    ppermute x8, starting transfers between devices, other_slabs(): lax.ppermute(value, 'line', [(i, (i + distance) % slabs) for i in range(s...  9.77 us
    pallas_call x1, Pallas kernels, take_pieces(): pl.pallas_call(functools.partial(take_and_edges_kernel, pieces, parts, la...  7.57 us
    unnamed x30, local copies, waits for them, and re-layouts  6.18 us
  transfers between devices with their start and end apart: 11, of which 4 were waited for; matrix products, arithmetic and copies ran while one was open for 1% of the time, Pallas kernels for 68%

profile of v8, /device:TPU:0, one launch (start us, length us, event | category | flops | bytes accessed | tf_op | source)
XLA Modules:
  0.0 141.7 jit_solution(1591154517692303733)
XLA Ops:
  0.6 1.2 take_first.1.after_ref
  1.9 3.0 %collective-permute-start.1 = (f32[512,512]{1,0:T(8,128)S(1)}, f32[512,512]{1,0:T(8,128)}, u32[]{:S(2)}, u32[]{:S(2)}) collective-permute-start(f32[512,512]{1,0:T(8,128)S(1)} %take_first.1.after_ref), channel_id=1, source_target_pairs={{0,4},{4,0},{1,5},{5,1},{2,6},{6,2},{3,7},{7,3},{8,12},{12,8},{9,1... | collective-permute-start | bytes 3145736 | tf_op jit(solution)/shard_map/ppermute | solution.py:513
  5.0 7.6 %take_pieces.1 = (f32[512,512]{1,0:T(8,128)}, f32[512,512]{1,0:T(8,128)}, f32[512,512]{1,0:T(8,128)}, f32[512,512]{1,0:T(8,128)}, f32[512,256]{1,0:T(8,128)S(1)}...) custom-call(f32[512,512]{1,0:T(8,128)S(1)} %take_first.1.after_ref, ...), custom_call_target="tpu_custom_call" | custom-call | bytes 10485760 | tf_op jit(solution)/shard_map/take_pieces/pallas_call | solution.py:162
  14.7 3.3 %all-to-all-start = ((f32[4,8,256]{2,1,0:T(8,128)}), f32[4,8,256]{2,1,0:T(8,128)S(1)}, u32[]{:S(2)}, u32[]{:S(2)}) async-start(f32[4,8,256]{2,1,0:T(8,128)} %get-tuple-element.34), calls=%async_computation | async-start | bytes 65536 | tf_op jit(solution)/shard_map/all_to_all | solution.py:536
  18.1 2.0 %collective-permute-start.3 = (f32[512,512]{1,0:T(8,128)}, f32[512,512]{1,0:T(8,128)}, u32[]{:S(2)}, u32[]{:S(2)}) collective-permute-start(f32[512,512]{1,0:T(8,128)} %get-tuple-element.43), channel_id=1, source_target_pairs={{0,4},{4,0},{1,5},{5,1},{2,6},{6,2},{3,7},{7,3},{8,12},{12,8},{9,1... | collective-permute-start | bytes 3145736 | tf_op jit(solution)/shard_map/ppermute | solution.py:513
  20.2 1.9 %collective-permute-start.5 = (f32[512,512]{1,0:T(8,128)}, f32[512,512]{1,0:T(8,128)S(1)}, u32[]{:S(2)}, u32[]{:S(2)}) collective-permute-start(f32[512,512]{1,0:T(8,128)} %get-tuple-element.49), channel_id=1, source_target_pairs={{0,4},{4,0},{1,5},{5,1},{2,6},{6,2},{3,7},{7,3},{8,12},{12,8},{9,1... | collective-permute-start | bytes 3145736 | tf_op jit(solution)/shard_map/ppermute | solution.py:513
  22.4 27.2 %donor_gather.1 = f32[4,2,8,128]{3,2,1,0:T(8,128)} custom-call(s32[4,4,256]{2,1,0:T(4,128)S(1)} %slice_convert_fusion.words_ref, f32[4,8,256]{2,1,0:T(8,128)S(1)} %all-to-all-done.weights_ref, f32[1,5,512,512]{3,2,1,0:T(8,128)} %elastic_ref.9, f32[1,3,512,512]{3,2,1,0:T(8,128)} %acoustic_ref.7), custom_call_target="tpu_custom_call" | custom-call | flops 1000000000 | bytes 8388608 | tf_op jit(solution)/shard_map/donor_gather/pallas_call | solution.py:541
  49.5 3.3 %all-to-all-start.1 = ((f32[4,2,8,128]{3,2,1,0:T(8,128)}), f32[4,2,8,128]{3,2,1,0:T(8,128)S(1)}, u32[]{:S(2)}, u32[]{:S(2)}) async-start(f32[4,2,8,128]{3,2,1,0:T(8,128)} %donor_gather.1), calls=%async_computation.1 | async-start | bytes 65536 | tf_op jit(solution)/shard_map/all_to_all | solution.py:551
  53.6 3.1 %all-to-all-done.1.interp_ref = f32[4,2,8,128]{3,2,1,0:T(8,128)S(1)} async-done(((f32[4,2,8,128]{3,2,1,0:T(8,128)}), f32[4,2,8,128]{3,2,1,0:T(8,128)S(1)}, u32[]{:S(2)}, u32[]{:S(2)}) %all-to-all-start.1) | async-done | bytes 32800 | tf_op jit(solution)/shard_map/all_to_all | solution.py:551
  56.7 4.9 %all-to-all-start.2 = ((f32[4,8,512]{2,1,0:T(8,128)}), f32[4,8,512]{2,1,0:T(8,128)S(1)}, u32[]{:S(2)}, u32[]{:S(2)}) async-start(f32[4,8,512]{2,1,0:T(8,128)} %get-tuple-element.36), calls=%async_computation.2 | async-start | bytes 131072 | tf_op jit(solution)/shard_map/all_to_all | solution.py:552
  63.1 12.6 %near_dx.1 = (f32[6,512,512]{2,1,0:T(8,128)}, bf16[512,1536]{1,0:T(8,128)(2,1)S(1)}) custom-call(s32[1]{0:T(128)} %bitcast.me_ref, f32[512,512]{1,0:T(8,128)} %constant.33.clone.own_ref, f32[2,512,512]{2,1,0:T(8,128)} %constant.34.clone.far_ref, f32[2,512,128]{2,1,0:T(8,128)} %constant.35.clone.tail_ref, f32[128,512]{1,0:T(8,128)S(1)} %copy-done.1, ...), custom_call_target="tpu_custom_call" | custom-call | flops 4831838208 | bytes 15728640 | tf_op jit(solution)/shard_map/near_dx/pallas_call | solution.py:245
  75.7 2.8 %copy-done = f32[6,512,512]{2,1,0:T(8,128)S(1)} copy-done((f32[6,512,512]{2,1,0:T(8,128)S(1)}, f32[6,512,512]{2,1,0:T(8,128)}, u32[]{:S(2)}) %copy-start) | copy-done | bytes 6291480
  78.5 24.6 %near_section.1 = (f32[1,5,512,512]{3,2,1,0:T(8,128)}, f32[1,3,512,512]{3,2,1,0:T(8,128)}, f32[512,512]{1,0:T(8,128)S(1)}) custom-call(s32[1,1,1,4,256]{4,3,2,1,0:T(4,128)S(1)} %copy-done.4, s32[1,1,1,4]{3,2,1,0:T(1,128)S(1)} %copy-done.7, f32[4,2,8,128]{3,2,1,0:T(8,128)S(1)} %all-to-all-done.1.interp_ref, f32[6,512,512]{2,1,0:T(8,128)S(1)} %copy-done, ...), custom_call_target="tpu_custom_call" | custom-call | flops 26214400 | bytes 29360128 | tf_op jit(solution)/shard_map/near_section/pallas_call | solution.py:555
  103.0 4.5 %add_far.7 = (f32[8,128]{1,0:T(8,128)S(1)}, f32[1,5,512,512]{3,2,1,0:T(8,128)}) custom-call(f32[8,128]{1,0:T(8,128)S(1)} %broadcast_in_dim.11.turn_ref, bf16[512,1536]{1,0:T(8,128)(2,1)S(1)} %get-tuple-element.32.d_ref, f32[512,512]{1,0:T(8,128)} %collective-permute-done.1.far_ref, ...), custom_call_target="tpu_custom_call", output_to_operand_aliasing={{0}: (0, {}), {1}: (5, {})} | custom-call | flops 805306368 | bytes 8388608 | tf_op jit(solution)/shard_map/add_far/pallas_call | solution.py:385
  107.6 3.4 %add_far.8 = (f32[8,128]{1,0:T(8,128)S(1)}, f32[1,3,512,512]{3,2,1,0:T(8,128)}) custom-call(f32[8,128]{1,0:T(8,128)S(1)} %get-tuple-element.39.turn_ref, bf16[512,1536]{1,0:T(8,128)(2,1)S(1)} %get-tuple-element.32.d_ref, f32[512,512]{1,0:T(8,128)} %collective-permute-done.2.far_ref, ...), custom_call_target="tpu_custom_call", output_to_operand_aliasing={{0}: (0, {}), {1}: (5, {})} | custom-call | flops 805306368 | bytes 5242880 | tf_op jit(solution)/shard_map/add_far/pallas_call | solution.py:385
  111.0 2.1 %collective-permute-start = (f32[512,128]{1,0:T(8,128)S(1)}, f32[512,128]{1,0:T(8,128)S(1)}, u32[]{:S(2)}, u32[]{:S(2)}) collective-permute-start(f32[512,128]{1,0:T(8,128)S(1)} %copy-done.10), channel_id=1, source_target_pairs={{0,4},{4,0},{1,5},{5,1},{2,6},{6,2},{3,7},{7,3},{8,12},{12,8},{9,1... | collective-permute-start | bytes 786440 | tf_op jit(solution)/shard_map/ppermute | solution.py:513
  113.0 3.3 %add_far.9 = (f32[8,128]{1,0:T(8,128)S(1)}, f32[1,3,512,512]{3,2,1,0:T(8,128)}) custom-call(f32[8,128]{1,0:T(8,128)S(1)} %get-tuple-element.42.turn_ref, bf16[512,1536]{1,0:T(8,128)(2,1)S(1)} %get-tuple-element.32.d_ref, f32[512,512]{1,0:T(8,128)} %collective-permute-done.3.far_ref, ...), custom_call_target="tpu_custom_call", output_to_operand_aliasing={{0}: (0, {}), {1}: (5, {})} | custom-call | flops 805306368 | bytes 5242880 | tf_op jit(solution)/shard_map/add_far/pallas_call | solution.py:385
  116.4 3.4 %add_far.10 = (f32[8,128]{1,0:T(8,128)S(1)}, f32[1,5,512,512]{3,2,1,0:T(8,128)}) custom-call(f32[8,128]{1,0:T(8,128)S(1)} %get-tuple-element.45.turn_ref, bf16[512,1536]{1,0:T(8,128)(2,1)S(1)} %get-tuple-element.32.d_ref, f32[512,512]{1,0:T(8,128)} %collective-permute-done.4.far_ref, ...), custom_call_target="tpu_custom_call", output_to_operand_aliasing={{0}: (0, {}), {1}: (5, {})} | custom-call | flops 805306368 | bytes 5242880 | tf_op jit(solution)/shard_map/add_far/pallas_call | solution.py:385
  119.8 3.2 %add_far.11 = (f32[8,128]{1,0:T(8,128)S(1)}, f32[1,5,512,512]{3,2,1,0:T(8,128)}) custom-call(f32[8,128]{1,0:T(8,128)S(1)} %get-tuple-element.48.turn_ref, bf16[512,1536]{1,0:T(8,128)(2,1)S(1)} %get-tuple-element.32.d_ref, f32[512,512]{1,0:T(8,128)S(1)} %collective-permute-done.5.far_ref, ...), custom_call_target="tpu_custom_call", output_to_operand_aliasing={{0}: (0, {}), {1}: (5, {})} | custom-call | flops 805306368 | bytes 5242880 | tf_op jit(solution)/shard_map/add_far/pallas_call | solution.py:385
  123.0 7.1 %collective-permute-done.6.far_ref = f32[512,256]{1,0:T(8,128)S(1)} collective-permute-done((f32[512,256]{1,0:T(8,128)}, f32[512,256]{1,0:T(8,128)S(1)}, u32[]{:S(2)}, u32[]{:S(2)}) %collective-permute-start.6) | collective-permute-done | bytes 524320 | tf_op jit(solution)/shard_map/ppermute | solution.py:513
  130.1 2.6 %add_far.12 = (f32[8,128]{1,0:T(8,128)S(1)}, f32[1,5,512,512]{3,2,1,0:T(8,128)}) custom-call(f32[8,128]{1,0:T(8,128)S(1)} %get-tuple-element.51.turn_ref, bf16[512,1536]{1,0:T(8,128)(2,1)S(1)} %get-tuple-element.32.d_ref, f32[512,256]{1,0:T(8,128)S(1)} %collective-permute-done.6.far_ref, ...), custom_call_target="tpu_custom_call", output_to_operand_aliasing={{0}: (0, {}), {1}: (5, {})} | custom-call | flops 402653184 | bytes 2621440 | tf_op jit(solution)/shard_map/add_far/pallas_call | solution.py:385
  132.6 3.0 %collective-permute-done.7.far_ref = f32[512,128]{1,0:T(8,128)S(1)} collective-permute-done((f32[512,128]{1,0:T(8,128)S(1)}, f32[512,128]{1,0:T(8,128)S(1)}, u32[]{:S(2)}, u32[]{:S(2)}) %collective-permute-start.7) | collective-permute-done | bytes 262176 | tf_op jit(solution)/shard_map/ppermute | solution.py:513
  135.7 2.3 %add_far.13 = (f32[8,128]{1,0:T(8,128)S(1)}, f32[1,5,512,512]{3,2,1,0:T(8,128)}) custom-call(f32[8,128]{1,0:T(8,128)S(1)} %get-tuple-element.54.turn_ref, bf16[512,1536]{1,0:T(8,128)(2,1)S(1)} %get-tuple-element.32.d_ref, f32[512,128]{1,0:T(8,128)S(1)} %collective-permute-done.7.far_ref, ...), custom_call_target="tpu_custom_call", output_to_operand_aliasing={{0}: (0, {}), {1}: (5, {})} | custom-call | flops 201326592 | bytes 1310720 | tf_op jit(solution)/shard_map/add_far/pallas_call | solution.py:385
  138.0 1.9 %prepare_last.1 = (f32[1,5,512,512]{3,2,1,0:T(8,128)}, f32[512,128]{1,0:T(8,128)S(1)}, f32[512,128]{1,0:T(8,128)S(1)}) custom-call(f32[1,5,512,512]{3,2,1,0:T(8,128)} %get-tuple-element.57.base_ref, f32[1,3,512,512]{3,2,1,0:T(8,128)} %media_ref.15, f32[512,512]{1,0:T(8,128)S(1)} %get-tuple-element.37.open_ref), custom_call_target="tpu_custom_call", output_to_operand_aliasing={{0}: (0, {})} | custom-call | flops 65536 | bytes 1310720 | tf_op jit(solution)/shard_map/prepare_last/pallas_call | solution.py:427
  (46 shorter events, 6.7 us)
Async XLA Ops:
  0.6 4.3 %copy-start.2 = (s32[1,1,1,4,4,256]{5,4,3,2,1,0:T(4,128)S(1)}, s32[1,1,1,4,4,256]{5,4,3,2,1,0:T(4,128)}, u32[]{:S(2)}) copy-start(s32[1,1,1,4,4,256]{5,4,3,2,1,0:T(4,128)} %cells_ref.2) | copy-start | bytes 49156
  0.6 4.3 %copy-start.3 = (f32[1,1,1,4,4,256]{5,4,3,2,1,0:T(4,128)S(1)}, f32[1,1,1,4,4,256]{5,4,3,2,1,0:T(4,128)}, u32[]{:S(2)}) copy-start(f32[1,1,1,4,4,256]{5,4,3,2,1,0:T(4,128)} %weights_ref.1) | copy-start | bytes 49156
  1.9 20.2 %copy-start.13 = (f32[128,20]{0,1:T(8,128)S(1)}, f32[128,20]{0,1:T(8,128)}, u32[]{:S(2)}) copy-start(f32[128,20]{0,1:T(8,128)} %param.18) | copy-start | bytes 30724
  1.9 59.7 %collective-permute-start.1 = (f32[512,512]{1,0:T(8,128)S(1)}, f32[512,512]{1,0:T(8,128)}, u32[]{:S(2)}, u32[]{:S(2)}) collective-permute-start(f32[512,512]{1,0:T(8,128)S(1)} %take_first.1.after_ref), channel_id=1, source_target_pairs={{0,4},{4,0},{1,5},{5,1},{2,6},{6,2},{3,7},{7,3},{8,12},{12,8},{9,1... | collective-permute-start | bytes 3145736 | tf_op jit(solution)/shard_map/ppermute | solution.py:513
  12.5 0.8 copy-start.8
  13.3 0.7 copy-start.9
  14.7 7.6 %all-to-all-start = ((f32[4,8,256]{2,1,0:T(8,128)}), f32[4,8,256]{2,1,0:T(8,128)S(1)}, u32[]{:S(2)}, u32[]{:S(2)}) async-start(f32[4,8,256]{2,1,0:T(8,128)} %get-tuple-element.34), calls=%async_computation | async-start | bytes 65536 | tf_op jit(solution)/shard_map/all_to_all | solution.py:536
  18.0 89.5 %collective-permute-start.2 = (f32[512,512]{1,0:T(8,128)}, f32[512,512]{1,0:T(8,128)}, u32[]{:S(2)}, u32[]{:S(2)}) collective-permute-start(f32[512,512]{1,0:T(8,128)} %get-tuple-element.40), channel_id=1, source_target_pairs={{0,4},{4,0},{1,5},{5,1},{2,6},{6,2},{3,7},{7,3},{8,12},{12,8},{9,1... | collective-permute-start | bytes 3145736 | tf_op jit(solution)/shard_map/ppermute | solution.py:513
  18.1 92.9 %collective-permute-start.3 = (f32[512,512]{1,0:T(8,128)}, f32[512,512]{1,0:T(8,128)}, u32[]{:S(2)}, u32[]{:S(2)}) collective-permute-start(f32[512,512]{1,0:T(8,128)} %get-tuple-element.43), channel_id=1, source_target_pairs={{0,4},{4,0},{1,5},{5,1},{2,6},{6,2},{3,7},{7,3},{8,12},{12,8},{9,1... | collective-permute-start | bytes 3145736 | tf_op jit(solution)/shard_map/ppermute | solution.py:513
  20.1 96.3 %collective-permute-start.4 = (f32[512,512]{1,0:T(8,128)}, f32[512,512]{1,0:T(8,128)}, u32[]{:S(2)}, u32[]{:S(2)}) collective-permute-start(f32[512,512]{1,0:T(8,128)} %get-tuple-element.46), channel_id=1, source_target_pairs={{0,4},{4,0},{1,5},{5,1},{2,6},{6,2},{3,7},{7,3},{8,12},{12,8},{9,1... | collective-permute-start | bytes 3145736 | tf_op jit(solution)/shard_map/ppermute | solution.py:513
  20.2 99.6 %collective-permute-start.5 = (f32[512,512]{1,0:T(8,128)}, f32[512,512]{1,0:T(8,128)S(1)}, u32[]{:S(2)}, u32[]{:S(2)}) collective-permute-start(f32[512,512]{1,0:T(8,128)} %get-tuple-element.49), channel_id=1, source_target_pairs={{0,4},{4,0},{1,5},{5,1},{2,6},{6,2},{3,7},{7,3},{8,12},{12,8},{9,1... | collective-permute-start | bytes 3145736 | tf_op jit(solution)/shard_map/ppermute | solution.py:513
  49.5 7.2 %all-to-all-start.1 = ((f32[4,2,8,128]{3,2,1,0:T(8,128)}), f32[4,2,8,128]{3,2,1,0:T(8,128)S(1)}, u32[]{:S(2)}, u32[]{:S(2)}) async-start(f32[4,2,8,128]{3,2,1,0:T(8,128)} %donor_gather.1), calls=%async_computation.1 | async-start | bytes 65536 | tf_op jit(solution)/shard_map/all_to_all | solution.py:551
  56.7 18.9 %all-to-all-start.2 = ((f32[4,8,512]{2,1,0:T(8,128)}), f32[4,8,512]{2,1,0:T(8,128)S(1)}, u32[]{:S(2)}, u32[]{:S(2)}) async-start(f32[4,8,512]{2,1,0:T(8,128)} %get-tuple-element.36), calls=%async_computation.2 | async-start | bytes 131072 | tf_op jit(solution)/shard_map/all_to_all | solution.py:552
  61.6 68.4 %collective-permute-start.6 = (f32[512,256]{1,0:T(8,128)}, f32[512,256]{1,0:T(8,128)S(1)}, u32[]{:S(2)}, u32[]{:S(2)}) collective-permute-start(f32[512,256]{1,0:T(8,128)} %copy-done.8), channel_id=1, source_target_pairs={{0,4},{4,0},{1,5},{5,1},{2,6},{6,2},{3,7},{7,3},{8,12},{12,8},{9,1... | collective-permute-start | bytes 1572872 | tf_op jit(solution)/shard_map/ppermute | solution.py:513
  62.1 0.9 copy-start.1
  63.0 12.6 %copy-start.4 = (s32[1,1,1,4,256]{4,3,2,1,0:T(4,128)S(1)}, s32[1,1,1,4,256]{4,3,2,1,0:T(4,128)}, u32[]{:S(2)}) copy-start(s32[1,1,1,4,256]{4,3,2,1,0:T(4,128)} %cells_ref.3) | copy-start | bytes 12292
  63.1 12.6 %copy-start.5 = (s32[1,512]{1,0:T(1,128)S(1)}, s32[1,512]{1,0:T(1,128)}, u32[]{:S(2)}) copy-start(s32[1,512]{1,0:T(1,128)} %el_pair_ref.1) | copy-start | bytes 6148
  63.1 12.6 %copy-start.6 = (s32[1,512]{1,0:T(1,128)S(1)}, s32[1,512]{1,0:T(1,128)}, u32[]{:S(2)}) copy-start(s32[1,512]{1,0:T(1,128)} %ac_pair_ref.1) | copy-start | bytes 6148
  63.1 12.6 %copy-start.7 = (s32[1,1,1,4]{3,2,1,0:T(1,128)S(1)}, s32[1,1,1,4]{3,2,1,0:T(1,128)}, u32[]{:S(2)}) copy-start(s32[1,1,1,4]{3,2,1,0:T(1,128)} %counts_ref.1) | copy-start | bytes 52
  75.7 2.8 %copy-start = (f32[6,512,512]{2,1,0:T(8,128)S(1)}, f32[6,512,512]{2,1,0:T(8,128)}, u32[]{:S(2)}) copy-start(f32[6,512,512]{2,1,0:T(8,128)} %get-tuple-element.35.dx_ref) | copy-start | bytes 18874372
  103.0 4.5 %copy-start.12 = (f32[512,128]{1,0:T(8,128)S(1)}, f32[512,128]{1,0:T(8,128)}, u32[]{:S(2)}) copy-start(f32[512,128]{1,0:T(8,128)} %copy-done.11) | copy-start | bytes 786436
  107.5 3.5 %copy-start.10 = (f32[512,128]{1,0:T(8,128)S(1)}, f32[512,128]{1,0:T(8,128)}, u32[]{:S(2)}) copy-start(f32[512,128]{1,0:T(8,128)} %copy-done.9) | copy-start | bytes 786436
  107.5 28.1 %collective-permute-start.7 = (f32[512,128]{1,0:T(8,128)S(1)}, f32[512,128]{1,0:T(8,128)S(1)}, u32[]{:S(2)}, u32[]{:S(2)}) collective-permute-start(f32[512,128]{1,0:T(8,128)S(1)} %copy-done.12), channel_id=1, source_target_pairs={{0,4},{4,0},{1,5},{5,1},{2,6},{6,2},{3,7},{7,3},{8,12},{12,8},{9,1... | collective-permute-start | bytes 786440 | tf_op jit(solution)/shard_map/ppermute | solution.py:513
  111.0 29.5 %collective-permute-start = (f32[512,128]{1,0:T(8,128)S(1)}, f32[512,128]{1,0:T(8,128)S(1)}, u32[]{:S(2)}, u32[]{:S(2)}) collective-permute-start(f32[512,128]{1,0:T(8,128)S(1)} %copy-done.10), channel_id=1, source_target_pairs={{0,4},{4,0},{1,5},{5,1},{2,6},{6,2},{3,7},{7,3},{8,12},{12,8},{9,1... | collective-permute-start | bytes 786440 | tf_op jit(solution)/shard_map/ppermute | solution.py:513
  (1 other events, 0.7 us)

commit v9 on v8

--- a/solution.py
+++ b/solution.py
@@ -543,7 +543,7 @@
         in_specs=[smem, smem, vmem, vmem],
         out_specs=vmem,
         out_shape=jax.ShapeDtypeStruct((patches, groups, 8, LANES), jnp.float32),
-        scratch_shapes=[pltpu.VMEM((8 * rows * (depth // LANES), LANES), jnp.float32)],
+        scratch_shapes=[pltpu.VMEM((8 * rows * (depth // LANES) + rows, LANES), jnp.float32)],
         compiler_params=pltpu.CompilerParams(vmem_limit_bytes=24 * MIB),
         cost_estimate=pl.CostEstimate(flops=10**9, bytes_accessed=32 * rows * depth, transcendentals=0),
         name="donor_gather",
@@ -597,17 +597,21 @@
     turn = jnp.zeros((8, LANES), jnp.float32)
     section = {"el": new_el, "ac": new_ac}
     media = {"el": el_media, "ac": ac_media}
-    for value, (_, _, at, _, target, first_media, n_media, first_field, coefficients) in zip(far[:-1], pieces):
+    *middle, closing = pieces
+    _, _, last_at, last_width, last_target, last_media, _, last_field, (last_coefficient,) = closing
+    for i, (_, _, at, _, target, first_media, n_media, first_field, coefficients) in enumerate(middle):
+        if i == len(middle) - 1:
+            section[last_target], old, scale = prepare_last(
+                section[last_target], media[last_target], last_media, last_field, last_coefficient,
+                opened, last_at, last_width,
+            )
         turn, section[target] = add_far(
-            section[target], far_operator, value, at,
+            section[target], far_operator, far[i], at,
             media[target], first_media, n_media, first_field, coefficients, opened, turn,
         )
-
-    _, _, at, width, target, first_media, _, field, (coefficient,) = pieces[-1]
-    base, old, scale = prepare_last(
-        section[target], media[target], first_media, field, coefficient, opened, at, width
+    section[last_target] = finish_last(
+        section[last_target], far_operator, far[-1], old, scale, last_field, last_at
     )
-    section[target] = finish_last(base, far_operator, far[-1], old, scale, field, at)
     return section["el"], section["ac"]
 
 

time: 143 us -> 143 us (level)
  transfers between devices with their start and end apart: 11 -> 11, of which waited for: 4 -> 4; matrix products, arithmetic and copies ran while one was open for 1% -> 1% of each run, Pallas kernels for 68% -> 67%
where the time goes in v9:
time: 143 us; the launch traced here: 142 us
  Pallas kernels  97.8 us (68%)
  starting transfers between devices  22.5 us (16%)
  waiting for transfers between devices  13.5 us (9%)
  local copies, waits for them, and re-layouts  6.19 us (4%)
    pallas_call x1, Pallas kernels, per_device(): pl.pallas_call(functools.partial(gather_kernel, 8, rows, depth), in_specs...  27.2 us
    pallas_call x1, Pallas kernels, per_device(): pl.pallas_call(functools.partial(section_kernel, layers, rows, depth, til...  23.4 us
    pallas_call x7, Pallas kernels, add_far(): pl.pallas_call(functools.partial(far_kernel, coefficients), grid=(width /...  22.7 us
    pallas_call x1, Pallas kernels, near_derivatives(): pl.pallas_call(functools.partial(near_kernel, 4), grid_spec=pltpu.Prefetc...  12.6 us
    ppermute x8, starting transfers between devices, other_slabs(): lax.ppermute(value, 'line', [(i, (i + distance) % slabs) for i in range(s...  11.1 us
    ppermute x8, waiting for transfers between devices, other_slabs(): lax.ppermute(value, 'line', [(i, (i + distance) % slabs) for i in range(s...  10.4 us
    pallas_call x1, Pallas kernels, take_pieces(): pl.pallas_call(functools.partial(take_and_edges_kernel, pieces, parts, la...  7.57 us
    unnamed x30, local copies, waits for them, and re-layouts  6.18 us
  transfers between devices with their start and end apart: 11, of which 4 were waited for; matrix products, arithmetic and copies ran while one was open for 1% of the time, Pallas kernels for 67%

profile of v9, /device:TPU:0, one launch (start us, length us, event | category | flops | bytes accessed | tf_op | source)
XLA Modules:
  0.0 141.7 jit_solution(7051336692655912922)
XLA Ops:
  0.6 1.2 take_first.1.after_ref
  1.9 3.0 %collective-permute-start.1 = (f32[512,512]{1,0:T(8,128)S(1)}, f32[512,512]{1,0:T(8,128)}, u32[]{:S(2)}, u32[]{:S(2)}) collective-permute-start(f32[512,512]{1,0:T(8,128)S(1)} %take_first.1.after_ref), channel_id=1, source_target_pairs={{0,4},{4,0},{1,5},{5,1},{2,6},{6,2},{3,7},{7,3},{8,12},{12,8},{9,1... | collective-permute-start | bytes 3145736 | tf_op jit(solution)/shard_map/ppermute | solution.py:513
  5.0 7.6 %take_pieces.1 = (f32[512,512]{1,0:T(8,128)}, f32[512,512]{1,0:T(8,128)}, f32[512,512]{1,0:T(8,128)}, f32[512,512]{1,0:T(8,128)}, f32[512,256]{1,0:T(8,128)S(1)}...) custom-call(f32[512,512]{1,0:T(8,128)S(1)} %take_first.1.after_ref, ...), custom_call_target="tpu_custom_call" | custom-call | bytes 10485760 | tf_op jit(solution)/shard_map/take_pieces/pallas_call | solution.py:162
  14.7 3.3 %all-to-all-start = ((f32[4,8,256]{2,1,0:T(8,128)}), f32[4,8,256]{2,1,0:T(8,128)S(1)}, u32[]{:S(2)}, u32[]{:S(2)}) async-start(f32[4,8,256]{2,1,0:T(8,128)} %get-tuple-element.34), calls=%async_computation | async-start | bytes 65536 | tf_op jit(solution)/shard_map/all_to_all | solution.py:536
  18.1 2.0 %collective-permute-start.3 = (f32[512,512]{1,0:T(8,128)}, f32[512,512]{1,0:T(8,128)}, u32[]{:S(2)}, u32[]{:S(2)}) collective-permute-start(f32[512,512]{1,0:T(8,128)} %get-tuple-element.43), channel_id=1, source_target_pairs={{0,4},{4,0},{1,5},{5,1},{2,6},{6,2},{3,7},{7,3},{8,12},{12,8},{9,1... | collective-permute-start | bytes 3145736 | tf_op jit(solution)/shard_map/ppermute | solution.py:513
  20.2 1.9 %collective-permute-start.5 = (f32[512,512]{1,0:T(8,128)}, f32[512,512]{1,0:T(8,128)S(1)}, u32[]{:S(2)}, u32[]{:S(2)}) collective-permute-start(f32[512,512]{1,0:T(8,128)} %get-tuple-element.49), channel_id=1, source_target_pairs={{0,4},{4,0},{1,5},{5,1},{2,6},{6,2},{3,7},{7,3},{8,12},{12,8},{9,1... | collective-permute-start | bytes 3145736 | tf_op jit(solution)/shard_map/ppermute | solution.py:513
  22.4 27.2 %donor_gather.1 = f32[4,2,8,128]{3,2,1,0:T(8,128)} custom-call(s32[4,4,256]{2,1,0:T(4,128)S(1)} %slice_convert_fusion.words_ref, f32[4,8,256]{2,1,0:T(8,128)S(1)} %all-to-all-done.weights_ref, f32[1,5,512,512]{3,2,1,0:T(8,128)} %elastic_ref.9, f32[1,3,512,512]{3,2,1,0:T(8,128)} %acoustic_ref.7), custom_call_target="tpu_custom_call" | custom-call | flops 1000000000 | bytes 8388608 | tf_op jit(solution)/shard_map/donor_gather/pallas_call | solution.py:541
  49.5 3.3 %all-to-all-start.1 = ((f32[4,2,8,128]{3,2,1,0:T(8,128)}), f32[4,2,8,128]{3,2,1,0:T(8,128)S(1)}, u32[]{:S(2)}, u32[]{:S(2)}) async-start(f32[4,2,8,128]{3,2,1,0:T(8,128)} %donor_gather.1), calls=%async_computation.1 | async-start | bytes 65536 | tf_op jit(solution)/shard_map/all_to_all | solution.py:551
  53.6 3.1 %all-to-all-done.1.interp_ref = f32[4,2,8,128]{3,2,1,0:T(8,128)S(1)} async-done(((f32[4,2,8,128]{3,2,1,0:T(8,128)}), f32[4,2,8,128]{3,2,1,0:T(8,128)S(1)}, u32[]{:S(2)}, u32[]{:S(2)}) %all-to-all-start.1) | async-done | bytes 32800 | tf_op jit(solution)/shard_map/all_to_all | solution.py:551
  56.7 4.9 %all-to-all-start.2 = ((f32[4,8,512]{2,1,0:T(8,128)}), f32[4,8,512]{2,1,0:T(8,128)S(1)}, u32[]{:S(2)}, u32[]{:S(2)}) async-start(f32[4,8,512]{2,1,0:T(8,128)} %get-tuple-element.36), calls=%async_computation.2 | async-start | bytes 131072 | tf_op jit(solution)/shard_map/all_to_all | solution.py:552
  63.1 12.6 %near_dx.1 = (f32[6,512,512]{2,1,0:T(8,128)}, bf16[512,1536]{1,0:T(8,128)(2,1)S(1)}) custom-call(s32[1]{0:T(128)} %bitcast.me_ref, f32[512,512]{1,0:T(8,128)} %constant.33.clone.own_ref, f32[2,512,512]{2,1,0:T(8,128)} %constant.34.clone.far_ref, f32[2,512,128]{2,1,0:T(8,128)} %constant.35.clone.tail_ref, f32[128,512]{1,0:T(8,128)S(1)} %copy-done.1, ...), custom_call_target="tpu_custom_call" | custom-call | flops 4831838208 | bytes 15728640 | tf_op jit(solution)/shard_map/near_dx/pallas_call | solution.py:245
  75.7 2.8 %copy-done = f32[6,512,512]{2,1,0:T(8,128)S(1)} copy-done((f32[6,512,512]{2,1,0:T(8,128)S(1)}, f32[6,512,512]{2,1,0:T(8,128)}, u32[]{:S(2)}) %copy-start) | copy-done | bytes 6291480
  78.5 23.4 %near_section.1 = (f32[1,5,512,512]{3,2,1,0:T(8,128)}, f32[1,3,512,512]{3,2,1,0:T(8,128)}, f32[512,512]{1,0:T(8,128)S(1)}) custom-call(s32[1,1,1,4,256]{4,3,2,1,0:T(4,128)S(1)} %copy-done.4, s32[1,1,1,4]{3,2,1,0:T(1,128)S(1)} %copy-done.7, f32[4,2,8,128]{3,2,1,0:T(8,128)S(1)} %all-to-all-done.1.interp_ref, f32[6,512,512]{2,1,0:T(8,128)S(1)} %copy-done, ...), custom_call_target="tpu_custom_call" | custom-call | flops 26214400 | bytes 29360128 | tf_op jit(solution)/shard_map/near_section/pallas_call | solution.py:555
  101.9 4.5 %add_far.7 = (f32[8,128]{1,0:T(8,128)S(1)}, f32[1,5,512,512]{3,2,1,0:T(8,128)}) custom-call(f32[8,128]{1,0:T(8,128)S(1)} %broadcast_in_dim.11.turn_ref, bf16[512,1536]{1,0:T(8,128)(2,1)S(1)} %get-tuple-element.32.d_ref, f32[512,512]{1,0:T(8,128)} %collective-permute-done.1.far_ref, ...), custom_call_target="tpu_custom_call", output_to_operand_aliasing={{0}: (0, {}), {1}: (5, {})} | custom-call | flops 805306368 | bytes 8388608 | tf_op jit(solution)/shard_map/add_far/pallas_call | solution.py:385
  106.4 3.4 %collective-permute-start.7 = (f32[512,128]{1,0:T(8,128)S(1)}, f32[512,128]{1,0:T(8,128)S(1)}, u32[]{:S(2)}, u32[]{:S(2)}) collective-permute-start(f32[512,128]{1,0:T(8,128)S(1)} %copy-done.12), channel_id=1, source_target_pairs={{0,4},{4,0},{1,5},{5,1},{2,6},{6,2},{3,7},{7,3},{8,12},{12,8},{9,1... | collective-permute-start | bytes 786440 | tf_op jit(solution)/shard_map/ppermute | solution.py:513
  109.8 3.4 %add_far.8 = (f32[8,128]{1,0:T(8,128)S(1)}, f32[1,3,512,512]{3,2,1,0:T(8,128)}) custom-call(f32[8,128]{1,0:T(8,128)S(1)} %get-tuple-element.39.turn_ref, bf16[512,1536]{1,0:T(8,128)(2,1)S(1)} %get-tuple-element.32.d_ref, f32[512,512]{1,0:T(8,128)} %collective-permute-done.2.far_ref, ...), custom_call_target="tpu_custom_call", output_to_operand_aliasing={{0}: (0, {}), {1}: (5, {})} | custom-call | flops 805306368 | bytes 5242880 | tf_op jit(solution)/shard_map/add_far/pallas_call | solution.py:385
  113.3 3.4 %add_far.9 = (f32[8,128]{1,0:T(8,128)S(1)}, f32[1,3,512,512]{3,2,1,0:T(8,128)}) custom-call(f32[8,128]{1,0:T(8,128)S(1)} %get-tuple-element.42.turn_ref, bf16[512,1536]{1,0:T(8,128)(2,1)S(1)} %get-tuple-element.32.d_ref, f32[512,512]{1,0:T(8,128)} %collective-permute-done.3.far_ref, ...), custom_call_target="tpu_custom_call", output_to_operand_aliasing={{0}: (0, {}), {1}: (5, {})} | custom-call | flops 805306368 | bytes 5242880 | tf_op jit(solution)/shard_map/add_far/pallas_call | solution.py:385
  116.6 3.4 %add_far.10 = (f32[8,128]{1,0:T(8,128)S(1)}, f32[1,5,512,512]{3,2,1,0:T(8,128)}) custom-call(f32[8,128]{1,0:T(8,128)S(1)} %get-tuple-element.45.turn_ref, bf16[512,1536]{1,0:T(8,128)(2,1)S(1)} %get-tuple-element.32.d_ref, f32[512,512]{1,0:T(8,128)} %collective-permute-done.4.far_ref, ...), custom_call_target="tpu_custom_call", output_to_operand_aliasing={{0}: (0, {}), {1}: (5, {})} | custom-call | flops 805306368 | bytes 5242880 | tf_op jit(solution)/shard_map/add_far/pallas_call | solution.py:385
  120.0 3.2 %add_far.11 = (f32[8,128]{1,0:T(8,128)S(1)}, f32[1,5,512,512]{3,2,1,0:T(8,128)}) custom-call(f32[8,128]{1,0:T(8,128)S(1)} %get-tuple-element.48.turn_ref, bf16[512,1536]{1,0:T(8,128)(2,1)S(1)} %get-tuple-element.32.d_ref, f32[512,512]{1,0:T(8,128)S(1)} %collective-permute-done.5.far_ref, ...), custom_call_target="tpu_custom_call", output_to_operand_aliasing={{0}: (0, {}), {1}: (5, {})} | custom-call | flops 805306368 | bytes 5242880 | tf_op jit(solution)/shard_map/add_far/pallas_call | solution.py:385
  123.2 6.8 %collective-permute-done.6.far_ref = f32[512,256]{1,0:T(8,128)S(1)} collective-permute-done((f32[512,256]{1,0:T(8,128)}, f32[512,256]{1,0:T(8,128)S(1)}, u32[]{:S(2)}, u32[]{:S(2)}) %collective-permute-start.6) | collective-permute-done | bytes 524320 | tf_op jit(solution)/shard_map/ppermute | solution.py:513
  130.1 2.6 %add_far.12 = (f32[8,128]{1,0:T(8,128)S(1)}, f32[1,5,512,512]{3,2,1,0:T(8,128)}) custom-call(f32[8,128]{1,0:T(8,128)S(1)} %get-tuple-element.51.turn_ref, bf16[512,1536]{1,0:T(8,128)(2,1)S(1)} %get-tuple-element.32.d_ref, f32[512,256]{1,0:T(8,128)S(1)} %collective-permute-done.6.far_ref, ...), custom_call_target="tpu_custom_call", output_to_operand_aliasing={{0}: (0, {}), {1}: (5, {})} | custom-call | flops 402653184 | bytes 2621440 | tf_op jit(solution)/shard_map/add_far/pallas_call | solution.py:385
  132.6 1.9 %prepare_last.1 = (f32[1,5,512,512]{3,2,1,0:T(8,128)}, f32[512,128]{1,0:T(8,128)S(1)}, f32[512,128]{1,0:T(8,128)S(1)}) custom-call(f32[1,5,512,512]{3,2,1,0:T(8,128)} %get-tuple-element.54.base_ref, f32[1,3,512,512]{3,2,1,0:T(8,128)} %media_ref.15, f32[512,512]{1,0:T(8,128)S(1)} %get-tuple-element.37.open_ref), custom_call_target="tpu_custom_call", output_to_operand_aliasing={{0}: (0, {})} | custom-call | flops 65536 | bytes 1310720 | tf_op jit(solution)/shard_map/prepare_last/pallas_call | solution.py:427
  135.7 2.3 %add_far.13 = (f32[8,128]{1,0:T(8,128)S(1)}, f32[1,5,512,512]{3,2,1,0:T(8,128)}) custom-call(f32[8,128]{1,0:T(8,128)S(1)} %get-tuple-element.57.turn_ref, bf16[512,1536]{1,0:T(8,128)(2,1)S(1)} %get-tuple-element.32.d_ref, f32[512,128]{1,0:T(8,128)S(1)} %collective-permute-done.7.far_ref, ...), custom_call_target="tpu_custom_call", output_to_operand_aliasing={{0}: (0, {}), {1}: (5, {})} | custom-call | flops 201326592 | bytes 1310720 | tf_op jit(solution)/shard_map/add_far/pallas_call | solution.py:385
  138.0 2.5 %collective-permute-done.far_ref = f32[512,128]{1,0:T(8,128)S(1)} collective-permute-done((f32[512,128]{1,0:T(8,128)S(1)}, f32[512,128]{1,0:T(8,128)S(1)}, u32[]{:S(2)}, u32[]{:S(2)}) %collective-permute-start) | collective-permute-done | bytes 262176 | tf_op jit(solution)/shard_map/ppermute | solution.py:513
  (46 shorter events, 7.3 us)
Async XLA Ops:
  0.6 4.3 %copy-start.2 = (s32[1,1,1,4,4,256]{5,4,3,2,1,0:T(4,128)S(1)}, s32[1,1,1,4,4,256]{5,4,3,2,1,0:T(4,128)}, u32[]{:S(2)}) copy-start(s32[1,1,1,4,4,256]{5,4,3,2,1,0:T(4,128)} %cells_ref.2) | copy-start | bytes 49156
  0.6 4.3 %copy-start.3 = (f32[1,1,1,4,4,256]{5,4,3,2,1,0:T(4,128)S(1)}, f32[1,1,1,4,4,256]{5,4,3,2,1,0:T(4,128)}, u32[]{:S(2)}) copy-start(f32[1,1,1,4,4,256]{5,4,3,2,1,0:T(4,128)} %weights_ref.1) | copy-start | bytes 49156
  1.9 20.2 %copy-start.13 = (f32[128,20]{0,1:T(8,128)S(1)}, f32[128,20]{0,1:T(8,128)}, u32[]{:S(2)}) copy-start(f32[128,20]{0,1:T(8,128)} %param.18) | copy-start | bytes 30724
  1.9 59.7 %collective-permute-start.1 = (f32[512,512]{1,0:T(8,128)S(1)}, f32[512,512]{1,0:T(8,128)}, u32[]{:S(2)}, u32[]{:S(2)}) collective-permute-start(f32[512,512]{1,0:T(8,128)S(1)} %take_first.1.after_ref), channel_id=1, source_target_pairs={{0,4},{4,0},{1,5},{5,1},{2,6},{6,2},{3,7},{7,3},{8,12},{12,8},{9,1... | collective-permute-start | bytes 3145736 | tf_op jit(solution)/shard_map/ppermute | solution.py:513
  12.5 0.8 copy-start.8
  13.3 0.7 copy-start.9
  14.7 7.6 %all-to-all-start = ((f32[4,8,256]{2,1,0:T(8,128)}), f32[4,8,256]{2,1,0:T(8,128)S(1)}, u32[]{:S(2)}, u32[]{:S(2)}) async-start(f32[4,8,256]{2,1,0:T(8,128)} %get-tuple-element.34), calls=%async_computation | async-start | bytes 65536 | tf_op jit(solution)/shard_map/all_to_all | solution.py:536
  18.0 88.4 %collective-permute-start.2 = (f32[512,512]{1,0:T(8,128)}, f32[512,512]{1,0:T(8,128)}, u32[]{:S(2)}, u32[]{:S(2)}) collective-permute-start(f32[512,512]{1,0:T(8,128)} %get-tuple-element.40), channel_id=1, source_target_pairs={{0,4},{4,0},{1,5},{5,1},{2,6},{6,2},{3,7},{7,3},{8,12},{12,8},{9,1... | collective-permute-start | bytes 3145736 | tf_op jit(solution)/shard_map/ppermute | solution.py:513
  18.1 95.1 %collective-permute-start.3 = (f32[512,512]{1,0:T(8,128)}, f32[512,512]{1,0:T(8,128)}, u32[]{:S(2)}, u32[]{:S(2)}) collective-permute-start(f32[512,512]{1,0:T(8,128)} %get-tuple-element.43), channel_id=1, source_target_pairs={{0,4},{4,0},{1,5},{5,1},{2,6},{6,2},{3,7},{7,3},{8,12},{12,8},{9,1... | collective-permute-start | bytes 3145736 | tf_op jit(solution)/shard_map/ppermute | solution.py:513
  20.1 96.5 %collective-permute-start.4 = (f32[512,512]{1,0:T(8,128)}, f32[512,512]{1,0:T(8,128)}, u32[]{:S(2)}, u32[]{:S(2)}) collective-permute-start(f32[512,512]{1,0:T(8,128)} %get-tuple-element.46), channel_id=1, source_target_pairs={{0,4},{4,0},{1,5},{5,1},{2,6},{6,2},{3,7},{7,3},{8,12},{12,8},{9,1... | collective-permute-start | bytes 3145736 | tf_op jit(solution)/shard_map/ppermute | solution.py:513
  20.2 99.8 %collective-permute-start.5 = (f32[512,512]{1,0:T(8,128)}, f32[512,512]{1,0:T(8,128)S(1)}, u32[]{:S(2)}, u32[]{:S(2)}) collective-permute-start(f32[512,512]{1,0:T(8,128)} %get-tuple-element.49), channel_id=1, source_target_pairs={{0,4},{4,0},{1,5},{5,1},{2,6},{6,2},{3,7},{7,3},{8,12},{12,8},{9,1... | collective-permute-start | bytes 3145736 | tf_op jit(solution)/shard_map/ppermute | solution.py:513
  49.5 7.2 %all-to-all-start.1 = ((f32[4,2,8,128]{3,2,1,0:T(8,128)}), f32[4,2,8,128]{3,2,1,0:T(8,128)S(1)}, u32[]{:S(2)}, u32[]{:S(2)}) async-start(f32[4,2,8,128]{3,2,1,0:T(8,128)} %donor_gather.1), calls=%async_computation.1 | async-start | bytes 65536 | tf_op jit(solution)/shard_map/all_to_all | solution.py:551
  56.7 18.9 %all-to-all-start.2 = ((f32[4,8,512]{2,1,0:T(8,128)}), f32[4,8,512]{2,1,0:T(8,128)S(1)}, u32[]{:S(2)}, u32[]{:S(2)}) async-start(f32[4,8,512]{2,1,0:T(8,128)} %get-tuple-element.36), calls=%async_computation.2 | async-start | bytes 131072 | tf_op jit(solution)/shard_map/all_to_all | solution.py:552
  61.6 68.4 %collective-permute-start.6 = (f32[512,256]{1,0:T(8,128)}, f32[512,256]{1,0:T(8,128)S(1)}, u32[]{:S(2)}, u32[]{:S(2)}) collective-permute-start(f32[512,256]{1,0:T(8,128)} %copy-done.8), channel_id=1, source_target_pairs={{0,4},{4,0},{1,5},{5,1},{2,6},{6,2},{3,7},{7,3},{8,12},{12,8},{9,1... | collective-permute-start | bytes 1572872 | tf_op jit(solution)/shard_map/ppermute | solution.py:513
  62.1 0.9 copy-start.1
  63.0 12.6 %copy-start.4 = (s32[1,1,1,4,256]{4,3,2,1,0:T(4,128)S(1)}, s32[1,1,1,4,256]{4,3,2,1,0:T(4,128)}, u32[]{:S(2)}) copy-start(s32[1,1,1,4,256]{4,3,2,1,0:T(4,128)} %cells_ref.3) | copy-start | bytes 12292
  63.1 12.6 %copy-start.5 = (s32[1,512]{1,0:T(1,128)S(1)}, s32[1,512]{1,0:T(1,128)}, u32[]{:S(2)}) copy-start(s32[1,512]{1,0:T(1,128)} %el_pair_ref.1) | copy-start | bytes 6148
  63.1 12.6 %copy-start.6 = (s32[1,512]{1,0:T(1,128)S(1)}, s32[1,512]{1,0:T(1,128)}, u32[]{:S(2)}) copy-start(s32[1,512]{1,0:T(1,128)} %ac_pair_ref.1) | copy-start | bytes 6148
  63.1 12.6 %copy-start.7 = (s32[1,1,1,4]{3,2,1,0:T(1,128)S(1)}, s32[1,1,1,4]{3,2,1,0:T(1,128)}, u32[]{:S(2)}) copy-start(s32[1,1,1,4]{3,2,1,0:T(1,128)} %counts_ref.1) | copy-start | bytes 52
  75.7 2.8 %copy-start = (f32[6,512,512]{2,1,0:T(8,128)S(1)}, f32[6,512,512]{2,1,0:T(8,128)}, u32[]{:S(2)}) copy-start(f32[6,512,512]{2,1,0:T(8,128)} %get-tuple-element.35.dx_ref) | copy-start | bytes 18874372
  101.9 4.5 %copy-start.12 = (f32[512,128]{1,0:T(8,128)S(1)}, f32[512,128]{1,0:T(8,128)}, u32[]{:S(2)}) copy-start(f32[512,128]{1,0:T(8,128)} %copy-done.11) | copy-start | bytes 786436
  106.4 6.8 %copy-start.10 = (f32[512,128]{1,0:T(8,128)S(1)}, f32[512,128]{1,0:T(8,128)}, u32[]{:S(2)}) copy-start(f32[512,128]{1,0:T(8,128)} %copy-done.9) | copy-start | bytes 786436
  106.4 29.3 %collective-permute-start.7 = (f32[512,128]{1,0:T(8,128)S(1)}, f32[512,128]{1,0:T(8,128)S(1)}, u32[]{:S(2)}, u32[]{:S(2)}) collective-permute-start(f32[512,128]{1,0:T(8,128)S(1)} %copy-done.12), channel_id=1, source_target_pairs={{0,4},{4,0},{1,5},{5,1},{2,6},{6,2},{3,7},{7,3},{8,12},{12,8},{9,1... | collective-permute-start | bytes 786440 | tf_op jit(solution)/shard_map/ppermute | solution.py:513
  113.2 27.3 %collective-permute-start = (f32[512,128]{1,0:T(8,128)S(1)}, f32[512,128]{1,0:T(8,128)S(1)}, u32[]{:S(2)}, u32[]{:S(2)}) collective-permute-start(f32[512,128]{1,0:T(8,128)S(1)} %copy-done.10), channel_id=1, source_target_pairs={{0,4},{4,0},{1,5},{5,1},{2,6},{6,2},{3,7},{7,3},{8,12},{12,8},{9,1... | collective-permute-start | bytes 786440 | tf_op jit(solution)/shard_map/ppermute | solution.py:513
  (1 other events, 0.7 us)

commit v10 on v9

--- a/solution.py
+++ b/solution.py
@@ -531,7 +531,12 @@
     *others, edges, asked = take_pieces(
         elastic, acoustic, travelling[1:], first, donor_cells, donor_weights, layers
     )
-    far = [other_slabs(value) for value in [first, *others]]
+    far = [other_slabs(value) for value in [first, *others[2:]]]
+    ocean_pair = lax.all_gather(jnp.concatenate(others[:2], axis=1), "line")
+    behind = [(me - distance) % slabs for distance in range(1, slabs)]
+    ocean_far = [lax.dynamic_index_in_dim(ocean_pair, source, 0, keepdims=False) for source in behind]
+    ocean_far = ocean_far[0] if slabs == 2 else jnp.concatenate(ocean_far, axis=0)
+    far[1:1] = [ocean_far[:, :depth], ocean_far[:, depth:]]
 
     asked = lax.all_to_all(asked, "patch", split_axis=0, concat_axis=0, tiled=True)
     asked_words = asked[:, :4].astype(jnp.int32)

time: 143 us -> 167 us (1.17)
  between operations: 0.78 us -> 14.2 us
  waiting for transfers between devices: 13.5 us -> 25.7 us
  starting transfers between devices: 22.5 us -> 20.5 us
    all_gather x0 -> x1, waiting for transfers between devices: none -> 9.62 us  [per_device(): ocean_pair = lax.all_gather(jnp.concatenate(others[:2], axis=1), 'line')]
    unnamed x30 -> x18, local copies, waits for them, and re-layouts: 6.18 us -> 3.03 us
    ppermute x8 -> x6, starting transfers between devices: 11.1 us -> 9.07 us  [other_slabs(): lax.ppermute(value, 'line', [(i, (i + distance) % slabs) for i in range(s...]
    ppermute x8 -> x6, waiting for transfers between devices: 10.4 us -> 12.2 us  [other_slabs(): lax.ppermute(value, 'line', [(i, (i + distance) % slabs) for i in range(s...]
    squeeze x0 -> x1, local copies, waits for them, and re-layouts: none -> 1.73 us  [per_device(): lax.dynamic_index_in_dim(ocean_pair, source, 0, keepdims=False)]
  transfers between devices with their start and end apart: 11 -> 10, of which waited for: 4 -> 6; matrix products, arithmetic and copies ran while one was open for 1% -> 1% of each run, Pallas kernels for 67% -> 53%
where the time goes in v10:
time: 167 us; the launch traced here: 166 us
  Pallas kernels  98.9 us (59%)
  waiting for transfers between devices  25.7 us (15%)
  starting transfers between devices  20.5 us (12%)
  between operations  14.2 us (9%)
  local copies, waits for them, and re-layouts  4.97 us (3%)
    pallas_call x1, Pallas kernels, per_device(): pl.pallas_call(functools.partial(gather_kernel, 8, rows, depth), in_specs...  28 us
    pallas_call x7, Pallas kernels, add_far(): pl.pallas_call(functools.partial(far_kernel, coefficients), grid=(width /...  22.5 us
    pallas_call x1, Pallas kernels, per_device(): pl.pallas_call(functools.partial(section_kernel, layers, rows, depth, til...  22.5 us
    pallas_call x1, Pallas kernels, near_derivatives(): pl.pallas_call(functools.partial(near_kernel, 4), grid_spec=pltpu.Prefetc...  12.6 us
    ppermute x6, waiting for transfers between devices, other_slabs(): lax.ppermute(value, 'line', [(i, (i + distance) % slabs) for i in range(s...  12.2 us
    all_gather x1, waiting for transfers between devices, per_device(): ocean_pair = lax.all_gather(jnp.concatenate(others[:2], axis=1), 'line')  9.62 us
    ppermute x6, starting transfers between devices, other_slabs(): lax.ppermute(value, 'line', [(i, (i + distance) % slabs) for i in range(s...  9.07 us
    pallas_call x1, Pallas kernels, take_pieces(): pl.pallas_call(functools.partial(take_and_edges_kernel, pieces, parts, la...  6.92 us
  transfers between devices with their start and end apart: 10, of which 6 were waited for; matrix products, arithmetic and copies ran while one was open for 1% of the time, Pallas kernels for 53%

profile of v10, /device:TPU:0, one launch (start us, length us, event | category | flops | bytes accessed | tf_op | source)
XLA Modules:
  0.0 165.9 jit_solution(13273769877709047474)
XLA Ops:
  7.2 2.2 %take_first.1.after_ref = f32[512,512]{1,0:T(8,128)} custom-call(f32[1,5,512,512]{3,2,1,0:T(8,128)} %elastic_ref.9), custom_call_target="tpu_custom_call" | custom-call | bytes 2097152 | tf_op jit(solution)/shard_map/take_first/pallas_call | solution.py:95
  9.5 6.9 %take_pieces.1 = (f32[512,512]{1,0:T(8,128)S(1)}, f32[512,512]{1,0:T(8,128)S(1)}, f32[512,512]{1,0:T(8,128)}, f32[512,512]{1,0:T(8,128)}, f32[512,256]{1,0:T(8,1...) custom-call(f32[512,512]{1,0:T(8,128)} %take_first.1.after_ref, ...), custom_call_target="tpu_custom_call" | custom-call | bytes 10485760 | tf_op jit(solution)/shard_map/take_pieces/pallas_call | solution.py:162
  18.0 3.0 %collective-permute-start.1 = (f32[512,512]{1,0:T(8,128)}, f32[512,512]{1,0:T(8,128)}, u32[]{:S(2)}, u32[]{:S(2)}) collective-permute-start(f32[512,512]{1,0:T(8,128)} %take_first.1.after_ref), channel_id=1, source_target_pairs={{0,4},{4,0},{1,5},{5,1},{2,6},{6,2},{3,7},{7,3},{8,12},{12,8},{9,1... | collective-permute-start | bytes 3145736 | tf_op jit(solution)/shard_map/ppermute | solution.py:513
  21.0 3.3 %all-to-all-start = ((f32[4,8,256]{2,1,0:T(8,128)}), f32[4,8,256]{2,1,0:T(8,128)S(1)}, u32[]{:S(2)}, u32[]{:S(2)}) async-start(f32[4,8,256]{2,1,0:T(8,128)} %get-tuple-element.34), calls=%async_computation | async-start | bytes 65536 | tf_op jit(solution)/shard_map/all_to_all | solution.py:541
  24.4 2.0 %collective-permute-start.3 = (f32[512,512]{1,0:T(8,128)}, f32[512,512]{1,0:T(8,128)}, u32[]{:S(2)}, u32[]{:S(2)}) collective-permute-start(f32[512,512]{1,0:T(8,128)} %get-tuple-element.49), channel_id=1, source_target_pairs={{0,4},{4,0},{1,5},{5,1},{2,6},{6,2},{3,7},{7,3},{8,12},{12,8},{9,1... | collective-permute-start | bytes 3145736 | tf_op jit(solution)/shard_map/ppermute | solution.py:513
  26.5 1.9 %collective-permute-start.5 = (f32[512,128]{1,0:T(8,128)}, f32[512,128]{1,0:T(8,128)S(1)}, u32[]{:S(2)}, u32[]{:S(2)}) collective-permute-start(f32[512,128]{1,0:T(8,128)} %get-tuple-element.58), channel_id=1, source_target_pairs={{0,4},{4,0},{1,5},{5,1},{2,6},{6,2},{3,7},{7,3},{8,12},{12,8},{9,1... | collective-permute-start | bytes 786440 | tf_op jit(solution)/shard_map/ppermute | solution.py:513
  28.7 28.0 %donor_gather.1 = f32[4,2,8,128]{3,2,1,0:T(8,128)} custom-call(s32[4,4,256]{2,1,0:T(4,128)S(1)} %slice_convert_fusion.words_ref, f32[4,8,256]{2,1,0:T(8,128)S(1)} %all-to-all-done.weights_ref, f32[1,5,512,512]{3,2,1,0:T(8,128)} %elastic_ref.9, f32[1,3,512,512]{3,2,1,0:T(8,128)} %acoustic_ref.7), custom_call_target="tpu_custom_call" | custom-call | flops 1000000000 | bytes 8388608 | tf_op jit(solution)/shard_map/donor_gather/pallas_call | solution.py:546
  56.7 3.3 %all-to-all-start.1 = ((f32[4,2,8,128]{3,2,1,0:T(8,128)}), f32[4,2,8,128]{3,2,1,0:T(8,128)S(1)}, u32[]{:S(2)}, u32[]{:S(2)}) async-start(f32[4,2,8,128]{3,2,1,0:T(8,128)} %donor_gather.1), calls=%async_computation.1 | async-start | bytes 65536 | tf_op jit(solution)/shard_map/all_to_all | solution.py:556
  60.0 3.8 %all-to-all-done.1.interp_ref = f32[4,2,8,128]{3,2,1,0:T(8,128)S(1)} async-done(((f32[4,2,8,128]{3,2,1,0:T(8,128)}), f32[4,2,8,128]{3,2,1,0:T(8,128)S(1)}, u32[]{:S(2)}, u32[]{:S(2)}) %all-to-all-start.1) | async-done | bytes 32800 | tf_op jit(solution)/shard_map/all_to_all | solution.py:556
  63.8 4.9 %all-to-all-start.2 = ((f32[4,8,512]{2,1,0:T(8,128)}), f32[4,8,512]{2,1,0:T(8,128)S(1)}, u32[]{:S(2)}, u32[]{:S(2)}) async-start(f32[4,8,512]{2,1,0:T(8,128)} %get-tuple-element.36), calls=%async_computation.2 | async-start | bytes 131072 | tf_op jit(solution)/shard_map/all_to_all | solution.py:557
  68.8 12.6 %near_dx.1 = (f32[6,512,512]{2,1,0:T(8,128)}, bf16[512,1536]{1,0:T(8,128)(2,1)S(1)}) custom-call(s32[1]{0:T(128)} %bitcast.me_ref, f32[512,512]{1,0:T(8,128)} %constant.39.clone.own_ref, f32[2,512,512]{2,1,0:T(8,128)} %constant.40.clone.far_ref, f32[2,512,128]{2,1,0:T(8,128)} %constant.41.clone.tail_ref, f32[128,512]{1,0:T(8,128)S(1)} %get-tuple-element.65.own_cont_ref, ...), custom_call_target="tpu_custom_call" | custom-call | flops 4831838208 | bytes 15728640 | tf_op jit(solution)/shard_map/near_dx/pallas_call | solution.py:245
  81.4 2.8 %copy-done = f32[6,512,512]{2,1,0:T(8,128)S(1)} copy-done((f32[6,512,512]{2,1,0:T(8,128)S(1)}, f32[6,512,512]{2,1,0:T(8,128)}, u32[]{:S(2)}) %copy-start) | copy-done | bytes 6291480
  84.2 22.5 %near_section.1 = (f32[1,5,512,512]{3,2,1,0:T(8,128)}, f32[1,3,512,512]{3,2,1,0:T(8,128)}, f32[512,512]{1,0:T(8,128)S(1)}) custom-call(s32[1,1,1,4,256]{4,3,2,1,0:T(4,128)S(1)} %copy-done.3, s32[1,1,1,4]{3,2,1,0:T(1,128)S(1)} %copy-done.6, f32[4,2,8,128]{3,2,1,0:T(8,128)S(1)} %all-to-all-done.1.interp_ref, f32[6,512,512]{2,1,0:T(8,128)S(1)} %copy-done, ...), custom_call_target="tpu_custom_call" | custom-call | flops 26214400 | bytes 29360128 | tf_op jit(solution)/shard_map/near_section/pallas_call | solution.py:560
  108.6 4.4 %add_far.7 = (f32[8,128]{1,0:T(8,128)S(1)}, f32[1,5,512,512]{3,2,1,0:T(8,128)}) custom-call(f32[8,128]{1,0:T(8,128)S(1)} %broadcast_in_dim.11.turn_ref, bf16[512,1536]{1,0:T(8,128)(2,1)S(1)} %get-tuple-element.32.d_ref, f32[512,512]{1,0:T(8,128)} %collective-permute-done.1.far_ref, ...), custom_call_target="tpu_custom_call", output_to_operand_aliasing={{0}: (0, {}), {1}: (5, {})} | custom-call | flops 805306368 | bytes 8388608 | tf_op jit(solution)/shard_map/add_far/pallas_call | solution.py:385
  113.1 9.6 %all-gather.3.cloned.1.call-done = f32[1024,1024]{1,0:T(8,128)} async-done(((f32[512,1024]{1,0:T(8,128)}), f32[1024,1024]{1,0:T(8,128)}) %all-gather.3.cloned.1.call-update) | async-done | bytes 4194320 | tf_op jit(solution)/shard_map/all_gather | solution.py:535
  124.6 3.2 %add_far.8 = (f32[8,128]{1,0:T(8,128)S(1)}, f32[1,3,512,512]{3,2,1,0:T(8,128)}) custom-call(f32[8,128]{1,0:T(8,128)S(1)} %get-tuple-element.39.turn_ref, bf16[512,1536]{1,0:T(8,128)(2,1)S(1)} %get-tuple-element.32.d_ref, f32[512,512]{1,0:T(8,128)S(1)} %get-tuple-element.63.far_ref, ...), custom_call_target="tpu_custom_call", output_to_operand_aliasing={{0}: (0, {}), {1}: (5, {})} | custom-call | flops 805306368 | bytes 5242880 | tf_op jit(solution)/shard_map/add_far/pallas_call | solution.py:385
  127.9 3.2 %add_far.9 = (f32[8,128]{1,0:T(8,128)S(1)}, f32[1,3,512,512]{3,2,1,0:T(8,128)}) custom-call(f32[8,128]{1,0:T(8,128)S(1)} %get-tuple-element.43.turn_ref, bf16[512,1536]{1,0:T(8,128)(2,1)S(1)} %get-tuple-element.32.d_ref, f32[512,512]{1,0:T(8,128)S(1)} %get-tuple-element.62.far_ref, ...), custom_call_target="tpu_custom_call", output_to_operand_aliasing={{0}: (0, {}), {1}: (5, {})} | custom-call | flops 805306368 | bytes 5242880 | tf_op jit(solution)/shard_map/add_far/pallas_call | solution.py:385
  131.1 3.4 %add_far.10 = (f32[8,128]{1,0:T(8,128)S(1)}, f32[1,5,512,512]{3,2,1,0:T(8,128)}) custom-call(f32[8,128]{1,0:T(8,128)S(1)} %get-tuple-element.45.turn_ref, bf16[512,1536]{1,0:T(8,128)(2,1)S(1)} %get-tuple-element.32.d_ref, f32[512,512]{1,0:T(8,128)} %collective-permute-done.2.far_ref, ...), custom_call_target="tpu_custom_call", output_to_operand_aliasing={{0}: (0, {}), {1}: (5, {})} | custom-call | flops 805306368 | bytes 5242880 | tf_op jit(solution)/shard_map/add_far/pallas_call | solution.py:385
  135.2 3.3 %add_far.11 = (f32[8,128]{1,0:T(8,128)S(1)}, f32[1,5,512,512]{3,2,1,0:T(8,128)}) custom-call(f32[8,128]{1,0:T(8,128)S(1)} %get-tuple-element.48.turn_ref, bf16[512,1536]{1,0:T(8,128)(2,1)S(1)} %get-tuple-element.32.d_ref, f32[512,512]{1,0:T(8,128)} %collective-permute-done.3.far_ref, ...), custom_call_target="tpu_custom_call", output_to_operand_aliasing={{0}: (0, {}), {1}: (5, {})} | custom-call | flops 805306368 | bytes 5242880 | tf_op jit(solution)/shard_map/add_far/pallas_call | solution.py:385
  138.6 7.8 %collective-permute-done.4.far_ref = f32[512,256]{1,0:T(8,128)S(1)} collective-permute-done((f32[512,256]{1,0:T(8,128)}, f32[512,256]{1,0:T(8,128)S(1)}, u32[]{:S(2)}, u32[]{:S(2)}) %collective-permute-start.4) | collective-permute-done | bytes 524320 | tf_op jit(solution)/shard_map/ppermute | solution.py:513
  146.4 2.6 %add_far.12 = (f32[8,128]{1,0:T(8,128)S(1)}, f32[1,5,512,512]{3,2,1,0:T(8,128)}) custom-call(f32[8,128]{1,0:T(8,128)S(1)} %get-tuple-element.51.turn_ref, bf16[512,1536]{1,0:T(8,128)(2,1)S(1)} %get-tuple-element.32.d_ref, f32[512,256]{1,0:T(8,128)S(1)} %collective-permute-done.4.far_ref, ...), custom_call_target="tpu_custom_call", output_to_operand_aliasing={{0}: (0, {}), {1}: (5, {})} | custom-call | flops 402653184 | bytes 2621440 | tf_op jit(solution)/shard_map/add_far/pallas_call | solution.py:385
  152.0 2.3 %add_far.13 = (f32[8,128]{1,0:T(8,128)S(1)}, f32[1,5,512,512]{3,2,1,0:T(8,128)}) custom-call(f32[8,128]{1,0:T(8,128)S(1)} %get-tuple-element.57.turn_ref, bf16[512,1536]{1,0:T(8,128)(2,1)S(1)} %get-tuple-element.32.d_ref, f32[512,128]{1,0:T(8,128)S(1)} %collective-permute-done.5.far_ref, ...), custom_call_target="tpu_custom_call", output_to_operand_aliasing={{0}: (0, {}), {1}: (5, {})} | custom-call | flops 201326592 | bytes 1310720 | tf_op jit(solution)/shard_map/add_far/pallas_call | solution.py:385
  154.3 2.6 %collective-permute-done.far_ref = f32[512,128]{1,0:T(8,128)} collective-permute-done((f32[512,128]{1,0:T(8,128)}, f32[512,128]{1,0:T(8,128)}, u32[]{:S(2)}, u32[]{:S(2)}) %collective-permute-start) | collective-permute-done | bytes 262176 | tf_op jit(solution)/shard_map/ppermute | solution.py:513
  156.9 2.2 %finish_last.1 = f32[1,5,512,512]{3,2,1,0:T(8,128)} custom-call(bf16[512,1536]{1,0:T(8,128)(2,1)S(1)} %get-tuple-element.32.d_ref, f32[512,128]{1,0:T(8,128)} %collective-permute-done.far_ref, f32[512,128]{1,0:T(8,128)S(1)} %get-tuple-element.55.old_ref, f32[512,128]{1,0:T(8,128)S(1)} %get-tuple-element.56.scale_ref, ...), custom_call_target="tpu_custom_call", output_to_operand_aliasing={{}: (4, {})} | custom-call | flops 201326592 | bytes 262144 | tf_op jit(solution)/shard_map/finish_last/pallas_call | solution.py:473
  (36 shorter events, 9.8 us)
Async XLA Ops:
  7.2 2.3 %copy-start.1 = (s32[1,1,1,4,4,256]{5,4,3,2,1,0:T(4,128)S(1)}, s32[1,1,1,4,4,256]{5,4,3,2,1,0:T(4,128)}, u32[]{:S(2)}) copy-start(s32[1,1,1,4,4,256]{5,4,3,2,1,0:T(4,128)} %cells_ref.2) | copy-start | bytes 49156
  7.2 2.3 %copy-start.2 = (f32[1,1,1,4,4,256]{5,4,3,2,1,0:T(4,128)S(1)}, f32[1,1,1,4,4,256]{5,4,3,2,1,0:T(4,128)}, u32[]{:S(2)}) copy-start(f32[1,1,1,4,4,256]{5,4,3,2,1,0:T(4,128)} %weights_ref.1) | copy-start | bytes 49156
  7.2 115.5 %all-gather.3.cloned.1.call-start = ((), (), s32[]{:S(2)}) async-start(), calls=%async_computation.3 | async-start | bytes 6291456 | tf_op jit(solution)/shard_map/all_gather | solution.py:535
  16.4 12.0 %copy-start.7 = (f32[128,20]{0,1:T(8,128)S(1)}, f32[128,20]{0,1:T(8,128)}, u32[]{:S(2)}) copy-start(f32[128,20]{0,1:T(8,128)} %param.18) | copy-start | bytes 30724
  18.0 88.7 %collective-permute-start.1 = (f32[512,512]{1,0:T(8,128)}, f32[512,512]{1,0:T(8,128)}, u32[]{:S(2)}, u32[]{:S(2)}) collective-permute-start(f32[512,512]{1,0:T(8,128)} %take_first.1.after_ref), channel_id=1, source_target_pairs={{0,4},{4,0},{1,5},{5,1},{2,6},{6,2},{3,7},{7,3},{8,12},{12,8},{9,1... | collective-permute-start | bytes 3145736 | tf_op jit(solution)/shard_map/ppermute | solution.py:513
  21.0 7.6 %all-to-all-start = ((f32[4,8,256]{2,1,0:T(8,128)}), f32[4,8,256]{2,1,0:T(8,128)S(1)}, u32[]{:S(2)}, u32[]{:S(2)}) async-start(f32[4,8,256]{2,1,0:T(8,128)} %get-tuple-element.34), calls=%async_computation | async-start | bytes 65536 | tf_op jit(solution)/shard_map/all_to_all | solution.py:541
  24.3 106.8 %collective-permute-start.2 = (f32[512,512]{1,0:T(8,128)}, f32[512,512]{1,0:T(8,128)}, u32[]{:S(2)}, u32[]{:S(2)}) collective-permute-start(f32[512,512]{1,0:T(8,128)} %get-tuple-element.46), channel_id=1, source_target_pairs={{0,4},{4,0},{1,5},{5,1},{2,6},{6,2},{3,7},{7,3},{8,12},{12,8},{9,1... | collective-permute-start | bytes 3145736 | tf_op jit(solution)/shard_map/ppermute | solution.py:513
  24.4 110.8 %collective-permute-start.3 = (f32[512,512]{1,0:T(8,128)}, f32[512,512]{1,0:T(8,128)}, u32[]{:S(2)}, u32[]{:S(2)}) collective-permute-start(f32[512,512]{1,0:T(8,128)} %get-tuple-element.49), channel_id=1, source_target_pairs={{0,4},{4,0},{1,5},{5,1},{2,6},{6,2},{3,7},{7,3},{8,12},{12,8},{9,1... | collective-permute-start | bytes 3145736 | tf_op jit(solution)/shard_map/ppermute | solution.py:513
  26.4 120.0 %collective-permute-start.4 = (f32[512,256]{1,0:T(8,128)}, f32[512,256]{1,0:T(8,128)S(1)}, u32[]{:S(2)}, u32[]{:S(2)}) collective-permute-start(f32[512,256]{1,0:T(8,128)} %get-tuple-element.52), channel_id=1, source_target_pairs={{0,4},{4,0},{1,5},{5,1},{2,6},{6,2},{3,7},{7,3},{8,12},{12,8},{9,1... | collective-permute-start | bytes 1572872 | tf_op jit(solution)/shard_map/ppermute | solution.py:513
  26.5 125.5 %collective-permute-start.5 = (f32[512,128]{1,0:T(8,128)}, f32[512,128]{1,0:T(8,128)S(1)}, u32[]{:S(2)}, u32[]{:S(2)}) collective-permute-start(f32[512,128]{1,0:T(8,128)} %get-tuple-element.58), channel_id=1, source_target_pairs={{0,4},{4,0},{1,5},{5,1},{2,6},{6,2},{3,7},{7,3},{8,12},{12,8},{9,1... | collective-permute-start | bytes 786440 | tf_op jit(solution)/shard_map/ppermute | solution.py:513
  56.7 7.2 %all-to-all-start.1 = ((f32[4,2,8,128]{3,2,1,0:T(8,128)}), f32[4,2,8,128]{3,2,1,0:T(8,128)S(1)}, u32[]{:S(2)}, u32[]{:S(2)}) async-start(f32[4,2,8,128]{3,2,1,0:T(8,128)} %donor_gather.1), calls=%async_computation.1 | async-start | bytes 65536 | tf_op jit(solution)/shard_map/all_to_all | solution.py:556
  63.8 17.5 %all-to-all-start.2 = ((f32[4,8,512]{2,1,0:T(8,128)}), f32[4,8,512]{2,1,0:T(8,128)S(1)}, u32[]{:S(2)}, u32[]{:S(2)}) async-start(f32[4,8,512]{2,1,0:T(8,128)} %get-tuple-element.36), calls=%async_computation.2 | async-start | bytes 131072 | tf_op jit(solution)/shard_map/all_to_all | solution.py:557
  68.7 12.6 %copy-start.3 = (s32[1,1,1,4,256]{4,3,2,1,0:T(4,128)S(1)}, s32[1,1,1,4,256]{4,3,2,1,0:T(4,128)}, u32[]{:S(2)}) copy-start(s32[1,1,1,4,256]{4,3,2,1,0:T(4,128)} %cells_ref.3) | copy-start | bytes 12292
  68.7 12.6 %copy-start.4 = (s32[1,512]{1,0:T(1,128)S(1)}, s32[1,512]{1,0:T(1,128)}, u32[]{:S(2)}) copy-start(s32[1,512]{1,0:T(1,128)} %el_pair_ref.1) | copy-start | bytes 6148
  68.7 12.6 %copy-start.5 = (s32[1,512]{1,0:T(1,128)S(1)}, s32[1,512]{1,0:T(1,128)}, u32[]{:S(2)}) copy-start(s32[1,512]{1,0:T(1,128)} %ac_pair_ref.1) | copy-start | bytes 6148
  68.8 12.6 %copy-start.6 = (s32[1,1,1,4]{3,2,1,0:T(1,128)S(1)}, s32[1,1,1,4]{3,2,1,0:T(1,128)}, u32[]{:S(2)}) copy-start(s32[1,1,1,4]{3,2,1,0:T(1,128)} %counts_ref.1) | copy-start | bytes 52
  81.4 2.8 %copy-start = (f32[6,512,512]{2,1,0:T(8,128)S(1)}, f32[6,512,512]{2,1,0:T(8,128)}, u32[]{:S(2)}) copy-start(f32[6,512,512]{2,1,0:T(8,128)} %get-tuple-element.35.dx_ref) | copy-start | bytes 18874372
  106.7 50.2 %collective-permute-start = (f32[512,128]{1,0:T(8,128)}, f32[512,128]{1,0:T(8,128)}, u32[]{:S(2)}, u32[]{:S(2)}) collective-permute-start(f32[512,128]{1,0:T(8,128)} %get-tuple-element.33), channel_id=1, source_target_pairs={{0,4},{4,0},{1,5},{5,1},{2,6},{6,2},{3,7},{7,3},{8,12},{12,8},{9,1... | collective-permute-start | bytes 786440 | tf_op jit(solution)/shard_map/ppermute | solution.py:513
Sparse Core Ops, SparseCore 0:
  18.1 104.5 all-gather.2

commit v11 on v9

--- a/solution.py
+++ b/solution.py
@@ -84,20 +84,26 @@
     return stores
 
 
-def take_first_kernel(field, elastic_ref, out_ref, semaphore):
-    copy = pltpu.make_async_copy(elastic_ref.at[0, field], out_ref, semaphore)
-    copy.start()
-    copy.wait()
+def take_first_kernel(field, parts, elastic_ref, out_ref, semaphores):
+    rows = out_ref.shape[0] // parts
+    copies = []
+    for part in range(parts):
+        here = pl.ds(part * rows, rows)
+        copies.append(pltpu.make_async_copy(elastic_ref.at[0, field, here], out_ref.at[here], semaphores.at[part]))
+        copies[-1].start()
+    for copy in copies:
+        copy.wait()
 
 
 def take_first(elastic, field):
     rows, depth = elastic.shape[2:]
+    parts = 4
     return pl.pallas_call(
-        functools.partial(take_first_kernel, field),
+        functools.partial(take_first_kernel, field, parts),
         in_specs=[pl.BlockSpec(memory_space=pl.ANY)],
         out_specs=pl.BlockSpec(memory_space=pltpu.VMEM),
         out_shape=pltpu.VMEM((rows, depth), jnp.float32),
-        scratch_shapes=[pltpu.SemaphoreType.DMA],
+        scratch_shapes=[pltpu.SemaphoreType.DMA((parts,))],
         compiler_params=pltpu.CompilerParams(vmem_limit_bytes=16 * MIB),
         cost_estimate=pl.CostEstimate(flops=0, bytes_accessed=8 * rows * depth, transcendentals=0),
         name="take_first",
@@ -467,7 +473,7 @@
 
 def finish_last(base, operator, far, old, scale, field, at):
     rows, width = old.shape
-    parts = 4
+    parts = 2
     anywhere = pl.BlockSpec(memory_space=pl.ANY)
     vmem = pl.BlockSpec(memory_space=pltpu.VMEM)
     return pl.pallas_call(

time: 143 us -> 143 us (level)
  no operation moved by 1% of the time
where the time goes in v11:
time: 143 us; the launch traced here: 142 us
  Pallas kernels  97.3 us (68%)
  starting transfers between devices  23.4 us (16%)
  waiting for transfers between devices  13.2 us (9%)
  local copies, waits for them, and re-layouts  6.19 us (4%)
    pallas_call x1, Pallas kernels, per_device(): pl.pallas_call(functools.partial(gather_kernel, 8, rows, depth), in_specs...  27.2 us
    pallas_call x1, Pallas kernels, per_device(): pl.pallas_call(functools.partial(section_kernel, layers, rows, depth, til...  22.9 us
    pallas_call x7, Pallas kernels, add_far(): pl.pallas_call(functools.partial(far_kernel, coefficients), grid=(width /...  22.7 us
    pallas_call x1, Pallas kernels, near_derivatives(): pl.pallas_call(functools.partial(near_kernel, 4), grid_spec=pltpu.Prefetc...  12.6 us
    ppermute x8, starting transfers between devices, other_slabs(): lax.ppermute(value, 'line', [(i, (i + distance) % slabs) for i in range(s...  12 us
    ppermute x8, waiting for transfers between devices, other_slabs(): lax.ppermute(value, 'line', [(i, (i + distance) % slabs) for i in range(s...  10.1 us
    pallas_call x1, Pallas kernels, take_pieces(): pl.pallas_call(functools.partial(take_and_edges_kernel, pieces, parts, la...  7.57 us
    unnamed x30, local copies, waits for them, and re-layouts  6.18 us
  transfers between devices with their start and end apart: 11, of which 4 were waited for; matrix products, arithmetic and copies ran while one was open for 1% of the time, Pallas kernels for 67%

profile of v11, /device:TPU:0, one launch (start us, length us, event | category | flops | bytes accessed | tf_op | source)
XLA Modules:
  0.0 141.7 jit_solution(984942265489569847)
XLA Ops:
  1.9 3.0 %collective-permute-start.1 = (f32[512,512]{1,0:T(8,128)S(1)}, f32[512,512]{1,0:T(8,128)}, u32[]{:S(2)}, u32[]{:S(2)}) collective-permute-start(f32[512,512]{1,0:T(8,128)S(1)} %take_first.1.after_ref), channel_id=1, source_target_pairs={{0,4},{4,0},{1,5},{5,1},{2,6},{6,2},{3,7},{7,3},{8,12},{12,8},{9,1... | collective-permute-start | bytes 3145736 | tf_op jit(solution)/shard_map/ppermute | solution.py:519
  4.9 7.6 %take_pieces.1 = (f32[512,512]{1,0:T(8,128)}, f32[512,512]{1,0:T(8,128)}, f32[512,512]{1,0:T(8,128)}, f32[512,512]{1,0:T(8,128)}, f32[512,256]{1,0:T(8,128)S(1)}...) custom-call(f32[512,512]{1,0:T(8,128)S(1)} %take_first.1.after_ref, ...), custom_call_target="tpu_custom_call" | custom-call | bytes 10485760 | tf_op jit(solution)/shard_map/take_pieces/pallas_call | solution.py:168
  14.7 3.3 %all-to-all-start = ((f32[4,8,256]{2,1,0:T(8,128)}), f32[4,8,256]{2,1,0:T(8,128)S(1)}, u32[]{:S(2)}, u32[]{:S(2)}) async-start(f32[4,8,256]{2,1,0:T(8,128)} %get-tuple-element.34), calls=%async_computation | async-start | bytes 65536 | tf_op jit(solution)/shard_map/all_to_all | solution.py:542
  18.1 2.0 %collective-permute-start.3 = (f32[512,512]{1,0:T(8,128)}, f32[512,512]{1,0:T(8,128)}, u32[]{:S(2)}, u32[]{:S(2)}) collective-permute-start(f32[512,512]{1,0:T(8,128)} %get-tuple-element.43), channel_id=1, source_target_pairs={{0,4},{4,0},{1,5},{5,1},{2,6},{6,2},{3,7},{7,3},{8,12},{12,8},{9,1... | collective-permute-start | bytes 3145736 | tf_op jit(solution)/shard_map/ppermute | solution.py:519
  20.2 1.9 %collective-permute-start.5 = (f32[512,512]{1,0:T(8,128)}, f32[512,512]{1,0:T(8,128)S(1)}, u32[]{:S(2)}, u32[]{:S(2)}) collective-permute-start(f32[512,512]{1,0:T(8,128)} %get-tuple-element.49), channel_id=1, source_target_pairs={{0,4},{4,0},{1,5},{5,1},{2,6},{6,2},{3,7},{7,3},{8,12},{12,8},{9,1... | collective-permute-start | bytes 3145736 | tf_op jit(solution)/shard_map/ppermute | solution.py:519
  22.4 27.2 %donor_gather.1 = f32[4,2,8,128]{3,2,1,0:T(8,128)} custom-call(s32[4,4,256]{2,1,0:T(4,128)S(1)} %slice_convert_fusion.words_ref, f32[4,8,256]{2,1,0:T(8,128)S(1)} %all-to-all-done.weights_ref, f32[1,5,512,512]{3,2,1,0:T(8,128)} %elastic_ref.9, f32[1,3,512,512]{3,2,1,0:T(8,128)} %acoustic_ref.7), custom_call_target="tpu_custom_call" | custom-call | flops 1000000000 | bytes 8388608 | tf_op jit(solution)/shard_map/donor_gather/pallas_call | solution.py:547
  49.5 3.3 %all-to-all-start.1 = ((f32[4,2,8,128]{3,2,1,0:T(8,128)}), f32[4,2,8,128]{3,2,1,0:T(8,128)S(1)}, u32[]{:S(2)}, u32[]{:S(2)}) async-start(f32[4,2,8,128]{3,2,1,0:T(8,128)} %donor_gather.1), calls=%async_computation.1 | async-start | bytes 65536 | tf_op jit(solution)/shard_map/all_to_all | solution.py:557
  53.6 3.1 %all-to-all-done.1.interp_ref = f32[4,2,8,128]{3,2,1,0:T(8,128)S(1)} async-done(((f32[4,2,8,128]{3,2,1,0:T(8,128)}), f32[4,2,8,128]{3,2,1,0:T(8,128)S(1)}, u32[]{:S(2)}, u32[]{:S(2)}) %all-to-all-start.1) | async-done | bytes 32800 | tf_op jit(solution)/shard_map/all_to_all | solution.py:557
  56.7 4.9 %all-to-all-start.2 = ((f32[4,8,512]{2,1,0:T(8,128)}), f32[4,8,512]{2,1,0:T(8,128)S(1)}, u32[]{:S(2)}, u32[]{:S(2)}) async-start(f32[4,8,512]{2,1,0:T(8,128)} %get-tuple-element.36), calls=%async_computation.2 | async-start | bytes 131072 | tf_op jit(solution)/shard_map/all_to_all | solution.py:558
  63.0 12.6 %near_dx.1 = (f32[6,512,512]{2,1,0:T(8,128)}, bf16[512,1536]{1,0:T(8,128)(2,1)S(1)}) custom-call(s32[1]{0:T(128)} %bitcast.me_ref, f32[512,512]{1,0:T(8,128)} %constant.33.clone.own_ref, f32[2,512,512]{2,1,0:T(8,128)} %constant.34.clone.far_ref, f32[2,512,128]{2,1,0:T(8,128)} %constant.35.clone.tail_ref, f32[128,512]{1,0:T(8,128)S(1)} %copy-done.1, ...), custom_call_target="tpu_custom_call" | custom-call | flops 4831838208 | bytes 15728640 | tf_op jit(solution)/shard_map/near_dx/pallas_call | solution.py:251
  75.7 2.8 %copy-done = f32[6,512,512]{2,1,0:T(8,128)S(1)} copy-done((f32[6,512,512]{2,1,0:T(8,128)S(1)}, f32[6,512,512]{2,1,0:T(8,128)}, u32[]{:S(2)}) %copy-start) | copy-done | bytes 6291480
  78.5 22.9 %near_section.1 = (f32[1,5,512,512]{3,2,1,0:T(8,128)}, f32[1,3,512,512]{3,2,1,0:T(8,128)}, f32[512,512]{1,0:T(8,128)S(1)}) custom-call(s32[1,1,1,4,256]{4,3,2,1,0:T(4,128)S(1)} %copy-done.4, s32[1,1,1,4]{3,2,1,0:T(1,128)S(1)} %copy-done.7, f32[4,2,8,128]{3,2,1,0:T(8,128)S(1)} %all-to-all-done.1.interp_ref, f32[6,512,512]{2,1,0:T(8,128)S(1)} %copy-done, ...), custom_call_target="tpu_custom_call" | custom-call | flops 26214400 | bytes 29360128 | tf_op jit(solution)/shard_map/near_section/pallas_call | solution.py:561
  101.4 4.5 %add_far.7 = (f32[8,128]{1,0:T(8,128)S(1)}, f32[1,5,512,512]{3,2,1,0:T(8,128)}) custom-call(f32[8,128]{1,0:T(8,128)S(1)} %broadcast_in_dim.11.turn_ref, bf16[512,1536]{1,0:T(8,128)(2,1)S(1)} %get-tuple-element.32.d_ref, f32[512,512]{1,0:T(8,128)} %collective-permute-done.1.far_ref, ...), custom_call_target="tpu_custom_call", output_to_operand_aliasing={{0}: (0, {}), {1}: (5, {})} | custom-call | flops 805306368 | bytes 8388608 | tf_op jit(solution)/shard_map/add_far/pallas_call | solution.py:391
  105.9 4.2 %collective-permute-start.7 = (f32[512,128]{1,0:T(8,128)S(1)}, f32[512,128]{1,0:T(8,128)S(1)}, u32[]{:S(2)}, u32[]{:S(2)}) collective-permute-start(f32[512,128]{1,0:T(8,128)S(1)} %copy-done.12), channel_id=1, source_target_pairs={{0,4},{4,0},{1,5},{5,1},{2,6},{6,2},{3,7},{7,3},{8,12},{12,8},{9,1... | collective-permute-start | bytes 786440 | tf_op jit(solution)/shard_map/ppermute | solution.py:519
  110.1 3.4 %add_far.8 = (f32[8,128]{1,0:T(8,128)S(1)}, f32[1,3,512,512]{3,2,1,0:T(8,128)}) custom-call(f32[8,128]{1,0:T(8,128)S(1)} %get-tuple-element.39.turn_ref, bf16[512,1536]{1,0:T(8,128)(2,1)S(1)} %get-tuple-element.32.d_ref, f32[512,512]{1,0:T(8,128)} %collective-permute-done.2.far_ref, ...), custom_call_target="tpu_custom_call", output_to_operand_aliasing={{0}: (0, {}), {1}: (5, {})} | custom-call | flops 805306368 | bytes 5242880 | tf_op jit(solution)/shard_map/add_far/pallas_call | solution.py:391
  113.6 3.4 %add_far.9 = (f32[8,128]{1,0:T(8,128)S(1)}, f32[1,3,512,512]{3,2,1,0:T(8,128)}) custom-call(f32[8,128]{1,0:T(8,128)S(1)} %get-tuple-element.42.turn_ref, bf16[512,1536]{1,0:T(8,128)(2,1)S(1)} %get-tuple-element.32.d_ref, f32[512,512]{1,0:T(8,128)} %collective-permute-done.3.far_ref, ...), custom_call_target="tpu_custom_call", output_to_operand_aliasing={{0}: (0, {}), {1}: (5, {})} | custom-call | flops 805306368 | bytes 5242880 | tf_op jit(solution)/shard_map/add_far/pallas_call | solution.py:391
  117.0 3.4 %add_far.10 = (f32[8,128]{1,0:T(8,128)S(1)}, f32[1,5,512,512]{3,2,1,0:T(8,128)}) custom-call(f32[8,128]{1,0:T(8,128)S(1)} %get-tuple-element.45.turn_ref, bf16[512,1536]{1,0:T(8,128)(2,1)S(1)} %get-tuple-element.32.d_ref, f32[512,512]{1,0:T(8,128)} %collective-permute-done.4.far_ref, ...), custom_call_target="tpu_custom_call", output_to_operand_aliasing={{0}: (0, {}), {1}: (5, {})} | custom-call | flops 805306368 | bytes 5242880 | tf_op jit(solution)/shard_map/add_far/pallas_call | solution.py:391
  120.3 3.2 %add_far.11 = (f32[8,128]{1,0:T(8,128)S(1)}, f32[1,5,512,512]{3,2,1,0:T(8,128)}) custom-call(f32[8,128]{1,0:T(8,128)S(1)} %get-tuple-element.48.turn_ref, bf16[512,1536]{1,0:T(8,128)(2,1)S(1)} %get-tuple-element.32.d_ref, f32[512,512]{1,0:T(8,128)S(1)} %collective-permute-done.5.far_ref, ...), custom_call_target="tpu_custom_call", output_to_operand_aliasing={{0}: (0, {}), {1}: (5, {})} | custom-call | flops 805306368 | bytes 5242880 | tf_op jit(solution)/shard_map/add_far/pallas_call | solution.py:391
  123.6 6.5 %collective-permute-done.6.far_ref = f32[512,256]{1,0:T(8,128)S(1)} collective-permute-done((f32[512,256]{1,0:T(8,128)}, f32[512,256]{1,0:T(8,128)S(1)}, u32[]{:S(2)}, u32[]{:S(2)}) %collective-permute-start.6) | collective-permute-done | bytes 524320 | tf_op jit(solution)/shard_map/ppermute | solution.py:519
  130.0 2.6 %add_far.12 = (f32[8,128]{1,0:T(8,128)S(1)}, f32[1,5,512,512]{3,2,1,0:T(8,128)}) custom-call(f32[8,128]{1,0:T(8,128)S(1)} %get-tuple-element.51.turn_ref, bf16[512,1536]{1,0:T(8,128)(2,1)S(1)} %get-tuple-element.32.d_ref, f32[512,256]{1,0:T(8,128)S(1)} %collective-permute-done.6.far_ref, ...), custom_call_target="tpu_custom_call", output_to_operand_aliasing={{0}: (0, {}), {1}: (5, {})} | custom-call | flops 402653184 | bytes 2621440 | tf_op jit(solution)/shard_map/add_far/pallas_call | solution.py:391
  132.6 1.9 %prepare_last.1 = (f32[1,5,512,512]{3,2,1,0:T(8,128)}, f32[512,128]{1,0:T(8,128)S(1)}, f32[512,128]{1,0:T(8,128)S(1)}) custom-call(f32[1,5,512,512]{3,2,1,0:T(8,128)} %get-tuple-element.54.base_ref, f32[1,3,512,512]{3,2,1,0:T(8,128)} %media_ref.15, f32[512,512]{1,0:T(8,128)S(1)} %get-tuple-element.37.open_ref), custom_call_target="tpu_custom_call", output_to_operand_aliasing={{0}: (0, {})} | custom-call | flops 65536 | bytes 1310720 | tf_op jit(solution)/shard_map/prepare_last/pallas_call | solution.py:433
  135.7 2.3 %add_far.13 = (f32[8,128]{1,0:T(8,128)S(1)}, f32[1,5,512,512]{3,2,1,0:T(8,128)}) custom-call(f32[8,128]{1,0:T(8,128)S(1)} %get-tuple-element.57.turn_ref, bf16[512,1536]{1,0:T(8,128)(2,1)S(1)} %get-tuple-element.32.d_ref, f32[512,128]{1,0:T(8,128)S(1)} %collective-permute-done.7.far_ref, ...), custom_call_target="tpu_custom_call", output_to_operand_aliasing={{0}: (0, {}), {1}: (5, {})} | custom-call | flops 201326592 | bytes 1310720 | tf_op jit(solution)/shard_map/add_far/pallas_call | solution.py:391
  138.0 2.5 %collective-permute-done.far_ref = f32[512,128]{1,0:T(8,128)S(1)} collective-permute-done((f32[512,128]{1,0:T(8,128)S(1)}, f32[512,128]{1,0:T(8,128)S(1)}, u32[]{:S(2)}, u32[]{:S(2)}) %collective-permute-start) | collective-permute-done | bytes 262176 | tf_op jit(solution)/shard_map/ppermute | solution.py:519
  140.4 1.2 finish_last.1
  (46 shorter events, 7.3 us)
Async XLA Ops:
  0.6 4.3 %copy-start.2 = (s32[1,1,1,4,4,256]{5,4,3,2,1,0:T(4,128)S(1)}, s32[1,1,1,4,4,256]{5,4,3,2,1,0:T(4,128)}, u32[]{:S(2)}) copy-start(s32[1,1,1,4,4,256]{5,4,3,2,1,0:T(4,128)} %cells_ref.2) | copy-start | bytes 49156
  0.6 4.3 %copy-start.3 = (f32[1,1,1,4,4,256]{5,4,3,2,1,0:T(4,128)S(1)}, f32[1,1,1,4,4,256]{5,4,3,2,1,0:T(4,128)}, u32[]{:S(2)}) copy-start(f32[1,1,1,4,4,256]{5,4,3,2,1,0:T(4,128)} %weights_ref.1) | copy-start | bytes 49156
  1.9 20.2 %copy-start.13 = (f32[128,20]{0,1:T(8,128)S(1)}, f32[128,20]{0,1:T(8,128)}, u32[]{:S(2)}) copy-start(f32[128,20]{0,1:T(8,128)} %param.18) | copy-start | bytes 30724
  1.9 59.7 %collective-permute-start.1 = (f32[512,512]{1,0:T(8,128)S(1)}, f32[512,512]{1,0:T(8,128)}, u32[]{:S(2)}, u32[]{:S(2)}) collective-permute-start(f32[512,512]{1,0:T(8,128)S(1)} %take_first.1.after_ref), channel_id=1, source_target_pairs={{0,4},{4,0},{1,5},{5,1},{2,6},{6,2},{3,7},{7,3},{8,12},{12,8},{9,1... | collective-permute-start | bytes 3145736 | tf_op jit(solution)/shard_map/ppermute | solution.py:519
  12.5 0.8 copy-start.8
  13.3 0.7 copy-start.9
  14.7 7.6 %all-to-all-start = ((f32[4,8,256]{2,1,0:T(8,128)}), f32[4,8,256]{2,1,0:T(8,128)S(1)}, u32[]{:S(2)}, u32[]{:S(2)}) async-start(f32[4,8,256]{2,1,0:T(8,128)} %get-tuple-element.34), calls=%async_computation | async-start | bytes 65536 | tf_op jit(solution)/shard_map/all_to_all | solution.py:542
  18.0 87.9 %collective-permute-start.2 = (f32[512,512]{1,0:T(8,128)}, f32[512,512]{1,0:T(8,128)}, u32[]{:S(2)}, u32[]{:S(2)}) collective-permute-start(f32[512,512]{1,0:T(8,128)} %get-tuple-element.40), channel_id=1, source_target_pairs={{0,4},{4,0},{1,5},{5,1},{2,6},{6,2},{3,7},{7,3},{8,12},{12,8},{9,1... | collective-permute-start | bytes 3145736 | tf_op jit(solution)/shard_map/ppermute | solution.py:519
  18.1 95.4 %collective-permute-start.3 = (f32[512,512]{1,0:T(8,128)}, f32[512,512]{1,0:T(8,128)}, u32[]{:S(2)}, u32[]{:S(2)}) collective-permute-start(f32[512,512]{1,0:T(8,128)} %get-tuple-element.43), channel_id=1, source_target_pairs={{0,4},{4,0},{1,5},{5,1},{2,6},{6,2},{3,7},{7,3},{8,12},{12,8},{9,1... | collective-permute-start | bytes 3145736 | tf_op jit(solution)/shard_map/ppermute | solution.py:519
  20.1 96.9 %collective-permute-start.4 = (f32[512,512]{1,0:T(8,128)}, f32[512,512]{1,0:T(8,128)}, u32[]{:S(2)}, u32[]{:S(2)}) collective-permute-start(f32[512,512]{1,0:T(8,128)} %get-tuple-element.46), channel_id=1, source_target_pairs={{0,4},{4,0},{1,5},{5,1},{2,6},{6,2},{3,7},{7,3},{8,12},{12,8},{9,1... | collective-permute-start | bytes 3145736 | tf_op jit(solution)/shard_map/ppermute | solution.py:519
  20.2 100.2 %collective-permute-start.5 = (f32[512,512]{1,0:T(8,128)}, f32[512,512]{1,0:T(8,128)S(1)}, u32[]{:S(2)}, u32[]{:S(2)}) collective-permute-start(f32[512,512]{1,0:T(8,128)} %get-tuple-element.49), channel_id=1, source_target_pairs={{0,4},{4,0},{1,5},{5,1},{2,6},{6,2},{3,7},{7,3},{8,12},{12,8},{9,1... | collective-permute-start | bytes 3145736 | tf_op jit(solution)/shard_map/ppermute | solution.py:519
  49.5 7.2 %all-to-all-start.1 = ((f32[4,2,8,128]{3,2,1,0:T(8,128)}), f32[4,2,8,128]{3,2,1,0:T(8,128)S(1)}, u32[]{:S(2)}, u32[]{:S(2)}) async-start(f32[4,2,8,128]{3,2,1,0:T(8,128)} %donor_gather.1), calls=%async_computation.1 | async-start | bytes 65536 | tf_op jit(solution)/shard_map/all_to_all | solution.py:557
  56.7 18.9 %all-to-all-start.2 = ((f32[4,8,512]{2,1,0:T(8,128)}), f32[4,8,512]{2,1,0:T(8,128)S(1)}, u32[]{:S(2)}, u32[]{:S(2)}) async-start(f32[4,8,512]{2,1,0:T(8,128)} %get-tuple-element.36), calls=%async_computation.2 | async-start | bytes 131072 | tf_op jit(solution)/shard_map/all_to_all | solution.py:558
  61.6 68.4 %collective-permute-start.6 = (f32[512,256]{1,0:T(8,128)}, f32[512,256]{1,0:T(8,128)S(1)}, u32[]{:S(2)}, u32[]{:S(2)}) collective-permute-start(f32[512,256]{1,0:T(8,128)} %copy-done.8), channel_id=1, source_target_pairs={{0,4},{4,0},{1,5},{5,1},{2,6},{6,2},{3,7},{7,3},{8,12},{12,8},{9,1... | collective-permute-start | bytes 1572872 | tf_op jit(solution)/shard_map/ppermute | solution.py:519
  62.1 0.9 copy-start.1
  63.0 12.6 %copy-start.4 = (s32[1,1,1,4,256]{4,3,2,1,0:T(4,128)S(1)}, s32[1,1,1,4,256]{4,3,2,1,0:T(4,128)}, u32[]{:S(2)}) copy-start(s32[1,1,1,4,256]{4,3,2,1,0:T(4,128)} %cells_ref.3) | copy-start | bytes 12292
  63.0 12.6 %copy-start.5 = (s32[1,512]{1,0:T(1,128)S(1)}, s32[1,512]{1,0:T(1,128)}, u32[]{:S(2)}) copy-start(s32[1,512]{1,0:T(1,128)} %el_pair_ref.1) | copy-start | bytes 6148
  63.0 12.6 %copy-start.6 = (s32[1,512]{1,0:T(1,128)S(1)}, s32[1,512]{1,0:T(1,128)}, u32[]{:S(2)}) copy-start(s32[1,512]{1,0:T(1,128)} %ac_pair_ref.1) | copy-start | bytes 6148
  63.0 12.6 %copy-start.7 = (s32[1,1,1,4]{3,2,1,0:T(1,128)S(1)}, s32[1,1,1,4]{3,2,1,0:T(1,128)}, u32[]{:S(2)}) copy-start(s32[1,1,1,4]{3,2,1,0:T(1,128)} %counts_ref.1) | copy-start | bytes 52
  75.7 2.8 %copy-start = (f32[6,512,512]{2,1,0:T(8,128)S(1)}, f32[6,512,512]{2,1,0:T(8,128)}, u32[]{:S(2)}) copy-start(f32[6,512,512]{2,1,0:T(8,128)} %get-tuple-element.35.dx_ref) | copy-start | bytes 18874372
  101.4 4.5 %copy-start.12 = (f32[512,128]{1,0:T(8,128)S(1)}, f32[512,128]{1,0:T(8,128)}, u32[]{:S(2)}) copy-start(f32[512,128]{1,0:T(8,128)} %copy-done.11) | copy-start | bytes 786436
  105.9 7.6 %copy-start.10 = (f32[512,128]{1,0:T(8,128)S(1)}, f32[512,128]{1,0:T(8,128)}, u32[]{:S(2)}) copy-start(f32[512,128]{1,0:T(8,128)} %copy-done.9) | copy-start | bytes 786436
  105.9 29.8 %collective-permute-start.7 = (f32[512,128]{1,0:T(8,128)S(1)}, f32[512,128]{1,0:T(8,128)S(1)}, u32[]{:S(2)}, u32[]{:S(2)}) collective-permute-start(f32[512,128]{1,0:T(8,128)S(1)} %copy-done.12), channel_id=1, source_target_pairs={{0,4},{4,0},{1,5},{5,1},{2,6},{6,2},{3,7},{7,3},{8,12},{12,8},{9,1... | collective-permute-start | bytes 786440 | tf_op jit(solution)/shard_map/ppermute | solution.py:519
  113.5 26.9 %collective-permute-start = (f32[512,128]{1,0:T(8,128)S(1)}, f32[512,128]{1,0:T(8,128)S(1)}, u32[]{:S(2)}, u32[]{:S(2)}) collective-permute-start(f32[512,128]{1,0:T(8,128)S(1)} %copy-done.10), channel_id=1, source_target_pairs={{0,4},{4,0},{1,5},{5,1},{2,6},{6,2},{3,7},{7,3},{8,12},{12,8},{9,1... | collective-permute-start | bytes 786440 | tf_op jit(solution)/shard_map/ppermute | solution.py:519
  (1 other events, 0.7 us)

commit v12 on v11

--- a/solution.py
+++ b/solution.py
@@ -84,30 +84,32 @@
     return stores
 
 
-def take_first_kernel(field, parts, elastic_ref, out_ref, semaphores):
+def take_field_kernel(field, parts, *refs):
+    fields_ref, out_ref, semaphores = refs[-3:]
     rows = out_ref.shape[0] // parts
     copies = []
     for part in range(parts):
         here = pl.ds(part * rows, rows)
-        copies.append(pltpu.make_async_copy(elastic_ref.at[0, field, here], out_ref.at[here], semaphores.at[part]))
+        copies.append(pltpu.make_async_copy(fields_ref.at[0, field, here], out_ref.at[here], semaphores.at[part]))
         copies[-1].start()
     for copy in copies:
         copy.wait()
 
 
-def take_first(elastic, field):
-    rows, depth = elastic.shape[2:]
+def take_field(fields, field, after=None):
+    rows, depth = fields.shape[2:]
     parts = 4
+    operands = (in_hbm(fields),) if after is None else (after, in_hbm(fields))
     return pl.pallas_call(
-        functools.partial(take_first_kernel, field, parts),
-        in_specs=[pl.BlockSpec(memory_space=pl.ANY)],
+        functools.partial(take_field_kernel, field, parts),
+        in_specs=[pl.BlockSpec(memory_space=pl.ANY)] * len(operands),
         out_specs=pl.BlockSpec(memory_space=pltpu.VMEM),
         out_shape=pltpu.VMEM((rows, depth), jnp.float32),
         scratch_shapes=[pltpu.SemaphoreType.DMA((parts,))],
         compiler_params=pltpu.CompilerParams(vmem_limit_bytes=16 * MIB),
         cost_estimate=pl.CostEstimate(flops=0, bytes_accessed=8 * rows * depth, transcendentals=0),
-        name="take_first",
-    )(in_hbm(elastic))
+        name="take_field",
+    )(*operands)
 
 
 def take_and_edges_kernel(
@@ -533,11 +535,15 @@
         ("el", 4, half + quarter, quarter, "el", 0, 1, 1, (lambda b: b,)),
     ]
     travelling = [piece[:4] for piece in pieces]
-    first = take_first(elastic, travelling[0][1])
+    whole = [piece for piece in travelling if piece[3] == depth]
+    fields = {"el": elastic, "ac": acoustic}
+    taken = [take_field(fields[whole[0][0]], whole[0][1])]
     *others, edges, asked = take_pieces(
-        elastic, acoustic, travelling[1:], first, donor_cells, donor_weights, layers
+        elastic, acoustic, travelling[len(whole) :], taken[0], donor_cells, donor_weights, layers
     )
-    far = [other_slabs(value) for value in [first, *others]]
+    for name, field, _, _ in whole[1:]:
+        taken.append(take_field(fields[name], field, edges if len(taken) == 1 else taken[-1]))
+    far = [other_slabs(value) for value in [*taken, *others]]
 
     asked = lax.all_to_all(asked, "patch", split_axis=0, concat_axis=0, tiled=True)
     asked_words = asked[:, :4].astype(jnp.int32)

time: 143 us -> 143 us (level)
  Pallas kernels: 97.3 us -> 103 us
  waiting for transfers between devices: 13.2 us -> 9.06 us
  starting transfers between devices: 23.4 us -> 21.7 us
    pallas_call x1 -> x5, Pallas kernels: 1.23 us -> 9.08 us  [take_field(): pl.pallas_call(functools.partial(take_field_kernel, field, parts), in_spe...]
    ppermute x8, waiting for transfers between devices: 10.1 us -> 5.93 us  [other_slabs(): lax.ppermute(value, 'line', [(i, (i + distance) % slabs) for i in range(s...]
    pallas_call x1, Pallas kernels: 7.57 us -> 4.7 us  [take_pieces(): pl.pallas_call(functools.partial(take_and_edges_kernel, pieces, parts, la...]
    ppermute x8, starting transfers between devices: 12 us -> 10.3 us  [other_slabs(): lax.ppermute(value, 'line', [(i, (i + distance) % slabs) for i in range(s...]
  transfers between devices with their start and end apart: 11 -> 11, of which waited for: 4 -> 4; matrix products, arithmetic and copies ran while one was open for 1% -> 1% of each run, Pallas kernels for 67% -> 71%
where the time goes in v12:
time: 143 us; the launch traced here: 142 us
  Pallas kernels  103 us (72%)
  starting transfers between devices  21.7 us (15%)
  waiting for transfers between devices  9.06 us (6%)
  local copies, waits for them, and re-layouts  6.19 us (4%)
    pallas_call x1, Pallas kernels, per_device(): pl.pallas_call(functools.partial(gather_kernel, 8, rows, depth), in_specs...  27.2 us
    pallas_call x1, Pallas kernels, per_device(): pl.pallas_call(functools.partial(section_kernel, layers, rows, depth, til...  23.6 us
    pallas_call x7, Pallas kernels, add_far(): pl.pallas_call(functools.partial(far_kernel, coefficients), grid=(width /...  22.8 us
    pallas_call x1, Pallas kernels, near_derivatives(): pl.pallas_call(functools.partial(near_kernel, 4), grid_spec=pltpu.Prefetc...  12.6 us
    ppermute x8, starting transfers between devices, other_slabs(): lax.ppermute(value, 'line', [(i, (i + distance) % slabs) for i in range(s...  10.3 us
    pallas_call x5, Pallas kernels, take_field(): pl.pallas_call(functools.partial(take_field_kernel, field, parts), in_spe...  9.08 us
    unnamed x30, local copies, waits for them, and re-layouts  6.18 us
    ppermute x8, waiting for transfers between devices, other_slabs(): lax.ppermute(value, 'line', [(i, (i + distance) % slabs) for i in range(s...  5.93 us
  transfers between devices with their start and end apart: 11, of which 4 were waited for; matrix products, arithmetic and copies ran while one was open for 1% of the time, Pallas kernels for 71%

profile of v12, /device:TPU:0, one launch (start us, length us, event | category | flops | bytes accessed | tf_op | source)
XLA Modules:
  0.0 141.7 jit_solution(11207969694854549410)
XLA Ops:
  1.9 3.0 %collective-permute-start.1 = (f32[512,512]{1,0:T(8,128)S(1)}, f32[512,512]{1,0:T(8,128)}, u32[]{:S(2)}, u32[]{:S(2)}) collective-permute-start(f32[512,512]{1,0:T(8,128)S(1)} %take_field.5.after_ref), channel_id=1, source_target_pairs={{0,4},{4,0},{1,5},{5,1},{2,6},{6,2},{3,7},{7,3},{8,12},{12,8},{9,1... | collective-permute-start | bytes 3145736 | tf_op jit(solution)/shard_map/ppermute | solution.py:521
  4.9 4.7 %take_pieces.1 = (f32[512,256]{1,0:T(8,128)S(1)}, f32[512,128]{1,0:T(8,128)S(1)}, f32[512,128]{1,0:T(8,128)S(1)}, f32[4,8,512]{2,1,0:T(8,128)}, f32[4,8,256]{2,1,0:T(8,128)}) custom-call(f32[512,512]{1,0:T(8,128)S(1)} %take_field.5.after_ref, f32[1,5,512,512]{3,2,1,0:T(8,128)} %refs_1_.7, f32[1,3,512,512]{3,2,1,0:T(8,128)} %refs_1_.5, ...), custom_call_target="tpu_custom_call" | custom-call | bytes 2097152 | tf_op jit(solution)/shard_map/take_pieces/pallas_call | solution.py:170
  11.8 3.3 %all-to-all-start = ((f32[4,8,256]{2,1,0:T(8,128)}), f32[4,8,256]{2,1,0:T(8,128)S(1)}, u32[]{:S(2)}, u32[]{:S(2)}) async-start(f32[4,8,256]{2,1,0:T(8,128)} %get-tuple-element.30), calls=%async_computation | async-start | bytes 65536 | tf_op jit(solution)/shard_map/all_to_all | solution.py:548
  15.1 2.2 %take_field.6.refs_0_ = f32[512,512]{1,0:T(8,128)} custom-call(f32[4,8,512]{2,1,0:T(8,128)} %get-tuple-element.32.refs_0_, f32[1,3,512,512]{3,2,1,0:T(8,128)} %refs_1_.5), custom_call_target="tpu_custom_call" | custom-call | bytes 2097152 | tf_op jit(solution)/shard_map/take_field/pallas_call | solution.py:103
  17.5 2.2 %take_field.7.refs_0_ = f32[512,512]{1,0:T(8,128)} custom-call(f32[512,512]{1,0:T(8,128)} %take_field.6.refs_0_, f32[1,3,512,512]{3,2,1,0:T(8,128)} %refs_1_.5), custom_call_target="tpu_custom_call" | custom-call | bytes 2097152 | tf_op jit(solution)/shard_map/take_field/pallas_call | solution.py:103
  19.6 2.1 %collective-permute-start.3 = (f32[512,512]{1,0:T(8,128)}, f32[512,512]{1,0:T(8,128)}, u32[]{:S(2)}, u32[]{:S(2)}) collective-permute-start(f32[512,512]{1,0:T(8,128)} %take_field.7.refs_0_), channel_id=1, source_target_pairs={{0,4},{4,0},{1,5},{5,1},{2,6},{6,2},{3,7},{7,3},{8,12},{12,8},{9,1... | collective-permute-start | bytes 3145736 | tf_op jit(solution)/shard_map/ppermute | solution.py:521
  23.0 2.2 %take_field.9 = f32[512,512]{1,0:T(8,128)} custom-call(f32[512,512]{1,0:T(8,128)S(1)} %take_field.8.refs_0_, f32[1,5,512,512]{3,2,1,0:T(8,128)} %refs_1_.7), custom_call_target="tpu_custom_call" | custom-call | bytes 2097152 | tf_op jit(solution)/shard_map/take_field/pallas_call | solution.py:103
  27.6 27.2 %donor_gather.1 = f32[4,2,8,128]{3,2,1,0:T(8,128)} custom-call(s32[4,4,256]{2,1,0:T(4,128)S(1)} %slice_convert_fusion.words_ref, f32[4,8,256]{2,1,0:T(8,128)S(1)} %all-to-all-done.weights_ref, f32[1,5,512,512]{3,2,1,0:T(8,128)} %refs_1_.7, f32[1,3,512,512]{3,2,1,0:T(8,128)} %refs_1_.5), custom_call_target="tpu_custom_call" | custom-call | flops 1000000000 | bytes 8388608 | tf_op jit(solution)/shard_map/donor_gather/pallas_call | solution.py:553
  54.7 3.3 %all-to-all-start.1 = ((f32[4,2,8,128]{3,2,1,0:T(8,128)}), f32[4,2,8,128]{3,2,1,0:T(8,128)S(1)}, u32[]{:S(2)}, u32[]{:S(2)}) async-start(f32[4,2,8,128]{3,2,1,0:T(8,128)} %donor_gather.1), calls=%async_computation.1 | async-start | bytes 65536 | tf_op jit(solution)/shard_map/all_to_all | solution.py:563
  58.8 3.1 %all-to-all-done.1.interp_ref = f32[4,2,8,128]{3,2,1,0:T(8,128)S(1)} async-done(((f32[4,2,8,128]{3,2,1,0:T(8,128)}), f32[4,2,8,128]{3,2,1,0:T(8,128)S(1)}, u32[]{:S(2)}, u32[]{:S(2)}) %all-to-all-start.1) | async-done | bytes 32800 | tf_op jit(solution)/shard_map/all_to_all | solution.py:563
  61.9 4.9 %all-to-all-start.2 = ((f32[4,8,512]{2,1,0:T(8,128)}), f32[4,8,512]{2,1,0:T(8,128)S(1)}, u32[]{:S(2)}, u32[]{:S(2)}) async-start(f32[4,8,512]{2,1,0:T(8,128)} %get-tuple-element.32.refs_0_), calls=%async_computation.2 | async-start | bytes 131072 | tf_op jit(solution)/shard_map/all_to_all | solution.py:564
  68.3 12.6 %near_dx.1 = (f32[6,512,512]{2,1,0:T(8,128)}, bf16[512,1536]{1,0:T(8,128)(2,1)S(1)}) custom-call(s32[1]{0:T(128)} %bitcast.me_ref, f32[512,512]{1,0:T(8,128)} %constant.33.clone.own_ref, f32[2,512,512]{2,1,0:T(8,128)} %constant.34.clone.far_ref, f32[2,512,128]{2,1,0:T(8,128)} %constant.35.clone.tail_ref, f32[128,512]{1,0:T(8,128)S(1)} %copy-done.1, ...), custom_call_target="tpu_custom_call" | custom-call | flops 4831838208 | bytes 15728640 | tf_op jit(solution)/shard_map/near_dx/pallas_call | solution.py:253
  80.9 2.8 %copy-done = f32[6,512,512]{2,1,0:T(8,128)S(1)} copy-done((f32[6,512,512]{2,1,0:T(8,128)S(1)}, f32[6,512,512]{2,1,0:T(8,128)}, u32[]{:S(2)}) %copy-start) | copy-done | bytes 6291480
  83.7 23.6 %near_section.1 = (f32[1,5,512,512]{3,2,1,0:T(8,128)}, f32[1,3,512,512]{3,2,1,0:T(8,128)}, f32[512,512]{1,0:T(8,128)S(1)}) custom-call(s32[1,1,1,4,256]{4,3,2,1,0:T(4,128)S(1)} %copy-done.4, s32[1,1,1,4]{3,2,1,0:T(1,128)S(1)} %copy-done.7, f32[4,2,8,128]{3,2,1,0:T(8,128)S(1)} %all-to-all-done.1.interp_ref, f32[6,512,512]{2,1,0:T(8,128)S(1)} %copy-done, ...), custom_call_target="tpu_custom_call" | custom-call | flops 26214400 | bytes 29360128 | tf_op jit(solution)/shard_map/near_section/pallas_call | solution.py:567
  107.3 4.5 %add_far.7 = (f32[8,128]{1,0:T(8,128)S(1)}, f32[1,5,512,512]{3,2,1,0:T(8,128)}) custom-call(f32[8,128]{1,0:T(8,128)S(1)} %broadcast_in_dim.11.turn_ref, bf16[512,1536]{1,0:T(8,128)(2,1)S(1)} %get-tuple-element.28.d_ref, f32[512,512]{1,0:T(8,128)} %collective-permute-done.1.far_ref, ...), custom_call_target="tpu_custom_call", output_to_operand_aliasing={{0}: (0, {}), {1}: (5, {})} | custom-call | flops 805306368 | bytes 8388608 | tf_op jit(solution)/shard_map/add_far/pallas_call | solution.py:393
  111.8 2.4 %collective-permute-start.7 = (f32[512,128]{1,0:T(8,128)S(1)}, f32[512,128]{1,0:T(8,128)S(1)}, u32[]{:S(2)}, u32[]{:S(2)}) collective-permute-start(f32[512,128]{1,0:T(8,128)S(1)} %copy-done.12), channel_id=1, source_target_pairs={{0,4},{4,0},{1,5},{5,1},{2,6},{6,2},{3,7},{7,3},{8,12},{12,8},{9,1... | collective-permute-start | bytes 786440 | tf_op jit(solution)/shard_map/ppermute | solution.py:521
  114.1 3.4 %add_far.8 = (f32[8,128]{1,0:T(8,128)S(1)}, f32[1,3,512,512]{3,2,1,0:T(8,128)}) custom-call(f32[8,128]{1,0:T(8,128)S(1)} %get-tuple-element.35.turn_ref, bf16[512,1536]{1,0:T(8,128)(2,1)S(1)} %get-tuple-element.28.d_ref, f32[512,512]{1,0:T(8,128)} %collective-permute-done.2.far_ref, ...), custom_call_target="tpu_custom_call", output_to_operand_aliasing={{0}: (0, {}), {1}: (5, {})} | custom-call | flops 805306368 | bytes 5242880 | tf_op jit(solution)/shard_map/add_far/pallas_call | solution.py:393
  117.6 3.4 %add_far.9 = (f32[8,128]{1,0:T(8,128)S(1)}, f32[1,3,512,512]{3,2,1,0:T(8,128)}) custom-call(f32[8,128]{1,0:T(8,128)S(1)} %get-tuple-element.37.turn_ref, bf16[512,1536]{1,0:T(8,128)(2,1)S(1)} %get-tuple-element.28.d_ref, f32[512,512]{1,0:T(8,128)} %collective-permute-done.3.far_ref, ...), custom_call_target="tpu_custom_call", output_to_operand_aliasing={{0}: (0, {}), {1}: (5, {})} | custom-call | flops 805306368 | bytes 5242880 | tf_op jit(solution)/shard_map/add_far/pallas_call | solution.py:393
  121.0 3.4 %add_far.10 = (f32[8,128]{1,0:T(8,128)S(1)}, f32[1,5,512,512]{3,2,1,0:T(8,128)}) custom-call(f32[8,128]{1,0:T(8,128)S(1)} %get-tuple-element.39.turn_ref, bf16[512,1536]{1,0:T(8,128)(2,1)S(1)} %get-tuple-element.28.d_ref, f32[512,512]{1,0:T(8,128)} %collective-permute-done.4.far_ref, ...), custom_call_target="tpu_custom_call", output_to_operand_aliasing={{0}: (0, {}), {1}: (5, {})} | custom-call | flops 805306368 | bytes 5242880 | tf_op jit(solution)/shard_map/add_far/pallas_call | solution.py:393
  124.3 3.4 %add_far.11 = (f32[8,128]{1,0:T(8,128)S(1)}, f32[1,5,512,512]{3,2,1,0:T(8,128)}) custom-call(f32[8,128]{1,0:T(8,128)S(1)} %get-tuple-element.41.turn_ref, bf16[512,1536]{1,0:T(8,128)(2,1)S(1)} %get-tuple-element.28.d_ref, f32[512,512]{1,0:T(8,128)} %collective-permute-done.5.far_ref, ...), custom_call_target="tpu_custom_call", output_to_operand_aliasing={{0}: (0, {}), {1}: (5, {})} | custom-call | flops 805306368 | bytes 5242880 | tf_op jit(solution)/shard_map/add_far/pallas_call | solution.py:393
  127.7 2.3 %collective-permute-done.6.far_ref = f32[512,256]{1,0:T(8,128)S(1)} collective-permute-done((f32[512,256]{1,0:T(8,128)}, f32[512,256]{1,0:T(8,128)S(1)}, u32[]{:S(2)}, u32[]{:S(2)}) %collective-permute-start.6) | collective-permute-done | bytes 524320 | tf_op jit(solution)/shard_map/ppermute | solution.py:521
  130.0 2.6 %add_far.12 = (f32[8,128]{1,0:T(8,128)S(1)}, f32[1,5,512,512]{3,2,1,0:T(8,128)}) custom-call(f32[8,128]{1,0:T(8,128)S(1)} %get-tuple-element.43.turn_ref, bf16[512,1536]{1,0:T(8,128)(2,1)S(1)} %get-tuple-element.28.d_ref, f32[512,256]{1,0:T(8,128)S(1)} %collective-permute-done.6.far_ref, ...), custom_call_target="tpu_custom_call", output_to_operand_aliasing={{0}: (0, {}), {1}: (5, {})} | custom-call | flops 402653184 | bytes 2621440 | tf_op jit(solution)/shard_map/add_far/pallas_call | solution.py:393
  135.6 2.3 %add_far.13 = (f32[8,128]{1,0:T(8,128)S(1)}, f32[1,5,512,512]{3,2,1,0:T(8,128)}) custom-call(f32[8,128]{1,0:T(8,128)S(1)} %get-tuple-element.49.turn_ref, bf16[512,1536]{1,0:T(8,128)(2,1)S(1)} %get-tuple-element.28.d_ref, f32[512,128]{1,0:T(8,128)S(1)} %collective-permute-done.7.far_ref, ...), custom_call_target="tpu_custom_call", output_to_operand_aliasing={{0}: (0, {}), {1}: (5, {})} | custom-call | flops 201326592 | bytes 1310720 | tf_op jit(solution)/shard_map/add_far/pallas_call | solution.py:393
  138.0 2.5 %collective-permute-done.far_ref = f32[512,128]{1,0:T(8,128)S(1)} collective-permute-done((f32[512,128]{1,0:T(8,128)S(1)}, f32[512,128]{1,0:T(8,128)S(1)}, u32[]{:S(2)}, u32[]{:S(2)}) %collective-permute-start) | collective-permute-done | bytes 262176 | tf_op jit(solution)/shard_map/ppermute | solution.py:521
  (50 shorter events, 13.8 us)
Async XLA Ops:
  0.6 4.3 %copy-start.2 = (s32[1,1,1,4,4,256]{5,4,3,2,1,0:T(4,128)S(1)}, s32[1,1,1,4,4,256]{5,4,3,2,1,0:T(4,128)}, u32[]{:S(2)}) copy-start(s32[1,1,1,4,4,256]{5,4,3,2,1,0:T(4,128)} %cells_ref.2) | copy-start | bytes 49156
  0.6 4.3 %copy-start.3 = (f32[1,1,1,4,4,256]{5,4,3,2,1,0:T(4,128)S(1)}, f32[1,1,1,4,4,256]{5,4,3,2,1,0:T(4,128)}, u32[]{:S(2)}) copy-start(f32[1,1,1,4,4,256]{5,4,3,2,1,0:T(4,128)} %weights_ref.1) | copy-start | bytes 49156
  1.9 64.9 %collective-permute-start.1 = (f32[512,512]{1,0:T(8,128)S(1)}, f32[512,512]{1,0:T(8,128)}, u32[]{:S(2)}, u32[]{:S(2)}) collective-permute-start(f32[512,512]{1,0:T(8,128)S(1)} %take_field.5.after_ref), channel_id=1, source_target_pairs={{0,4},{4,0},{1,5},{5,1},{2,6},{6,2},{3,7},{7,3},{8,12},{12,8},{9,1... | collective-permute-start | bytes 3145736 | tf_op jit(solution)/shard_map/ppermute | solution.py:521
  9.6 0.8 copy-start.8
  10.4 0.7 copy-start.9
  11.8 15.7 %all-to-all-start = ((f32[4,8,256]{2,1,0:T(8,128)}), f32[4,8,256]{2,1,0:T(8,128)S(1)}, u32[]{:S(2)}, u32[]{:S(2)}) async-start(f32[4,8,256]{2,1,0:T(8,128)} %get-tuple-element.30), calls=%async_computation | async-start | bytes 65536 | tf_op jit(solution)/shard_map/all_to_all | solution.py:548
  17.4 94.4 %collective-permute-start.2 = (f32[512,512]{1,0:T(8,128)}, f32[512,512]{1,0:T(8,128)}, u32[]{:S(2)}, u32[]{:S(2)}) collective-permute-start(f32[512,512]{1,0:T(8,128)} %take_field.6.refs_0_), channel_id=1, source_target_pairs={{0,4},{4,0},{1,5},{5,1},{2,6},{6,2},{3,7},{7,3},{8,12},{12,8},{9,1... | collective-permute-start | bytes 3145736 | tf_op jit(solution)/shard_map/ppermute | solution.py:521
  19.6 97.9 %collective-permute-start.3 = (f32[512,512]{1,0:T(8,128)}, f32[512,512]{1,0:T(8,128)}, u32[]{:S(2)}, u32[]{:S(2)}) collective-permute-start(f32[512,512]{1,0:T(8,128)} %take_field.7.refs_0_), channel_id=1, source_target_pairs={{0,4},{4,0},{1,5},{5,1},{2,6},{6,2},{3,7},{7,3},{8,12},{12,8},{9,1... | collective-permute-start | bytes 3145736 | tf_op jit(solution)/shard_map/ppermute | solution.py:521
  22.9 4.4 %copy-start.13 = (f32[128,20]{0,1:T(8,128)S(1)}, f32[128,20]{0,1:T(8,128)}, u32[]{:S(2)}) copy-start(f32[128,20]{0,1:T(8,128)} %param.18) | copy-start | bytes 30724
  22.9 98.0 %collective-permute-start.4 = (f32[512,512]{1,0:T(8,128)S(1)}, f32[512,512]{1,0:T(8,128)}, u32[]{:S(2)}, u32[]{:S(2)}) collective-permute-start(f32[512,512]{1,0:T(8,128)S(1)} %take_field.8.refs_0_), channel_id=1, source_target_pairs={{0,4},{4,0},{1,5},{5,1},{2,6},{6,2},{3,7},{7,3},{8,12},{12,8},{9,1... | collective-permute-start | bytes 3145736 | tf_op jit(solution)/shard_map/ppermute | solution.py:521
  25.3 99.1 %collective-permute-start.5 = (f32[512,512]{1,0:T(8,128)}, f32[512,512]{1,0:T(8,128)}, u32[]{:S(2)}, u32[]{:S(2)}) collective-permute-start(f32[512,512]{1,0:T(8,128)} %take_field.9), channel_id=1, source_target_pairs={{0,4},{4,0},{1,5},{5,1},{2,6},{6,2},{3,7},{7,3},{8,12},{12,8},{9,1... | collective-permute-start | bytes 3145736 | tf_op jit(solution)/shard_map/ppermute | solution.py:521
  54.7 7.2 %all-to-all-start.1 = ((f32[4,2,8,128]{3,2,1,0:T(8,128)}), f32[4,2,8,128]{3,2,1,0:T(8,128)S(1)}, u32[]{:S(2)}, u32[]{:S(2)}) async-start(f32[4,2,8,128]{3,2,1,0:T(8,128)} %donor_gather.1), calls=%async_computation.1 | async-start | bytes 65536 | tf_op jit(solution)/shard_map/all_to_all | solution.py:563
  61.9 18.9 %all-to-all-start.2 = ((f32[4,8,512]{2,1,0:T(8,128)}), f32[4,8,512]{2,1,0:T(8,128)S(1)}, u32[]{:S(2)}, u32[]{:S(2)}) async-start(f32[4,8,512]{2,1,0:T(8,128)} %get-tuple-element.32.refs_0_), calls=%async_computation.2 | async-start | bytes 131072 | tf_op jit(solution)/shard_map/all_to_all | solution.py:564
  66.8 63.2 %collective-permute-start.6 = (f32[512,256]{1,0:T(8,128)}, f32[512,256]{1,0:T(8,128)S(1)}, u32[]{:S(2)}, u32[]{:S(2)}) collective-permute-start(f32[512,256]{1,0:T(8,128)} %copy-done.8), channel_id=1, source_target_pairs={{0,4},{4,0},{1,5},{5,1},{2,6},{6,2},{3,7},{7,3},{8,12},{12,8},{9,1... | collective-permute-start | bytes 1572872 | tf_op jit(solution)/shard_map/ppermute | solution.py:521
  67.3 0.9 copy-start.1
  68.3 12.6 %copy-start.4 = (s32[1,1,1,4,256]{4,3,2,1,0:T(4,128)S(1)}, s32[1,1,1,4,256]{4,3,2,1,0:T(4,128)}, u32[]{:S(2)}) copy-start(s32[1,1,1,4,256]{4,3,2,1,0:T(4,128)} %cells_ref.3) | copy-start | bytes 12292
  68.3 12.6 %copy-start.5 = (s32[1,512]{1,0:T(1,128)S(1)}, s32[1,512]{1,0:T(1,128)}, u32[]{:S(2)}) copy-start(s32[1,512]{1,0:T(1,128)} %el_pair_ref.1) | copy-start | bytes 6148
  68.3 12.6 %copy-start.6 = (s32[1,512]{1,0:T(1,128)S(1)}, s32[1,512]{1,0:T(1,128)}, u32[]{:S(2)}) copy-start(s32[1,512]{1,0:T(1,128)} %ac_pair_ref.1) | copy-start | bytes 6148
  68.3 12.6 %copy-start.7 = (s32[1,1,1,4]{3,2,1,0:T(1,128)S(1)}, s32[1,1,1,4]{3,2,1,0:T(1,128)}, u32[]{:S(2)}) copy-start(s32[1,1,1,4]{3,2,1,0:T(1,128)} %counts_ref.1) | copy-start | bytes 52
  80.9 2.8 %copy-start = (f32[6,512,512]{2,1,0:T(8,128)S(1)}, f32[6,512,512]{2,1,0:T(8,128)}, u32[]{:S(2)}) copy-start(f32[6,512,512]{2,1,0:T(8,128)} %get-tuple-element.31.dx_ref) | copy-start | bytes 18874372
  107.3 4.5 %copy-start.12 = (f32[512,128]{1,0:T(8,128)S(1)}, f32[512,128]{1,0:T(8,128)}, u32[]{:S(2)}) copy-start(f32[512,128]{1,0:T(8,128)} %copy-done.11) | copy-start | bytes 786436
  111.8 5.7 %copy-start.10 = (f32[512,128]{1,0:T(8,128)S(1)}, f32[512,128]{1,0:T(8,128)}, u32[]{:S(2)}) copy-start(f32[512,128]{1,0:T(8,128)} %copy-done.9) | copy-start | bytes 786436
  111.8 23.9 %collective-permute-start.7 = (f32[512,128]{1,0:T(8,128)S(1)}, f32[512,128]{1,0:T(8,128)S(1)}, u32[]{:S(2)}, u32[]{:S(2)}) collective-permute-start(f32[512,128]{1,0:T(8,128)S(1)} %copy-done.12), channel_id=1, source_target_pairs={{0,4},{4,0},{1,5},{5,1},{2,6},{6,2},{3,7},{7,3},{8,12},{12,8},{9,1... | collective-permute-start | bytes 786440 | tf_op jit(solution)/shard_map/ppermute | solution.py:521
  117.5 22.9 %collective-permute-start = (f32[512,128]{1,0:T(8,128)S(1)}, f32[512,128]{1,0:T(8,128)S(1)}, u32[]{:S(2)}, u32[]{:S(2)}) collective-permute-start(f32[512,128]{1,0:T(8,128)S(1)} %copy-done.10), channel_id=1, source_target_pairs={{0,4},{4,0},{1,5},{5,1},{2,6},{6,2},{3,7},{7,3},{8,12},{12,8},{9,1... | collective-permute-start | bytes 786440 | tf_op jit(solution)/shard_map/ppermute | solution.py:521
  (1 other events, 0.7 us)

commit v13 on v11

--- a/solution.py
+++ b/solution.py
@@ -65,15 +65,15 @@
 def take_kernel(pieces, parts, elastic_ref, acoustic_ref, *refs):
     n = len(pieces)
     outs, held, in_semaphores, out_semaphores = refs[:n], refs[n : 2 * n], refs[-2], refs[-1]
-    rows = elastic_ref.shape[2]
     loads, stores = [], []
-    for i, (name, field, at, width) in enumerate(pieces):
+    for i, (name, field, at, width, row, count) in enumerate(pieces):
         source = elastic_ref if name == "el" else acoustic_ref
         for part in range(parts):
-            here = pl.ds(part * (rows // parts), rows // parts)
+            size = count // parts
+            here, there = pl.ds(part * size, size), pl.ds(row + part * size, size)
             k = i * parts + part
             loads.append(
-                pltpu.make_async_copy(source.at[0, field, here, pl.ds(at, width)], held[i].at[here], in_semaphores.at[k])
+                pltpu.make_async_copy(source.at[0, field, there, pl.ds(at, width)], held[i].at[here], in_semaphores.at[k])
             )
             stores.append(pltpu.make_async_copy(held[i].at[here], outs[i].at[here], out_semaphores.at[k]))
     for load in loads:
@@ -156,15 +156,15 @@
     rows = elastic.shape[2]
     anywhere = pl.BlockSpec(memory_space=pl.ANY)
     vmem = pl.BlockSpec(memory_space=pltpu.VMEM)
-    out_shape = [jax.ShapeDtypeStruct((rows, width), jnp.float32) for _, _, _, width in pieces]
+    out_shape = [jax.ShapeDtypeStruct((count, width), jnp.float32) for _, _, _, width, _, count in pieces]
     parts = 2
     scratch = [pltpu.VMEM((2, 8, rows, LANES), jnp.float32), pltpu.SemaphoreType.DMA((4,))]
-    scratch += [pltpu.VMEM((rows, width), jnp.float32) for _, _, _, width in pieces]
+    scratch += [pltpu.VMEM((count, width), jnp.float32) for _, _, _, width, _, count in pieces]
     scratch += [pltpu.SemaphoreType.DMA((len(pieces) * parts,))] * 2
     patches, corners, slots = cells.shape[3:]
     out_shape.append(jax.ShapeDtypeStruct((layers, 8, rows), jnp.float32))
     out_shape.append(jax.ShapeDtypeStruct((patches, 2 * corners, slots), jnp.float32))
-    cost = sum(width for _, _, _, width in pieces) * rows
+    cost = sum(width * count for _, _, _, width, _, count in pieces)
     return pl.pallas_call(
         functools.partial(take_and_edges_kernel, pieces, parts, layers),
         in_specs=[anywhere] * 3 + [vmem] * 2,
@@ -452,14 +452,44 @@
     )(base, in_hbm(media), opened)
 
 
-def finish_kernel(field, at, parts, d_ref, far_ref, old_ref, scale_ref, base_ref, out_ref, held, semaphores):
+def operator_part(d_ref, here, first, count):
+    reach = d_ref.shape[1] // 3
+    if count == reach:
+        return d_ref[here, :]
+    return jnp.concatenate([d_ref[here, pl.ds(k * reach + first, count)] for k in range(3)], axis=1)
+
+
+def fold_kernel(first, turn_ref, d_ref, far_ref, old_ref, scale_ref, out_ref):
+    del turn_ref
+    left = operator_part(d_ref, slice(None), first, far_ref.shape[0])
+    far = jnp.dot(left, three_right(far_ref[...]), preferred_element_type=jnp.float32)
+    out_ref[...] = old_ref[...] + scale_ref[...] * far
+
+
+def fold_part(operator, far, old, scale, first, turn):
+    vmem = pl.BlockSpec(memory_space=pltpu.VMEM)
+    return pl.pallas_call(
+        functools.partial(fold_kernel, first),
+        in_specs=[pl.BlockSpec(memory_space=pl.ANY)] + [vmem] * 4,
+        out_specs=vmem,
+        out_shape=pltpu.VMEM(old.shape, jnp.float32),
+        compiler_params=pltpu.CompilerParams(vmem_limit_bytes=16 * MIB),
+        cost_estimate=pl.CostEstimate(
+            flops=6 * old.size * far.shape[0], bytes_accessed=16 * old.size, transcendentals=0
+        ),
+        name="fold_part",
+    )(turn, operator, far, old, scale)
+
+
+def finish_kernel(field, at, first, parts, d_ref, far_ref, old_ref, scale_ref, base_ref, out_ref, held, semaphores):
     del base_ref
     rows, width = old_ref.shape[0] // parts, old_ref.shape[1]
     far_field = three_right(far_ref[...])
     stores = []
     for part in range(parts):
         here = pl.ds(part * rows, rows)
-        far = jnp.dot(d_ref[here, :], far_field, preferred_element_type=jnp.float32)
+        left = operator_part(d_ref, here, first, far_ref.shape[0])
+        far = jnp.dot(left, far_field, preferred_element_type=jnp.float32)
         held[here, :] = old_ref[here, :] + scale_ref[here, :] * far
         stores.append(
             pltpu.make_async_copy(
@@ -471,13 +501,13 @@
         store.wait()
 
 
-def finish_last(base, operator, far, old, scale, field, at):
+def finish_last(base, operator, far, old, scale, field, at, first):
     rows, width = old.shape
     parts = 2
     anywhere = pl.BlockSpec(memory_space=pl.ANY)
     vmem = pl.BlockSpec(memory_space=pltpu.VMEM)
     return pl.pallas_call(
-        functools.partial(finish_kernel, field, at, parts),
+        functools.partial(finish_kernel, field, at, first, parts),
         in_specs=[vmem] * 4 + [anywhere],
         out_specs=anywhere,
         out_shape=jax.ShapeDtypeStruct(base.shape, base.dtype),
@@ -485,7 +515,7 @@
         input_output_aliases={4: 0},
         compiler_params=pltpu.CompilerParams(vmem_limit_bytes=16 * MIB),
         cost_estimate=pl.CostEstimate(
-            flops=2 * rows * operator.shape[1] * width, bytes_accessed=4 * rows * width, transcendentals=0
+            flops=6 * rows * far.shape[0] * width, bytes_accessed=4 * rows * width, transcendentals=0
         ),
         name="finish_last",
     )(operator, far, old, scale, base)
@@ -532,7 +562,11 @@
         ("el", 4, half, quarter, "el", 0, 1, 1, (lambda b: b,)),
         ("el", 4, half + quarter, quarter, "el", 0, 1, 1, (lambda b: b,)),
     ]
-    travelling = [piece[:4] for piece in pieces]
+    travelling = [piece[:4] + (0, rows) for piece in pieces]
+    late = rows // 4
+    if slabs == 2 and late % LANES == 0:
+        last = travelling.pop()[:4]
+        travelling += [last + (0, rows - late), last + (rows - late, late)]
     first = take_first(elastic, travelling[0][1])
     *others, edges, asked = take_pieces(
         elastic, acoustic, travelling[1:], first, donor_cells, donor_weights, layers
@@ -615,8 +649,13 @@
             section[target], far_operator, far[i], at,
             media[target], first_media, n_media, first_field, coefficients, opened, turn,
         )
+    *folded, closing_far = far[len(middle) :]
+    first_row = 0
+    for part in folded:
+        old = fold_part(far_operator, part, old, scale, first_row, turn)
+        first_row += part.shape[0]
     section[last_target] = finish_last(
-        section[last_target], far_operator, far[-1], old, scale, last_field, last_at
+        section[last_target], far_operator, closing_far, old, scale, last_field, last_at, first_row
     )
     return section["el"], section["ac"]
 

time: 143 us -> 142 us (level)
  starting transfers between devices: 23.4 us -> 25.6 us
  waiting for transfers between devices: 13.2 us -> 11 us
    ppermute x8 -> x9, starting transfers between devices: 12 us -> 14.2 us  [other_slabs(): lax.ppermute(value, 'line', [(i, (i + distance) % slabs) for i in range(s...]
    ppermute x8 -> x9, waiting for transfers between devices: 10.1 us -> 7.86 us  [other_slabs(): lax.ppermute(value, 'line', [(i, (i + distance) % slabs) for i in range(s...]
    unnamed x30 -> x34, local copies, waits for them, and re-layouts: 6.18 us -> 6.8 us
  transfers between devices with their start and end apart: 11 -> 12, of which waited for: 4 -> 5; matrix products, arithmetic and copies ran while one was open for 1% -> 1% of each run, Pallas kernels for 67% -> 67%
where the time goes in v13:
time: 142 us; the launch traced here: 141 us
  Pallas kernels  96.4 us (68%)
  starting transfers between devices  25.6 us (18%)
  waiting for transfers between devices  11 us (8%)
  local copies, waits for them, and re-layouts  6.8 us (5%)
    pallas_call x1, Pallas kernels, per_device(): pl.pallas_call(functools.partial(gather_kernel, 8, rows, depth), in_specs...  27.2 us
    pallas_call x7, Pallas kernels, add_far(): pl.pallas_call(functools.partial(far_kernel, coefficients), grid=(width /...  22.7 us
    pallas_call x1, Pallas kernels, per_device(): pl.pallas_call(functools.partial(section_kernel, layers, rows, depth, til...  21.9 us
    ppermute x9, starting transfers between devices, other_slabs(): lax.ppermute(value, 'line', [(i, (i + distance) % slabs) for i in range(s...  14.2 us
    pallas_call x1, Pallas kernels, near_derivatives(): pl.pallas_call(functools.partial(near_kernel, 4), grid_spec=pltpu.Prefetc...  12.6 us
    ppermute x9, waiting for transfers between devices, other_slabs(): lax.ppermute(value, 'line', [(i, (i + distance) % slabs) for i in range(s...  7.86 us
    pallas_call x1, Pallas kernels, take_pieces(): pl.pallas_call(functools.partial(take_and_edges_kernel, pieces, parts, la...  7.49 us
    unnamed x34, local copies, waits for them, and re-layouts  6.8 us
  transfers between devices with their start and end apart: 12, of which 5 were waited for; matrix products, arithmetic and copies ran while one was open for 1% of the time, Pallas kernels for 67%

profile of v13, /device:TPU:0, one launch (start us, length us, event | category | flops | bytes accessed | tf_op | source)
XLA Modules:
  0.0 141.4 jit_solution(18164859248756645108)
XLA Ops:
  1.9 3.0 %collective-permute-start.1 = (f32[512,512]{1,0:T(8,128)S(1)}, f32[512,512]{1,0:T(8,128)}, u32[]{:S(2)}, u32[]{:S(2)}) collective-permute-start(f32[512,512]{1,0:T(8,128)S(1)} %take_first.1.after_ref), channel_id=1, source_target_pairs={{0,4},{4,0},{1,5},{5,1},{2,6},{6,2},{3,7},{7,3},{8,12},{12,8},{9,1... | collective-permute-start | bytes 3145736 | tf_op jit(solution)/shard_map/ppermute | solution.py:549
  4.9 7.5 %take_pieces.1 = (f32[512,512]{1,0:T(8,128)}, f32[512,512]{1,0:T(8,128)}, f32[512,512]{1,0:T(8,128)}, f32[512,512]{1,0:T(8,128)}, f32[512,256]{1,0:T(8,128)S(1)}...) custom-call(f32[512,512]{1,0:T(8,128)S(1)} %take_first.1.after_ref, ...), custom_call_target="tpu_custom_call" | custom-call | bytes 10485760 | tf_op jit(solution)/shard_map/take_pieces/pallas_call | solution.py:168
  15.3 3.3 %all-to-all-start = ((f32[4,8,256]{2,1,0:T(8,128)}), f32[4,8,256]{2,1,0:T(8,128)S(1)}, u32[]{:S(2)}, u32[]{:S(2)}) async-start(f32[4,8,256]{2,1,0:T(8,128)} %get-tuple-element.36), calls=%async_computation | async-start | bytes 65536 | tf_op jit(solution)/shard_map/all_to_all | solution.py:576
  18.6 2.0 %collective-permute-start.3 = (f32[512,512]{1,0:T(8,128)}, f32[512,512]{1,0:T(8,128)}, u32[]{:S(2)}, u32[]{:S(2)}) collective-permute-start(f32[512,512]{1,0:T(8,128)} %get-tuple-element.45), channel_id=1, source_target_pairs={{0,4},{4,0},{1,5},{5,1},{2,6},{6,2},{3,7},{7,3},{8,12},{12,8},{9,1... | collective-permute-start | bytes 3145736 | tf_op jit(solution)/shard_map/ppermute | solution.py:549
  20.7 1.9 %collective-permute-start.5 = (f32[512,512]{1,0:T(8,128)}, f32[512,512]{1,0:T(8,128)S(1)}, u32[]{:S(2)}, u32[]{:S(2)}) collective-permute-start(f32[512,512]{1,0:T(8,128)} %get-tuple-element.51), channel_id=1, source_target_pairs={{0,4},{4,0},{1,5},{5,1},{2,6},{6,2},{3,7},{7,3},{8,12},{12,8},{9,1... | collective-permute-start | bytes 3145736 | tf_op jit(solution)/shard_map/ppermute | solution.py:549
  22.9 27.2 %donor_gather.1 = f32[4,2,8,128]{3,2,1,0:T(8,128)} custom-call(s32[4,4,256]{2,1,0:T(4,128)S(1)} %slice_convert_fusion.words_ref, f32[4,8,256]{2,1,0:T(8,128)S(1)} %all-to-all-done.weights_ref, f32[1,5,512,512]{3,2,1,0:T(8,128)} %elastic_ref.9, f32[1,3,512,512]{3,2,1,0:T(8,128)} %acoustic_ref.7), custom_call_target="tpu_custom_call" | custom-call | flops 1000000000 | bytes 8388608 | tf_op jit(solution)/shard_map/donor_gather/pallas_call | solution.py:581
  50.1 3.3 %all-to-all-start.1 = ((f32[4,2,8,128]{3,2,1,0:T(8,128)}), f32[4,2,8,128]{3,2,1,0:T(8,128)S(1)}, u32[]{:S(2)}, u32[]{:S(2)}) async-start(f32[4,2,8,128]{3,2,1,0:T(8,128)} %donor_gather.1), calls=%async_computation.1 | async-start | bytes 65536 | tf_op jit(solution)/shard_map/all_to_all | solution.py:591
  54.1 3.1 %all-to-all-done.1.interp_ref = f32[4,2,8,128]{3,2,1,0:T(8,128)S(1)} async-done(((f32[4,2,8,128]{3,2,1,0:T(8,128)}), f32[4,2,8,128]{3,2,1,0:T(8,128)S(1)}, u32[]{:S(2)}, u32[]{:S(2)}) %all-to-all-start.1) | async-done | bytes 32800 | tf_op jit(solution)/shard_map/all_to_all | solution.py:591
  57.2 4.9 %all-to-all-start.2 = ((f32[4,8,512]{2,1,0:T(8,128)}), f32[4,8,512]{2,1,0:T(8,128)S(1)}, u32[]{:S(2)}, u32[]{:S(2)}) async-start(f32[4,8,512]{2,1,0:T(8,128)} %get-tuple-element.38), calls=%async_computation.2 | async-start | bytes 131072 | tf_op jit(solution)/shard_map/all_to_all | solution.py:592
  63.6 12.6 %near_dx.1 = (f32[6,512,512]{2,1,0:T(8,128)}, bf16[512,1536]{1,0:T(8,128)(2,1)S(1)}) custom-call(s32[1]{0:T(128)} %bitcast.me_ref, f32[512,512]{1,0:T(8,128)} %constant.33.clone.own_ref, f32[2,512,512]{2,1,0:T(8,128)} %constant.34.clone.far_ref, f32[2,512,128]{2,1,0:T(8,128)} %constant.35.clone.tail_ref, f32[128,512]{1,0:T(8,128)S(1)} %copy-done.1, ...), custom_call_target="tpu_custom_call" | custom-call | flops 4831838208 | bytes 15728640 | tf_op jit(solution)/shard_map/near_dx/pallas_call | solution.py:251
  76.2 2.8 %copy-done = f32[6,512,512]{2,1,0:T(8,128)S(1)} copy-done((f32[6,512,512]{2,1,0:T(8,128)S(1)}, f32[6,512,512]{2,1,0:T(8,128)}, u32[]{:S(2)}) %copy-start) | copy-done | bytes 6291480
  79.0 21.9 %near_section.1 = (f32[1,5,512,512]{3,2,1,0:T(8,128)}, f32[1,3,512,512]{3,2,1,0:T(8,128)}, f32[512,512]{1,0:T(8,128)S(1)}) custom-call(s32[1,1,1,4,256]{4,3,2,1,0:T(4,128)S(1)} %copy-done.4, s32[1,1,1,4]{3,2,1,0:T(1,128)S(1)} %copy-done.7, f32[4,2,8,128]{3,2,1,0:T(8,128)S(1)} %all-to-all-done.1.interp_ref, f32[6,512,512]{2,1,0:T(8,128)S(1)} %copy-done, ...), custom_call_target="tpu_custom_call" | custom-call | flops 26214400 | bytes 29360128 | tf_op jit(solution)/shard_map/near_section/pallas_call | solution.py:595
  100.9 4.5 %add_far.7 = (f32[8,128]{1,0:T(8,128)S(1)}, f32[1,5,512,512]{3,2,1,0:T(8,128)}) custom-call(f32[8,128]{1,0:T(8,128)S(1)} %broadcast_in_dim.11.turn_ref, bf16[512,1536]{1,0:T(8,128)(2,1)S(1)} %get-tuple-element.34.d_ref, f32[512,512]{1,0:T(8,128)} %collective-permute-done.1.far_ref, ...), custom_call_target="tpu_custom_call", output_to_operand_aliasing={{0}: (0, {}), {1}: (5, {})} | custom-call | flops 805306368 | bytes 8388608 | tf_op jit(solution)/shard_map/add_far/pallas_call | solution.py:391
  105.4 4.4 %collective-permute-start.7 = (f32[512,128]{1,0:T(8,128)S(1)}, f32[512,128]{1,0:T(8,128)S(1)}, u32[]{:S(2)}, u32[]{:S(2)}) collective-permute-start(f32[512,128]{1,0:T(8,128)S(1)} %copy-done.10), channel_id=1, source_target_pairs={{0,4},{4,0},{1,5},{5,1},{2,6},{6,2},{3,7},{7,3},{8,12},{12,8},{9,1... | collective-permute-start | bytes 786440 | tf_op jit(solution)/shard_map/ppermute | solution.py:549
  109.8 3.4 %add_far.8 = (f32[8,128]{1,0:T(8,128)S(1)}, f32[1,3,512,512]{3,2,1,0:T(8,128)}) custom-call(f32[8,128]{1,0:T(8,128)S(1)} %get-tuple-element.41.turn_ref, bf16[512,1536]{1,0:T(8,128)(2,1)S(1)} %get-tuple-element.34.d_ref, f32[512,512]{1,0:T(8,128)} %collective-permute-done.2.far_ref, ...), custom_call_target="tpu_custom_call", output_to_operand_aliasing={{0}: (0, {}), {1}: (5, {})} | custom-call | flops 805306368 | bytes 5242880 | tf_op jit(solution)/shard_map/add_far/pallas_call | solution.py:391
  113.3 3.4 %add_far.9 = (f32[8,128]{1,0:T(8,128)S(1)}, f32[1,3,512,512]{3,2,1,0:T(8,128)}) custom-call(f32[8,128]{1,0:T(8,128)S(1)} %get-tuple-element.44.turn_ref, bf16[512,1536]{1,0:T(8,128)(2,1)S(1)} %get-tuple-element.34.d_ref, f32[512,512]{1,0:T(8,128)} %collective-permute-done.3.far_ref, ...), custom_call_target="tpu_custom_call", output_to_operand_aliasing={{0}: (0, {}), {1}: (5, {})} | custom-call | flops 805306368 | bytes 5242880 | tf_op jit(solution)/shard_map/add_far/pallas_call | solution.py:391
  116.6 2.1 %collective-permute-start = (f32[128,128]{1,0:T(8,128)S(1)}, f32[128,128]{1,0:T(8,128)S(1)}, u32[]{:S(2)}, u32[]{:S(2)}) collective-permute-start(f32[128,128]{1,0:T(8,128)S(1)} %copy-done.14), channel_id=1, source_target_pairs={{0,4},{4,0},{1,5},{5,1},{2,6},{6,2},{3,7},{7,3},{8,12},{12,8},{9,1... | collective-permute-start | bytes 196616 | tf_op jit(solution)/shard_map/ppermute | solution.py:549
  118.7 3.3 %add_far.10 = (f32[8,128]{1,0:T(8,128)S(1)}, f32[1,5,512,512]{3,2,1,0:T(8,128)}) custom-call(f32[8,128]{1,0:T(8,128)S(1)} %get-tuple-element.47.turn_ref, bf16[512,1536]{1,0:T(8,128)(2,1)S(1)} %get-tuple-element.34.d_ref, f32[512,512]{1,0:T(8,128)} %collective-permute-done.4.far_ref, ...), custom_call_target="tpu_custom_call", output_to_operand_aliasing={{0}: (0, {}), {1}: (5, {})} | custom-call | flops 805306368 | bytes 5242880 | tf_op jit(solution)/shard_map/add_far/pallas_call | solution.py:391
  122.0 3.2 %add_far.11 = (f32[8,128]{1,0:T(8,128)S(1)}, f32[1,5,512,512]{3,2,1,0:T(8,128)}) custom-call(f32[8,128]{1,0:T(8,128)S(1)} %get-tuple-element.50.turn_ref, bf16[512,1536]{1,0:T(8,128)(2,1)S(1)} %get-tuple-element.34.d_ref, f32[512,512]{1,0:T(8,128)S(1)} %collective-permute-done.5.far_ref, ...), custom_call_target="tpu_custom_call", output_to_operand_aliasing={{0}: (0, {}), {1}: (5, {})} | custom-call | flops 805306368 | bytes 5242880 | tf_op jit(solution)/shard_map/add_far/pallas_call | solution.py:391
  125.3 4.8 %collective-permute-done.6.far_ref = f32[512,256]{1,0:T(8,128)S(1)} collective-permute-done((f32[512,256]{1,0:T(8,128)}, f32[512,256]{1,0:T(8,128)S(1)}, u32[]{:S(2)}, u32[]{:S(2)}) %collective-permute-start.6) | collective-permute-done | bytes 524320 | tf_op jit(solution)/shard_map/ppermute | solution.py:549
  130.0 2.6 %add_far.12 = (f32[8,128]{1,0:T(8,128)S(1)}, f32[1,5,512,512]{3,2,1,0:T(8,128)}) custom-call(f32[8,128]{1,0:T(8,128)S(1)} %get-tuple-element.53.turn_ref, bf16[512,1536]{1,0:T(8,128)(2,1)S(1)} %get-tuple-element.34.d_ref, f32[512,256]{1,0:T(8,128)S(1)} %collective-permute-done.6.far_ref, ...), custom_call_target="tpu_custom_call", output_to_operand_aliasing={{0}: (0, {}), {1}: (5, {})} | custom-call | flops 402653184 | bytes 2621440 | tf_op jit(solution)/shard_map/add_far/pallas_call | solution.py:391
  132.6 1.9 %prepare_last.1 = (f32[1,5,512,512]{3,2,1,0:T(8,128)}, f32[512,128]{1,0:T(8,128)S(1)}, f32[512,128]{1,0:T(8,128)S(1)}) custom-call(f32[1,5,512,512]{3,2,1,0:T(8,128)} %get-tuple-element.58.base_ref, f32[1,3,512,512]{3,2,1,0:T(8,128)} %media_ref.15, f32[512,512]{1,0:T(8,128)S(1)} %get-tuple-element.39.open_ref), custom_call_target="tpu_custom_call", output_to_operand_aliasing={{0}: (0, {})} | custom-call | flops 65536 | bytes 1310720 | tf_op jit(solution)/shard_map/prepare_last/pallas_call | solution.py:433
  135.7 2.3 %add_far.13 = (f32[8,128]{1,0:T(8,128)S(1)}, f32[1,5,512,512]{3,2,1,0:T(8,128)}) custom-call(f32[8,128]{1,0:T(8,128)S(1)} %get-tuple-element.56.turn_ref, bf16[512,1536]{1,0:T(8,128)(2,1)S(1)} %get-tuple-element.34.d_ref, f32[512,128]{1,0:T(8,128)S(1)} %collective-permute-done.7.far_ref, ...), custom_call_target="tpu_custom_call", output_to_operand_aliasing={{0}: (0, {}), {1}: (5, {})} | custom-call | flops 201326592 | bytes 1310720 | tf_op jit(solution)/shard_map/add_far/pallas_call | solution.py:391
  138.0 1.8 %collective-permute-done.8.far_ref = f32[384,128]{1,0:T(8,128)S(1)} collective-permute-done((f32[384,128]{1,0:T(8,128)S(1)}, f32[384,128]{1,0:T(8,128)S(1)}, u32[]{:S(2)}, u32[]{:S(2)}) %collective-permute-start.8) | collective-permute-done | bytes 196640 | tf_op jit(solution)/shard_map/ppermute | solution.py:549
  (53 shorter events, 9.6 us)
Async XLA Ops:
  0.6 4.3 %copy-start.2 = (s32[1,1,1,4,4,256]{5,4,3,2,1,0:T(4,128)S(1)}, s32[1,1,1,4,4,256]{5,4,3,2,1,0:T(4,128)}, u32[]{:S(2)}) copy-start(s32[1,1,1,4,4,256]{5,4,3,2,1,0:T(4,128)} %cells_ref.2) | copy-start | bytes 49156
  0.6 4.3 %copy-start.3 = (f32[1,1,1,4,4,256]{5,4,3,2,1,0:T(4,128)S(1)}, f32[1,1,1,4,4,256]{5,4,3,2,1,0:T(4,128)}, u32[]{:S(2)}) copy-start(f32[1,1,1,4,4,256]{5,4,3,2,1,0:T(4,128)} %weights_ref.1) | copy-start | bytes 49156
  1.9 20.8 %copy-start.15 = (f32[128,20]{0,1:T(8,128)S(1)}, f32[128,20]{0,1:T(8,128)}, u32[]{:S(2)}) copy-start(f32[128,20]{0,1:T(8,128)} %param.18) | copy-start | bytes 30724
  1.9 60.2 %collective-permute-start.1 = (f32[512,512]{1,0:T(8,128)S(1)}, f32[512,512]{1,0:T(8,128)}, u32[]{:S(2)}, u32[]{:S(2)}) collective-permute-start(f32[512,512]{1,0:T(8,128)S(1)} %take_first.1.after_ref), channel_id=1, source_target_pairs={{0,4},{4,0},{1,5},{5,1},{2,6},{6,2},{3,7},{7,3},{8,12},{12,8},{9,1... | collective-permute-start | bytes 3145736 | tf_op jit(solution)/shard_map/ppermute | solution.py:549
  15.3 7.6 %all-to-all-start = ((f32[4,8,256]{2,1,0:T(8,128)}), f32[4,8,256]{2,1,0:T(8,128)S(1)}, u32[]{:S(2)}, u32[]{:S(2)}) async-start(f32[4,8,256]{2,1,0:T(8,128)} %get-tuple-element.36), calls=%async_computation | async-start | bytes 65536 | tf_op jit(solution)/shard_map/all_to_all | solution.py:576
  18.5 86.9 %collective-permute-start.2 = (f32[512,512]{1,0:T(8,128)}, f32[512,512]{1,0:T(8,128)}, u32[]{:S(2)}, u32[]{:S(2)}) collective-permute-start(f32[512,512]{1,0:T(8,128)} %get-tuple-element.42), channel_id=1, source_target_pairs={{0,4},{4,0},{1,5},{5,1},{2,6},{6,2},{3,7},{7,3},{8,12},{12,8},{9,1... | collective-permute-start | bytes 3145736 | tf_op jit(solution)/shard_map/ppermute | solution.py:549
  18.6 94.5 %collective-permute-start.3 = (f32[512,512]{1,0:T(8,128)}, f32[512,512]{1,0:T(8,128)}, u32[]{:S(2)}, u32[]{:S(2)}) collective-permute-start(f32[512,512]{1,0:T(8,128)} %get-tuple-element.45), channel_id=1, source_target_pairs={{0,4},{4,0},{1,5},{5,1},{2,6},{6,2},{3,7},{7,3},{8,12},{12,8},{9,1... | collective-permute-start | bytes 3145736 | tf_op jit(solution)/shard_map/ppermute | solution.py:549
  20.6 96.0 %collective-permute-start.4 = (f32[512,512]{1,0:T(8,128)}, f32[512,512]{1,0:T(8,128)}, u32[]{:S(2)}, u32[]{:S(2)}) collective-permute-start(f32[512,512]{1,0:T(8,128)} %get-tuple-element.48), channel_id=1, source_target_pairs={{0,4},{4,0},{1,5},{5,1},{2,6},{6,2},{3,7},{7,3},{8,12},{12,8},{9,1... | collective-permute-start | bytes 3145736 | tf_op jit(solution)/shard_map/ppermute | solution.py:549
  20.7 101.3 %collective-permute-start.5 = (f32[512,512]{1,0:T(8,128)}, f32[512,512]{1,0:T(8,128)S(1)}, u32[]{:S(2)}, u32[]{:S(2)}) collective-permute-start(f32[512,512]{1,0:T(8,128)} %get-tuple-element.51), channel_id=1, source_target_pairs={{0,4},{4,0},{1,5},{5,1},{2,6},{6,2},{3,7},{7,3},{8,12},{12,8},{9,1... | collective-permute-start | bytes 3145736 | tf_op jit(solution)/shard_map/ppermute | solution.py:549
  50.1 7.2 %all-to-all-start.1 = ((f32[4,2,8,128]{3,2,1,0:T(8,128)}), f32[4,2,8,128]{3,2,1,0:T(8,128)S(1)}, u32[]{:S(2)}, u32[]{:S(2)}) async-start(f32[4,2,8,128]{3,2,1,0:T(8,128)} %donor_gather.1), calls=%async_computation.1 | async-start | bytes 65536 | tf_op jit(solution)/shard_map/all_to_all | solution.py:591
  57.2 18.9 %all-to-all-start.2 = ((f32[4,8,512]{2,1,0:T(8,128)}), f32[4,8,512]{2,1,0:T(8,128)S(1)}, u32[]{:S(2)}, u32[]{:S(2)}) async-start(f32[4,8,512]{2,1,0:T(8,128)} %get-tuple-element.38), calls=%async_computation.2 | async-start | bytes 131072 | tf_op jit(solution)/shard_map/all_to_all | solution.py:592
  62.1 67.9 %collective-permute-start.6 = (f32[512,256]{1,0:T(8,128)}, f32[512,256]{1,0:T(8,128)S(1)}, u32[]{:S(2)}, u32[]{:S(2)}) collective-permute-start(f32[512,256]{1,0:T(8,128)} %copy-done.8), channel_id=1, source_target_pairs={{0,4},{4,0},{1,5},{5,1},{2,6},{6,2},{3,7},{7,3},{8,12},{12,8},{9,1... | collective-permute-start | bytes 1572872 | tf_op jit(solution)/shard_map/ppermute | solution.py:549
  62.6 0.9 copy-start.1
  63.6 12.6 %copy-start.4 = (s32[1,1,1,4,256]{4,3,2,1,0:T(4,128)S(1)}, s32[1,1,1,4,256]{4,3,2,1,0:T(4,128)}, u32[]{:S(2)}) copy-start(s32[1,1,1,4,256]{4,3,2,1,0:T(4,128)} %cells_ref.3) | copy-start | bytes 12292
  63.6 12.6 %copy-start.5 = (s32[1,512]{1,0:T(1,128)S(1)}, s32[1,512]{1,0:T(1,128)}, u32[]{:S(2)}) copy-start(s32[1,512]{1,0:T(1,128)} %el_pair_ref.1) | copy-start | bytes 6148
  63.6 12.6 %copy-start.6 = (s32[1,512]{1,0:T(1,128)S(1)}, s32[1,512]{1,0:T(1,128)}, u32[]{:S(2)}) copy-start(s32[1,512]{1,0:T(1,128)} %ac_pair_ref.1) | copy-start | bytes 6148
  63.6 12.6 %copy-start.7 = (s32[1,1,1,4]{3,2,1,0:T(1,128)S(1)}, s32[1,1,1,4]{3,2,1,0:T(1,128)}, u32[]{:S(2)}) copy-start(s32[1,1,1,4]{3,2,1,0:T(1,128)} %counts_ref.1) | copy-start | bytes 52
  76.2 2.8 %copy-start = (f32[6,512,512]{2,1,0:T(8,128)S(1)}, f32[6,512,512]{2,1,0:T(8,128)}, u32[]{:S(2)}) copy-start(f32[6,512,512]{2,1,0:T(8,128)} %get-tuple-element.37.dx_ref) | copy-start | bytes 18874372
  100.9 4.5 %copy-start.10 = (f32[512,128]{1,0:T(8,128)S(1)}, f32[512,128]{1,0:T(8,128)}, u32[]{:S(2)}) copy-start(f32[512,128]{1,0:T(8,128)} %copy-done.9) | copy-start | bytes 786436
  105.4 7.8 %copy-start.12 = (f32[384,128]{1,0:T(8,128)S(1)}, f32[384,128]{1,0:T(8,128)}, u32[]{:S(2)}) copy-start(f32[384,128]{1,0:T(8,128)} %copy-done.11) | copy-start | bytes 589828
  105.4 30.3 %collective-permute-start.7 = (f32[512,128]{1,0:T(8,128)S(1)}, f32[512,128]{1,0:T(8,128)S(1)}, u32[]{:S(2)}, u32[]{:S(2)}) collective-permute-start(f32[512,128]{1,0:T(8,128)S(1)} %copy-done.10), channel_id=1, source_target_pairs={{0,4},{4,0},{1,5},{5,1},{2,6},{6,2},{3,7},{7,3},{8,12},{12,8},{9,1... | collective-permute-start | bytes 786440 | tf_op jit(solution)/shard_map/ppermute | solution.py:549
  113.2 3.5 %copy-start.14 = (f32[128,128]{1,0:T(8,128)S(1)}, f32[128,128]{1,0:T(8,128)}, u32[]{:S(2)}) copy-start(f32[128,128]{1,0:T(8,128)} %copy-done.13) | copy-start | bytes 196612
  113.2 26.6 %collective-permute-start.8 = (f32[384,128]{1,0:T(8,128)S(1)}, f32[384,128]{1,0:T(8,128)S(1)}, u32[]{:S(2)}, u32[]{:S(2)}) collective-permute-start(f32[384,128]{1,0:T(8,128)S(1)} %copy-done.12), channel_id=1, source_target_pairs={{0,4},{4,0},{1,5},{5,1},{2,6},{6,2},{3,7},{7,3},{8,12},{12,8},{9,1... | collective-permute-start | bytes 589832 | tf_op jit(solution)/shard_map/ppermute | solution.py:549
  116.6 23.8 %collective-permute-start = (f32[128,128]{1,0:T(8,128)S(1)}, f32[128,128]{1,0:T(8,128)S(1)}, u32[]{:S(2)}, u32[]{:S(2)}) collective-permute-start(f32[128,128]{1,0:T(8,128)S(1)} %copy-done.14), channel_id=1, source_target_pairs={{0,4},{4,0},{1,5},{5,1},{2,6},{6,2},{3,7},{7,3},{8,12},{12,8},{9,1... | collective-permute-start | bytes 196616 | tf_op jit(solution)/shard_map/ppermute | solution.py:549
  (4 other events, 2.8 us)
